TPU v7x, 256 devices: a whole 4x4x8 slice. The times are simulated.
256 devices in a mesh: queue: 32 (over y, x, core), tok: 8 (over z).
Axes of the slice: x: 4, y: 4, z: 8, core: 2. Of those that a mesh axis runs over, the one named last changes fastest.
Arguments:
- queue_tokens: bfloat16 [64, 512, 1152], P('queue', 'tok'), may hold values from -6 to 6
- fresh_frame: bfloat16 [512, 1152], P('tok'), may hold values from -6 to 6
- levels: int32 [64], P('queue'), may hold values from 0 to 63
- mod_table: float32 [64, 6912], replicated, may hold values from -3 to 3
- w_qkv_spatial: bfloat16 [3, 1152, 1152], P(None, None, 'tok'), may hold values from -1 to 1
- w_out_spatial: bfloat16 [1152, 1152], P('tok'), may hold values from -0.1875 to 0.1875
- w_qkv_temporal: bfloat16 [3, 1152, 1152], P(None, None, 'tok'), may hold values from -1 to 1
- w_out_temporal: bfloat16 [1152, 1152], P('tok'), may hold values from -0.1875 to 0.1875
Outputs:
- next_queue: bfloat16 [64, 512, 1152], P('queue', 'tok')
All inputs are finite; a program needn't handle non-finite values.
Results may differ from a plain program's by a relative error of at most 0.013.
Values may be sent and summed in bfloat16 or wider, within the bound.
No kernel may reach another device: no remote copies, remote signals or barrier semaphores. Data moves between devices by JAX's collectives and lax.ppermute only.
A program may use at most 128 MiB of HBM per device.

v0:
```python
import jax
import jax.numpy as jnp
from jax import lax
from jax.experimental import pallas as pl
from jax.experimental.pallas import tpu as pltpu
from jax.sharding import PartitionSpec as P

HEADS = 16
HDIM = 72
EPS = 1e-06
FACTOR = HDIM ** (-0.5)
BF16 = jnp.bfloat16
F32 = jnp.float32
VMEM = pltpu.VMEM


def params(mib):
    return pltpu.CompilerParams(vmem_limit_bytes=mib * 1024 * 1024)


def vspec():
    return pl.BlockSpec(memory_space=VMEM)


def normalize(values):
    mean = jnp.mean(values, axis=-1, keepdims=True)
    centered = values - mean
    variance = jnp.mean(centered * centered, axis=-1, keepdims=True)
    return centered * lax.rsqrt(variance + EPS)


def turned(values, matrix):
    return lax.dot_general(values, matrix, (((1,), (1,)), ((), ())), preferred_element_type=F32)


def first_kernel(levels_ref, table_ref, tokens_ref, chunk_ref, mods_ref, h0_ref, h1_ref):
    rows, width = tokens_ref.shape[1:]
    for j, out in enumerate((h0_ref, h1_ref)):
        row = table_ref[pl.ds(levels_ref[j], 1), :]
        mods_ref[j : j + 1, :] = row
        values = normalize(tokens_ref[j].astype(F32))
        out[:rows] = (values * (1.0 + row[:, width : 2 * width]) + row[:, :width]).astype(BF16)
    h0_ref[rows:] = chunk_ref[...]


def first(levels, table, tokens, chunk):
    _, rows, width = tokens.shape
    return pl.pallas_call(
        first_kernel,
        out_shape=(
            jax.ShapeDtypeStruct((2, table.shape[1]), F32),
            jax.ShapeDtypeStruct((rows + chunk.shape[0], width), BF16),
            jax.ShapeDtypeStruct((rows, width), BF16),
        ),
        in_specs=[pl.BlockSpec(memory_space=pltpu.SMEM), vspec(), vspec(), vspec()],
        out_specs=(vspec(), vspec(), vspec()),
        compiler_params=params(8),
        cost_estimate=pl.CostEstimate(flops=4000000, bytes_accessed=3000000, transcendentals=0),
        name="first",
    )(levels, table, tokens, chunk)


def stack_kernel(size, *refs):
    pieces = [ref[ref.shape[0] - size :].astype(F32) for ref in refs[:-1]]
    refs[-1][...] = jnp.concatenate(pieces, axis=0).astype(BF16)


def stack(size, blocks):
    return pl.pallas_call(
        lambda *refs: stack_kernel(size, *refs),
        out_shape=jax.ShapeDtypeStruct((size * len(blocks), blocks[0].shape[1]), BF16),
        in_specs=[vspec()] * len(blocks),
        out_specs=vspec(),
        compiler_params=params(8),
        cost_estimate=pl.CostEstimate(flops=0, bytes_accessed=700000, transcendentals=0),
        name="stack",
    )(*blocks)


def spatial_kernel(rows, wq_ref, wo_ref, *refs):
    blocks, outs = refs[: len(refs) // 2], refs[len(refs) // 2 :]
    hidden = jnp.concatenate([ref[:rows] for ref in blocks], axis=0)
    query, keyed, valued = [turned(hidden, wq_ref[m]).astype(BF16) for m in range(3)]
    heads = []
    for h in range(query.shape[1] // HDIM):
        cut = slice(h * HDIM, (h + 1) * HDIM)
        scores = FACTOR * turned(query[:, cut], keyed[:, cut])
        weights = jnp.exp(scores - jnp.max(scores, axis=-1, keepdims=True))
        total = jnp.sum(weights, axis=-1, keepdims=True)
        mixed = jnp.dot(weights.astype(BF16), valued[:, cut], preferred_element_type=F32)
        heads.append((mixed / total).astype(BF16))
    attended = jnp.concatenate(heads, axis=1)
    for n, out in enumerate(outs):
        piece = attended[n * rows : (n + 1) * rows]
        out[...] = jnp.dot(piece, wo_ref[...], preferred_element_type=F32).astype(BF16)


def spatial(rows, w_qkv, w_out, blocks):
    width = blocks[0].shape[1]
    whole = rows * len(blocks)
    return pl.pallas_call(
        lambda *refs: spatial_kernel(rows, *refs),
        out_shape=[jax.ShapeDtypeStruct((rows, width), BF16) for _ in blocks],
        in_specs=[vspec()] * (2 + len(blocks)),
        out_specs=[vspec()] * len(blocks),
        compiler_params=params(16),
        cost_estimate=pl.CostEstimate(
            flops=2 * whole * width * 144 * 4 + 4 * whole * whole * 256,
            bytes_accessed=5000000,
            transcendentals=2 * whole * whole,
        ),
        name="spatial",
    )(w_qkv, w_out, *blocks)


def middle_kernel(tokens_ref, mods_ref, *refs):
    parts, (x1_ref, h2_ref, pack_ref) = refs[:-3], refs[-3:]
    rows, width = x1_ref.shape[1:]
    for j in range(2):
        own, one, two = [parts[3 * j + k][...].astype(F32) for k in range(3)]
        branch = own + one + two

        def row(n):
            return mods_ref[j : j + 1, n * width : (n + 1) * width]

        x1 = tokens_ref[j].astype(F32) + row(2) * branch
        x1_ref[j] = x1
        h2_ref[j] = (normalize(x1) * (1.0 + row(4)) + row(3)).astype(BF16)
        if j == 0:
            pack_ref[:rows] = x1
            pack_ref[rows:] = jnp.broadcast_to(row(5), (8, width))


def middle(tokens, mods, parts):
    _, rows, width = tokens.shape
    return pl.pallas_call(
        middle_kernel,
        out_shape=(
            jax.ShapeDtypeStruct(tokens.shape, F32),
            jax.ShapeDtypeStruct(tokens.shape, BF16),
            jax.ShapeDtypeStruct((rows + 8, width), F32),
        ),
        in_specs=[vspec()] * (2 + len(parts)),
        out_specs=(vspec(), vspec(), vspec()),
        compiler_params=params(8),
        cost_estimate=pl.CostEstimate(flops=4000000, bytes_accessed=3000000, transcendentals=0),
        name="middle",
    )(tokens, mods, *parts)


def temporal_kernel(ring, size, per, hidden_ref, weights_ref, out_ref, held, sems):
    pieces, depth, width = weights_ref.shape
    some = pieces // 8

    def copy(n):
        part = pl.ds(n * some, some)
        return pltpu.make_async_copy(weights_ref.at[part], held.at[part], sems.at[n])

    for n in range(8):
        copy(n).start()
    hidden = hidden_ref[...]
    rows = hidden.shape[0]
    half = width // 2

    def matrix(m, s):
        n = 2 * m + s
        copy(n).wait()
        return held[n * some : (n + 1) * some].reshape(half, width)

    lane = lax.broadcasted_iota(jnp.int32, (1, half), 1)
    owned = []
    for z in range(ring):
        mask = jnp.zeros((1, half), jnp.bool_)
        for a in range(some):
            low = a * depth + z * size
            mask = mask | ((lane >= low) & (lane < low + size))
        owned.append(mask)
    along = lax.broadcasted_iota(jnp.int32, (ring * rows, rows), 0) % per
    across = lax.broadcasted_iota(jnp.int32, (ring * rows, rows), 1) % per
    same = along == across

    query = [turned(hidden, matrix(0, s)) for s in range(2)]
    keyed = [turned(hidden, matrix(1, s)).astype(BF16) for s in range(2)]
    valued = [turned(hidden, matrix(2, s)).astype(BF16) for s in range(2)]
    branch = jnp.zeros((rows, width), F32)
    for s in range(2):
        spread = jnp.concatenate([jnp.where(m, query[s], 0.0) for m in owned], axis=0).astype(BF16)
        scores = jnp.where(same, FACTOR * turned(spread, keyed[s]), -jnp.inf)
        weights = jnp.exp(scores - jnp.max(scores, axis=-1, keepdims=True))
        total = jnp.sum(weights, axis=-1, keepdims=True)
        mixed = jnp.dot(weights.astype(BF16), valued[s], preferred_element_type=F32) / total
        attended = jnp.zeros((rows, half), F32)
        for z, m in enumerate(owned):
            attended = jnp.where(m, mixed[z * rows : (z + 1) * rows], attended)
        branch += jnp.dot(attended.astype(BF16), matrix(3, s), preferred_element_type=F32)
    out_ref[...] = jnp.concatenate([branch[per:], branch[:per]], axis=0).astype(BF16)


def temporal(ring, per, hidden, weights):
    pieces, depth, width = weights.shape
    rows = hidden.shape[0]
    return pl.pallas_call(
        lambda *refs: temporal_kernel(ring, depth // ring, per, *refs),
        out_shape=jax.ShapeDtypeStruct((rows, width), BF16),
        in_specs=[vspec(), pl.BlockSpec(memory_space=pl.ANY)],
        out_specs=vspec(),
        scratch_shapes=[
            VMEM((pieces, depth, width), BF16),
            pltpu.SemaphoreType.DMA((8,)),
        ],
        compiler_params=params(50),
        cost_estimate=pl.CostEstimate(
            flops=2 * rows * width * width * 4, bytes_accessed=12000000, transcendentals=16 * rows * rows
        ),
        name="temporal",
    )(hidden, weights)


def last_kernel(tail_ref, x1_ref, mods_ref, pack_ref, branch_ref, fresh_ref, out_ref):
    rows, width = x1_ref.shape[1:]
    gate = mods_ref[1:2, 5 * width :]
    out_ref[0] = (x1_ref[1] + gate * branch_ref[0].astype(F32)).astype(BF16)
    moved = (pack_ref[:rows] + pack_ref[rows : rows + 1] * branch_ref[1].astype(F32)).astype(BF16)

    @pl.when(tail_ref[0] == 0)
    def _():
        out_ref[1] = moved

    @pl.when(tail_ref[0] != 0)
    def _():
        out_ref[1] = fresh_ref[...]


def last(at_tail, x1, mods, pack, branch, fresh):
    return pl.pallas_call(
        last_kernel,
        out_shape=jax.ShapeDtypeStruct(x1.shape, BF16),
        in_specs=[pl.BlockSpec(memory_space=pltpu.SMEM)] + [vspec()] * 5,
        out_specs=vspec(),
        compiler_params=params(8),
        cost_estimate=pl.CostEstimate(flops=1000000, bytes_accessed=2000000, transcendentals=0),
        name="last",
    )(at_tail, x1, mods, pack, branch, fresh)


def per_device(
    queue_tokens,
    fresh_frame,
    levels,
    mod_table,
    w_qkv_spatial,
    w_out_spatial,
    w_qkv_temporal,
    w_out_temporal,
):
    _, rows, width = queue_tokens.shape
    ring = lax.axis_size("tok")
    line = lax.axis_size("queue")
    spot = lax.axis_index("queue")
    up = [(i, (i + 1) % ring) for i in range(ring)]
    down = [(i, (i - 1) % ring) for i in range(ring)]

    def send_up(v):
        return lax.ppermute(v, "tok", up)

    def send_down(v):
        return lax.ppermute(v, "tok", down)

    turned_qkv = jnp.swapaxes(w_qkv_temporal, 1, 2)
    side = w_out_temporal.shape[0]
    size = 4 * side // line
    start = spot * size
    chunk = jnp.where(
        start >= 3 * side,
        lax.dynamic_slice(w_out_temporal, (jnp.maximum(start - 3 * side, 0), 0), (size, width)),
        lax.dynamic_slice(
            turned_qkv.reshape(3 * side, width), (jnp.minimum(start, 3 * side - size), 0), (size, width)
        ),
    )

    mods, *hidden = first(levels, mod_table, queue_tokens, chunk)
    frames = [{0: h} for h in hidden]
    reach = ((4, 3), (3, 4))
    for step in range(1, 5):
        for j in range(2):
            if step <= reach[j][0]:
                frames[j][-step] = send_up(frames[j][1 - step])
            if step <= reach[j][1]:
                frames[j][step] = send_down(frames[j][step - 1])
    order = [[0, 1, 2, 3, -4, -3, -2, -1], [0, 1, 2, 3, 4, -3, -2, -1]]
    *tied, _, _ = lax.optimization_barrier(
        tuple(frames[0][o] for o in order[0]) + (frames[1][4], frames[1][-3])
    )
    pieces = stack(size, tied)
    weights = lax.all_gather(pieces, "queue", axis=0, tiled=False)

    w_spatial = jnp.swapaxes(w_qkv_spatial, 1, 2)
    parts = []

    def add(value, other):
        return (value.astype(F32) + other.astype(F32)).astype(BF16)

    done, rise, fall = [None] * 2, [None] * 2, [None] * 2
    for j in range(2):
        blocks = [frames[j][o] for o in order[j]]
        done[j] = dict(zip(order[j], spatial(rows, w_spatial, w_out_spatial, blocks)))
        far_up, far_down = reach[j]
        rise[j] = send_up(done[j][far_up if far_up < 4 else -4])
        fall[j] = send_down(done[j][-far_down if far_down < 4 else 4])
    rise[0], fall[0], *rest = lax.optimization_barrier((rise[0], fall[0], *[done[1][o] for o in order[1]]))
    done[1] = dict(zip(order[1], rest))
    for j in range(2):
        far_up, far_down = reach[j]
        for o in range(far_up - 1, 0, -1):
            rise[j] = send_up(add(done[j][o], rise[j]))
        for o in range(far_down - 1, 0, -1):
            fall[j] = send_down(add(done[j][-o], fall[j]))
        parts += [done[j][0], rise[j], fall[j]]

    x1, h2, pack = middle(queue_tokens, mods, parts)
    pack = lax.ppermute(pack, "queue", [(i, i - 1) for i in range(1, line)])
    per = rows // line
    sent = jnp.transpose(h2.reshape(2, line, per, width), (1, 0, 2, 3)).reshape(line, 2 * per, width)
    got = lax.all_to_all(sent, "queue", 0, 0, tiled=True)
    branch = temporal(ring, per, got.reshape(line * 2 * per, width), weights)
    got = lax.all_to_all(branch.reshape(line, 2 * per, width), "queue", 0, 0, tiled=True)
    branch = jnp.transpose(got.reshape(line, 2, per, width), (1, 0, 2, 3)).reshape(2, rows, width)
    at_tail = (spot == line - 1).astype(jnp.int32)[None]
    return last(at_tail, x1, mods, pack, branch, fresh_frame)


def solution(mesh):
    return jax.shard_map(
        per_device,
        mesh=mesh,
        in_specs=(
            P("queue", "tok", None),
            P("tok", None),
            P("queue"),
            P(),
            P(None, None, "tok"),
            P("tok", None),
            P(None, None, "tok"),
            P("tok", None),
        ),
        out_specs=P("queue", "tok", None),
        check_vma=False,
    )
```

profile of v0, /device:TPU:1, one launch (start us, length us, event | category | flops | bytes accessed | tf_op | source)
XLA Modules:
  0.0 150.4 jit_solution(17782887412659940162)
XLA Ops:
  6.5 1.0 dynamic-slice_select_fusion.chunk_ref
  7.5 1.5 copy-done
  9.0 1.0 copy-done.1
  9.9 0.7 copy-done.4
  10.6 0.8 first.1
  11.4 2.5 %collective-permute-start.3 = (bf16[82,1152]{1,0:T(8,128)(2,1)S(1)}, bf16[82,1152]{1,0:T(8,128)(2,1)S(1)}, u32[]{:S(2)}, u32[]{:S(2)}) collective-permute-start(bf16[82,1152]{1,0:T(8,128)(2,1)S(1)} %get-tuple-element.73.refs_2_.refs_0_), channel_id=1, source_target_pairs={{0,1},{1,2},{2,3},{3,4},{4,5},{5,6},{6,7},{7,0},{8,9},{9,10},{10,1... | collective-permute-start | bytes 566792 | tf_op jit(solution)/shard_map/ppermute | solution.py:264
  14.0 4.0 %collective-permute-start.9 = (bf16[64,1152]{1,0:T(8,128)(2,1)S(1)}, bf16[64,1152]{1,0:T(8,128)(2,1)S(1)}, u32[]{:S(2)}, u32[]{:S(2)}) collective-permute-start(bf16[64,1152]{1,0:T(8,128)(2,1)S(1)} %get-tuple-element.51.refs_2_), channel_id=1, source_target_pairs={{0,7},{1,0},{2,1},{3,2},{4,3},{5,4},{6,5},{7,6},{8,15},{9,8},{10,9... | collective-permute-start | bytes 442376 | tf_op jit(solution)/shard_map/ppermute | solution.py:267
  18.0 1.4 collective-permute-start
  19.4 3.3 %collective-permute-done.3.refs_9_.refs_7_ = bf16[82,1152]{1,0:T(8,128)(2,1)S(1)} collective-permute-done((bf16[82,1152]{1,0:T(8,128)(2,1)S(1)}, bf16[82,1152]{1,0:T(8,128)(2,1)S(1)}, u32[]{:S(2)}, u32[]{:S(2)}) %collective-permute-start.3) | collective-permute-done | bytes 188960 | tf_op jit(solution)/shard_map/ppermute | solution.py:264
  22.7 2.7 %collective-permute-start.10 = (bf16[64,1152]{1,0:T(8,128)(2,1)S(1)}, bf16[64,1152]{1,0:T(8,128)(2,1)S(1)}, u32[]{:S(2)}, u32[]{:S(2)}) collective-permute-start(bf16[64,1152]{1,0:T(8,128)(2,1)S(1)} %collective-permute-done.9.refs_3_), channel_id=1, source_target_pairs={{0,7},{1,0},{2,1},{3,2},{4,3},{5,4},{6,5},{7,6},{8,15},{9,8},{10,9... | collective-permute-start | bytes 442376 | tf_op jit(solution)/shard_map/ppermute | solution.py:267
  25.4 2.9 %collective-permute-start.1 = (bf16[82,1152]{1,0:T(8,128)(2,1)S(1)}, bf16[82,1152]{1,0:T(8,128)(2,1)S(1)}, u32[]{:S(2)}, u32[]{:S(2)}) collective-permute-start(bf16[82,1152]{1,0:T(8,128)(2,1)S(1)} %collective-permute-done.refs_3_.refs_1_), channel_id=1, source_target_pairs={{0,7},{1,0},{2,1},{3,2},{4,3},{5,4},{6,5},{7,6},{8,15},{9,8},{10,9... | collective-permute-start | bytes 566792 | tf_op jit(solution)/shard_map/ppermute | solution.py:267
  28.3 0.9 collective-permute-done.4.refs_8_.refs_6_
  29.2 3.2 %collective-permute-done.13.refs_9_ = bf16[64,1152]{1,0:T(8,128)(2,1)S(1)} collective-permute-done((bf16[64,1152]{1,0:T(8,128)(2,1)S(1)}, bf16[64,1152]{1,0:T(8,128)(2,1)S(1)}, u32[]{:S(2)}, u32[]{:S(2)}) %collective-permute-start.13) | collective-permute-done | bytes 147488 | tf_op jit(solution)/shard_map/ppermute | solution.py:264
  32.3 2.7 %collective-permute-start.11 = (bf16[64,1152]{1,0:T(8,128)(2,1)S(1)}, bf16[64,1152]{1,0:T(8,128)(2,1)S(1)}, u32[]{:S(2)}, u32[]{:S(2)}) collective-permute-start(bf16[64,1152]{1,0:T(8,128)(2,1)S(1)} %collective-permute-done.10.refs_4_), channel_id=1, source_target_pairs={{0,7},{1,0},{2,1},{3,2},{4,3},{5,4},{6,5},{7,6},{8,15},{9,8},{10,9... | collective-permute-start | bytes 442376 | tf_op jit(solution)/shard_map/ppermute | solution.py:267
  35.0 0.7 collective-permute-start.2
  36.0 0.5 collective-permute-start.6
  36.5 1.8 %collective-permute-done.14.refs_8_ = bf16[64,1152]{1,0:T(8,128)(2,1)S(1)} collective-permute-done((bf16[64,1152]{1,0:T(8,128)(2,1)S(1)}, bf16[64,1152]{1,0:T(8,128)(2,1)S(1)}, u32[]{:S(2)}, u32[]{:S(2)}) %collective-permute-start.14) | collective-permute-done | bytes 147488 | tf_op jit(solution)/shard_map/ppermute | solution.py:264
  38.3 2.7 %collective-permute-start.12 = (bf16[64,1152]{1,0:T(8,128)(2,1)S(1)}, bf16[64,1152]{1,0:T(8,128)(2,1)S(1)}, u32[]{:S(2)}, u32[]{:S(2)}) collective-permute-start(bf16[64,1152]{1,0:T(8,128)(2,1)S(1)} %collective-permute-done.11.refs_5_), channel_id=1, source_target_pairs={{0,7},{1,0},{2,1},{3,2},{4,3},{5,4},{6,5},{7,6},{8,15},{9,8},{10,9... | collective-permute-start | bytes 442376 | tf_op jit(solution)/shard_map/ppermute | solution.py:267
  41.0 4.8 %collective-permute-done.15.refs_7_ = bf16[64,1152]{1,0:T(8,128)(2,1)S(1)} collective-permute-done((bf16[64,1152]{1,0:T(8,128)(2,1)S(1)}, bf16[64,1152]{1,0:T(8,128)(2,1)S(1)}, u32[]{:S(2)}, u32[]{:S(2)}) %collective-permute-start.15) | collective-permute-done | bytes 147488 | tf_op jit(solution)/shard_map/ppermute | solution.py:264
  45.8 0.8 stack.1
  46.6 1.2 copy-done.5
  47.8 1.0 copy-done.7
  48.8 3.1 %spatial.2 = (bf16[64,1152]{1,0:T(8,128)(2,1)S(1)}, bf16[64,1152]{1,0:T(8,128)(2,1)S(1)}, bf16[64,1152]{1,0:T(8,128)(2,1)S(1)}, bf16[64,1152]{1,0:T(8,128)(2,1)S...) custom-call(bf16[3,144,1152]{2,1,0:T(8,128)(2,1)S(1)} %bitcast.10, ...), custom_call_target="tpu_custom_call" | custom-call | flops 947912704 | bytes 5000000 | tf_op jit(solution)/shard_map/spatial/pallas_call | solution.py:101
  52.0 2.7 %collective-permute-start.8 = (bf16[64,1152]{1,0:T(8,128)(2,1)S(1)}, bf16[64,1152]{1,0:T(8,128)(2,1)S(1)}, u32[]{:S(2)}, u32[]{:S(2)}) collective-permute-start(bf16[64,1152]{1,0:T(8,128)(2,1)S(1)} %get-tuple-element.50), channel_id=1, source_target_pairs={{0,7},{1,0},{2,1},{3,2},{4,3},{5,4},{6,5},{7,6},{8,15},{9,8},{10,9... | collective-permute-start | bytes 442376 | tf_op jit(solution)/shard_map/ppermute | solution.py:267
  54.6 1.2 copy-done.6
  55.8 1.0 copy-done.8
  56.8 3.1 %spatial.3 = (bf16[64,1152]{1,0:T(8,128)(2,1)S(1)}, bf16[64,1152]{1,0:T(8,128)(2,1)S(1)}, bf16[64,1152]{1,0:T(8,128)(2,1)S(1)}, bf16[64,1152]{1,0:T(8,128)(2,1)S...) custom-call(bf16[3,144,1152]{2,1,0:T(8,128)(2,1)S(1)} %bitcast.11, ...), custom_call_target="tpu_custom_call" | custom-call | flops 947912704 | bytes 5000000 | tf_op jit(solution)/shard_map/spatial/pallas_call | solution.py:101
  59.9 1.1 collective-permute-start.24
  61.8 2.6 %collective-permute-start.19 = (bf16[64,1152]{1,0:T(8,128)(2,1)S(1)}, bf16[64,1152]{1,0:T(8,128)(2,1)S(1)}, u32[]{:S(2)}, u32[]{:S(2)}) collective-permute-start(bf16[64,1152]{1,0:T(8,128)(2,1)S(1)} %add_convert_fusion.6), channel_id=1, source_target_pairs={{0,7},{1,0},{2,1},{3,2},{4,3},{5,4},{6,5},{7,6},{8,15},{9,8},{10,9... | collective-permute-start | bytes 442376 | tf_op jit(solution)/shard_map/ppermute | solution.py:267
  64.3 1.8 %collective-permute-done.21 = bf16[64,1152]{1,0:T(8,128)(2,1)S(1)} collective-permute-done((bf16[64,1152]{1,0:T(8,128)(2,1)S(1)}, bf16[64,1152]{1,0:T(8,128)(2,1)S(1)}, u32[]{:S(2)}, u32[]{:S(2)}) %collective-permute-start.21) | collective-permute-done | bytes 147488 | tf_op jit(solution)/shard_map/ppermute | solution.py:264
  66.3 2.7 %collective-permute-start.25 = (bf16[64,1152]{1,0:T(8,128)(2,1)S(1)}, bf16[64,1152]{1,0:T(8,128)(2,1)S(1)}, u32[]{:S(2)}, u32[]{:S(2)}) collective-permute-start(bf16[64,1152]{1,0:T(8,128)(2,1)S(1)} %get-tuple-element.81), channel_id=1, source_target_pairs={{0,7},{1,0},{2,1},{3,2},{4,3},{5,4},{6,5},{7,6},{8,15},{9,8},{10,9... | collective-permute-start | bytes 442376 | tf_op jit(solution)/shard_map/ppermute | solution.py:267
  69.2 2.9 %collective-permute-start.20 = (bf16[64,1152]{1,0:T(8,128)(2,1)S(1)}, bf16[64,1152]{1,0:T(8,128)(2,1)S(1)}, u32[]{:S(2)}, u32[]{:S(2)}) collective-permute-start(bf16[64,1152]{1,0:T(8,128)(2,1)S(1)} %add_convert_fusion.5), channel_id=1, source_target_pairs={{0,7},{1,0},{2,1},{3,2},{4,3},{5,4},{6,5},{7,6},{8,15},{9,8},{10,9... | collective-permute-start | bytes 442376 | tf_op jit(solution)/shard_map/ppermute | solution.py:267
  72.7 2.7 %collective-permute-start.26 = (bf16[64,1152]{1,0:T(8,128)(2,1)S(1)}, bf16[64,1152]{1,0:T(8,128)(2,1)S(1)}, u32[]{:S(2)}, u32[]{:S(2)}) collective-permute-start(bf16[64,1152]{1,0:T(8,128)(2,1)S(1)} %add_convert_fusion.1), channel_id=1, source_target_pairs={{0,7},{1,0},{2,1},{3,2},{4,3},{5,4},{6,5},{7,6},{8,15},{9,8},{10,9... | collective-permute-start | bytes 442376 | tf_op jit(solution)/shard_map/ppermute | solution.py:267
  75.5 0.9 collective-permute-done.17
  76.5 1.1 collective-permute-done.26
  77.6 3.2 %collective-permute-start.27 = (bf16[64,1152]{1,0:T(8,128)(2,1)S(1)}, bf16[64,1152]{1,0:T(8,128)(2,1)S(1)}, u32[]{:S(2)}, u32[]{:S(2)}) collective-permute-start(bf16[64,1152]{1,0:T(8,128)(2,1)S(1)} %add_convert_fusion), channel_id=1, source_target_pairs={{0,7},{1,0},{2,1},{3,2},{4,3},{5,4},{6,5},{7,6},{8,15},{9,8},{10,9... | collective-permute-start | bytes 442376 | tf_op jit(solution)/shard_map/ppermute | solution.py:267
  80.8 0.9 collective-permute-done.18.refs_1_
  81.7 2.2 %collective-permute-done.27.refs_5_ = bf16[64,1152]{1,0:T(8,128)(2,1)S(1)} collective-permute-done((bf16[64,1152]{1,0:T(8,128)(2,1)S(1)}, bf16[64,1152]{1,0:T(8,128)(2,1)S(1)}, u32[]{:S(2)}, u32[]{:S(2)}) %collective-permute-start.27) | collective-permute-done | bytes 147488 | tf_op jit(solution)/shard_map/ppermute | solution.py:267
  84.6 0.8 reshape.23
  85.4 17.2 %all-to-all-start = ((bf16[32,4,1152]{2,1,0:T(4,128)(2,1)}), bf16[32,4,1152]{2,1,0:T(4,128)(2,1)S(1)}, u32[]{:S(2)}, u32[]{:S(2)}) async-start(bf16[32,4,1152]{2,1,0:T(4,128)(2,1)} %reshape.23), calls=%async_computation | async-start | bytes 589824 | tf_op jit(solution)/shard_map/all_to_all | solution.py:324
  102.7 2.1 %collective-permute-start.28 = (f32[72,1152]{1,0:T(8,128)S(1)}, f32[72,1152]{1,0:T(8,128)S(1)}, u32[]{:S(2)}, u32[]{:S(2)}) collective-permute-start(f32[72,1152]{1,0:T(8,128)S(1)} %get-tuple-element.71), channel_id=1, source_target_pairs={{8,0},{16,8},{24,16},{32,24},{40,32},{48,40},{56,48},{64,56},{72,6... | collective-permute-start | bytes 995336 | tf_op jit(solution)/shard_map/ppermute | solution.py:321
  104.8 9.8 %all-to-all-done = bf16[32,4,1152]{2,1,0:T(4,128)(2,1)S(1)} async-done(((bf16[32,4,1152]{2,1,0:T(4,128)(2,1)}), bf16[32,4,1152]{2,1,0:T(4,128)(2,1)S(1)}, u32[]{:S(2)}, u32[]{:S(2)}) %all-to-all-start) | async-done | bytes 294944 | tf_op jit(solution)/shard_map/all_to_all | solution.py:324
  114.7 2.6 %all-gather.3.cloned.1.call-done = bf16[4608,1152]{1,0:T(8,128)(2,1)} async-done(((bf16[144,1152]{1,0:T(8,128)(2,1)}), bf16[4608,1152]{1,0:T(8,128)(2,1)}) %all-gather.3.cloned.1.call-update) | async-done | bytes 10616848 | tf_op jit(solution)/shard_map/all_gather | solution.py:295
  117.4 8.1 %temporal.1 = bf16[128,1152]{1,0:T(8,128)(2,1)S(1)} custom-call(bf16[128,1152]{1,0:T(8,128)(2,1)S(1)} %reshape.24.refs_0_, bf16[32,144,1152]{2,1,0:T(8,128)(2,1)} %bitcast.12), custom_call_target="tpu_custom_call" | custom-call | flops 1358954496 | bytes 12000000 | tf_op jit(solution)/shard_map/temporal/pallas_call | solution.py:202
  125.5 0.8 reshape.25
  126.3 6.8 %all-to-all-start.1 = ((bf16[32,4,1152]{2,1,0:T(4,128)(2,1)}), bf16[32,4,1152]{2,1,0:T(4,128)(2,1)S(1)}, u32[]{:S(2)}, u32[]{:S(2)}) async-start(bf16[32,4,1152]{2,1,0:T(4,128)(2,1)} %reshape.25), calls=%async_computation.1 | async-start | bytes 589824 | tf_op jit(solution)/shard_map/all_to_all | solution.py:326
  133.1 9.2 %all-to-all-done.1 = bf16[32,4,1152]{2,1,0:T(4,128)(2,1)S(1)} async-done(((bf16[32,4,1152]{2,1,0:T(4,128)(2,1)}), bf16[32,4,1152]{2,1,0:T(4,128)(2,1)S(1)}, u32[]{:S(2)}, u32[]{:S(2)}) %all-to-all-start.1) | async-done | bytes 294944 | tf_op jit(solution)/shard_map/all_to_all | solution.py:326
  142.7 0.8 last.1
  (60 shorter events, 3.4 us)
Async XLA Ops:
  6.5 110.8 %all-gather.3.cloned.1.call-start = ((), (), s32[]{:S(2)}) async-start(), calls=%async_computation.2 | async-start | bytes 10948608 | tf_op jit(solution)/shard_map/all_gather | solution.py:295
  7.5 1.5 copy-start
  9.0 1.0 copy-start.1
  9.9 0.7 copy-start.4
  10.6 73.3 %copy-start.2 = (bf16[2,64,1152]{2,1,0:T(8,128)(2,1)S(1)}, bf16[2,64,1152]{2,1,0:T(8,128)(2,1)}, u32[]{:S(2)}) copy-start(bf16[2,64,1152]{2,1,0:T(8,128)(2,1)} %tokens_ref.3) | copy-start | bytes 884740
  11.4 11.2 %collective-permute-start.3 = (bf16[82,1152]{1,0:T(8,128)(2,1)S(1)}, bf16[82,1152]{1,0:T(8,128)(2,1)S(1)}, u32[]{:S(2)}, u32[]{:S(2)}) collective-permute-start(bf16[82,1152]{1,0:T(8,128)(2,1)S(1)} %get-tuple-element.73.refs_2_.refs_0_), channel_id=1, source_target_pairs={{0,1},{1,2},{2,3},{3,4},{4,5},{5,6},{6,7},{7,0},{8,9},{9,10},{10,1... | collective-permute-start | bytes 566792 | tf_op jit(solution)/shard_map/ppermute | solution.py:264
  14.0 8.7 %collective-permute-start.9 = (bf16[64,1152]{1,0:T(8,128)(2,1)S(1)}, bf16[64,1152]{1,0:T(8,128)(2,1)S(1)}, u32[]{:S(2)}, u32[]{:S(2)}) collective-permute-start(bf16[64,1152]{1,0:T(8,128)(2,1)S(1)} %get-tuple-element.51.refs_2_), channel_id=1, source_target_pairs={{0,7},{1,0},{2,1},{3,2},{4,3},{5,4},{6,5},{7,6},{8,15},{9,8},{10,9... | collective-permute-start | bytes 442376 | tf_op jit(solution)/shard_map/ppermute | solution.py:267
  18.0 7.4 %collective-permute-start = (bf16[82,1152]{1,0:T(8,128)(2,1)S(1)}, bf16[82,1152]{1,0:T(8,128)(2,1)S(1)}, u32[]{:S(2)}, u32[]{:S(2)}) collective-permute-start(bf16[82,1152]{1,0:T(8,128)(2,1)S(1)} %get-tuple-element.73.refs_2_.refs_0_), channel_id=1, source_target_pairs={{0,7},{1,0},{2,1},{3,2},{4,3},{5,4},{6,5},{7,6},{8,15},{9,8},{10,9... | collective-permute-start | bytes 566792 | tf_op jit(solution)/shard_map/ppermute | solution.py:267
  22.7 6.5 %collective-permute-start.4 = (bf16[82,1152]{1,0:T(8,128)(2,1)S(1)}, bf16[82,1152]{1,0:T(8,128)(2,1)S(1)}, u32[]{:S(2)}, u32[]{:S(2)}) collective-permute-start(bf16[82,1152]{1,0:T(8,128)(2,1)S(1)} %collective-permute-done.3.refs_9_.refs_7_), channel_id=1, source_target_pairs={{0,1},{1,2},{2,3},{3,4},{4,5},{5,6},{6,7},{7,0},{8,9},{9,10},{10,1... | collective-permute-start | bytes 566792 | tf_op jit(solution)/shard_map/ppermute | solution.py:264
  22.7 9.7 %collective-permute-start.13 = (bf16[64,1152]{1,0:T(8,128)(2,1)S(1)}, bf16[64,1152]{1,0:T(8,128)(2,1)S(1)}, u32[]{:S(2)}, u32[]{:S(2)}) collective-permute-start(bf16[64,1152]{1,0:T(8,128)(2,1)S(1)} %get-tuple-element.51.refs_2_), channel_id=1, source_target_pairs={{0,1},{1,2},{2,3},{3,4},{4,5},{5,6},{6,7},{7,0},{8,9},{9,10},{10,1... | collective-permute-start | bytes 442376 | tf_op jit(solution)/shard_map/ppermute | solution.py:264
  22.7 9.7 %collective-permute-start.10 = (bf16[64,1152]{1,0:T(8,128)(2,1)S(1)}, bf16[64,1152]{1,0:T(8,128)(2,1)S(1)}, u32[]{:S(2)}, u32[]{:S(2)}) collective-permute-start(bf16[64,1152]{1,0:T(8,128)(2,1)S(1)} %collective-permute-done.9.refs_3_), channel_id=1, source_target_pairs={{0,7},{1,0},{2,1},{3,2},{4,3},{5,4},{6,5},{7,6},{8,15},{9,8},{10,9... | collective-permute-start | bytes 442376 | tf_op jit(solution)/shard_map/ppermute | solution.py:267
  25.4 9.6 %collective-permute-start.1 = (bf16[82,1152]{1,0:T(8,128)(2,1)S(1)}, bf16[82,1152]{1,0:T(8,128)(2,1)S(1)}, u32[]{:S(2)}, u32[]{:S(2)}) collective-permute-start(bf16[82,1152]{1,0:T(8,128)(2,1)S(1)} %collective-permute-done.refs_3_.refs_1_), channel_id=1, source_target_pairs={{0,7},{1,0},{2,1},{3,2},{4,3},{5,4},{6,5},{7,6},{8,15},{9,8},{10,9... | collective-permute-start | bytes 566792 | tf_op jit(solution)/shard_map/ppermute | solution.py:267
  29.2 6.8 %collective-permute-start.5 = (bf16[82,1152]{1,0:T(8,128)(2,1)S(1)}, bf16[82,1152]{1,0:T(8,128)(2,1)S(1)}, u32[]{:S(2)}, u32[]{:S(2)}) collective-permute-start(bf16[82,1152]{1,0:T(8,128)(2,1)S(1)} %collective-permute-done.4.refs_8_.refs_6_), channel_id=1, source_target_pairs={{0,1},{1,2},{2,3},{3,4},{4,5},{5,6},{6,7},{7,0},{8,9},{9,10},{10,1... | collective-permute-start | bytes 566792 | tf_op jit(solution)/shard_map/ppermute | solution.py:264
  32.3 6.0 %collective-permute-start.14 = (bf16[64,1152]{1,0:T(8,128)(2,1)S(1)}, bf16[64,1152]{1,0:T(8,128)(2,1)S(1)}, u32[]{:S(2)}, u32[]{:S(2)}) collective-permute-start(bf16[64,1152]{1,0:T(8,128)(2,1)S(1)} %collective-permute-done.13.refs_9_), channel_id=1, source_target_pairs={{0,1},{1,2},{2,3},{3,4},{4,5},{5,6},{6,7},{7,0},{8,9},{9,10},{10,1... | collective-permute-start | bytes 442376 | tf_op jit(solution)/shard_map/ppermute | solution.py:264
  32.3 6.0 %collective-permute-start.11 = (bf16[64,1152]{1,0:T(8,128)(2,1)S(1)}, bf16[64,1152]{1,0:T(8,128)(2,1)S(1)}, u32[]{:S(2)}, u32[]{:S(2)}) collective-permute-start(bf16[64,1152]{1,0:T(8,128)(2,1)S(1)} %collective-permute-done.10.refs_4_), channel_id=1, source_target_pairs={{0,7},{1,0},{2,1},{3,2},{4,3},{5,4},{6,5},{7,6},{8,15},{9,8},{10,9... | collective-permute-start | bytes 442376 | tf_op jit(solution)/shard_map/ppermute | solution.py:267
  35.0 10.8 %collective-permute-start.2 = (bf16[82,1152]{1,0:T(8,128)(2,1)S(1)}, bf16[82,1152]{1,0:T(8,128)(2,1)S(1)}, u32[]{:S(2)}, u32[]{:S(2)}) collective-permute-start(bf16[82,1152]{1,0:T(8,128)(2,1)S(1)} %collective-permute-done.1.refs_4_.refs_2_), channel_id=1, source_target_pairs={{0,7},{1,0},{2,1},{3,2},{4,3},{5,4},{6,5},{7,6},{8,15},{9,8},{10,9... | collective-permute-start | bytes 566792 | tf_op jit(solution)/shard_map/ppermute | solution.py:267
  36.0 9.8 %collective-permute-start.6 = (bf16[82,1152]{1,0:T(8,128)(2,1)S(1)}, bf16[82,1152]{1,0:T(8,128)(2,1)S(1)}, u32[]{:S(2)}, u32[]{:S(2)}) collective-permute-start(bf16[82,1152]{1,0:T(8,128)(2,1)S(1)} %collective-permute-done.5.refs_7_.refs_5_), channel_id=1, source_target_pairs={{0,1},{1,2},{2,3},{3,4},{4,5},{5,6},{6,7},{7,0},{8,9},{9,10},{10,1... | collective-permute-start | bytes 566792 | tf_op jit(solution)/shard_map/ppermute | solution.py:264
  38.3 7.4 %collective-permute-start.15 = (bf16[64,1152]{1,0:T(8,128)(2,1)S(1)}, bf16[64,1152]{1,0:T(8,128)(2,1)S(1)}, u32[]{:S(2)}, u32[]{:S(2)}) collective-permute-start(bf16[64,1152]{1,0:T(8,128)(2,1)S(1)} %collective-permute-done.14.refs_8_), channel_id=1, source_target_pairs={{0,1},{1,2},{2,3},{3,4},{4,5},{5,6},{6,7},{7,0},{8,9},{9,10},{10,1... | collective-permute-start | bytes 442376 | tf_op jit(solution)/shard_map/ppermute | solution.py:264
  38.3 7.4 %collective-permute-start.12 = (bf16[64,1152]{1,0:T(8,128)(2,1)S(1)}, bf16[64,1152]{1,0:T(8,128)(2,1)S(1)}, u32[]{:S(2)}, u32[]{:S(2)}) collective-permute-start(bf16[64,1152]{1,0:T(8,128)(2,1)S(1)} %collective-permute-done.11.refs_5_), channel_id=1, source_target_pairs={{0,7},{1,0},{2,1},{3,2},{4,3},{5,4},{6,5},{7,6},{8,15},{9,8},{10,9... | collective-permute-start | bytes 442376 | tf_op jit(solution)/shard_map/ppermute | solution.py:267
  46.6 1.2 copy-start.5
  47.8 1.0 copy-start.7
  51.9 9.6 %collective-permute-start.7 = (bf16[64,1152]{1,0:T(8,128)(2,1)S(1)}, bf16[64,1152]{1,0:T(8,128)(2,1)S(1)}, u32[]{:S(2)}, u32[]{:S(2)}) collective-permute-start(bf16[64,1152]{1,0:T(8,128)(2,1)S(1)} %get-tuple-element.49), channel_id=1, source_target_pairs={{0,1},{1,2},{2,3},{3,4},{4,5},{5,6},{6,7},{7,0},{8,9},{9,10},{10,1... | collective-permute-start | bytes 442376 | tf_op jit(solution)/shard_map/ppermute | solution.py:264
  52.0 9.5 %collective-permute-start.8 = (bf16[64,1152]{1,0:T(8,128)(2,1)S(1)}, bf16[64,1152]{1,0:T(8,128)(2,1)S(1)}, u32[]{:S(2)}, u32[]{:S(2)}) collective-permute-start(bf16[64,1152]{1,0:T(8,128)(2,1)S(1)} %get-tuple-element.50), channel_id=1, source_target_pairs={{0,7},{1,0},{2,1},{3,2},{4,3},{5,4},{6,5},{7,6},{8,15},{9,8},{10,9... | collective-permute-start | bytes 442376 | tf_op jit(solution)/shard_map/ppermute | solution.py:267
  54.6 1.2 copy-start.6
  55.8 1.0 copy-start.8
  59.9 4.5 %collective-permute-start.24 = (bf16[64,1152]{1,0:T(8,128)(2,1)S(1)}, bf16[64,1152]{1,0:T(8,128)(2,1)S(1)}, u32[]{:S(2)}, u32[]{:S(2)}) collective-permute-start(bf16[64,1152]{1,0:T(8,128)(2,1)S(1)} %get-tuple-element.56), channel_id=1, source_target_pairs={{0,7},{1,0},{2,1},{3,2},{4,3},{5,4},{6,5},{7,6},{8,15},{9,8},{10,9... | collective-permute-start | bytes 442376 | tf_op jit(solution)/shard_map/ppermute | solution.py:267
  61.0 5.2 %collective-permute-start.21 = (bf16[64,1152]{1,0:T(8,128)(2,1)S(1)}, bf16[64,1152]{1,0:T(8,128)(2,1)S(1)}, u32[]{:S(2)}, u32[]{:S(2)}) collective-permute-start(bf16[64,1152]{1,0:T(8,128)(2,1)S(1)} %get-tuple-element.55), channel_id=1, source_target_pairs={{0,1},{1,2},{2,3},{3,4},{4,5},{5,6},{6,7},{7,0},{8,9},{9,10},{10,1... | collective-permute-start | bytes 442376 | tf_op jit(solution)/shard_map/ppermute | solution.py:264
  61.5 7.5 %collective-permute-start.16 = (bf16[64,1152]{1,0:T(8,128)(2,1)S(1)}, bf16[64,1152]{1,0:T(8,128)(2,1)S(1)}, u32[]{:S(2)}, u32[]{:S(2)}) collective-permute-start(bf16[64,1152]{1,0:T(8,128)(2,1)S(1)} %add_convert_fusion.9), channel_id=1, source_target_pairs={{0,1},{1,2},{2,3},{3,4},{4,5},{5,6},{6,7},{7,0},{8,9},{9,10},{10,1... | collective-permute-start | bytes 442376 | tf_op jit(solution)/shard_map/ppermute | solution.py:264
  61.8 7.4 %collective-permute-start.19 = (bf16[64,1152]{1,0:T(8,128)(2,1)S(1)}, bf16[64,1152]{1,0:T(8,128)(2,1)S(1)}, u32[]{:S(2)}, u32[]{:S(2)}) collective-permute-start(bf16[64,1152]{1,0:T(8,128)(2,1)S(1)} %add_convert_fusion.6), channel_id=1, source_target_pairs={{0,7},{1,0},{2,1},{3,2},{4,3},{5,4},{6,5},{7,6},{8,15},{9,8},{10,9... | collective-permute-start | bytes 442376 | tf_op jit(solution)/shard_map/ppermute | solution.py:267
  66.2 76.5 %copy-start.3 = (bf16[64,1152]{1,0:T(8,128)(2,1)S(1)}, bf16[64,1152]{1,0:T(8,128)(2,1)}, u32[]{:S(2)}) copy-start(bf16[64,1152]{1,0:T(8,128)(2,1)} %fresh_ref.1) | copy-start | bytes 442372
  66.3 6.3 %collective-permute-start.22 = (bf16[64,1152]{1,0:T(8,128)(2,1)S(1)}, bf16[64,1152]{1,0:T(8,128)(2,1)S(1)}, u32[]{:S(2)}, u32[]{:S(2)}) collective-permute-start(bf16[64,1152]{1,0:T(8,128)(2,1)S(1)} %get-tuple-element.82), channel_id=1, source_target_pairs={{0,1},{1,2},{2,3},{3,4},{4,5},{5,6},{6,7},{7,0},{8,9},{9,10},{10,1... | collective-permute-start | bytes 442376 | tf_op jit(solution)/shard_map/ppermute | solution.py:264
  66.3 6.3 %collective-permute-start.25 = (bf16[64,1152]{1,0:T(8,128)(2,1)S(1)}, bf16[64,1152]{1,0:T(8,128)(2,1)S(1)}, u32[]{:S(2)}, u32[]{:S(2)}) collective-permute-start(bf16[64,1152]{1,0:T(8,128)(2,1)S(1)} %get-tuple-element.81), channel_id=1, source_target_pairs={{0,7},{1,0},{2,1},{3,2},{4,3},{5,4},{6,5},{7,6},{8,15},{9,8},{10,9... | collective-permute-start | bytes 442376 | tf_op jit(solution)/shard_map/ppermute | solution.py:267
  69.1 7.3 %collective-permute-start.17 = (bf16[64,1152]{1,0:T(8,128)(2,1)S(1)}, bf16[64,1152]{1,0:T(8,128)(2,1)S(1)}, u32[]{:S(2)}, u32[]{:S(2)}) collective-permute-start(bf16[64,1152]{1,0:T(8,128)(2,1)S(1)} %add_convert_fusion.8), channel_id=1, source_target_pairs={{0,1},{1,2},{2,3},{3,4},{4,5},{5,6},{6,7},{7,0},{8,9},{9,10},{10,1... | collective-permute-start | bytes 442376 | tf_op jit(solution)/shard_map/ppermute | solution.py:264
  69.2 11.6 %collective-permute-start.20 = (bf16[64,1152]{1,0:T(8,128)(2,1)S(1)}, bf16[64,1152]{1,0:T(8,128)(2,1)S(1)}, u32[]{:S(2)}, u32[]{:S(2)}) collective-permute-start(bf16[64,1152]{1,0:T(8,128)(2,1)S(1)} %add_convert_fusion.5), channel_id=1, source_target_pairs={{0,7},{1,0},{2,1},{3,2},{4,3},{5,4},{6,5},{7,6},{8,15},{9,8},{10,9... | collective-permute-start | bytes 442376 | tf_op jit(solution)/shard_map/ppermute | solution.py:267
  72.6 8.2 %collective-permute-start.23 = (bf16[64,1152]{1,0:T(8,128)(2,1)S(1)}, bf16[64,1152]{1,0:T(8,128)(2,1)S(1)}, u32[]{:S(2)}, u32[]{:S(2)}) collective-permute-start(bf16[64,1152]{1,0:T(8,128)(2,1)S(1)} %add_convert_fusion.3), channel_id=1, source_target_pairs={{0,1},{1,2},{2,3},{3,4},{4,5},{5,6},{6,7},{7,0},{8,9},{9,10},{10,1... | collective-permute-start | bytes 442376 | tf_op jit(solution)/shard_map/ppermute | solution.py:264
  72.7 4.8 %collective-permute-start.26 = (bf16[64,1152]{1,0:T(8,128)(2,1)S(1)}, bf16[64,1152]{1,0:T(8,128)(2,1)S(1)}, u32[]{:S(2)}, u32[]{:S(2)}) collective-permute-start(bf16[64,1152]{1,0:T(8,128)(2,1)S(1)} %add_convert_fusion.1), channel_id=1, source_target_pairs={{0,7},{1,0},{2,1},{3,2},{4,3},{5,4},{6,5},{7,6},{8,15},{9,8},{10,9... | collective-permute-start | bytes 442376 | tf_op jit(solution)/shard_map/ppermute | solution.py:267
  76.4 5.3 %collective-permute-start.18 = (bf16[64,1152]{1,0:T(8,128)(2,1)S(1)}, bf16[64,1152]{1,0:T(8,128)(2,1)S(1)}, u32[]{:S(2)}, u32[]{:S(2)}) collective-permute-start(bf16[64,1152]{1,0:T(8,128)(2,1)S(1)} %add_convert_fusion.7), channel_id=1, source_target_pairs={{0,1},{1,2},{2,3},{3,4},{4,5},{5,6},{6,7},{7,0},{8,9},{9,10},{10,1... | collective-permute-start | bytes 442376 | tf_op jit(solution)/shard_map/ppermute | solution.py:264
  77.6 6.3 %collective-permute-start.27 = (bf16[64,1152]{1,0:T(8,128)(2,1)S(1)}, bf16[64,1152]{1,0:T(8,128)(2,1)S(1)}, u32[]{:S(2)}, u32[]{:S(2)}) collective-permute-start(bf16[64,1152]{1,0:T(8,128)(2,1)S(1)} %add_convert_fusion), channel_id=1, source_target_pairs={{0,7},{1,0},{2,1},{3,2},{4,3},{5,4},{6,5},{7,6},{8,15},{9,8},{10,9... | collective-permute-start | bytes 442376 | tf_op jit(solution)/shard_map/ppermute | solution.py:267
  85.4 29.2 %all-to-all-start = ((bf16[32,4,1152]{2,1,0:T(4,128)(2,1)}), bf16[32,4,1152]{2,1,0:T(4,128)(2,1)S(1)}, u32[]{:S(2)}, u32[]{:S(2)}) async-start(bf16[32,4,1152]{2,1,0:T(4,128)(2,1)} %reshape.23), calls=%async_computation | async-start | bytes 589824 | tf_op jit(solution)/shard_map/all_to_all | solution.py:324
  102.7 40.1 %collective-permute-start.28 = (f32[72,1152]{1,0:T(8,128)S(1)}, f32[72,1152]{1,0:T(8,128)S(1)}, u32[]{:S(2)}, u32[]{:S(2)}) collective-permute-start(f32[72,1152]{1,0:T(8,128)S(1)} %get-tuple-element.71), channel_id=1, source_target_pairs={{8,0},{16,8},{24,16},{32,24},{40,32},{48,40},{56,48},{64,56},{72,6... | collective-permute-start | bytes 995336 | tf_op jit(solution)/shard_map/ppermute | solution.py:321
  126.3 16.0 %all-to-all-start.1 = ((bf16[32,4,1152]{2,1,0:T(4,128)(2,1)}), bf16[32,4,1152]{2,1,0:T(4,128)(2,1)S(1)}, u32[]{:S(2)}, u32[]{:S(2)}) async-start(bf16[32,4,1152]{2,1,0:T(4,128)(2,1)} %reshape.25), calls=%async_computation.1 | async-start | bytes 589824 | tf_op jit(solution)/shard_map/all_to_all | solution.py:326
Sparse Core Ops, SparseCore 0:
  46.7 70.5 all-gather.2
where the time goes:
time: 151 us; the launch traced here: 150 us
  starting transfers between devices  65.3 us (43%)
  waiting for transfers between devices  43.3 us (29%)
  Pallas kernels  17.1 us (11%)
  between operations  13.7 us (9%)
  local copies, waits for them, and re-layouts  9.83 us (7%)
    ppermute x14, starting transfers between devices, send_down(): return lax.ppermute(v, 'tok', down)  34.9 us
    ppermute x14, waiting for transfers between devices, send_up(): return lax.ppermute(v, 'tok', up)  18.2 us
    all_to_all x1, starting transfers between devices, per_device(): got = lax.all_to_all(sent, 'queue', 0, 0, tiled=True)  17.2 us
    all_to_all x1, waiting for transfers between devices, per_device(): got = lax.all_to_all(sent, 'queue', 0, 0, tiled=True)  9.84 us
    all_to_all x1, waiting for transfers between devices, per_device(): lax.all_to_all(branch.reshape(line, 2 * per, width), 'queue', 0, 0, tiled...  9.21 us
    pallas_call x1, Pallas kernels, temporal(): pl.pallas_call(lambda *refs: temporal_kernel(ring, depth // ring, per, *r...  8.14 us
    unnamed x18, local copies, waits for them, and re-layouts  7.45 us
    all_to_all x1, starting transfers between devices, per_device(): lax.all_to_all(branch.reshape(line, 2 * per, width), 'queue', 0, 0, tiled...  6.79 us
  transfers between devices with their start and end apart: 32, of which 15 were waited for; matrix products, arithmetic and copies ran while one was open for 2% of the time, Pallas kernels for 10%

commit v1 on v0

--- a/solution.py
+++ b/solution.py
@@ -33,53 +33,71 @@
     return lax.dot_general(values, matrix, (((1,), (1,)), ((), ())), preferred_element_type=F32)
 
 
-def first_kernel(levels_ref, table_ref, tokens_ref, chunk_ref, mods_ref, h0_ref, h1_ref):
+def first_kernel(levels_ref, table_ref, tokens_ref, mods_ref, h0_ref, h1_ref, near, held, sems):
     rows, width = tokens_ref.shape[1:]
+    copies = [pltpu.make_async_copy(tokens_ref, held, sems.at[2])]
+    for j in range(2):
+        base = pl.multiple_of(levels_ref[j] // 8 * 8, 8)
+        copies.append(pltpu.make_async_copy(table_ref.at[pl.ds(base, 8)], near.at[j], sems.at[j]))
+    for copy in copies:
+        copy.start()
+    for copy in copies:
+        copy.wait()
     for j, out in enumerate((h0_ref, h1_ref)):
-        row = table_ref[pl.ds(levels_ref[j], 1), :]
+        row = near[j, pl.ds(levels_ref[j] % 8, 1), :]
         mods_ref[j : j + 1, :] = row
-        values = normalize(tokens_ref[j].astype(F32))
-        out[:rows] = (values * (1.0 + row[:, width : 2 * width]) + row[:, :width]).astype(BF16)
-    h0_ref[rows:] = chunk_ref[...]
-
-
-def first(levels, table, tokens, chunk):
+        values = normalize(held[j].astype(F32))
+        out[...] = (values * (1.0 + row[:, width : 2 * width]) + row[:, :width]).astype(BF16)
+
+
+def first(levels, table, tokens):
     _, rows, width = tokens.shape
+    block = jax.ShapeDtypeStruct((rows, width), BF16)
     return pl.pallas_call(
         first_kernel,
-        out_shape=(
-            jax.ShapeDtypeStruct((2, table.shape[1]), F32),
-            jax.ShapeDtypeStruct((rows + chunk.shape[0], width), BF16),
-            jax.ShapeDtypeStruct((rows, width), BF16),
-        ),
-        in_specs=[pl.BlockSpec(memory_space=pltpu.SMEM), vspec(), vspec(), vspec()],
+        out_shape=(jax.ShapeDtypeStruct((2, table.shape[1]), F32), block, block),
+        in_specs=[pl.BlockSpec(memory_space=pltpu.SMEM)] + [pl.BlockSpec(memory_space=pl.ANY)] * 2,
         out_specs=(vspec(), vspec(), vspec()),
-        compiler_params=params(8),
+        scratch_shapes=[
+            VMEM((2, 8, table.shape[1]), F32),
+            VMEM(tokens.shape, BF16),
+            pltpu.SemaphoreType.DMA((3,)),
+        ],
+        compiler_params=params(50),
         cost_estimate=pl.CostEstimate(flops=4000000, bytes_accessed=3000000, transcendentals=0),
         name="first",
-    )(levels, table, tokens, chunk)
-
-
-def stack_kernel(size, *refs):
-    pieces = [ref[ref.shape[0] - size :].astype(F32) for ref in refs[:-1]]
-    refs[-1][...] = jnp.concatenate(pieces, axis=0).astype(BF16)
-
-
-def stack(size, blocks):
-    return pl.pallas_call(
-        lambda *refs: stack_kernel(size, *refs),
-        out_shape=jax.ShapeDtypeStruct((size * len(blocks), blocks[0].shape[1]), BF16),
-        in_specs=[vspec()] * len(blocks),
+    )(levels, table, tokens)
+
+
+def stack_kernel(in_ref, out_ref):
+    count, size, width = in_ref.shape
+    pieces = [in_ref[n].astype(F32) for n in range(count)]
+    out_ref[...] = jnp.concatenate(pieces, axis=0).astype(BF16)
+
+
+def stack(blocks):
+    count, size, width = blocks.shape
+    return pl.pallas_call(
+        stack_kernel,
+        out_shape=jax.ShapeDtypeStruct((count * size, width), BF16),
+        in_specs=[vspec()],
         out_specs=vspec(),
         compiler_params=params(8),
         cost_estimate=pl.CostEstimate(flops=0, bytes_accessed=700000, transcendentals=0),
         name="stack",
-    )(*blocks)
-
-
-def spatial_kernel(rows, wq_ref, wo_ref, *refs):
+    )(blocks)
+
+
+def spatial_kernel(wq_hbm, wo_hbm, *refs):
+    *refs, wq_ref, wo_ref, sems = refs
+    first_copy = pltpu.make_async_copy(wq_hbm, wq_ref, sems.at[0])
+    later_copy = pltpu.make_async_copy(wo_hbm, wo_ref, sems.at[1])
+    first_copy.start()
+    later_copy.start()
     blocks, outs = refs[: len(refs) // 2], refs[len(refs) // 2 :]
-    hidden = jnp.concatenate([ref[:rows] for ref in blocks], axis=0)
+    rows = blocks[0].shape[0]
+    hidden = jnp.concatenate([ref[...] for ref in blocks], axis=0)
+    first_copy.wait()
     query, keyed, valued = [turned(hidden, wq_ref[m]).astype(BF16) for m in range(3)]
     heads = []
     for h in range(query.shape[1] // HDIM):
@@ -90,20 +108,26 @@
         mixed = jnp.dot(weights.astype(BF16), valued[:, cut], preferred_element_type=F32)
         heads.append((mixed / total).astype(BF16))
     attended = jnp.concatenate(heads, axis=1)
+    later_copy.wait()
     for n, out in enumerate(outs):
         piece = attended[n * rows : (n + 1) * rows]
         out[...] = jnp.dot(piece, wo_ref[...], preferred_element_type=F32).astype(BF16)
 
 
-def spatial(rows, w_qkv, w_out, blocks):
-    width = blocks[0].shape[1]
+def spatial(w_qkv, w_out, blocks):
+    rows, width = blocks[0].shape
     whole = rows * len(blocks)
     return pl.pallas_call(
-        lambda *refs: spatial_kernel(rows, *refs),
+        spatial_kernel,
         out_shape=[jax.ShapeDtypeStruct((rows, width), BF16) for _ in blocks],
-        in_specs=[vspec()] * (2 + len(blocks)),
+        in_specs=[pl.BlockSpec(memory_space=pl.ANY)] * 2 + [vspec()] * len(blocks),
         out_specs=[vspec()] * len(blocks),
-        compiler_params=params(16),
+        scratch_shapes=[
+            VMEM(w_qkv.shape, BF16),
+            VMEM(w_out.shape, BF16),
+            pltpu.SemaphoreType.DMA((2,)),
+        ],
+        compiler_params=params(40),
         cost_estimate=pl.CostEstimate(
             flops=2 * whole * width * 144 * 4 + 4 * whole * whole * 256,
             bytes_accessed=5000000,
@@ -277,8 +301,12 @@
             turned_qkv.reshape(3 * side, width), (jnp.minimum(start, 3 * side - size), 0), (size, width)
         ),
     )
-
-    mods, *hidden = first(levels, mod_table, queue_tokens, chunk)
+    chunks = lax.all_to_all(
+        jnp.broadcast_to(chunk[None], (ring, size, width)), "tok", 0, 0, tiled=True
+    )
+    weights = lax.all_gather(stack(chunks), "queue", axis=0, tiled=False)
+
+    mods, *hidden = first(levels, mod_table, queue_tokens)
     frames = [{0: h} for h in hidden]
     reach = ((4, 3), (3, 4))
     for step in range(1, 5):
@@ -288,11 +316,6 @@
             if step <= reach[j][1]:
                 frames[j][step] = send_down(frames[j][step - 1])
     order = [[0, 1, 2, 3, -4, -3, -2, -1], [0, 1, 2, 3, 4, -3, -2, -1]]
-    *tied, _, _ = lax.optimization_barrier(
-        tuple(frames[0][o] for o in order[0]) + (frames[1][4], frames[1][-3])
-    )
-    pieces = stack(size, tied)
-    weights = lax.all_gather(pieces, "queue", axis=0, tiled=False)
 
     w_spatial = jnp.swapaxes(w_qkv_spatial, 1, 2)
     parts = []
@@ -303,7 +326,7 @@
     done, rise, fall = [None] * 2, [None] * 2, [None] * 2
     for j in range(2):
         blocks = [frames[j][o] for o in order[j]]
-        done[j] = dict(zip(order[j], spatial(rows, w_spatial, w_out_spatial, blocks)))
+        done[j] = dict(zip(order[j], spatial(w_spatial, w_out_spatial, blocks)))
         far_up, far_down = reach[j]
         rise[j] = send_up(done[j][far_up if far_up < 4 else -4])
         fall[j] = send_down(done[j][-far_down if far_down < 4 else 4])

time: 151 us -> 156 us (1.033)
  blocking collectives: 0 us -> 22.9 us
  starting transfers between devices: 65.3 us -> 56.3 us
  waiting for transfers between devices: 43.3 us -> 34.4 us
  local copies, waits for them, and re-layouts: 9.83 us -> 7.68 us
  Pallas kernels: 17.1 us -> 18.9 us
    all_to_all x0 -> x1, blocking collectives: none -> 22.9 us  [per_device(): lax.all_to_all(jnp.broadcast_to(chunk[None], (ring, size, width)), 'tok',...]
    ppermute x14, starting transfers between devices: 34.9 us -> 29.7 us  [send_down(): return lax.ppermute(v, 'tok', down)]
    ppermute x14, waiting for transfers between devices: 3.3 us -> 0.04 us  [send_down(): return lax.ppermute(v, 'tok', down)]
    all_to_all x1, starting transfers between devices: 6.79 us -> 3.79 us  [per_device(): lax.all_to_all(branch.reshape(line, 2 * per, width), 'queue', 0, 0, tiled...]
    all_to_all x1, waiting for transfers between devices: 9.84 us -> 7.07 us  [per_device(): got = lax.all_to_all(sent, 'queue', 0, 0, tiled=True)]
    all_gather x1, waiting for transfers between devices: 2.64 us -> 0.02 us  [per_device(): weights = lax.all_gather(stack(chunks), 'queue', axis=0, tiled=False)]
    unnamed x18 -> x12, local copies, waits for them, and re-layouts: 7.45 us -> 5.27 us
    ppermute x14, starting transfers between devices: 4.21 us -> 2.51 us  [send_up(): return lax.ppermute(v, 'tok', up)]
  transfers between devices with their start and end apart: 32 -> 32, of which waited for: 15 -> 12; matrix products, arithmetic and copies ran while one was open for 2% -> 2% of each run, Pallas kernels for 10% -> 11%
where the time goes in v1:
time: 156 us; the launch traced here: 155 us
  starting transfers between devices  56.3 us (36%)
  waiting for transfers between devices  34.4 us (22%)
  blocking collectives  22.9 us (15%)
  Pallas kernels  18.9 us (12%)
  between operations  13.7 us (9%)
  local copies, waits for them, and re-layouts  7.68 us (5%)
    ppermute x14, starting transfers between devices, send_down(): return lax.ppermute(v, 'tok', down)  29.7 us
    all_to_all x1, blocking collectives, per_device(): lax.all_to_all(jnp.broadcast_to(chunk[None], (ring, size, width)), 'tok',...  22.9 us
    all_to_all x1, starting transfers between devices, per_device(): got = lax.all_to_all(sent, 'queue', 0, 0, tiled=True)  18.2 us
    ppermute x14, waiting for transfers between devices, send_up(): return lax.ppermute(v, 'tok', up)  17.9 us
    all_to_all x1, waiting for transfers between devices, per_device(): lax.all_to_all(branch.reshape(line, 2 * per, width), 'queue', 0, 0, tiled...  9.32 us
    pallas_call x1, Pallas kernels, temporal(): pl.pallas_call(lambda *refs: temporal_kernel(ring, depth // ring, per, *r...  8.13 us
    pallas_call x2, Pallas kernels, spatial(): pl.pallas_call(spatial_kernel, out_shape=[jax.ShapeDtypeStruct((rows, wid...  7.26 us
    all_to_all x1, waiting for transfers between devices, per_device(): got = lax.all_to_all(sent, 'queue', 0, 0, tiled=True)  7.07 us
  transfers between devices with their start and end apart: 32, of which 12 were waited for; matrix products, arithmetic and copies ran while one was open for 2% of the time, Pallas kernels for 11%

profile of v1, /device:TPU:1, one launch (start us, length us, event | category | flops | bytes accessed | tf_op | source)
XLA Modules:
  0.0 155.2 jit_solution(12332601900204965396)
XLA Ops:
  6.5 1.0 dynamic-slice_select_fusion
  7.5 22.9 %all_to_all.15.in_ref = bf16[8,18,1152]{2,1,0:T(8,128)(2,1)S(1)} all-to-all(bf16[8,18,1152]{2,1,0:T(8,128)(2,1)S(1)} %broadcast_in_dim.13), channel_id=1, replica_groups=mesh['queue'=32,'tok'=8] {'tok'}, dimensions={0} | all-to-all | bytes 663552 | tf_op jit(solution)/shard_map/all_to_all | solution.py:304
  30.5 0.8 stack.1
  31.3 1.5 copy-done
  32.8 1.0 copy-done.1
  33.7 0.7 copy-done.3
  34.4 1.5 first.1
  35.9 0.3 collective-permute-start.3
  36.2 2.4 %collective-permute-start.9 = (bf16[64,1152]{1,0:T(8,128)(2,1)S(1)}, bf16[64,1152]{1,0:T(8,128)(2,1)S(1)}, u32[]{:S(2)}, u32[]{:S(2)}) collective-permute-start(bf16[64,1152]{1,0:T(8,128)(2,1)S(1)} %get-tuple-element.43.refs_0_), channel_id=1, source_target_pairs={{0,7},{1,0},{2,1},{3,2},{4,3},{5,4},{6,5},{7,6},{8,15},{9,8},{10,9... | collective-permute-start | bytes 442376 | tf_op jit(solution)/shard_map/ppermute | solution.py:291
  38.7 2.5 %collective-permute-done.3.refs_7_ = bf16[64,1152]{1,0:T(8,128)(2,1)S(1)} collective-permute-done((bf16[64,1152]{1,0:T(8,128)(2,1)S(1)}, bf16[64,1152]{1,0:T(8,128)(2,1)S(1)}, u32[]{:S(2)}, u32[]{:S(2)}) %collective-permute-start.3) | collective-permute-done | bytes 147488 | tf_op jit(solution)/shard_map/ppermute | solution.py:288
  41.2 2.7 %collective-permute-start.10 = (bf16[64,1152]{1,0:T(8,128)(2,1)S(1)}, bf16[64,1152]{1,0:T(8,128)(2,1)S(1)}, u32[]{:S(2)}, u32[]{:S(2)}) collective-permute-start(bf16[64,1152]{1,0:T(8,128)(2,1)S(1)} %collective-permute-done.9.refs_1_), channel_id=1, source_target_pairs={{0,7},{1,0},{2,1},{3,2},{4,3},{5,4},{6,5},{7,6},{8,15},{9,8},{10,9... | collective-permute-start | bytes 442376 | tf_op jit(solution)/shard_map/ppermute | solution.py:291
  43.9 1.5 collective-permute-start.1
  45.4 0.9 collective-permute-done.4.refs_6_
  46.4 2.0 %collective-permute-done.13.refs_7_ = bf16[64,1152]{1,0:T(8,128)(2,1)S(1)} collective-permute-done((bf16[64,1152]{1,0:T(8,128)(2,1)S(1)}, bf16[64,1152]{1,0:T(8,128)(2,1)S(1)}, u32[]{:S(2)}, u32[]{:S(2)}) %collective-permute-start.13) | collective-permute-done | bytes 147488 | tf_op jit(solution)/shard_map/ppermute | solution.py:288
  48.4 2.7 %collective-permute-start.11 = (bf16[64,1152]{1,0:T(8,128)(2,1)S(1)}, bf16[64,1152]{1,0:T(8,128)(2,1)S(1)}, u32[]{:S(2)}, u32[]{:S(2)}) collective-permute-start(bf16[64,1152]{1,0:T(8,128)(2,1)S(1)} %collective-permute-done.10.refs_2_), channel_id=1, source_target_pairs={{0,7},{1,0},{2,1},{3,2},{4,3},{5,4},{6,5},{7,6},{8,15},{9,8},{10,9... | collective-permute-start | bytes 442376 | tf_op jit(solution)/shard_map/ppermute | solution.py:291
  51.0 0.9 collective-permute-start.2
  51.9 1.6 %collective-permute-done.5.refs_5_ = bf16[64,1152]{1,0:T(8,128)(2,1)S(1)} collective-permute-done((bf16[64,1152]{1,0:T(8,128)(2,1)S(1)}, bf16[64,1152]{1,0:T(8,128)(2,1)S(1)}, u32[]{:S(2)}, u32[]{:S(2)}) %collective-permute-start.5) | collective-permute-done | bytes 147488 | tf_op jit(solution)/shard_map/ppermute | solution.py:288
  53.6 2.1 %collective-permute-done.14.refs_6_ = bf16[64,1152]{1,0:T(8,128)(2,1)S(1)} collective-permute-done((bf16[64,1152]{1,0:T(8,128)(2,1)S(1)}, bf16[64,1152]{1,0:T(8,128)(2,1)S(1)}, u32[]{:S(2)}, u32[]{:S(2)}) %collective-permute-start.14) | collective-permute-done | bytes 147488 | tf_op jit(solution)/shard_map/ppermute | solution.py:288
  55.7 2.7 %collective-permute-start.12 = (bf16[64,1152]{1,0:T(8,128)(2,1)S(1)}, bf16[64,1152]{1,0:T(8,128)(2,1)S(1)}, u32[]{:S(2)}, u32[]{:S(2)}) collective-permute-start(bf16[64,1152]{1,0:T(8,128)(2,1)S(1)} %collective-permute-done.11.refs_3_), channel_id=1, source_target_pairs={{0,7},{1,0},{2,1},{3,2},{4,3},{5,4},{6,5},{7,6},{8,15},{9,8},{10,9... | collective-permute-start | bytes 442376 | tf_op jit(solution)/shard_map/ppermute | solution.py:291
  58.4 0.7 collective-permute-done.6.refs_4_
  59.1 1.2 copy-done.4
  60.3 1.0 copy-done.5
  61.2 3.6 %spatial.2 = (bf16[64,1152]{1,0:T(8,128)(2,1)S(1)}, bf16[64,1152]{1,0:T(8,128)(2,1)S(1)}, bf16[64,1152]{1,0:T(8,128)(2,1)S(1)}, bf16[64,1152]{1,0:T(8,128)(2,1)S...) custom-call(bf16[3,144,1152]{2,1,0:T(8,128)(2,1)S(1)} %bitcast.10, ...), custom_call_target="tpu_custom_call" | custom-call | flops 947912704 | bytes 5000000 | tf_op jit(solution)/shard_map/spatial/pallas_call | solution.py:120
  65.0 2.7 %collective-permute-start.8 = (bf16[64,1152]{1,0:T(8,128)(2,1)S(1)}, bf16[64,1152]{1,0:T(8,128)(2,1)S(1)}, u32[]{:S(2)}, u32[]{:S(2)}) collective-permute-start(bf16[64,1152]{1,0:T(8,128)(2,1)S(1)} %get-tuple-element.42), channel_id=1, source_target_pairs={{0,7},{1,0},{2,1},{3,2},{4,3},{5,4},{6,5},{7,6},{8,15},{9,8},{10,9... | collective-permute-start | bytes 442376 | tf_op jit(solution)/shard_map/ppermute | solution.py:291
  67.6 3.6 %spatial.3 = (bf16[64,1152]{1,0:T(8,128)(2,1)S(1)}, bf16[64,1152]{1,0:T(8,128)(2,1)S(1)}, bf16[64,1152]{1,0:T(8,128)(2,1)S(1)}, bf16[64,1152]{1,0:T(8,128)(2,1)S...) custom-call(bf16[3,144,1152]{2,1,0:T(8,128)(2,1)S(1)} %bitcast.11, ...), custom_call_target="tpu_custom_call" | custom-call | flops 947912704 | bytes 5000000 | tf_op jit(solution)/shard_map/spatial/pallas_call | solution.py:120
  71.4 2.7 %collective-permute-start.24 = (bf16[64,1152]{1,0:T(8,128)(2,1)S(1)}, bf16[64,1152]{1,0:T(8,128)(2,1)S(1)}, u32[]{:S(2)}, u32[]{:S(2)}) collective-permute-start(bf16[64,1152]{1,0:T(8,128)(2,1)S(1)} %get-tuple-element.48), channel_id=1, source_target_pairs={{0,7},{1,0},{2,1},{3,2},{4,3},{5,4},{6,5},{7,6},{8,15},{9,8},{10,9... | collective-permute-start | bytes 442376 | tf_op jit(solution)/shard_map/ppermute | solution.py:291
  74.2 1.5 collective-permute-start.16
  75.8 1.5 collective-permute-done.21
  77.4 2.4 %collective-permute-start.25 = (bf16[64,1152]{1,0:T(8,128)(2,1)S(1)}, bf16[64,1152]{1,0:T(8,128)(2,1)S(1)}, u32[]{:S(2)}, u32[]{:S(2)}) collective-permute-start(bf16[64,1152]{1,0:T(8,128)(2,1)S(1)} %get-tuple-element.65), channel_id=1, source_target_pairs={{0,7},{1,0},{2,1},{3,2},{4,3},{5,4},{6,5},{7,6},{8,15},{9,8},{10,9... | collective-permute-start | bytes 442376 | tf_op jit(solution)/shard_map/ppermute | solution.py:291
  79.9 3.1 %collective-permute-start.20 = (bf16[64,1152]{1,0:T(8,128)(2,1)S(1)}, bf16[64,1152]{1,0:T(8,128)(2,1)S(1)}, u32[]{:S(2)}, u32[]{:S(2)}) collective-permute-start(bf16[64,1152]{1,0:T(8,128)(2,1)S(1)} %add_convert_fusion.5), channel_id=1, source_target_pairs={{0,7},{1,0},{2,1},{3,2},{4,3},{5,4},{6,5},{7,6},{8,15},{9,8},{10,9... | collective-permute-start | bytes 442376 | tf_op jit(solution)/shard_map/ppermute | solution.py:291
  83.0 0.3 collective-permute-start.17
  83.3 2.7 %collective-permute-start.26 = (bf16[64,1152]{1,0:T(8,128)(2,1)S(1)}, bf16[64,1152]{1,0:T(8,128)(2,1)S(1)}, u32[]{:S(2)}, u32[]{:S(2)}) collective-permute-start(bf16[64,1152]{1,0:T(8,128)(2,1)S(1)} %add_convert_fusion.1), channel_id=1, source_target_pairs={{0,7},{1,0},{2,1},{3,2},{4,3},{5,4},{6,5},{7,6},{8,15},{9,8},{10,9... | collective-permute-start | bytes 442376 | tf_op jit(solution)/shard_map/ppermute | solution.py:291
  86.1 0.7 collective-permute-done.22
  86.9 2.8 %collective-permute-done.17 = bf16[64,1152]{1,0:T(8,128)(2,1)S(1)} collective-permute-done((bf16[64,1152]{1,0:T(8,128)(2,1)S(1)}, bf16[64,1152]{1,0:T(8,128)(2,1)S(1)}, u32[]{:S(2)}, u32[]{:S(2)}) %collective-permute-start.17) | collective-permute-done | bytes 147488 | tf_op jit(solution)/shard_map/ppermute | solution.py:288
  89.8 3.2 %collective-permute-start.27 = (bf16[64,1152]{1,0:T(8,128)(2,1)S(1)}, bf16[64,1152]{1,0:T(8,128)(2,1)S(1)}, u32[]{:S(2)}, u32[]{:S(2)}) collective-permute-start(bf16[64,1152]{1,0:T(8,128)(2,1)S(1)} %add_convert_fusion), channel_id=1, source_target_pairs={{0,7},{1,0},{2,1},{3,2},{4,3},{5,4},{6,5},{7,6},{8,15},{9,8},{10,9... | collective-permute-start | bytes 442376 | tf_op jit(solution)/shard_map/ppermute | solution.py:291
  93.0 3.0 %collective-permute-done.18.refs_1_ = bf16[64,1152]{1,0:T(8,128)(2,1)S(1)} collective-permute-done((bf16[64,1152]{1,0:T(8,128)(2,1)S(1)}, bf16[64,1152]{1,0:T(8,128)(2,1)S(1)}, u32[]{:S(2)}, u32[]{:S(2)}) %collective-permute-start.18) | collective-permute-done | bytes 147488 | tf_op jit(solution)/shard_map/ppermute | solution.py:288
  96.0 0.4 middle.1
  96.5 0.2 copy.13
  96.7 0.8 reshape.23
  97.5 18.2 %all-to-all-start = ((bf16[32,4,1152]{2,1,0:T(4,128)(2,1)}), bf16[32,4,1152]{2,1,0:T(4,128)(2,1)S(1)}, u32[]{:S(2)}, u32[]{:S(2)}) async-start(bf16[32,4,1152]{2,1,0:T(4,128)(2,1)} %reshape.23), calls=%async_computation | async-start | bytes 589824 | tf_op jit(solution)/shard_map/all_to_all | solution.py:347
  115.7 2.1 %collective-permute-start.28 = (f32[72,1152]{1,0:T(8,128)S(1)}, f32[72,1152]{1,0:T(8,128)S(1)}, u32[]{:S(2)}, u32[]{:S(2)}) collective-permute-start(f32[72,1152]{1,0:T(8,128)S(1)} %get-tuple-element.63), channel_id=1, source_target_pairs={{8,0},{16,8},{24,16},{32,24},{40,32},{48,40},{56,48},{64,56},{72,6... | collective-permute-start | bytes 995336 | tf_op jit(solution)/shard_map/ppermute | solution.py:344
  117.9 7.1 %all-to-all-done = bf16[32,4,1152]{2,1,0:T(4,128)(2,1)S(1)} async-done(((bf16[32,4,1152]{2,1,0:T(4,128)(2,1)}), bf16[32,4,1152]{2,1,0:T(4,128)(2,1)S(1)}, u32[]{:S(2)}, u32[]{:S(2)}) %all-to-all-start) | async-done | bytes 294944 | tf_op jit(solution)/shard_map/all_to_all | solution.py:347
  125.0 8.1 %temporal.1 = bf16[128,1152]{1,0:T(8,128)(2,1)S(1)} custom-call(bf16[128,1152]{1,0:T(8,128)(2,1)S(1)} %reshape.24.refs_0_, bf16[32,144,1152]{2,1,0:T(8,128)(2,1)} %bitcast.12), custom_call_target="tpu_custom_call" | custom-call | flops 1358954496 | bytes 12000000 | tf_op jit(solution)/shard_map/temporal/pallas_call | solution.py:226
  133.2 0.8 reshape.26
  134.0 3.8 %all-to-all-start.2 = ((bf16[32,4,1152]{2,1,0:T(4,128)(2,1)}), bf16[32,4,1152]{2,1,0:T(4,128)(2,1)S(1)}, u32[]{:S(2)}, u32[]{:S(2)}) async-start(bf16[32,4,1152]{2,1,0:T(4,128)(2,1)} %reshape.26), calls=%async_computation.2 | async-start | bytes 589824 | tf_op jit(solution)/shard_map/all_to_all | solution.py:349
  137.8 9.3 %all-to-all-done.2 = bf16[32,4,1152]{2,1,0:T(4,128)(2,1)S(1)} async-done(((bf16[32,4,1152]{2,1,0:T(4,128)(2,1)}), bf16[32,4,1152]{2,1,0:T(4,128)(2,1)S(1)}, u32[]{:S(2)}, u32[]{:S(2)}) %all-to-all-start.2) | async-done | bytes 294944 | tf_op jit(solution)/shard_map/all_to_all | solution.py:349
  147.1 0.2 copy.15
  147.5 0.8 last.1
  (56 shorter events, 1.3 us)
Async XLA Ops:
  6.5 118.5 %all-gather.3.cloned.1.call-start = ((), (), s32[]{:S(2)}) async-start(), calls=%async_computation.3 | async-start | bytes 10948608 | tf_op jit(solution)/shard_map/all_gather | solution.py:307
  31.3 1.5 copy-start
  32.8 1.0 copy-start.1
  33.7 0.7 copy-start.3
  35.9 5.3 %collective-permute-start.3 = (bf16[64,1152]{1,0:T(8,128)(2,1)S(1)}, bf16[64,1152]{1,0:T(8,128)(2,1)S(1)}, u32[]{:S(2)}, u32[]{:S(2)}) collective-permute-start(bf16[64,1152]{1,0:T(8,128)(2,1)S(1)} %get-tuple-element.36.refs_0_), channel_id=1, source_target_pairs={{0,1},{1,2},{2,3},{3,4},{4,5},{5,6},{6,7},{7,0},{8,9},{9,10},{10,1... | collective-permute-start | bytes 442376 | tf_op jit(solution)/shard_map/ppermute | solution.py:288
  36.2 5.0 %collective-permute-start.9 = (bf16[64,1152]{1,0:T(8,128)(2,1)S(1)}, bf16[64,1152]{1,0:T(8,128)(2,1)S(1)}, u32[]{:S(2)}, u32[]{:S(2)}) collective-permute-start(bf16[64,1152]{1,0:T(8,128)(2,1)S(1)} %get-tuple-element.43.refs_0_), channel_id=1, source_target_pairs={{0,7},{1,0},{2,1},{3,2},{4,3},{5,4},{6,5},{7,6},{8,15},{9,8},{10,9... | collective-permute-start | bytes 442376 | tf_op jit(solution)/shard_map/ppermute | solution.py:291
  38.6 5.2 %collective-permute-start = (bf16[64,1152]{1,0:T(8,128)(2,1)S(1)}, bf16[64,1152]{1,0:T(8,128)(2,1)S(1)}, u32[]{:S(2)}, u32[]{:S(2)}) collective-permute-start(bf16[64,1152]{1,0:T(8,128)(2,1)S(1)} %get-tuple-element.36.refs_0_), channel_id=1, source_target_pairs={{0,7},{1,0},{2,1},{3,2},{4,3},{5,4},{6,5},{7,6},{8,15},{9,8},{10,9... | collective-permute-start | bytes 442376 | tf_op jit(solution)/shard_map/ppermute | solution.py:291
  41.2 5.2 %collective-permute-start.4 = (bf16[64,1152]{1,0:T(8,128)(2,1)S(1)}, bf16[64,1152]{1,0:T(8,128)(2,1)S(1)}, u32[]{:S(2)}, u32[]{:S(2)}) collective-permute-start(bf16[64,1152]{1,0:T(8,128)(2,1)S(1)} %collective-permute-done.3.refs_7_), channel_id=1, source_target_pairs={{0,1},{1,2},{2,3},{3,4},{4,5},{5,6},{6,7},{7,0},{8,9},{9,10},{10,1... | collective-permute-start | bytes 442376 | tf_op jit(solution)/shard_map/ppermute | solution.py:288
  41.2 7.2 %collective-permute-start.13 = (bf16[64,1152]{1,0:T(8,128)(2,1)S(1)}, bf16[64,1152]{1,0:T(8,128)(2,1)S(1)}, u32[]{:S(2)}, u32[]{:S(2)}) collective-permute-start(bf16[64,1152]{1,0:T(8,128)(2,1)S(1)} %get-tuple-element.43.refs_0_), channel_id=1, source_target_pairs={{0,1},{1,2},{2,3},{3,4},{4,5},{5,6},{6,7},{7,0},{8,9},{9,10},{10,1... | collective-permute-start | bytes 442376 | tf_op jit(solution)/shard_map/ppermute | solution.py:288
  41.2 7.2 %collective-permute-start.10 = (bf16[64,1152]{1,0:T(8,128)(2,1)S(1)}, bf16[64,1152]{1,0:T(8,128)(2,1)S(1)}, u32[]{:S(2)}, u32[]{:S(2)}) collective-permute-start(bf16[64,1152]{1,0:T(8,128)(2,1)S(1)} %collective-permute-done.9.refs_1_), channel_id=1, source_target_pairs={{0,7},{1,0},{2,1},{3,2},{4,3},{5,4},{6,5},{7,6},{8,15},{9,8},{10,9... | collective-permute-start | bytes 442376 | tf_op jit(solution)/shard_map/ppermute | solution.py:291
  43.9 7.2 %collective-permute-start.1 = (bf16[64,1152]{1,0:T(8,128)(2,1)S(1)}, bf16[64,1152]{1,0:T(8,128)(2,1)S(1)}, u32[]{:S(2)}, u32[]{:S(2)}) collective-permute-start(bf16[64,1152]{1,0:T(8,128)(2,1)S(1)} %collective-permute-done.refs_1_), channel_id=1, source_target_pairs={{0,7},{1,0},{2,1},{3,2},{4,3},{5,4},{6,5},{7,6},{8,15},{9,8},{10,9... | collective-permute-start | bytes 442376 | tf_op jit(solution)/shard_map/ppermute | solution.py:291
  46.4 7.2 %collective-permute-start.5 = (bf16[64,1152]{1,0:T(8,128)(2,1)S(1)}, bf16[64,1152]{1,0:T(8,128)(2,1)S(1)}, u32[]{:S(2)}, u32[]{:S(2)}) collective-permute-start(bf16[64,1152]{1,0:T(8,128)(2,1)S(1)} %collective-permute-done.4.refs_6_), channel_id=1, source_target_pairs={{0,1},{1,2},{2,3},{3,4},{4,5},{5,6},{6,7},{7,0},{8,9},{9,10},{10,1... | collective-permute-start | bytes 442376 | tf_op jit(solution)/shard_map/ppermute | solution.py:288
  48.4 7.4 %collective-permute-start.14 = (bf16[64,1152]{1,0:T(8,128)(2,1)S(1)}, bf16[64,1152]{1,0:T(8,128)(2,1)S(1)}, u32[]{:S(2)}, u32[]{:S(2)}) collective-permute-start(bf16[64,1152]{1,0:T(8,128)(2,1)S(1)} %collective-permute-done.13.refs_7_), channel_id=1, source_target_pairs={{0,1},{1,2},{2,3},{3,4},{4,5},{5,6},{6,7},{7,0},{8,9},{9,10},{10,1... | collective-permute-start | bytes 442376 | tf_op jit(solution)/shard_map/ppermute | solution.py:288
  48.4 7.4 %collective-permute-start.11 = (bf16[64,1152]{1,0:T(8,128)(2,1)S(1)}, bf16[64,1152]{1,0:T(8,128)(2,1)S(1)}, u32[]{:S(2)}, u32[]{:S(2)}) collective-permute-start(bf16[64,1152]{1,0:T(8,128)(2,1)S(1)} %collective-permute-done.10.refs_2_), channel_id=1, source_target_pairs={{0,7},{1,0},{2,1},{3,2},{4,3},{5,4},{6,5},{7,6},{8,15},{9,8},{10,9... | collective-permute-start | bytes 442376 | tf_op jit(solution)/shard_map/ppermute | solution.py:291
  51.0 7.4 %collective-permute-start.2 = (bf16[64,1152]{1,0:T(8,128)(2,1)S(1)}, bf16[64,1152]{1,0:T(8,128)(2,1)S(1)}, u32[]{:S(2)}, u32[]{:S(2)}) collective-permute-start(bf16[64,1152]{1,0:T(8,128)(2,1)S(1)} %collective-permute-done.1.refs_2_), channel_id=1, source_target_pairs={{0,7},{1,0},{2,1},{3,2},{4,3},{5,4},{6,5},{7,6},{8,15},{9,8},{10,9... | collective-permute-start | bytes 442376 | tf_op jit(solution)/shard_map/ppermute | solution.py:291
  53.6 5.5 %collective-permute-start.6 = (bf16[64,1152]{1,0:T(8,128)(2,1)S(1)}, bf16[64,1152]{1,0:T(8,128)(2,1)S(1)}, u32[]{:S(2)}, u32[]{:S(2)}) collective-permute-start(bf16[64,1152]{1,0:T(8,128)(2,1)S(1)} %collective-permute-done.5.refs_5_), channel_id=1, source_target_pairs={{0,1},{1,2},{2,3},{3,4},{4,5},{5,6},{6,7},{7,0},{8,9},{9,10},{10,1... | collective-permute-start | bytes 442376 | tf_op jit(solution)/shard_map/ppermute | solution.py:288
  55.7 11.9 %collective-permute-start.15 = (bf16[64,1152]{1,0:T(8,128)(2,1)S(1)}, bf16[64,1152]{1,0:T(8,128)(2,1)S(1)}, u32[]{:S(2)}, u32[]{:S(2)}) collective-permute-start(bf16[64,1152]{1,0:T(8,128)(2,1)S(1)} %collective-permute-done.14.refs_6_), channel_id=1, source_target_pairs={{0,1},{1,2},{2,3},{3,4},{4,5},{5,6},{6,7},{7,0},{8,9},{9,10},{10,1... | collective-permute-start | bytes 442376 | tf_op jit(solution)/shard_map/ppermute | solution.py:288
  55.7 11.9 %collective-permute-start.12 = (bf16[64,1152]{1,0:T(8,128)(2,1)S(1)}, bf16[64,1152]{1,0:T(8,128)(2,1)S(1)}, u32[]{:S(2)}, u32[]{:S(2)}) collective-permute-start(bf16[64,1152]{1,0:T(8,128)(2,1)S(1)} %collective-permute-done.11.refs_3_), channel_id=1, source_target_pairs={{0,7},{1,0},{2,1},{3,2},{4,3},{5,4},{6,5},{7,6},{8,15},{9,8},{10,9... | collective-permute-start | bytes 442376 | tf_op jit(solution)/shard_map/ppermute | solution.py:291
  59.1 1.2 copy-start.4
  60.3 1.0 copy-start.5
  64.9 9.2 %collective-permute-start.7 = (bf16[64,1152]{1,0:T(8,128)(2,1)S(1)}, bf16[64,1152]{1,0:T(8,128)(2,1)S(1)}, u32[]{:S(2)}, u32[]{:S(2)}) collective-permute-start(bf16[64,1152]{1,0:T(8,128)(2,1)S(1)} %get-tuple-element.41), channel_id=1, source_target_pairs={{0,1},{1,2},{2,3},{3,4},{4,5},{5,6},{6,7},{7,0},{8,9},{9,10},{10,1... | collective-permute-start | bytes 442376 | tf_op jit(solution)/shard_map/ppermute | solution.py:288
  65.0 9.1 %collective-permute-start.8 = (bf16[64,1152]{1,0:T(8,128)(2,1)S(1)}, bf16[64,1152]{1,0:T(8,128)(2,1)S(1)}, u32[]{:S(2)}, u32[]{:S(2)}) collective-permute-start(bf16[64,1152]{1,0:T(8,128)(2,1)S(1)} %get-tuple-element.42), channel_id=1, source_target_pairs={{0,7},{1,0},{2,1},{3,2},{4,3},{5,4},{6,5},{7,6},{8,15},{9,8},{10,9... | collective-permute-start | bytes 442376 | tf_op jit(solution)/shard_map/ppermute | solution.py:291
  71.3 6.0 %collective-permute-start.21 = (bf16[64,1152]{1,0:T(8,128)(2,1)S(1)}, bf16[64,1152]{1,0:T(8,128)(2,1)S(1)}, u32[]{:S(2)}, u32[]{:S(2)}) collective-permute-start(bf16[64,1152]{1,0:T(8,128)(2,1)S(1)} %get-tuple-element.47), channel_id=1, source_target_pairs={{0,1},{1,2},{2,3},{3,4},{4,5},{5,6},{6,7},{7,0},{8,9},{9,10},{10,1... | collective-permute-start | bytes 442376 | tf_op jit(solution)/shard_map/ppermute | solution.py:288
  71.4 5.9 %collective-permute-start.24 = (bf16[64,1152]{1,0:T(8,128)(2,1)S(1)}, bf16[64,1152]{1,0:T(8,128)(2,1)S(1)}, u32[]{:S(2)}, u32[]{:S(2)}) collective-permute-start(bf16[64,1152]{1,0:T(8,128)(2,1)S(1)} %get-tuple-element.48), channel_id=1, source_target_pairs={{0,7},{1,0},{2,1},{3,2},{4,3},{5,4},{6,5},{7,6},{8,15},{9,8},{10,9... | collective-permute-start | bytes 442376 | tf_op jit(solution)/shard_map/ppermute | solution.py:291
  74.1 5.7 %collective-permute-start.19 = (bf16[64,1152]{1,0:T(8,128)(2,1)S(1)}, bf16[64,1152]{1,0:T(8,128)(2,1)S(1)}, u32[]{:S(2)}, u32[]{:S(2)}) collective-permute-start(bf16[64,1152]{1,0:T(8,128)(2,1)S(1)} %add_convert_fusion.6), channel_id=1, source_target_pairs={{0,7},{1,0},{2,1},{3,2},{4,3},{5,4},{6,5},{7,6},{8,15},{9,8},{10,9... | collective-permute-start | bytes 442376 | tf_op jit(solution)/shard_map/ppermute | solution.py:291
  74.2 8.7 %collective-permute-start.16 = (bf16[64,1152]{1,0:T(8,128)(2,1)S(1)}, bf16[64,1152]{1,0:T(8,128)(2,1)S(1)}, u32[]{:S(2)}, u32[]{:S(2)}) collective-permute-start(bf16[64,1152]{1,0:T(8,128)(2,1)S(1)} %add_convert_fusion.9), channel_id=1, source_target_pairs={{0,1},{1,2},{2,3},{3,4},{4,5},{5,6},{6,7},{7,0},{8,9},{9,10},{10,1... | collective-permute-start | bytes 442376 | tf_op jit(solution)/shard_map/ppermute | solution.py:288
  77.3 70.2 %copy-start.2 = (bf16[64,1152]{1,0:T(8,128)(2,1)S(1)}, bf16[64,1152]{1,0:T(8,128)(2,1)}, u32[]{:S(2)}) copy-start(bf16[64,1152]{1,0:T(8,128)(2,1)} %fresh_ref.1) | copy-start | bytes 442372
  77.4 5.9 %collective-permute-start.25 = (bf16[64,1152]{1,0:T(8,128)(2,1)S(1)}, bf16[64,1152]{1,0:T(8,128)(2,1)S(1)}, u32[]{:S(2)}, u32[]{:S(2)}) collective-permute-start(bf16[64,1152]{1,0:T(8,128)(2,1)S(1)} %get-tuple-element.65), channel_id=1, source_target_pairs={{0,7},{1,0},{2,1},{3,2},{4,3},{5,4},{6,5},{7,6},{8,15},{9,8},{10,9... | collective-permute-start | bytes 442376 | tf_op jit(solution)/shard_map/ppermute | solution.py:291
  79.8 7.0 %collective-permute-start.22 = (bf16[64,1152]{1,0:T(8,128)(2,1)S(1)}, bf16[64,1152]{1,0:T(8,128)(2,1)S(1)}, u32[]{:S(2)}, u32[]{:S(2)}) collective-permute-start(bf16[64,1152]{1,0:T(8,128)(2,1)S(1)} %get-tuple-element.66), channel_id=1, source_target_pairs={{0,1},{1,2},{2,3},{3,4},{4,5},{5,6},{6,7},{7,0},{8,9},{9,10},{10,1... | collective-permute-start | bytes 442376 | tf_op jit(solution)/shard_map/ppermute | solution.py:288
  79.9 13.1 %collective-permute-start.20 = (bf16[64,1152]{1,0:T(8,128)(2,1)S(1)}, bf16[64,1152]{1,0:T(8,128)(2,1)S(1)}, u32[]{:S(2)}, u32[]{:S(2)}) collective-permute-start(bf16[64,1152]{1,0:T(8,128)(2,1)S(1)} %add_convert_fusion.5), channel_id=1, source_target_pairs={{0,7},{1,0},{2,1},{3,2},{4,3},{5,4},{6,5},{7,6},{8,15},{9,8},{10,9... | collective-permute-start | bytes 442376 | tf_op jit(solution)/shard_map/ppermute | solution.py:291
  83.0 6.7 %collective-permute-start.17 = (bf16[64,1152]{1,0:T(8,128)(2,1)S(1)}, bf16[64,1152]{1,0:T(8,128)(2,1)S(1)}, u32[]{:S(2)}, u32[]{:S(2)}) collective-permute-start(bf16[64,1152]{1,0:T(8,128)(2,1)S(1)} %add_convert_fusion.8), channel_id=1, source_target_pairs={{0,1},{1,2},{2,3},{3,4},{4,5},{5,6},{6,7},{7,0},{8,9},{9,10},{10,1... | collective-permute-start | bytes 442376 | tf_op jit(solution)/shard_map/ppermute | solution.py:288
  83.3 6.5 %collective-permute-start.26 = (bf16[64,1152]{1,0:T(8,128)(2,1)S(1)}, bf16[64,1152]{1,0:T(8,128)(2,1)S(1)}, u32[]{:S(2)}, u32[]{:S(2)}) collective-permute-start(bf16[64,1152]{1,0:T(8,128)(2,1)S(1)} %add_convert_fusion.1), channel_id=1, source_target_pairs={{0,7},{1,0},{2,1},{3,2},{4,3},{5,4},{6,5},{7,6},{8,15},{9,8},{10,9... | collective-permute-start | bytes 442376 | tf_op jit(solution)/shard_map/ppermute | solution.py:291
  86.8 6.2 %collective-permute-start.23 = (bf16[64,1152]{1,0:T(8,128)(2,1)S(1)}, bf16[64,1152]{1,0:T(8,128)(2,1)S(1)}, u32[]{:S(2)}, u32[]{:S(2)}) collective-permute-start(bf16[64,1152]{1,0:T(8,128)(2,1)S(1)} %add_convert_fusion.3), channel_id=1, source_target_pairs={{0,1},{1,2},{2,3},{3,4},{4,5},{5,6},{6,7},{7,0},{8,9},{9,10},{10,1... | collective-permute-start | bytes 442376 | tf_op jit(solution)/shard_map/ppermute | solution.py:288
  89.7 6.3 %collective-permute-start.18 = (bf16[64,1152]{1,0:T(8,128)(2,1)S(1)}, bf16[64,1152]{1,0:T(8,128)(2,1)S(1)}, u32[]{:S(2)}, u32[]{:S(2)}) collective-permute-start(bf16[64,1152]{1,0:T(8,128)(2,1)S(1)} %add_convert_fusion.7), channel_id=1, source_target_pairs={{0,1},{1,2},{2,3},{3,4},{4,5},{5,6},{6,7},{7,0},{8,9},{9,10},{10,1... | collective-permute-start | bytes 442376 | tf_op jit(solution)/shard_map/ppermute | solution.py:288
  89.8 6.2 %collective-permute-start.27 = (bf16[64,1152]{1,0:T(8,128)(2,1)S(1)}, bf16[64,1152]{1,0:T(8,128)(2,1)S(1)}, u32[]{:S(2)}, u32[]{:S(2)}) collective-permute-start(bf16[64,1152]{1,0:T(8,128)(2,1)S(1)} %add_convert_fusion), channel_id=1, source_target_pairs={{0,7},{1,0},{2,1},{3,2},{4,3},{5,4},{6,5},{7,6},{8,15},{9,8},{10,9... | collective-permute-start | bytes 442376 | tf_op jit(solution)/shard_map/ppermute | solution.py:291
  97.5 27.4 %all-to-all-start = ((bf16[32,4,1152]{2,1,0:T(4,128)(2,1)}), bf16[32,4,1152]{2,1,0:T(4,128)(2,1)S(1)}, u32[]{:S(2)}, u32[]{:S(2)}) async-start(bf16[32,4,1152]{2,1,0:T(4,128)(2,1)} %reshape.23), calls=%async_computation | async-start | bytes 589824 | tf_op jit(solution)/shard_map/all_to_all | solution.py:347
  115.7 31.8 %collective-permute-start.28 = (f32[72,1152]{1,0:T(8,128)S(1)}, f32[72,1152]{1,0:T(8,128)S(1)}, u32[]{:S(2)}, u32[]{:S(2)}) collective-permute-start(f32[72,1152]{1,0:T(8,128)S(1)} %get-tuple-element.63), channel_id=1, source_target_pairs={{8,0},{16,8},{24,16},{32,24},{40,32},{48,40},{56,48},{64,56},{72,6... | collective-permute-start | bytes 995336 | tf_op jit(solution)/shard_map/ppermute | solution.py:344
  134.0 13.1 %all-to-all-start.2 = ((bf16[32,4,1152]{2,1,0:T(4,128)(2,1)}), bf16[32,4,1152]{2,1,0:T(4,128)(2,1)S(1)}, u32[]{:S(2)}, u32[]{:S(2)}) async-start(bf16[32,4,1152]{2,1,0:T(4,128)(2,1)} %reshape.26), calls=%async_computation.2 | async-start | bytes 589824 | tf_op jit(solution)/shard_map/all_to_all | solution.py:349
Sparse Core Ops, SparseCore 0:
  31.4 61.8 all-gather.2

commit v2 on v1

--- a/solution.py
+++ b/solution.py
@@ -20,6 +20,10 @@
 
 def vspec():
     return pl.BlockSpec(memory_space=VMEM)
+
+
+def in_hbm(values):
+    return pltpu.with_memory_space_constraint(values, pltpu.HBM)
 
 
 def normalize(values):
@@ -63,29 +67,10 @@
             VMEM(tokens.shape, BF16),
             pltpu.SemaphoreType.DMA((3,)),
         ],
-        compiler_params=params(50),
+        compiler_params=params(24),
         cost_estimate=pl.CostEstimate(flops=4000000, bytes_accessed=3000000, transcendentals=0),
         name="first",
-    )(levels, table, tokens)
-
-
-def stack_kernel(in_ref, out_ref):
-    count, size, width = in_ref.shape
-    pieces = [in_ref[n].astype(F32) for n in range(count)]
-    out_ref[...] = jnp.concatenate(pieces, axis=0).astype(BF16)
-
-
-def stack(blocks):
-    count, size, width = blocks.shape
-    return pl.pallas_call(
-        stack_kernel,
-        out_shape=jax.ShapeDtypeStruct((count * size, width), BF16),
-        in_specs=[vspec()],
-        out_specs=vspec(),
-        compiler_params=params(8),
-        cost_estimate=pl.CostEstimate(flops=0, bytes_accessed=700000, transcendentals=0),
-        name="stack",
-    )(blocks)
+    )(levels, in_hbm(table), in_hbm(tokens))
 
 
 def spatial_kernel(wq_hbm, wo_hbm, *refs):
@@ -127,14 +112,14 @@
             VMEM(w_out.shape, BF16),
             pltpu.SemaphoreType.DMA((2,)),
         ],
-        compiler_params=params(40),
+        compiler_params=params(20),
         cost_estimate=pl.CostEstimate(
             flops=2 * whole * width * 144 * 4 + 4 * whole * whole * 256,
             bytes_accessed=5000000,
             transcendentals=2 * whole * whole,
         ),
         name="spatial",
-    )(w_qkv, w_out, *blocks)
+    )(in_hbm(w_qkv), in_hbm(w_out), *blocks)
 
 
 def middle_kernel(tokens_ref, mods_ref, *refs):
@@ -172,7 +157,7 @@
     )(tokens, mods, *parts)
 
 
-def temporal_kernel(ring, size, per, hidden_ref, weights_ref, out_ref, held, sems):
+def temporal_kernel(per, hidden_ref, weights_ref, out_ref, held, sems):
     pieces, depth, width = weights_ref.shape
     some = pieces // 8
 
@@ -185,6 +170,7 @@
     hidden = hidden_ref[...]
     rows = hidden.shape[0]
     half = width // 2
+    heads = half // HDIM
 
     def matrix(m, s):
         n = 2 * m + s
@@ -192,15 +178,9 @@
         return held[n * some : (n + 1) * some].reshape(half, width)
 
     lane = lax.broadcasted_iota(jnp.int32, (1, half), 1)
-    owned = []
-    for z in range(ring):
-        mask = jnp.zeros((1, half), jnp.bool_)
-        for a in range(some):
-            low = a * depth + z * size
-            mask = mask | ((lane >= low) & (lane < low + size))
-        owned.append(mask)
-    along = lax.broadcasted_iota(jnp.int32, (ring * rows, rows), 0) % per
-    across = lax.broadcasted_iota(jnp.int32, (ring * rows, rows), 1) % per
+    owned = [(lane >= h * HDIM) & (lane < (h + 1) * HDIM) for h in range(heads)]
+    along = lax.broadcasted_iota(jnp.int32, (heads * rows, rows), 0) % per
+    across = lax.broadcasted_iota(jnp.int32, (heads * rows, rows), 1) % per
     same = along == across
 
     query = [turned(hidden, matrix(0, s)) for s in range(2)]
@@ -214,17 +194,17 @@
         total = jnp.sum(weights, axis=-1, keepdims=True)
         mixed = jnp.dot(weights.astype(BF16), valued[s], preferred_element_type=F32) / total
         attended = jnp.zeros((rows, half), F32)
-        for z, m in enumerate(owned):
-            attended = jnp.where(m, mixed[z * rows : (z + 1) * rows], attended)
+        for h, m in enumerate(owned):
+            attended = jnp.where(m, mixed[h * rows : (h + 1) * rows], attended)
         branch += jnp.dot(attended.astype(BF16), matrix(3, s), preferred_element_type=F32)
     out_ref[...] = jnp.concatenate([branch[per:], branch[:per]], axis=0).astype(BF16)
 
 
-def temporal(ring, per, hidden, weights):
+def temporal(per, hidden, weights):
     pieces, depth, width = weights.shape
     rows = hidden.shape[0]
     return pl.pallas_call(
-        lambda *refs: temporal_kernel(ring, depth // ring, per, *refs),
+        lambda *refs: temporal_kernel(per, *refs),
         out_shape=jax.ShapeDtypeStruct((rows, width), BF16),
         in_specs=[vspec(), pl.BlockSpec(memory_space=pl.ANY)],
         out_specs=vspec(),
@@ -232,12 +212,12 @@
             VMEM((pieces, depth, width), BF16),
             pltpu.SemaphoreType.DMA((8,)),
         ],
-        compiler_params=params(50),
+        compiler_params=params(24),
         cost_estimate=pl.CostEstimate(
             flops=2 * rows * width * width * 4, bytes_accessed=12000000, transcendentals=16 * rows * rows
         ),
         name="temporal",
-    )(hidden, weights)
+    )(hidden, in_hbm(weights))
 
 
 def last_kernel(tail_ref, x1_ref, mods_ref, pack_ref, branch_ref, fresh_ref, out_ref):
@@ -291,20 +271,13 @@
         return lax.ppermute(v, "tok", down)
 
     turned_qkv = jnp.swapaxes(w_qkv_temporal, 1, 2)
-    side = w_out_temporal.shape[0]
-    size = 4 * side // line
-    start = spot * size
+    which = spot // ring
     chunk = jnp.where(
-        start >= 3 * side,
-        lax.dynamic_slice(w_out_temporal, (jnp.maximum(start - 3 * side, 0), 0), (size, width)),
-        lax.dynamic_slice(
-            turned_qkv.reshape(3 * side, width), (jnp.minimum(start, 3 * side - size), 0), (size, width)
-        ),
+        which == 3, w_out_temporal, lax.dynamic_index_in_dim(turned_qkv, jnp.minimum(which, 2), keepdims=False)
     )
-    chunks = lax.all_to_all(
-        jnp.broadcast_to(chunk[None], (ring, size, width)), "tok", 0, 0, tiled=True
-    )
-    weights = lax.all_gather(stack(chunks), "queue", axis=0, tiled=False)
+    far = [n // 2 + n % 2 * (ring // 2) for n in range(ring)]
+    pairs = [(q * ring + z, q * ring + (z - far[q % ring]) % ring) for q in range(line) for z in range(ring)]
+    chunk = lax.ppermute(chunk, ("queue", "tok"), pairs)
 
     mods, *hidden = first(levels, mod_table, queue_tokens)
     frames = [{0: h} for h in hidden]
@@ -315,6 +288,9 @@
                 frames[j][-step] = send_up(frames[j][1 - step])
             if step <= reach[j][1]:
                 frames[j][step] = send_down(frames[j][step - 1])
+    chunk, *_ = lax.optimization_barrier((chunk, *[frames[j][o] for j in range(2) for o in (-2, 2)]))
+    weights = lax.all_gather(chunk, "queue", axis=0, tiled=False)
+
     order = [[0, 1, 2, 3, -4, -3, -2, -1], [0, 1, 2, 3, 4, -3, -2, -1]]
 
     w_spatial = jnp.swapaxes(w_qkv_spatial, 1, 2)
@@ -345,7 +321,7 @@
     per = rows // line
     sent = jnp.transpose(h2.reshape(2, line, per, width), (1, 0, 2, 3)).reshape(line, 2 * per, width)
     got = lax.all_to_all(sent, "queue", 0, 0, tiled=True)
-    branch = temporal(ring, per, got.reshape(line * 2 * per, width), weights)
+    branch = temporal(per, got.reshape(line * 2 * per, width), weights)
     got = lax.all_to_all(branch.reshape(line, 2 * per, width), "queue", 0, 0, tiled=True)
     branch = jnp.transpose(got.reshape(line, 2, per, width), (1, 0, 2, 3)).reshape(2, rows, width)
     at_tail = (spot == line - 1).astype(jnp.int32)[None]

time: 156 us -> 152 us (0.974)
  blocking collectives: 22.9 us -> 0 us
  starting transfers between devices: 56.3 us -> 69.9 us
  waiting for transfers between devices: 34.4 us -> 42.9 us
  local copies, waits for them, and re-layouts: 7.68 us -> 3.76 us
    all_to_all x1 -> x0, blocking collectives: 22.9 us -> none  [per_device(): lax.all_to_all(jnp.broadcast_to(chunk[None], (ring, size, width)), 'tok',...]
    ppermute x14, waiting for transfers between devices: 0.04 us -> 12.1 us  [send_down(): return lax.ppermute(v, 'tok', down)]
    ppermute x0 -> x1, starting transfers between devices: none -> 9.65 us  [per_device(): chunk = lax.ppermute(chunk, ('queue', 'tok'), pairs)]
    unnamed x12 -> x8, local copies, waits for them, and re-layouts: 5.27 us -> 1.38 us
    ppermute x14, waiting for transfers between devices: 17.9 us -> 14.3 us  [send_up(): return lax.ppermute(v, 'tok', up)]
    all_to_all x1, starting transfers between devices: 18.2 us -> 21.4 us  [per_device(): got = lax.all_to_all(sent, 'queue', 0, 0, tiled=True)]
    pallas_call x2 -> x1, Pallas kernels: 8.93 us -> 8.12 us  [temporal(): pl.pallas_call(lambda *refs: temporal_kernel(per, *refs), out_shape=jax.S...]
  transfers between devices with their start and end apart: 32 -> 33, of which waited for: 12 -> 13; matrix products, arithmetic and copies ran while one was open for 2% -> 2% of each run, Pallas kernels for 11% -> 13%
where the time goes in v2:
time: 152 us; the launch traced here: 151 us
  starting transfers between devices  69.9 us (46%)
  waiting for transfers between devices  42.9 us (28%)
  Pallas kernels  19.8 us (13%)
  between operations  13.7 us (9%)
  local copies, waits for them, and re-layouts  3.76 us (2%)
    ppermute x14, starting transfers between devices, send_down(): return lax.ppermute(v, 'tok', down)  29.1 us
    all_to_all x1, starting transfers between devices, per_device(): got = lax.all_to_all(sent, 'queue', 0, 0, tiled=True)  21.4 us
    ppermute x14, waiting for transfers between devices, send_up(): return lax.ppermute(v, 'tok', up)  14.3 us
    ppermute x14, waiting for transfers between devices, send_down(): return lax.ppermute(v, 'tok', down)  12.1 us
    ppermute x1, starting transfers between devices, per_device(): chunk = lax.ppermute(chunk, ('queue', 'tok'), pairs)  9.65 us
    all_to_all x1, waiting for transfers between devices, per_device(): lax.all_to_all(branch.reshape(line, 2 * per, width), 'queue', 0, 0, tiled...  9.33 us
    pallas_call x2, Pallas kernels, spatial(): pl.pallas_call(spatial_kernel, out_shape=[jax.ShapeDtypeStruct((rows, wid...  8.54 us
    pallas_call x1, Pallas kernels, temporal(): pl.pallas_call(lambda *refs: temporal_kernel(per, *refs), out_shape=jax.S...  8.12 us
  transfers between devices with their start and end apart: 33, of which 13 were waited for; matrix products, arithmetic and copies ran while one was open for 2% of the time, Pallas kernels for 13%

profile of v2, /device:TPU:1, one launch (start us, length us, event | category | flops | bytes accessed | tf_op | source)
XLA Modules:
  0.0 151.5 jit_solution(14136150919702903085)
XLA Ops:
  6.5 1.1 bitcast_select_fusion
  7.6 9.6 %collective-permute-start.29 = (bf16[144,1152]{1,0:T(8,128)(2,1)S(1)}, bf16[144,1152]{1,0:T(8,128)(2,1)S(1)}, u32[]{:S(2)}, u32[]{:S(2)}) collective-permute-start(bf16[144,1152]{1,0:T(8,128)(2,1)S(1)} %bitcast_select_fusion), channel_id=1, source_target_pairs={{0,0},{1,1},{2,2},{3,3},{4,4},{5,5},{6,6},{7,7},{8,12},{9,13},{10,... | collective-permute-start | bytes 995336 | tf_op jit(solution)/shard_map/ppermute | solution.py:280
  17.3 0.6 copy-done.2
  17.9 2.0 %first.1 = (f32[2,6912]{1,0:T(2,128)S(1)}, bf16[64,1152]{1,0:T(8,128)(2,1)S(1)}, bf16[64,1152]{1,0:T(8,128)(2,1)S(1)}) custom-call(s32[2]{0:T(128)S(1)} %copy-done.2, f32[64,6912]{1,0:T(8,128)} %table_ref.1, bf16[2,64,1152]{2,1,0:T(8,128)(2,1)} %tokens_ref.3), custom_call_target="tpu_custom_call" | custom-call | flops 4000000 | bytes 3000000 | tf_op jit(solution)/shard_map/first/pallas_call | solution.py:60
  20.0 1.5 collective-permute-start.3
  21.4 1.3 collective-permute-start.9
  22.7 0.2 collective-permute-start.13
  22.9 6.6 %collective-permute-done.refs_1_ = bf16[64,1152]{1,0:T(8,128)(2,1)S(1)} collective-permute-done((bf16[64,1152]{1,0:T(8,128)(2,1)S(1)}, bf16[64,1152]{1,0:T(8,128)(2,1)S(1)}, u32[]{:S(2)}, u32[]{:S(2)}) %collective-permute-start) | collective-permute-done | bytes 147488 | tf_op jit(solution)/shard_map/ppermute | solution.py:271
  29.5 2.5 %collective-permute-start.1 = (bf16[64,1152]{1,0:T(8,128)(2,1)S(1)}, bf16[64,1152]{1,0:T(8,128)(2,1)S(1)}, u32[]{:S(2)}, u32[]{:S(2)}) collective-permute-start(bf16[64,1152]{1,0:T(8,128)(2,1)S(1)} %collective-permute-done.refs_1_), channel_id=1, source_target_pairs={{0,7},{1,0},{2,1},{3,2},{4,3},{5,4},{6,5},{7,6},{8,15},{9,8},{10,9... | collective-permute-start | bytes 442376 | tf_op jit(solution)/shard_map/ppermute | solution.py:271
  32.0 3.0 %collective-permute-start.10 = (bf16[64,1152]{1,0:T(8,128)(2,1)S(1)}, bf16[64,1152]{1,0:T(8,128)(2,1)S(1)}, u32[]{:S(2)}, u32[]{:S(2)}) collective-permute-start(bf16[64,1152]{1,0:T(8,128)(2,1)S(1)} %collective-permute-done.9.refs_1_), channel_id=1, source_target_pairs={{0,7},{1,0},{2,1},{3,2},{4,3},{5,4},{6,5},{7,6},{8,15},{9,8},{10,9... | collective-permute-start | bytes 442376 | tf_op jit(solution)/shard_map/ppermute | solution.py:271
  35.0 3.1 %collective-permute-done.4.refs_6_ = bf16[64,1152]{1,0:T(8,128)(2,1)S(1)} collective-permute-done((bf16[64,1152]{1,0:T(8,128)(2,1)S(1)}, bf16[64,1152]{1,0:T(8,128)(2,1)S(1)}, u32[]{:S(2)}, u32[]{:S(2)}) %collective-permute-start.4) | collective-permute-done | bytes 147488 | tf_op jit(solution)/shard_map/ppermute | solution.py:268
  38.1 3.0 %collective-permute-done.14.refs_6_ = bf16[64,1152]{1,0:T(8,128)(2,1)S(1)} collective-permute-done((bf16[64,1152]{1,0:T(8,128)(2,1)S(1)}, bf16[64,1152]{1,0:T(8,128)(2,1)S(1)}, u32[]{:S(2)}, u32[]{:S(2)}) %collective-permute-start.14) | collective-permute-done | bytes 147488 | tf_op jit(solution)/shard_map/ppermute | solution.py:268
  41.2 0.7 copy-done.3
  42.0 2.7 %collective-permute-start.11 = (bf16[64,1152]{1,0:T(8,128)(2,1)S(1)}, bf16[64,1152]{1,0:T(8,128)(2,1)S(1)}, u32[]{:S(2)}, u32[]{:S(2)}) collective-permute-start(bf16[64,1152]{1,0:T(8,128)(2,1)S(1)} %collective-permute-done.10.refs_2_), channel_id=1, source_target_pairs={{0,7},{1,0},{2,1},{3,2},{4,3},{5,4},{6,5},{7,6},{8,15},{9,8},{10,9... | collective-permute-start | bytes 442376 | tf_op jit(solution)/shard_map/ppermute | solution.py:271
  44.7 2.5 %collective-permute-done.5.refs_5_ = bf16[64,1152]{1,0:T(8,128)(2,1)S(1)} collective-permute-done((bf16[64,1152]{1,0:T(8,128)(2,1)S(1)}, bf16[64,1152]{1,0:T(8,128)(2,1)S(1)}, u32[]{:S(2)}, u32[]{:S(2)}) %collective-permute-start.5) | collective-permute-done | bytes 147488 | tf_op jit(solution)/shard_map/ppermute | solution.py:268
  47.2 2.7 %collective-permute-start.12 = (bf16[64,1152]{1,0:T(8,128)(2,1)S(1)}, bf16[64,1152]{1,0:T(8,128)(2,1)S(1)}, u32[]{:S(2)}, u32[]{:S(2)}) collective-permute-start(bf16[64,1152]{1,0:T(8,128)(2,1)S(1)} %collective-permute-done.11.refs_3_), channel_id=1, source_target_pairs={{0,7},{1,0},{2,1},{3,2},{4,3},{5,4},{6,5},{7,6},{8,15},{9,8},{10,9... | collective-permute-start | bytes 442376 | tf_op jit(solution)/shard_map/ppermute | solution.py:271
  49.9 2.5 %collective-permute-done.6.refs_4_ = bf16[64,1152]{1,0:T(8,128)(2,1)S(1)} collective-permute-done((bf16[64,1152]{1,0:T(8,128)(2,1)S(1)}, bf16[64,1152]{1,0:T(8,128)(2,1)S(1)}, u32[]{:S(2)}, u32[]{:S(2)}) %collective-permute-start.6) | collective-permute-done | bytes 147488 | tf_op jit(solution)/shard_map/ppermute | solution.py:268
  52.4 4.3 %spatial.2 = (bf16[64,1152]{1,0:T(8,128)(2,1)S(1)}, bf16[64,1152]{1,0:T(8,128)(2,1)S(1)}, bf16[64,1152]{1,0:T(8,128)(2,1)S(1)}, bf16[64,1152]{1,0:T(8,128)(2,1)S...) custom-call(bf16[3,144,1152]{2,1,0:T(8,128)(2,1)} %bitcast.14, ...), custom_call_target="tpu_custom_call" | custom-call | flops 947912704 | bytes 5000000 | tf_op jit(solution)/shard_map/spatial/pallas_call | solution.py:105
  56.8 2.7 %collective-permute-start.8 = (bf16[64,1152]{1,0:T(8,128)(2,1)S(1)}, bf16[64,1152]{1,0:T(8,128)(2,1)S(1)}, u32[]{:S(2)}, u32[]{:S(2)}) collective-permute-start(bf16[64,1152]{1,0:T(8,128)(2,1)S(1)} %get-tuple-element.43), channel_id=1, source_target_pairs={{0,7},{1,0},{2,1},{3,2},{4,3},{5,4},{6,5},{7,6},{8,15},{9,8},{10,9... | collective-permute-start | bytes 442376 | tf_op jit(solution)/shard_map/ppermute | solution.py:271
  59.4 4.3 %spatial.3 = (bf16[64,1152]{1,0:T(8,128)(2,1)S(1)}, bf16[64,1152]{1,0:T(8,128)(2,1)S(1)}, bf16[64,1152]{1,0:T(8,128)(2,1)S(1)}, bf16[64,1152]{1,0:T(8,128)(2,1)S...) custom-call(bf16[3,144,1152]{2,1,0:T(8,128)(2,1)} %bitcast.15, ...), custom_call_target="tpu_custom_call" | custom-call | flops 947912704 | bytes 5000000 | tf_op jit(solution)/shard_map/spatial/pallas_call | solution.py:105
  63.7 0.1 collective-permute-start.24
  63.8 1.4 collective-permute-start.21
  65.3 0.1 collective-permute-start.16
  65.4 2.7 %collective-permute-start.19 = (bf16[64,1152]{1,0:T(8,128)(2,1)S(1)}, bf16[64,1152]{1,0:T(8,128)(2,1)S(1)}, u32[]{:S(2)}, u32[]{:S(2)}) collective-permute-start(bf16[64,1152]{1,0:T(8,128)(2,1)S(1)} %add_convert_fusion.6), channel_id=1, source_target_pairs={{0,7},{1,0},{2,1},{3,2},{4,3},{5,4},{6,5},{7,6},{8,15},{9,8},{10,9... | collective-permute-start | bytes 442376 | tf_op jit(solution)/shard_map/ppermute | solution.py:271
  68.2 1.3 collective-permute-done.21
  69.6 0.2 collective-permute-start.22
  69.8 2.5 %collective-permute-start.25 = (bf16[64,1152]{1,0:T(8,128)(2,1)S(1)}, bf16[64,1152]{1,0:T(8,128)(2,1)S(1)}, u32[]{:S(2)}, u32[]{:S(2)}) collective-permute-start(bf16[64,1152]{1,0:T(8,128)(2,1)S(1)} %get-tuple-element.67), channel_id=1, source_target_pairs={{0,7},{1,0},{2,1},{3,2},{4,3},{5,4},{6,5},{7,6},{8,15},{9,8},{10,9... | collective-permute-start | bytes 442376 | tf_op jit(solution)/shard_map/ppermute | solution.py:271
  72.5 2.9 %collective-permute-start.20 = (bf16[64,1152]{1,0:T(8,128)(2,1)S(1)}, bf16[64,1152]{1,0:T(8,128)(2,1)S(1)}, u32[]{:S(2)}, u32[]{:S(2)}) collective-permute-start(bf16[64,1152]{1,0:T(8,128)(2,1)S(1)} %add_convert_fusion.5), channel_id=1, source_target_pairs={{0,7},{1,0},{2,1},{3,2},{4,3},{5,4},{6,5},{7,6},{8,15},{9,8},{10,9... | collective-permute-start | bytes 442376 | tf_op jit(solution)/shard_map/ppermute | solution.py:271
  75.5 1.2 collective-permute-done.22
  76.9 2.7 %collective-permute-start.26 = (bf16[64,1152]{1,0:T(8,128)(2,1)S(1)}, bf16[64,1152]{1,0:T(8,128)(2,1)S(1)}, u32[]{:S(2)}, u32[]{:S(2)}) collective-permute-start(bf16[64,1152]{1,0:T(8,128)(2,1)S(1)} %add_convert_fusion.1), channel_id=1, source_target_pairs={{0,7},{1,0},{2,1},{3,2},{4,3},{5,4},{6,5},{7,6},{8,15},{9,8},{10,9... | collective-permute-start | bytes 442376 | tf_op jit(solution)/shard_map/ppermute | solution.py:271
  79.8 2.9 %collective-permute-done.26 = bf16[64,1152]{1,0:T(8,128)(2,1)S(1)} collective-permute-done((bf16[64,1152]{1,0:T(8,128)(2,1)S(1)}, bf16[64,1152]{1,0:T(8,128)(2,1)S(1)}, u32[]{:S(2)}, u32[]{:S(2)}) %collective-permute-start.26) | collective-permute-done | bytes 147488 | tf_op jit(solution)/shard_map/ppermute | solution.py:271
  82.7 3.2 %collective-permute-start.27 = (bf16[64,1152]{1,0:T(8,128)(2,1)S(1)}, bf16[64,1152]{1,0:T(8,128)(2,1)S(1)}, u32[]{:S(2)}, u32[]{:S(2)}) collective-permute-start(bf16[64,1152]{1,0:T(8,128)(2,1)S(1)} %add_convert_fusion), channel_id=1, source_target_pairs={{0,7},{1,0},{2,1},{3,2},{4,3},{5,4},{6,5},{7,6},{8,15},{9,8},{10,9... | collective-permute-start | bytes 442376 | tf_op jit(solution)/shard_map/ppermute | solution.py:271
  85.9 0.7 collective-permute-done.18.refs_1_
  86.6 2.5 %collective-permute-done.27.refs_5_ = bf16[64,1152]{1,0:T(8,128)(2,1)S(1)} collective-permute-done((bf16[64,1152]{1,0:T(8,128)(2,1)S(1)}, bf16[64,1152]{1,0:T(8,128)(2,1)S(1)}, u32[]{:S(2)}, u32[]{:S(2)}) %collective-permute-start.27) | collective-permute-done | bytes 147488 | tf_op jit(solution)/shard_map/ppermute | solution.py:271
  89.1 0.4 middle.1
  89.4 0.1 reshape.18
  89.6 0.2 copy.13
  89.8 0.8 reshape.19
  90.6 21.4 %all-to-all-start = ((bf16[32,4,1152]{2,1,0:T(4,128)(2,1)}), bf16[32,4,1152]{2,1,0:T(4,128)(2,1)S(1)}, u32[]{:S(2)}, u32[]{:S(2)}) async-start(bf16[32,4,1152]{2,1,0:T(4,128)(2,1)} %reshape.19), calls=%async_computation | async-start | bytes 589824 | tf_op jit(solution)/shard_map/all_to_all | solution.py:323
  112.1 2.1 %collective-permute-start.28 = (f32[72,1152]{1,0:T(8,128)S(1)}, f32[72,1152]{1,0:T(8,128)S(1)}, u32[]{:S(2)}, u32[]{:S(2)}) collective-permute-start(f32[72,1152]{1,0:T(8,128)S(1)} %get-tuple-element.64), channel_id=1, source_target_pairs={{8,0},{16,8},{24,16},{32,24},{40,32},{48,40},{56,48},{64,56},{72,6... | collective-permute-start | bytes 995336 | tf_op jit(solution)/shard_map/ppermute | solution.py:320
  114.2 7.1 %all-to-all-done = bf16[32,4,1152]{2,1,0:T(4,128)(2,1)S(1)} async-done(((bf16[32,4,1152]{2,1,0:T(4,128)(2,1)}), bf16[32,4,1152]{2,1,0:T(4,128)(2,1)S(1)}, u32[]{:S(2)}, u32[]{:S(2)}) %all-to-all-start) | async-done | bytes 294944 | tf_op jit(solution)/shard_map/all_to_all | solution.py:323
  121.4 8.1 %temporal.1 = bf16[128,1152]{1,0:T(8,128)(2,1)S(1)} custom-call(bf16[128,1152]{1,0:T(8,128)(2,1)S(1)} %reshape.20.refs_0_, bf16[32,144,1152]{2,1,0:T(8,128)(2,1)} %bitcast.11), custom_call_target="tpu_custom_call" | custom-call | flops 1358954496 | bytes 12000000 | tf_op jit(solution)/shard_map/temporal/pallas_call | solution.py:206
  129.5 0.8 reshape.21
  130.3 3.8 %all-to-all-start.1 = ((bf16[32,4,1152]{2,1,0:T(4,128)(2,1)}), bf16[32,4,1152]{2,1,0:T(4,128)(2,1)S(1)}, u32[]{:S(2)}, u32[]{:S(2)}) async-start(bf16[32,4,1152]{2,1,0:T(4,128)(2,1)} %reshape.21), calls=%async_computation.1 | async-start | bytes 589824 | tf_op jit(solution)/shard_map/all_to_all | solution.py:325
  134.1 9.3 %all-to-all-done.1 = bf16[32,4,1152]{2,1,0:T(4,128)(2,1)S(1)} async-done(((bf16[32,4,1152]{2,1,0:T(4,128)(2,1)}), bf16[32,4,1152]{2,1,0:T(4,128)(2,1)S(1)}, u32[]{:S(2)}, u32[]{:S(2)}) %all-to-all-start.1) | async-done | bytes 294944 | tf_op jit(solution)/shard_map/all_to_all | solution.py:325
  143.5 0.2 copy.15
  143.7 0.1 reshape.23.branch_ref
  143.8 0.8 last.1
  (51 shorter events, 1.2 us)
Async XLA Ops:
  6.5 82.5 %copy-start = (bf16[2,64,1152]{2,1,0:T(8,128)(2,1)S(1)}, bf16[2,64,1152]{2,1,0:T(8,128)(2,1)}, u32[]{:S(2)}) copy-start(bf16[2,64,1152]{2,1,0:T(8,128)(2,1)} %tokens_ref.3) | copy-start | bytes 884740
  6.5 114.8 %all-gather.3.cloned.1.call-start = ((), (), s32[]{:S(2)}) async-start(), calls=%async_computation.2 | async-start | bytes 10948608 | tf_op jit(solution)/shard_map/all_gather | solution.py:292
  7.6 33.6 %collective-permute-start.29 = (bf16[144,1152]{1,0:T(8,128)(2,1)S(1)}, bf16[144,1152]{1,0:T(8,128)(2,1)S(1)}, u32[]{:S(2)}, u32[]{:S(2)}) collective-permute-start(bf16[144,1152]{1,0:T(8,128)(2,1)S(1)} %bitcast_select_fusion), channel_id=1, source_target_pairs={{0,0},{1,1},{2,2},{3,3},{4,4},{5,5},{6,6},{7,7},{8,12},{9,13},{10,... | collective-permute-start | bytes 995336 | tf_op jit(solution)/shard_map/ppermute | solution.py:280
  17.3 0.7 copy-start.2
  19.9 9.6 %collective-permute-start = (bf16[64,1152]{1,0:T(8,128)(2,1)S(1)}, bf16[64,1152]{1,0:T(8,128)(2,1)S(1)}, u32[]{:S(2)}, u32[]{:S(2)}) collective-permute-start(bf16[64,1152]{1,0:T(8,128)(2,1)S(1)} %get-tuple-element.37.refs_0_), channel_id=1, source_target_pairs={{0,7},{1,0},{2,1},{3,2},{4,3},{5,4},{6,5},{7,6},{8,15},{9,8},{10,9... | collective-permute-start | bytes 442376 | tf_op jit(solution)/shard_map/ppermute | solution.py:271
  20.0 12.0 %collective-permute-start.3 = (bf16[64,1152]{1,0:T(8,128)(2,1)S(1)}, bf16[64,1152]{1,0:T(8,128)(2,1)S(1)}, u32[]{:S(2)}, u32[]{:S(2)}) collective-permute-start(bf16[64,1152]{1,0:T(8,128)(2,1)S(1)} %get-tuple-element.37.refs_0_), channel_id=1, source_target_pairs={{0,1},{1,2},{2,3},{3,4},{4,5},{5,6},{6,7},{7,0},{8,9},{9,10},{10,1... | collective-permute-start | bytes 442376 | tf_op jit(solution)/shard_map/ppermute | solution.py:268
  21.4 10.5 %collective-permute-start.9 = (bf16[64,1152]{1,0:T(8,128)(2,1)S(1)}, bf16[64,1152]{1,0:T(8,128)(2,1)S(1)}, u32[]{:S(2)}, u32[]{:S(2)}) collective-permute-start(bf16[64,1152]{1,0:T(8,128)(2,1)S(1)} %get-tuple-element.44.refs_0_), channel_id=1, source_target_pairs={{0,7},{1,0},{2,1},{3,2},{4,3},{5,4},{6,5},{7,6},{8,15},{9,8},{10,9... | collective-permute-start | bytes 442376 | tf_op jit(solution)/shard_map/ppermute | solution.py:271
  22.7 12.2 %collective-permute-start.13 = (bf16[64,1152]{1,0:T(8,128)(2,1)S(1)}, bf16[64,1152]{1,0:T(8,128)(2,1)S(1)}, u32[]{:S(2)}, u32[]{:S(2)}) collective-permute-start(bf16[64,1152]{1,0:T(8,128)(2,1)S(1)} %get-tuple-element.44.refs_0_), channel_id=1, source_target_pairs={{0,1},{1,2},{2,3},{3,4},{4,5},{5,6},{6,7},{7,0},{8,9},{9,10},{10,1... | collective-permute-start | bytes 442376 | tf_op jit(solution)/shard_map/ppermute | solution.py:268
  29.5 5.5 %collective-permute-start.1 = (bf16[64,1152]{1,0:T(8,128)(2,1)S(1)}, bf16[64,1152]{1,0:T(8,128)(2,1)S(1)}, u32[]{:S(2)}, u32[]{:S(2)}) collective-permute-start(bf16[64,1152]{1,0:T(8,128)(2,1)S(1)} %collective-permute-done.refs_1_), channel_id=1, source_target_pairs={{0,7},{1,0},{2,1},{3,2},{4,3},{5,4},{6,5},{7,6},{8,15},{9,8},{10,9... | collective-permute-start | bytes 442376 | tf_op jit(solution)/shard_map/ppermute | solution.py:271
  32.0 6.1 %collective-permute-start.4 = (bf16[64,1152]{1,0:T(8,128)(2,1)S(1)}, bf16[64,1152]{1,0:T(8,128)(2,1)S(1)}, u32[]{:S(2)}, u32[]{:S(2)}) collective-permute-start(bf16[64,1152]{1,0:T(8,128)(2,1)S(1)} %collective-permute-done.3.refs_7_), channel_id=1, source_target_pairs={{0,1},{1,2},{2,3},{3,4},{4,5},{5,6},{6,7},{7,0},{8,9},{9,10},{10,1... | collective-permute-start | bytes 442376 | tf_op jit(solution)/shard_map/ppermute | solution.py:268
  32.0 6.1 %collective-permute-start.10 = (bf16[64,1152]{1,0:T(8,128)(2,1)S(1)}, bf16[64,1152]{1,0:T(8,128)(2,1)S(1)}, u32[]{:S(2)}, u32[]{:S(2)}) collective-permute-start(bf16[64,1152]{1,0:T(8,128)(2,1)S(1)} %collective-permute-done.9.refs_1_), channel_id=1, source_target_pairs={{0,7},{1,0},{2,1},{3,2},{4,3},{5,4},{6,5},{7,6},{8,15},{9,8},{10,9... | collective-permute-start | bytes 442376 | tf_op jit(solution)/shard_map/ppermute | solution.py:271
  34.9 6.2 %collective-permute-start.14 = (bf16[64,1152]{1,0:T(8,128)(2,1)S(1)}, bf16[64,1152]{1,0:T(8,128)(2,1)S(1)}, u32[]{:S(2)}, u32[]{:S(2)}) collective-permute-start(bf16[64,1152]{1,0:T(8,128)(2,1)S(1)} %collective-permute-done.13.refs_7_), channel_id=1, source_target_pairs={{0,1},{1,2},{2,3},{3,4},{4,5},{5,6},{6,7},{7,0},{8,9},{9,10},{10,1... | collective-permute-start | bytes 442376 | tf_op jit(solution)/shard_map/ppermute | solution.py:268
  41.2 0.7 copy-start.3
  41.9 5.3 %collective-permute-start.5 = (bf16[64,1152]{1,0:T(8,128)(2,1)S(1)}, bf16[64,1152]{1,0:T(8,128)(2,1)S(1)}, u32[]{:S(2)}, u32[]{:S(2)}) collective-permute-start(bf16[64,1152]{1,0:T(8,128)(2,1)S(1)} %collective-permute-done.4.refs_6_), channel_id=1, source_target_pairs={{0,1},{1,2},{2,3},{3,4},{4,5},{5,6},{6,7},{7,0},{8,9},{9,10},{10,1... | collective-permute-start | bytes 442376 | tf_op jit(solution)/shard_map/ppermute | solution.py:268
  42.0 5.2 %collective-permute-start.11 = (bf16[64,1152]{1,0:T(8,128)(2,1)S(1)}, bf16[64,1152]{1,0:T(8,128)(2,1)S(1)}, u32[]{:S(2)}, u32[]{:S(2)}) collective-permute-start(bf16[64,1152]{1,0:T(8,128)(2,1)S(1)} %collective-permute-done.10.refs_2_), channel_id=1, source_target_pairs={{0,7},{1,0},{2,1},{3,2},{4,3},{5,4},{6,5},{7,6},{8,15},{9,8},{10,9... | collective-permute-start | bytes 442376 | tf_op jit(solution)/shard_map/ppermute | solution.py:271
  44.7 5.2 %collective-permute-start.2 = (bf16[64,1152]{1,0:T(8,128)(2,1)S(1)}, bf16[64,1152]{1,0:T(8,128)(2,1)S(1)}, u32[]{:S(2)}, u32[]{:S(2)}) collective-permute-start(bf16[64,1152]{1,0:T(8,128)(2,1)S(1)} %collective-permute-done.1.refs_2_), channel_id=1, source_target_pairs={{0,7},{1,0},{2,1},{3,2},{4,3},{5,4},{6,5},{7,6},{8,15},{9,8},{10,9... | collective-permute-start | bytes 442376 | tf_op jit(solution)/shard_map/ppermute | solution.py:271
  47.2 5.2 %collective-permute-start.6 = (bf16[64,1152]{1,0:T(8,128)(2,1)S(1)}, bf16[64,1152]{1,0:T(8,128)(2,1)S(1)}, u32[]{:S(2)}, u32[]{:S(2)}) collective-permute-start(bf16[64,1152]{1,0:T(8,128)(2,1)S(1)} %collective-permute-done.5.refs_5_), channel_id=1, source_target_pairs={{0,1},{1,2},{2,3},{3,4},{4,5},{5,6},{6,7},{7,0},{8,9},{9,10},{10,1... | collective-permute-start | bytes 442376 | tf_op jit(solution)/shard_map/ppermute | solution.py:268
  47.2 12.2 %collective-permute-start.15 = (bf16[64,1152]{1,0:T(8,128)(2,1)S(1)}, bf16[64,1152]{1,0:T(8,128)(2,1)S(1)}, u32[]{:S(2)}, u32[]{:S(2)}) collective-permute-start(bf16[64,1152]{1,0:T(8,128)(2,1)S(1)} %collective-permute-done.14.refs_6_), channel_id=1, source_target_pairs={{0,1},{1,2},{2,3},{3,4},{4,5},{5,6},{6,7},{7,0},{8,9},{9,10},{10,1... | collective-permute-start | bytes 442376 | tf_op jit(solution)/shard_map/ppermute | solution.py:268
  47.2 12.2 %collective-permute-start.12 = (bf16[64,1152]{1,0:T(8,128)(2,1)S(1)}, bf16[64,1152]{1,0:T(8,128)(2,1)S(1)}, u32[]{:S(2)}, u32[]{:S(2)}) collective-permute-start(bf16[64,1152]{1,0:T(8,128)(2,1)S(1)} %collective-permute-done.11.refs_3_), channel_id=1, source_target_pairs={{0,7},{1,0},{2,1},{3,2},{4,3},{5,4},{6,5},{7,6},{8,15},{9,8},{10,9... | collective-permute-start | bytes 442376 | tf_op jit(solution)/shard_map/ppermute | solution.py:271
  56.7 8.6 %collective-permute-start.7 = (bf16[64,1152]{1,0:T(8,128)(2,1)S(1)}, bf16[64,1152]{1,0:T(8,128)(2,1)S(1)}, u32[]{:S(2)}, u32[]{:S(2)}) collective-permute-start(bf16[64,1152]{1,0:T(8,128)(2,1)S(1)} %get-tuple-element.42), channel_id=1, source_target_pairs={{0,1},{1,2},{2,3},{3,4},{4,5},{5,6},{6,7},{7,0},{8,9},{9,10},{10,1... | collective-permute-start | bytes 442376 | tf_op jit(solution)/shard_map/ppermute | solution.py:268
  56.8 8.5 %collective-permute-start.8 = (bf16[64,1152]{1,0:T(8,128)(2,1)S(1)}, bf16[64,1152]{1,0:T(8,128)(2,1)S(1)}, u32[]{:S(2)}, u32[]{:S(2)}) collective-permute-start(bf16[64,1152]{1,0:T(8,128)(2,1)S(1)} %get-tuple-element.43), channel_id=1, source_target_pairs={{0,7},{1,0},{2,1},{3,2},{4,3},{5,4},{6,5},{7,6},{8,15},{9,8},{10,9... | collective-permute-start | bytes 442376 | tf_op jit(solution)/shard_map/ppermute | solution.py:271
  63.7 4.5 %collective-permute-start.24 = (bf16[64,1152]{1,0:T(8,128)(2,1)S(1)}, bf16[64,1152]{1,0:T(8,128)(2,1)S(1)}, u32[]{:S(2)}, u32[]{:S(2)}) collective-permute-start(bf16[64,1152]{1,0:T(8,128)(2,1)S(1)} %get-tuple-element.49), channel_id=1, source_target_pairs={{0,7},{1,0},{2,1},{3,2},{4,3},{5,4},{6,5},{7,6},{8,15},{9,8},{10,9... | collective-permute-start | bytes 442376 | tf_op jit(solution)/shard_map/ppermute | solution.py:271
  63.8 5.7 %collective-permute-start.21 = (bf16[64,1152]{1,0:T(8,128)(2,1)S(1)}, bf16[64,1152]{1,0:T(8,128)(2,1)S(1)}, u32[]{:S(2)}, u32[]{:S(2)}) collective-permute-start(bf16[64,1152]{1,0:T(8,128)(2,1)S(1)} %get-tuple-element.48), channel_id=1, source_target_pairs={{0,1},{1,2},{2,3},{3,4},{4,5},{5,6},{6,7},{7,0},{8,9},{9,10},{10,1... | collective-permute-start | bytes 442376 | tf_op jit(solution)/shard_map/ppermute | solution.py:268
  65.3 7.0 %collective-permute-start.16 = (bf16[64,1152]{1,0:T(8,128)(2,1)S(1)}, bf16[64,1152]{1,0:T(8,128)(2,1)S(1)}, u32[]{:S(2)}, u32[]{:S(2)}) collective-permute-start(bf16[64,1152]{1,0:T(8,128)(2,1)S(1)} %add_convert_fusion.9), channel_id=1, source_target_pairs={{0,1},{1,2},{2,3},{3,4},{4,5},{5,6},{6,7},{7,0},{8,9},{9,10},{10,1... | collective-permute-start | bytes 442376 | tf_op jit(solution)/shard_map/ppermute | solution.py:268
  65.4 7.0 %collective-permute-start.19 = (bf16[64,1152]{1,0:T(8,128)(2,1)S(1)}, bf16[64,1152]{1,0:T(8,128)(2,1)S(1)}, u32[]{:S(2)}, u32[]{:S(2)}) collective-permute-start(bf16[64,1152]{1,0:T(8,128)(2,1)S(1)} %add_convert_fusion.6), channel_id=1, source_target_pairs={{0,7},{1,0},{2,1},{3,2},{4,3},{5,4},{6,5},{7,6},{8,15},{9,8},{10,9... | collective-permute-start | bytes 442376 | tf_op jit(solution)/shard_map/ppermute | solution.py:271
  69.6 74.3 %copy-start.1 = (bf16[64,1152]{1,0:T(8,128)(2,1)S(1)}, bf16[64,1152]{1,0:T(8,128)(2,1)}, u32[]{:S(2)}) copy-start(bf16[64,1152]{1,0:T(8,128)(2,1)} %fresh_ref.1) | copy-start | bytes 442372
  69.6 7.1 %collective-permute-start.22 = (bf16[64,1152]{1,0:T(8,128)(2,1)S(1)}, bf16[64,1152]{1,0:T(8,128)(2,1)S(1)}, u32[]{:S(2)}, u32[]{:S(2)}) collective-permute-start(bf16[64,1152]{1,0:T(8,128)(2,1)S(1)} %get-tuple-element.68), channel_id=1, source_target_pairs={{0,1},{1,2},{2,3},{3,4},{4,5},{5,6},{6,7},{7,0},{8,9},{9,10},{10,1... | collective-permute-start | bytes 442376 | tf_op jit(solution)/shard_map/ppermute | solution.py:268
  69.8 7.0 %collective-permute-start.25 = (bf16[64,1152]{1,0:T(8,128)(2,1)S(1)}, bf16[64,1152]{1,0:T(8,128)(2,1)S(1)}, u32[]{:S(2)}, u32[]{:S(2)}) collective-permute-start(bf16[64,1152]{1,0:T(8,128)(2,1)S(1)} %get-tuple-element.67), channel_id=1, source_target_pairs={{0,7},{1,0},{2,1},{3,2},{4,3},{5,4},{6,5},{7,6},{8,15},{9,8},{10,9... | collective-permute-start | bytes 442376 | tf_op jit(solution)/shard_map/ppermute | solution.py:271
  72.4 7.3 %collective-permute-start.17 = (bf16[64,1152]{1,0:T(8,128)(2,1)S(1)}, bf16[64,1152]{1,0:T(8,128)(2,1)S(1)}, u32[]{:S(2)}, u32[]{:S(2)}) collective-permute-start(bf16[64,1152]{1,0:T(8,128)(2,1)S(1)} %add_convert_fusion.8), channel_id=1, source_target_pairs={{0,1},{1,2},{2,3},{3,4},{4,5},{5,6},{6,7},{7,0},{8,9},{9,10},{10,1... | collective-permute-start | bytes 442376 | tf_op jit(solution)/shard_map/ppermute | solution.py:268
  72.5 13.3 %collective-permute-start.20 = (bf16[64,1152]{1,0:T(8,128)(2,1)S(1)}, bf16[64,1152]{1,0:T(8,128)(2,1)S(1)}, u32[]{:S(2)}, u32[]{:S(2)}) collective-permute-start(bf16[64,1152]{1,0:T(8,128)(2,1)S(1)} %add_convert_fusion.5), channel_id=1, source_target_pairs={{0,7},{1,0},{2,1},{3,2},{4,3},{5,4},{6,5},{7,6},{8,15},{9,8},{10,9... | collective-permute-start | bytes 442376 | tf_op jit(solution)/shard_map/ppermute | solution.py:271
  76.8 9.1 %collective-permute-start.23 = (bf16[64,1152]{1,0:T(8,128)(2,1)S(1)}, bf16[64,1152]{1,0:T(8,128)(2,1)S(1)}, u32[]{:S(2)}, u32[]{:S(2)}) collective-permute-start(bf16[64,1152]{1,0:T(8,128)(2,1)S(1)} %add_convert_fusion.3), channel_id=1, source_target_pairs={{0,1},{1,2},{2,3},{3,4},{4,5},{5,6},{6,7},{7,0},{8,9},{9,10},{10,1... | collective-permute-start | bytes 442376 | tf_op jit(solution)/shard_map/ppermute | solution.py:268
  76.9 5.7 %collective-permute-start.26 = (bf16[64,1152]{1,0:T(8,128)(2,1)S(1)}, bf16[64,1152]{1,0:T(8,128)(2,1)S(1)}, u32[]{:S(2)}, u32[]{:S(2)}) collective-permute-start(bf16[64,1152]{1,0:T(8,128)(2,1)S(1)} %add_convert_fusion.1), channel_id=1, source_target_pairs={{0,7},{1,0},{2,1},{3,2},{4,3},{5,4},{6,5},{7,6},{8,15},{9,8},{10,9... | collective-permute-start | bytes 442376 | tf_op jit(solution)/shard_map/ppermute | solution.py:271
  79.7 6.9 %collective-permute-start.18 = (bf16[64,1152]{1,0:T(8,128)(2,1)S(1)}, bf16[64,1152]{1,0:T(8,128)(2,1)S(1)}, u32[]{:S(2)}, u32[]{:S(2)}) collective-permute-start(bf16[64,1152]{1,0:T(8,128)(2,1)S(1)} %add_convert_fusion.7), channel_id=1, source_target_pairs={{0,1},{1,2},{2,3},{3,4},{4,5},{5,6},{6,7},{7,0},{8,9},{9,10},{10,1... | collective-permute-start | bytes 442376 | tf_op jit(solution)/shard_map/ppermute | solution.py:268
  82.7 6.4 %collective-permute-start.27 = (bf16[64,1152]{1,0:T(8,128)(2,1)S(1)}, bf16[64,1152]{1,0:T(8,128)(2,1)S(1)}, u32[]{:S(2)}, u32[]{:S(2)}) collective-permute-start(bf16[64,1152]{1,0:T(8,128)(2,1)S(1)} %add_convert_fusion), channel_id=1, source_target_pairs={{0,7},{1,0},{2,1},{3,2},{4,3},{5,4},{6,5},{7,6},{8,15},{9,8},{10,9... | collective-permute-start | bytes 442376 | tf_op jit(solution)/shard_map/ppermute | solution.py:271
  90.6 30.7 %all-to-all-start = ((bf16[32,4,1152]{2,1,0:T(4,128)(2,1)}), bf16[32,4,1152]{2,1,0:T(4,128)(2,1)S(1)}, u32[]{:S(2)}, u32[]{:S(2)}) async-start(bf16[32,4,1152]{2,1,0:T(4,128)(2,1)} %reshape.19), calls=%async_computation | async-start | bytes 589824 | tf_op jit(solution)/shard_map/all_to_all | solution.py:323
  112.1 31.8 %collective-permute-start.28 = (f32[72,1152]{1,0:T(8,128)S(1)}, f32[72,1152]{1,0:T(8,128)S(1)}, u32[]{:S(2)}, u32[]{:S(2)}) collective-permute-start(f32[72,1152]{1,0:T(8,128)S(1)} %get-tuple-element.64), channel_id=1, source_target_pairs={{8,0},{16,8},{24,16},{32,24},{40,32},{48,40},{56,48},{64,56},{72,6... | collective-permute-start | bytes 995336 | tf_op jit(solution)/shard_map/ppermute | solution.py:320
  130.3 13.1 %all-to-all-start.1 = ((bf16[32,4,1152]{2,1,0:T(4,128)(2,1)}), bf16[32,4,1152]{2,1,0:T(4,128)(2,1)S(1)}, u32[]{:S(2)}, u32[]{:S(2)}) async-start(bf16[32,4,1152]{2,1,0:T(4,128)(2,1)} %reshape.21), calls=%async_computation.1 | async-start | bytes 589824 | tf_op jit(solution)/shard_map/all_to_all | solution.py:325
Sparse Core Ops, SparseCore 0:
  42.0 67.1 all-gather.2

commit v3 on v2

v3 whole, which is shorter than its diff:
```python
import jax
import jax.numpy as jnp
from jax import lax
from jax.experimental import pallas as pl
from jax.experimental.pallas import tpu as pltpu
from jax.sharding import PartitionSpec as P

HEADS = 16
HDIM = 72
EPS = 1e-06
FACTOR = HDIM ** (-0.5)
BF16 = jnp.bfloat16
F32 = jnp.float32
VMEM = pltpu.VMEM


def params(mib):
    return pltpu.CompilerParams(vmem_limit_bytes=mib * 1024 * 1024)


def vspec():
    return pl.BlockSpec(memory_space=VMEM)


def in_hbm(values):
    return pltpu.with_memory_space_constraint(values, pltpu.HBM)


def normalize(values):
    mean = jnp.mean(values, axis=-1, keepdims=True)
    centered = values - mean
    variance = jnp.mean(centered * centered, axis=-1, keepdims=True)
    return centered * lax.rsqrt(variance + EPS)


def turned(values, matrix):
    return lax.dot_general(values, matrix, (((1,), (1,)), ((), ())), preferred_element_type=F32)


def first_kernel(levels_ref, table_ref, tokens_ref, h0_ref, h1_ref, near, held, sems):
    rows, width = tokens_ref.shape[1:]
    copies = [pltpu.make_async_copy(tokens_ref, held, sems.at[2])]
    for j in range(2):
        base = pl.multiple_of(levels_ref[j] // 8 * 8, 8)
        copies.append(pltpu.make_async_copy(table_ref.at[pl.ds(base, 8), pl.ds(0, 2 * width)], near.at[j], sems.at[j]))
    for copy in copies:
        copy.start()
    for copy in copies:
        copy.wait()
    for j, out in enumerate((h0_ref, h1_ref)):
        row = near[j, pl.ds(levels_ref[j] % 8, 1), :]
        values = normalize(held[j].astype(F32))
        out[...] = (values * (1.0 + row[:, width : 2 * width]) + row[:, :width]).astype(BF16)


def first(levels, table, tokens):
    _, rows, width = tokens.shape
    block = jax.ShapeDtypeStruct((rows, width), BF16)
    return pl.pallas_call(
        first_kernel,
        out_shape=(block, block),
        in_specs=[pl.BlockSpec(memory_space=pltpu.SMEM)] + [pl.BlockSpec(memory_space=pl.ANY)] * 2,
        out_specs=(vspec(), vspec()),
        scratch_shapes=[
            VMEM((2, 8, 2 * width), F32),
            VMEM(tokens.shape, BF16),
            pltpu.SemaphoreType.DMA((3,)),
        ],
        compiler_params=params(24),
        cost_estimate=pl.CostEstimate(flops=4000000, bytes_accessed=3000000, transcendentals=0),
        name="first",
    )(levels, in_hbm(table), in_hbm(tokens))


def spatial_kernel(offsets, place_ref, w_hbm, *refs):
    *refs, out_ref, w_ref, sem = refs
    copy = pltpu.make_async_copy(w_hbm, w_ref, sem)
    copy.start()
    rows = refs[0].shape[0]
    ring = len(offsets[0])
    copy.wait()
    for j in range(2):
        hidden = jnp.concatenate([ref[...] for ref in refs[j * ring : (j + 1) * ring]], axis=0)
        query = turned(w_ref[0], hidden).astype(BF16)
        keyed = turned(hidden, w_ref[1]).astype(BF16)
        valued = turned(w_ref[2], hidden).astype(BF16)
        heads = []
        for h in range(query.shape[0] // HDIM):
            cut = slice(h * HDIM, (h + 1) * HDIM)
            scores = FACTOR * jnp.dot(keyed[:, cut], query[cut], preferred_element_type=F32)
            weights = jnp.exp(scores - jnp.max(scores, axis=0, keepdims=True))
            total = jnp.sum(weights, axis=0, keepdims=True)
            mixed = jnp.dot(valued[cut], weights.astype(BF16), preferred_element_type=F32)
            heads.append((mixed / total).astype(BF16))
        attended = jnp.concatenate(heads, axis=0)
        for n, offset in enumerate(offsets[j]):
            owner = lax.rem(place_ref[0] + offset + ring, ring)
            out_ref[owner, :, j * rows : (j + 1) * rows] = attended[:, n * rows : (n + 1) * rows]


def spatial(offsets, place, w_qkv, blocks):
    rows, width = blocks[0].shape
    ring = len(offsets[0])
    whole = rows * ring
    return pl.pallas_call(
        lambda *refs: spatial_kernel(offsets, *refs),
        out_shape=jax.ShapeDtypeStruct((ring, w_qkv.shape[1], 2 * rows), BF16),
        in_specs=[pl.BlockSpec(memory_space=pltpu.SMEM), pl.BlockSpec(memory_space=pl.ANY)]
        + [vspec()] * len(blocks),
        out_specs=vspec(),
        scratch_shapes=[VMEM(w_qkv.shape, BF16), pltpu.SemaphoreType.DMA],
        compiler_params=params(20),
        cost_estimate=pl.CostEstimate(
            flops=4 * whole * width * 144 * 3 + 8 * whole * whole * 256,
            bytes_accessed=5000000,
            transcendentals=4 * whole * whole,
        ),
        name="spatial",
    )(place, in_hbm(w_qkv), *blocks)


def bundle_kernel(line, size, levels_ref, mixed_ref, tokens_ref, out_ref):
    ring, side, rows = mixed_ref.shape
    width = ring * side
    per = rows // (2 * line)
    mixed = jnp.concatenate(
        [mixed_ref[z, a * size : (a + 1) * size].astype(F32) for a in range(side // size) for z in range(ring)],
        axis=0,
    ).astype(BF16)
    spot = lax.broadcasted_iota(jnp.int32, (rows, rows), 0)
    frame = spot // per % 2
    source = frame * (rows // 2) + spot // (2 * per) * per + spot % per
    moved = (lax.broadcasted_iota(jnp.int32, (rows, rows), 1) == source).astype(BF16)
    out_ref[:, :width] = turned(moved, mixed).astype(BF16)
    tokens = tokens_ref[...].reshape(rows, width)
    out_ref[:, width : 2 * width] = jnp.dot(moved, tokens, preferred_element_type=F32).astype(BF16)
    lanes = out_ref.shape[1] - 2 * width
    one, two = levels_ref[0].astype(F32), levels_ref[1].astype(F32)
    out_ref[:, 2 * width :] = jnp.where(frame[:, :lanes] == 0, one, two).astype(BF16)


def bundle(line, size, levels, mixed, tokens):
    ring, side, rows = mixed.shape
    return pl.pallas_call(
        lambda *refs: bundle_kernel(line, size, *refs),
        out_shape=jax.ShapeDtypeStruct((rows, 2 * ring * side + 128), BF16),
        in_specs=[pl.BlockSpec(memory_space=pltpu.SMEM), vspec(), vspec()],
        out_specs=vspec(),
        compiler_params=params(12),
        cost_estimate=pl.CostEstimate(flops=80000000, bytes_accessed=1500000, transcendentals=0),
        name="bundle",
    )(levels, mixed, tokens)


def temporal_kernel(ring, size, per, got_ref, table_hbm, weights_hbm, out_ref, held, table_ref, sems):
    depth, width = held.shape[1:]
    some = 6 // 2
    half = width // 2

    def copy(n):
        part = pl.ds(n * some, some)
        return pltpu.make_async_copy(weights_hbm.at[part], held.at[part], sems.at[n])

    table_copy = pltpu.make_async_copy(table_hbm.at[:, pl.ds(2 * width, 4 * width)], table_ref, sems.at[10])
    for n in (8, 9):
        copy(n).start()
    table_copy.start()
    for n in range(8):
        copy(n).start()
    rows = got_ref.shape[0]

    def matrix(m, s):
        n = 2 * m + s
        copy(n).wait()
        return held[n * some : (n + 1) * some].reshape(half, width)

    branch = jnp.zeros((rows, width), F32)
    for s in range(2):
        branch += jnp.dot(got_ref[:, s * half : (s + 1) * half], matrix(4, s), preferred_element_type=F32)
    level = got_ref[:, 2 * width :].astype(F32)[:, : table_ref.shape[0]]
    column = lax.broadcasted_iota(jnp.int32, level.shape, 1).astype(F32)
    onehot = (level == column).astype(BF16)
    table_copy.wait()

    def mods(n):
        values = table_ref[:, n * width : (n + 1) * width]
        large = values.astype(BF16)
        small = (values - large.astype(F32)).astype(BF16)
        return jnp.dot(onehot, large, preferred_element_type=F32) + jnp.dot(
            onehot, small, preferred_element_type=F32
        )

    x1 = got_ref[:, width : 2 * width].astype(F32) + mods(0) * branch
    hidden = (normalize(x1) * (1.0 + mods(2)) + mods(1)).astype(BF16)

    lane = lax.broadcasted_iota(jnp.int32, (1, half), 1)
    owned = []
    for z in range(ring):
        mask = jnp.zeros((1, half), jnp.bool_)
        for a in range(some):
            low = a * depth + z * size
            mask = mask | ((lane >= low) & (lane < low + size))
        owned.append(mask)
    along = lax.broadcasted_iota(jnp.int32, (ring * rows, rows), 0) % per
    across = lax.broadcasted_iota(jnp.int32, (ring * rows, rows), 1) % per
    same = along == across

    query = [turned(hidden, matrix(0, s)) for s in range(2)]
    keyed = [turned(hidden, matrix(1, s)).astype(BF16) for s in range(2)]
    valued = [turned(hidden, matrix(2, s)).astype(BF16) for s in range(2)]
    branch = jnp.zeros((rows, width), F32)
    for s in range(2):
        spread = jnp.concatenate([jnp.where(m, query[s], 0.0) for m in owned], axis=0).astype(BF16)
        scores = jnp.where(same, FACTOR * turned(spread, keyed[s]), -jnp.inf)
        weights = jnp.exp(scores - jnp.max(scores, axis=-1, keepdims=True))
        total = jnp.sum(weights, axis=-1, keepdims=True)
        mixed = jnp.dot(weights.astype(BF16), valued[s], preferred_element_type=F32) / total
        attended = jnp.zeros((rows, half), F32)
        for z, m in enumerate(owned):
            attended = jnp.where(m, mixed[z * rows : (z + 1) * rows], attended)
        branch += jnp.dot(attended.astype(BF16), matrix(3, s), preferred_element_type=F32)
    y = x1 + mods(3) * branch
    out_ref[...] = jnp.concatenate([y[per:], y[:per]], axis=0).astype(BF16)


def temporal(ring, size, per, got, table, weights):
    _, depth, width = weights.shape
    rows = got.shape[0]
    return pl.pallas_call(
        lambda *refs: temporal_kernel(ring, size, per, *refs),
        out_shape=jax.ShapeDtypeStruct((rows, width), BF16),
        in_specs=[vspec(), pl.BlockSpec(memory_space=pl.ANY), pl.BlockSpec(memory_space=pl.ANY)],
        out_specs=vspec(),
        scratch_shapes=[
            VMEM((30, depth, width), BF16),
            VMEM((table.shape[0], 4 * width), F32),
            pltpu.SemaphoreType.DMA((11,)),
        ],
        compiler_params=params(40),
        cost_estimate=pl.CostEstimate(
            flops=2 * rows * width * width * 5, bytes_accessed=15000000, transcendentals=16 * rows * rows
        ),
        name="temporal",
    )(got, in_hbm(table), in_hbm(weights))


def per_device(
    queue_tokens,
    fresh_frame,
    levels,
    mod_table,
    w_qkv_spatial,
    w_out_spatial,
    w_qkv_temporal,
    w_out_temporal,
):
    _, rows, width = queue_tokens.shape
    ring = lax.axis_size("tok")
    line = lax.axis_size("queue")
    spot = lax.axis_index("queue")
    up = [(i, (i + 1) % ring) for i in range(ring)]
    down = [(i, (i - 1) % ring) for i in range(ring)]

    def send_up(v):
        return lax.ppermute(v, "tok", up)

    def send_down(v):
        return lax.ppermute(v, "tok", down)

    side = w_out_temporal.shape[0]
    size = side // 6
    start = spot * size
    turned_qkv = jnp.swapaxes(w_qkv_temporal, 1, 2).reshape(3 * side, width)

    def rows_from(matrix, first_row):
        at = jnp.clip(start - first_row, 0, matrix.shape[0] - size)
        return lax.dynamic_slice(matrix, (at, 0), (size, width))

    chunk = jnp.where(
        start < 3 * side,
        rows_from(turned_qkv, 0),
        jnp.where(start < 4 * side, rows_from(w_out_temporal, 3 * side), rows_from(w_out_spatial, 4 * side)),
    )
    chunks = lax.all_to_all(
        jnp.broadcast_to(chunk[None], (ring, size, width)), "tok", 0, 0, tiled=True
    )
    weights = lax.all_gather(chunks.reshape(ring * size, width), "queue", axis=0, tiled=False)

    hidden = first(levels, mod_table, queue_tokens)
    frames = [{0: h} for h in hidden]
    reach = ((4, 3), (3, 4))
    for step in range(1, 5):
        for j in range(2):
            if step <= reach[j][0]:
                frames[j][-step] = send_up(frames[j][1 - step])
            if step <= reach[j][1]:
                frames[j][step] = send_down(frames[j][step - 1])
    offsets = [[0, 1, 2, 3, -4, -3, -2, -1], [0, 1, 2, 3, 4, -3, -2, -1]]
    place = lax.axis_index("tok").astype(jnp.int32)[None]
    mixed = spatial(
        offsets,
        place,
        jnp.swapaxes(w_qkv_spatial, 1, 2),
        [frames[j][o] for j in range(2) for o in offsets[j]],
    )
    mixed = lax.all_to_all(mixed, "tok", 0, 0, tiled=True)

    per = rows // line
    sent = bundle(line, size, levels, mixed, queue_tokens)
    got = lax.all_to_all(sent.reshape(line, 2 * per, sent.shape[1]), "queue", 0, 0, tiled=True)
    moved = temporal(ring, size, per, got.reshape(sent.shape), mod_table, weights)
    got = lax.all_to_all(moved.reshape(line, 2 * per, width), "queue", 0, 0, tiled=True)
    got = jnp.transpose(got.reshape(line, 2, per, width), (1, 0, 2, 3)).reshape(2, rows, width)
    tail = jnp.where(spot == line - 1, fresh_frame, got[1])
    return jnp.stack([got[0], tail])


def solution(mesh):
    return jax.shard_map(
        per_device,
        mesh=mesh,
        in_specs=(
            P("queue", "tok", None),
            P("tok", None),
            P("queue"),
            P(),
            P(None, None, "tok"),
            P("tok", None),
            P(None, None, "tok"),
            P("tok", None),
        ),
        out_specs=P("queue", "tok", None),
        check_vma=False,
    )
```

time: 152 us -> 141 us (0.928)
  blocking collectives: 0 us -> 64.3 us
  starting transfers between devices: 69.9 us -> 20.2 us
  waiting for transfers between devices: 42.9 us -> 18.7 us
    all_to_all x0 -> x3, blocking collectives: none -> 64.3 us  [the longest x1 27.9 us: per_device(): lax.all_to_all(sent.reshape(line, 2 * per, sent.shape[1]), 'queue', 0, 0,...]
    all_to_all x2 -> x1, starting transfers between devices: 25.2 us -> 4.05 us  [per_device(): lax.all_to_all(moved.reshape(line, 2 * per, width), 'queue', 0, 0, tiled=...]
    ppermute x14 -> x7, starting transfers between devices: 29.1 us -> 14.1 us  [send_down(): return lax.ppermute(v, 'tok', down)]
    ppermute x2 -> x0, starting transfers between devices: 11.8 us -> none  [the longest x1 9.65 us: per_device(): chunk = lax.ppermute(chunk, ('queue', 'tok'), pairs)]
    ppermute x14 -> x7, waiting for transfers between devices: 12.1 us -> 0.99 us  [send_down(): return lax.ppermute(v, 'tok', down)]
    all_to_all x2 -> x1, waiting for transfers between devices: 16.4 us -> 9.33 us  [per_device(): lax.all_to_all(moved.reshape(line, 2 * per, width), 'queue', 0, 0, tiled=...]
    ppermute x14 -> x7, waiting for transfers between devices: 14.3 us -> 8.31 us  [send_up(): return lax.ppermute(v, 'tok', up)]
    ppermute x14 -> x7, starting transfers between devices: 3.82 us -> 2.02 us  [send_up(): return lax.ppermute(v, 'tok', up)]
  transfers between devices with their start and end apart: 33 -> 16, of which waited for: 13 -> 7; matrix products, arithmetic and copies ran while one was open for 2% -> 0% of each run, Pallas kernels for 13% -> 6%
where the time goes in v3:
time: 141 us
  blocking collectives  64.3 us (46%)
  starting transfers between devices  20.2 us (14%)
  waiting for transfers between devices  18.7 us (13%)
  Pallas kernels  18.5 us (13%)
  between operations  13.5 us (10%)
  local copies, waits for them, and re-layouts  4.09 us (3%)
  other arithmetic  1.77 us (1%)
    all_to_all x1, blocking collectives, per_device(): lax.all_to_all(sent.reshape(line, 2 * per, sent.shape[1]), 'queue', 0, 0,...  27.9 us
    all_to_all x1, blocking collectives, per_device(): lax.all_to_all(jnp.broadcast_to(chunk[None], (ring, size, width)), 'tok',...  23 us
    ppermute x7, starting transfers between devices, send_down(): return lax.ppermute(v, 'tok', down)  14.1 us
    all_to_all x1, blocking collectives, per_device(): mixed = lax.all_to_all(mixed, 'tok', 0, 0, tiled=True)  13.4 us
    pallas_call x1, Pallas kernels, temporal(): pl.pallas_call(lambda *refs: temporal_kernel(ring, size, per, *refs), out...  10.2 us
    all_to_all x1, waiting for transfers between devices, per_device(): lax.all_to_all(moved.reshape(line, 2 * per, width), 'queue', 0, 0, tiled=...  9.33 us
    ppermute x7, waiting for transfers between devices, send_up(): return lax.ppermute(v, 'tok', up)  8.31 us
    pallas_call x1, Pallas kernels, spatial(): pl.pallas_call(lambda *refs: spatial_kernel(offsets, *refs), out_shape=ja...  5.6 us
  transfers between devices with their start and end apart: 16, of which 7 were waited for; matrix products, arithmetic and copies ran while one was open for 0% of the time, Pallas kernels for 6%

profile of v3, /device:TPU:1, one launch (start us, length us, event | category | flops | bytes accessed | tf_op | source)
XLA Modules:
  0.0 141.1 jit_solution(13081333629461697075)
XLA Ops:
  6.5 1.0 select_select_fusion
  7.6 23.0 %all_to_all.20 = bf16[8,24,1152]{2,1,0:T(8,128)(2,1)} all-to-all(bf16[8,24,1152]{2,1,0:T(8,128)(2,1)S(1)} %broadcast_in_dim.10), channel_id=1, replica_groups=mesh['queue'=32,'tok'=8] {'tok'}, dimensions={0} | all-to-all | bytes 884736 | tf_op jit(solution)/shard_map/all_to_all | solution.py:284
  30.6 0.0 all-gather.2.cloned.1.call-update
  30.6 0.0 copy-start.1
  30.7 0.6 copy-done.1
  31.3 1.8 %first.1 = (bf16[64,1152]{1,0:T(8,128)(2,1)S(1)}, bf16[64,1152]{1,0:T(8,128)(2,1)S(1)}) custom-call(s32[2]{0:T(128)S(1)} %copy-done.1, f32[64,6912]{1,0:T(8,128)} %refs_1_.1, bf16[2,64,1152]{2,1,0:T(8,128)(2,1)} %refs_2_.1), custom_call_target="tpu_custom_call" | custom-call | flops 4000000 | bytes 3000000 | tf_op jit(solution)/shard_map/first/pallas_call | solution.py:59
  33.2 0.3 collective-permute-start.3
  33.5 2.4 %collective-permute-start.7 = (bf16[64,1152]{1,0:T(8,128)(2,1)S(1)}, bf16[64,1152]{1,0:T(8,128)(2,1)S(1)}, u32[]{:S(2)}, u32[]{:S(2)}) collective-permute-start(bf16[64,1152]{1,0:T(8,128)(2,1)S(1)} %get-tuple-element.8.refs_10_), channel_id=1, source_target_pairs={{0,7},{1,0},{2,1},{3,2},{4,3},{5,4},{6,5},{7,6},{8,15},{9,8},{10,9... | collective-permute-start | bytes 442376 | tf_op jit(solution)/shard_map/ppermute | solution.py:268
  35.9 0.0 collective-permute-start
  35.9 1.4 %collective-permute-start.11 = (bf16[64,1152]{1,0:T(8,128)(2,1)S(1)}, bf16[64,1152]{1,0:T(8,128)(2,1)S(1)}, u32[]{:S(2)}, u32[]{:S(2)}) collective-permute-start(bf16[64,1152]{1,0:T(8,128)(2,1)S(1)} %get-tuple-element.8.refs_10_), channel_id=1, source_target_pairs={{0,1},{1,2},{2,3},{3,4},{4,5},{5,6},{6,7},{7,0},{8,9},{9,10},{10,1... | collective-permute-start | bytes 442376 | tf_op jit(solution)/shard_map/ppermute | solution.py:265
  37.4 1.1 collective-permute-done.3.refs_9_
  38.4 0.0 collective-permute-start.4
  38.4 0.0 collective-permute-done.7.refs_11_
  38.4 2.7 %collective-permute-start.8 = (bf16[64,1152]{1,0:T(8,128)(2,1)S(1)}, bf16[64,1152]{1,0:T(8,128)(2,1)S(1)}, u32[]{:S(2)}, u32[]{:S(2)}) collective-permute-start(bf16[64,1152]{1,0:T(8,128)(2,1)S(1)} %collective-permute-done.7.refs_11_), channel_id=1, source_target_pairs={{0,7},{1,0},{2,1},{3,2},{4,3},{5,4},{6,5},{7,6},{8,15},{9,8},{10,9... | collective-permute-start | bytes 442376 | tf_op jit(solution)/shard_map/ppermute | solution.py:268
  41.1 0.0 collective-permute-done.refs_3_
  41.1 1.6 %collective-permute-start.1 = (bf16[64,1152]{1,0:T(8,128)(2,1)S(1)}, bf16[64,1152]{1,0:T(8,128)(2,1)S(1)}, u32[]{:S(2)}, u32[]{:S(2)}) collective-permute-start(bf16[64,1152]{1,0:T(8,128)(2,1)S(1)} %collective-permute-done.refs_3_), channel_id=1, source_target_pairs={{0,7},{1,0},{2,1},{3,2},{4,3},{5,4},{6,5},{7,6},{8,15},{9,8},{10,9... | collective-permute-start | bytes 442376 | tf_op jit(solution)/shard_map/ppermute | solution.py:268
  42.7 3.0 %collective-permute-done.4.refs_8_ = bf16[64,1152]{1,0:T(8,128)(2,1)S(1)} collective-permute-done((bf16[64,1152]{1,0:T(8,128)(2,1)S(1)}, bf16[64,1152]{1,0:T(8,128)(2,1)S(1)}, u32[]{:S(2)}, u32[]{:S(2)}) %collective-permute-start.4) | collective-permute-done | bytes 147488 | tf_op jit(solution)/shard_map/ppermute | solution.py:265
  45.7 2.7 %collective-permute-start.9 = (bf16[64,1152]{1,0:T(8,128)(2,1)S(1)}, bf16[64,1152]{1,0:T(8,128)(2,1)S(1)}, u32[]{:S(2)}, u32[]{:S(2)}) collective-permute-start(bf16[64,1152]{1,0:T(8,128)(2,1)S(1)} %collective-permute-done.8.refs_12_), channel_id=1, source_target_pairs={{0,7},{1,0},{2,1},{3,2},{4,3},{5,4},{6,5},{7,6},{8,15},{9,8},{10,9... | collective-permute-start | bytes 442376 | tf_op jit(solution)/shard_map/ppermute | solution.py:268
  48.4 0.0 collective-permute-done.1.refs_4_
  48.4 1.2 collective-permute-start.2
  49.6 0.0 collective-permute-done.12.refs_16_
  49.6 0.2 collective-permute-start.13
  49.8 1.2 collective-permute-done.5.refs_7_
  51.1 0.0 collective-permute-start.6
  51.1 1.0 collective-permute-done.9.refs_13_
  52.0 3.5 %collective-permute-start.10 = (bf16[64,1152]{1,0:T(8,128)(2,1)S(1)}, bf16[64,1152]{1,0:T(8,128)(2,1)S(1)}, u32[]{:S(2)}, u32[]{:S(2)}) collective-permute-start(bf16[64,1152]{1,0:T(8,128)(2,1)S(1)} %collective-permute-done.9.refs_13_), channel_id=1, source_target_pairs={{0,7},{1,0},{2,1},{3,2},{4,3},{5,4},{6,5},{7,6},{8,15},{9,8},{10,9... | collective-permute-start | bytes 442376 | tf_op jit(solution)/shard_map/ppermute | solution.py:268
  55.6 1.2 collective-permute-done.13.refs_15_
  56.8 1.8 %collective-permute-done.6.refs_6_ = bf16[64,1152]{1,0:T(8,128)(2,1)S(1)} collective-permute-done((bf16[64,1152]{1,0:T(8,128)(2,1)S(1)}, bf16[64,1152]{1,0:T(8,128)(2,1)S(1)}, u32[]{:S(2)}, u32[]{:S(2)}) %collective-permute-start.6) | collective-permute-done | bytes 147488 | tf_op jit(solution)/shard_map/ppermute | solution.py:265
  58.6 5.6 %spatial.1 = bf16[8,144,128]{2,1,0:T(8,128)(2,1)S(1)} custom-call(s32[1]{0:T(128)} %bitcast.refs_0_, bf16[3,144,1152]{2,1,0:T(8,128)(2,1)} %bitcast.14, bf16[64,1152]{1,0:T(8,128)(2,1)S(1)} %get-tuple-element.7.refs_2_, bf16[64,1152]{1,0:T(8,128)(2,1)S(1)} %collective-permute-done.refs_3_, bf16[64,1152]{1,0:T(8,128)(2,1)S(1)} %collective-permute-done.1.refs_4_, ...), custom_call_target="tpu_custom_call" | custom-call | flops 1556086784 | bytes 5000000 | tf_op jit(solution)/shard_map/spatial/pallas_call | solution.py:105
  64.2 0.0 copy-start.3
  64.2 13.4 %all_to_all.21.refs_1_ = bf16[8,144,128]{2,1,0:T(8,128)(2,1)S(1)} all-to-all(bf16[8,144,128]{2,1,0:T(8,128)(2,1)S(1)} %spatial.1), channel_id=1, replica_groups=mesh['queue'=32,'tok'=8] {'tok'}, dimensions={0} | all-to-all | bytes 589824 | tf_op jit(solution)/shard_map/all_to_all | solution.py:306
  77.6 1.0 copy-done
  78.6 0.7 copy-done.2
  79.3 0.9 bundle.1
  80.1 0.1 reshape.20
  80.3 27.9 %all_to_all.22 = bf16[32,4,2432]{2,1,0:T(4,128)(2,1)S(1)} all-to-all(bf16[32,4,2432]{2,1,0:T(4,128)(2,1)S(1)} %reshape.20), channel_id=1, replica_groups=mesh['queue'=32,'tok'=8] {'queue'}, dimensions={0} | all-to-all | bytes 1245184 | tf_op jit(solution)/shard_map/all_to_all | solution.py:310
  108.2 0.1 reshape.21.refs_0_
  108.4 0.0 all-gather.2.cloned.1.call-done.refs_2_
  108.4 10.2 %temporal.1 = bf16[128,1152]{1,0:T(8,128)(2,1)S(1)} custom-call(bf16[128,2432]{1,0:T(8,128)(2,1)S(1)} %reshape.21.refs_0_, f32[64,6912]{1,0:T(8,128)} %refs_1_.1, bf16[32,192,1152]{2,1,0:T(8,128)(2,1)} %all-gather.2.cloned.1.call-done.refs_2_), custom_call_target="tpu_custom_call" | custom-call | flops 1698693120 | bytes 15000000 | tf_op jit(solution)/shard_map/temporal/pallas_call | solution.py:229
  118.6 0.8 reshape.23
  119.4 4.1 %all-to-all-start.3 = ((bf16[32,4,1152]{2,1,0:T(4,128)(2,1)}), bf16[32,4,1152]{2,1,0:T(4,128)(2,1)S(1)}, u32[]{:S(2)}, u32[]{:S(2)}) async-start(bf16[32,4,1152]{2,1,0:T(4,128)(2,1)} %reshape.23), calls=%async_computation.3 | async-start | bytes 589824 | tf_op jit(solution)/shard_map/all_to_all | solution.py:312
  123.4 9.3 %all-to-all-done.3 = bf16[32,4,1152]{2,1,0:T(4,128)(2,1)S(1)} async-done(((bf16[32,4,1152]{2,1,0:T(4,128)(2,1)}), bf16[32,4,1152]{2,1,0:T(4,128)(2,1)S(1)}, u32[]{:S(2)}, u32[]{:S(2)}) %all-to-all-start.3) | async-done | bytes 294944 | tf_op jit(solution)/shard_map/all_to_all | solution.py:312
  132.8 0.1 reshape.24
  132.9 0.2 copy.12
  133.1 0.2 fusion
  133.3 0.1 slice.11
  133.4 0.1 squeeze.3
  133.5 0.7 pad_maximum_fusion
  (12 shorter events, 0.1 us)
Async XLA Ops:
  6.5 101.9 %all-gather.2.cloned.1.call-start = ((), (), s32[]{:S(2)}) async-start(), calls=%async_computation.4 | async-start | bytes 14598144 | tf_op jit(solution)/shard_map/all_gather | solution.py:287
  30.6 0.7 copy-start.1
  33.2 5.3 %collective-permute-start.3 = (bf16[64,1152]{1,0:T(8,128)(2,1)S(1)}, bf16[64,1152]{1,0:T(8,128)(2,1)S(1)}, u32[]{:S(2)}, u32[]{:S(2)}) collective-permute-start(bf16[64,1152]{1,0:T(8,128)(2,1)S(1)} %get-tuple-element.7.refs_2_), channel_id=1, source_target_pairs={{0,1},{1,2},{2,3},{3,4},{4,5},{5,6},{6,7},{7,0},{8,9},{9,10},{10,1... | collective-permute-start | bytes 442376 | tf_op jit(solution)/shard_map/ppermute | solution.py:265
  33.5 5.0 %collective-permute-start.7 = (bf16[64,1152]{1,0:T(8,128)(2,1)S(1)}, bf16[64,1152]{1,0:T(8,128)(2,1)S(1)}, u32[]{:S(2)}, u32[]{:S(2)}) collective-permute-start(bf16[64,1152]{1,0:T(8,128)(2,1)S(1)} %get-tuple-element.8.refs_10_), channel_id=1, source_target_pairs={{0,7},{1,0},{2,1},{3,2},{4,3},{5,4},{6,5},{7,6},{8,15},{9,8},{10,9... | collective-permute-start | bytes 442376 | tf_op jit(solution)/shard_map/ppermute | solution.py:268
  35.9 5.2 %collective-permute-start = (bf16[64,1152]{1,0:T(8,128)(2,1)S(1)}, bf16[64,1152]{1,0:T(8,128)(2,1)S(1)}, u32[]{:S(2)}, u32[]{:S(2)}) collective-permute-start(bf16[64,1152]{1,0:T(8,128)(2,1)S(1)} %get-tuple-element.7.refs_2_), channel_id=1, source_target_pairs={{0,7},{1,0},{2,1},{3,2},{4,3},{5,4},{6,5},{7,6},{8,15},{9,8},{10,9... | collective-permute-start | bytes 442376 | tf_op jit(solution)/shard_map/ppermute | solution.py:268
  35.9 6.8 %collective-permute-start.11 = (bf16[64,1152]{1,0:T(8,128)(2,1)S(1)}, bf16[64,1152]{1,0:T(8,128)(2,1)S(1)}, u32[]{:S(2)}, u32[]{:S(2)}) collective-permute-start(bf16[64,1152]{1,0:T(8,128)(2,1)S(1)} %get-tuple-element.8.refs_10_), channel_id=1, source_target_pairs={{0,1},{1,2},{2,3},{3,4},{4,5},{5,6},{6,7},{7,0},{8,9},{9,10},{10,1... | collective-permute-start | bytes 442376 | tf_op jit(solution)/shard_map/ppermute | solution.py:265
  38.4 7.2 %collective-permute-start.4 = (bf16[64,1152]{1,0:T(8,128)(2,1)S(1)}, bf16[64,1152]{1,0:T(8,128)(2,1)S(1)}, u32[]{:S(2)}, u32[]{:S(2)}) collective-permute-start(bf16[64,1152]{1,0:T(8,128)(2,1)S(1)} %collective-permute-done.3.refs_9_), channel_id=1, source_target_pairs={{0,1},{1,2},{2,3},{3,4},{4,5},{5,6},{6,7},{7,0},{8,9},{9,10},{10,1... | collective-permute-start | bytes 442376 | tf_op jit(solution)/shard_map/ppermute | solution.py:265
  38.4 7.2 %collective-permute-start.8 = (bf16[64,1152]{1,0:T(8,128)(2,1)S(1)}, bf16[64,1152]{1,0:T(8,128)(2,1)S(1)}, u32[]{:S(2)}, u32[]{:S(2)}) collective-permute-start(bf16[64,1152]{1,0:T(8,128)(2,1)S(1)} %collective-permute-done.7.refs_11_), channel_id=1, source_target_pairs={{0,7},{1,0},{2,1},{3,2},{4,3},{5,4},{6,5},{7,6},{8,15},{9,8},{10,9... | collective-permute-start | bytes 442376 | tf_op jit(solution)/shard_map/ppermute | solution.py:268
  41.1 7.2 %collective-permute-start.1 = (bf16[64,1152]{1,0:T(8,128)(2,1)S(1)}, bf16[64,1152]{1,0:T(8,128)(2,1)S(1)}, u32[]{:S(2)}, u32[]{:S(2)}) collective-permute-start(bf16[64,1152]{1,0:T(8,128)(2,1)S(1)} %collective-permute-done.refs_3_), channel_id=1, source_target_pairs={{0,7},{1,0},{2,1},{3,2},{4,3},{5,4},{6,5},{7,6},{8,15},{9,8},{10,9... | collective-permute-start | bytes 442376 | tf_op jit(solution)/shard_map/ppermute | solution.py:268
  42.7 6.9 %collective-permute-start.12 = (bf16[64,1152]{1,0:T(8,128)(2,1)S(1)}, bf16[64,1152]{1,0:T(8,128)(2,1)S(1)}, u32[]{:S(2)}, u32[]{:S(2)}) collective-permute-start(bf16[64,1152]{1,0:T(8,128)(2,1)S(1)} %collective-permute-done.11.refs_17_), channel_id=1, source_target_pairs={{0,1},{1,2},{2,3},{3,4},{4,5},{5,6},{6,7},{7,0},{8,9},{9,10},{10,1... | collective-permute-start | bytes 442376 | tf_op jit(solution)/shard_map/ppermute | solution.py:265
  45.7 5.4 %collective-permute-start.5 = (bf16[64,1152]{1,0:T(8,128)(2,1)S(1)}, bf16[64,1152]{1,0:T(8,128)(2,1)S(1)}, u32[]{:S(2)}, u32[]{:S(2)}) collective-permute-start(bf16[64,1152]{1,0:T(8,128)(2,1)S(1)} %collective-permute-done.4.refs_8_), channel_id=1, source_target_pairs={{0,1},{1,2},{2,3},{3,4},{4,5},{5,6},{6,7},{7,0},{8,9},{9,10},{10,1... | collective-permute-start | bytes 442376 | tf_op jit(solution)/shard_map/ppermute | solution.py:265
  45.7 6.4 %collective-permute-start.9 = (bf16[64,1152]{1,0:T(8,128)(2,1)S(1)}, bf16[64,1152]{1,0:T(8,128)(2,1)S(1)}, u32[]{:S(2)}, u32[]{:S(2)}) collective-permute-start(bf16[64,1152]{1,0:T(8,128)(2,1)S(1)} %collective-permute-done.8.refs_12_), channel_id=1, source_target_pairs={{0,7},{1,0},{2,1},{3,2},{4,3},{5,4},{6,5},{7,6},{8,15},{9,8},{10,9... | collective-permute-start | bytes 442376 | tf_op jit(solution)/shard_map/ppermute | solution.py:268
  48.4 7.2 %collective-permute-start.2 = (bf16[64,1152]{1,0:T(8,128)(2,1)S(1)}, bf16[64,1152]{1,0:T(8,128)(2,1)S(1)}, u32[]{:S(2)}, u32[]{:S(2)}) collective-permute-start(bf16[64,1152]{1,0:T(8,128)(2,1)S(1)} %collective-permute-done.1.refs_4_), channel_id=1, source_target_pairs={{0,7},{1,0},{2,1},{3,2},{4,3},{5,4},{6,5},{7,6},{8,15},{9,8},{10,9... | collective-permute-start | bytes 442376 | tf_op jit(solution)/shard_map/ppermute | solution.py:268
  49.6 7.2 %collective-permute-start.13 = (bf16[64,1152]{1,0:T(8,128)(2,1)S(1)}, bf16[64,1152]{1,0:T(8,128)(2,1)S(1)}, u32[]{:S(2)}, u32[]{:S(2)}) collective-permute-start(bf16[64,1152]{1,0:T(8,128)(2,1)S(1)} %collective-permute-done.12.refs_16_), channel_id=1, source_target_pairs={{0,1},{1,2},{2,3},{3,4},{4,5},{5,6},{6,7},{7,0},{8,9},{9,10},{10,1... | collective-permute-start | bytes 442376 | tf_op jit(solution)/shard_map/ppermute | solution.py:265
  51.1 7.5 %collective-permute-start.6 = (bf16[64,1152]{1,0:T(8,128)(2,1)S(1)}, bf16[64,1152]{1,0:T(8,128)(2,1)S(1)}, u32[]{:S(2)}, u32[]{:S(2)}) collective-permute-start(bf16[64,1152]{1,0:T(8,128)(2,1)S(1)} %collective-permute-done.5.refs_7_), channel_id=1, source_target_pairs={{0,1},{1,2},{2,3},{3,4},{4,5},{5,6},{6,7},{7,0},{8,9},{9,10},{10,1... | collective-permute-start | bytes 442376 | tf_op jit(solution)/shard_map/ppermute | solution.py:265
  52.0 6.6 %collective-permute-start.10 = (bf16[64,1152]{1,0:T(8,128)(2,1)S(1)}, bf16[64,1152]{1,0:T(8,128)(2,1)S(1)}, u32[]{:S(2)}, u32[]{:S(2)}) collective-permute-start(bf16[64,1152]{1,0:T(8,128)(2,1)S(1)} %collective-permute-done.9.refs_13_), channel_id=1, source_target_pairs={{0,7},{1,0},{2,1},{3,2},{4,3},{5,4},{6,5},{7,6},{8,15},{9,8},{10,9... | collective-permute-start | bytes 442376 | tf_op jit(solution)/shard_map/ppermute | solution.py:268
  64.2 69.2 %copy-start.3 = (bf16[64,1152]{1,0:T(8,128)(2,1)S(1)}, bf16[64,1152]{1,0:T(8,128)(2,1)}, u32[]{:S(2)}) copy-start(bf16[64,1152]{1,0:T(8,128)(2,1)} %param.9) | copy-start | bytes 442372
  77.6 1.0 copy-start
  78.6 0.7 copy-start.2
  119.4 13.4 %all-to-all-start.3 = ((bf16[32,4,1152]{2,1,0:T(4,128)(2,1)}), bf16[32,4,1152]{2,1,0:T(4,128)(2,1)S(1)}, u32[]{:S(2)}, u32[]{:S(2)}) async-start(bf16[32,4,1152]{2,1,0:T(4,128)(2,1)} %reshape.23), calls=%async_computation.3 | async-start | bytes 589824 | tf_op jit(solution)/shard_map/all_to_all | solution.py:312
Sparse Core Ops, SparseCore 0:
  30.8 70.0 all-gather.1

commit v4 on v3

--- a/solution.py
+++ b/solution.py
@@ -37,39 +37,55 @@
     return lax.dot_general(values, matrix, (((1,), (1,)), ((), ())), preferred_element_type=F32)
 
 
-def first_kernel(levels_ref, table_ref, tokens_ref, h0_ref, h1_ref, near, held, sems):
-    rows, width = tokens_ref.shape[1:]
-    copies = [pltpu.make_async_copy(tokens_ref, held, sems.at[2])]
-    for j in range(2):
-        base = pl.multiple_of(levels_ref[j] // 8 * 8, 8)
-        copies.append(pltpu.make_async_copy(table_ref.at[pl.ds(base, 8), pl.ds(0, 2 * width)], near.at[j], sems.at[j]))
+def first_kernel(line, levels_hbm, table_hbm, tokens_hbm, h0_ref, h1_ref, side_ref, table_ref, held, levels_ref, sems):
+    _, rows, width = held.shape
+    copies = [
+        pltpu.make_async_copy(levels_hbm, levels_ref, sems.at[0]),
+        pltpu.make_async_copy(tokens_hbm, held, sems.at[1]),
+        pltpu.make_async_copy(table_hbm.at[:, pl.ds(0, 2 * width)], table_ref, sems.at[2]),
+    ]
     for copy in copies:
         copy.start()
     for copy in copies:
         copy.wait()
     for j, out in enumerate((h0_ref, h1_ref)):
-        row = near[j, pl.ds(levels_ref[j] % 8, 1), :]
+        row = table_ref[pl.ds(levels_ref[j], 1), :]
         values = normalize(held[j].astype(F32))
-        out[...] = (values * (1.0 + row[:, width : 2 * width]) + row[:, :width]).astype(BF16)
-
-
-def first(levels, table, tokens):
+        out[...] = (values * (1.0 + row[:, width:]) + row[:, :width]).astype(BF16)
+    moved, frame = order_matrix(line, 2 * rows)
+    tokens = held[...].reshape(2 * rows, width)
+    side_ref[:, :width] = jnp.dot(moved, tokens, preferred_element_type=F32).astype(BF16)
+    one, two = levels_ref[0].astype(F32), levels_ref[1].astype(F32)
+    side_ref[:, width:] = jnp.where(frame == 0, one, two).astype(BF16)
+
+
+def order_matrix(line, rows):
+    per = rows // (2 * line)
+    spot = lax.broadcasted_iota(jnp.int32, (rows, rows), 0)
+    frame = spot // per % 2
+    source = frame * (rows // 2) + spot // (2 * per) * per + spot % per
+    moved = (lax.broadcasted_iota(jnp.int32, (rows, rows), 1) == source).astype(BF16)
+    return moved, frame
+
+
+def first(line, levels, table, tokens):
     _, rows, width = tokens.shape
     block = jax.ShapeDtypeStruct((rows, width), BF16)
     return pl.pallas_call(
-        first_kernel,
-        out_shape=(block, block),
-        in_specs=[pl.BlockSpec(memory_space=pltpu.SMEM)] + [pl.BlockSpec(memory_space=pl.ANY)] * 2,
-        out_specs=(vspec(), vspec()),
+        lambda *refs: first_kernel(line, *refs),
+        out_shape=(block, block, jax.ShapeDtypeStruct((2 * rows, width + 2 * rows), BF16)),
+        in_specs=[pl.BlockSpec(memory_space=pl.ANY)] * 3,
+        out_specs=(vspec(), vspec(), vspec()),
         scratch_shapes=[
-            VMEM((2, 8, 2 * width), F32),
+            VMEM((table.shape[0], 2 * width), F32),
             VMEM(tokens.shape, BF16),
+            pltpu.SMEM(levels.shape, jnp.int32),
             pltpu.SemaphoreType.DMA((3,)),
         ],
-        compiler_params=params(24),
-        cost_estimate=pl.CostEstimate(flops=4000000, bytes_accessed=3000000, transcendentals=0),
+        compiler_params=params(12),
+        cost_estimate=pl.CostEstimate(flops=40000000, bytes_accessed=1500000, transcendentals=0),
         name="first",
-    )(levels, in_hbm(table), in_hbm(tokens))
+    )(in_hbm(levels), in_hbm(table), in_hbm(tokens))
 
 
 def spatial_kernel(offsets, place_ref, w_hbm, *refs):
@@ -119,37 +135,29 @@
     )(place, in_hbm(w_qkv), *blocks)
 
 
-def bundle_kernel(line, size, levels_ref, mixed_ref, tokens_ref, out_ref):
+def bundle_kernel(line, size, mixed_ref, side_ref, out_ref):
     ring, side, rows = mixed_ref.shape
     width = ring * side
-    per = rows // (2 * line)
     mixed = jnp.concatenate(
         [mixed_ref[z, a * size : (a + 1) * size].astype(F32) for a in range(side // size) for z in range(ring)],
         axis=0,
     ).astype(BF16)
-    spot = lax.broadcasted_iota(jnp.int32, (rows, rows), 0)
-    frame = spot // per % 2
-    source = frame * (rows // 2) + spot // (2 * per) * per + spot % per
-    moved = (lax.broadcasted_iota(jnp.int32, (rows, rows), 1) == source).astype(BF16)
+    moved, _ = order_matrix(line, rows)
     out_ref[:, :width] = turned(moved, mixed).astype(BF16)
-    tokens = tokens_ref[...].reshape(rows, width)
-    out_ref[:, width : 2 * width] = jnp.dot(moved, tokens, preferred_element_type=F32).astype(BF16)
-    lanes = out_ref.shape[1] - 2 * width
-    one, two = levels_ref[0].astype(F32), levels_ref[1].astype(F32)
-    out_ref[:, 2 * width :] = jnp.where(frame[:, :lanes] == 0, one, two).astype(BF16)
-
-
-def bundle(line, size, levels, mixed, tokens):
+    out_ref[:, width:] = side_ref[...]
+
+
+def bundle(line, size, mixed, tokens):
     ring, side, rows = mixed.shape
     return pl.pallas_call(
         lambda *refs: bundle_kernel(line, size, *refs),
-        out_shape=jax.ShapeDtypeStruct((rows, 2 * ring * side + 128), BF16),
-        in_specs=[pl.BlockSpec(memory_space=pltpu.SMEM), vspec(), vspec()],
+        out_shape=jax.ShapeDtypeStruct((rows, ring * side + tokens.shape[1]), BF16),
+        in_specs=[vspec(), vspec()],
         out_specs=vspec(),
         compiler_params=params(12),
-        cost_estimate=pl.CostEstimate(flops=80000000, bytes_accessed=1500000, transcendentals=0),
+        cost_estimate=pl.CostEstimate(flops=40000000, bytes_accessed=1500000, transcendentals=0),
         name="bundle",
-    )(levels, mixed, tokens)
+    )(mixed, tokens)
 
 
 def temporal_kernel(ring, size, per, got_ref, table_hbm, weights_hbm, out_ref, held, table_ref, sems):
@@ -284,9 +292,8 @@
     chunks = lax.all_to_all(
         jnp.broadcast_to(chunk[None], (ring, size, width)), "tok", 0, 0, tiled=True
     )
-    weights = lax.all_gather(chunks.reshape(ring * size, width), "queue", axis=0, tiled=False)
-
-    hidden = first(levels, mod_table, queue_tokens)
+
+    *hidden, side_rows = first(line, levels, mod_table, queue_tokens)
     frames = [{0: h} for h in hidden]
     reach = ((4, 3), (3, 4))
     for step in range(1, 5):
@@ -295,6 +302,9 @@
                 frames[j][-step] = send_up(frames[j][1 - step])
             if step <= reach[j][1]:
                 frames[j][step] = send_down(frames[j][step - 1])
+    chunks, *_ = lax.optimization_barrier((chunks, *[frames[j][o] for j in range(2) for o in (-1, 1)]))
+    weights = lax.all_gather(chunks.reshape(ring * size, width), "queue", axis=0, tiled=False)
+
     offsets = [[0, 1, 2, 3, -4, -3, -2, -1], [0, 1, 2, 3, 4, -3, -2, -1]]
     place = lax.axis_index("tok").astype(jnp.int32)[None]
     mixed = spatial(
@@ -306,7 +316,7 @@
     mixed = lax.all_to_all(mixed, "tok", 0, 0, tiled=True)
 
     per = rows // line
-    sent = bundle(line, size, levels, mixed, queue_tokens)
+    sent = bundle(line, size, mixed, side_rows)
     got = lax.all_to_all(sent.reshape(line, 2 * per, sent.shape[1]), "queue", 0, 0, tiled=True)
     moved = temporal(ring, size, per, got.reshape(sent.shape), mod_table, weights)
     got = lax.all_to_all(moved.reshape(line, 2 * per, width), "queue", 0, 0, tiled=True)

time: 141 us -> 150 us (1.064)
  blocking collectives: 64.3 us -> 44.8 us
  waiting for transfers between devices: 18.7 us -> 38 us
  starting transfers between devices: 20.2 us -> 30.6 us
    all_to_all x1 -> x0, blocking collectives: 23 us -> none  [per_device(): lax.all_to_all(jnp.broadcast_to(chunk[None], (ring, size, width)), 'tok',...]
    all_to_all x0 -> x1, starting transfers between devices: none -> 9.01 us  [per_device(): lax.all_to_all(jnp.broadcast_to(chunk[None], (ring, size, width)), 'tok',...]
    ppermute x7, waiting for transfers between devices: 0.99 us -> 8.93 us  [send_down(): return lax.ppermute(v, 'tok', down)]
    all_gather x1, waiting for transfers between devices: 0.02 us -> 7.46 us  [per_device(): lax.all_gather(chunks.reshape(ring * size, width), 'queue', axis=0, tiled...]
    ppermute x7, waiting for transfers between devices: 8.31 us -> 12.4 us  [send_up(): return lax.ppermute(v, 'tok', up)]
    all_to_all x1, blocking collectives: 13.4 us -> 15.5 us  [per_device(): mixed = lax.all_to_all(mixed, 'tok', 0, 0, tiled=True)]
    unnamed x8 -> x4, local copies, waits for them, and re-layouts: 2.35 us -> 0.79 us
  transfers between devices with their start and end apart: 16 -> 17, of which waited for: 7 -> 9; matrix products, arithmetic and copies ran while one was open for 0% -> 0% of each run, Pallas kernels for 6% -> 5%
where the time goes in v4:
time: 150 us; the launch traced here: 149 us
  blocking collectives  44.8 us (30%)
  waiting for transfers between devices  38 us (25%)
  starting transfers between devices  30.6 us (20%)
  Pallas kernels  17.5 us (12%)
  between operations  13.5 us (9%)
  local copies, waits for them, and re-layouts  3.3 us (2%)
  other arithmetic  1.77 us (1%)
    all_to_all x1, blocking collectives, per_device(): lax.all_to_all(sent.reshape(line, 2 * per, sent.shape[1]), 'queue', 0, 0,...  29.3 us
    all_to_all x1, blocking collectives, per_device(): mixed = lax.all_to_all(mixed, 'tok', 0, 0, tiled=True)  15.5 us
    ppermute x7, starting transfers between devices, send_down(): return lax.ppermute(v, 'tok', down)  15.3 us
    ppermute x7, waiting for transfers between devices, send_up(): return lax.ppermute(v, 'tok', up)  12.4 us
    pallas_call x1, Pallas kernels, temporal(): pl.pallas_call(lambda *refs: temporal_kernel(ring, size, per, *refs), out...  10.2 us
    all_to_all x1, waiting for transfers between devices, per_device(): lax.all_to_all(moved.reshape(line, 2 * per, width), 'queue', 0, 0, tiled=...  9.21 us
    all_to_all x1, starting transfers between devices, per_device(): lax.all_to_all(jnp.broadcast_to(chunk[None], (ring, size, width)), 'tok',...  9.01 us
    ppermute x7, waiting for transfers between devices, send_down(): return lax.ppermute(v, 'tok', down)  8.93 us
  transfers between devices with their start and end apart: 17, of which 9 were waited for; matrix products, arithmetic and copies ran while one was open for 0% of the time, Pallas kernels for 5%

profile of v4, /device:TPU:1, one launch (start us, length us, event | category | flops | bytes accessed | tf_op | source)
XLA Modules:
  0.0 149.4 jit_solution(11160763325195523185)
XLA Ops:
  6.5 1.0 select_select_fusion
  7.5 0.8 broadcast_in_dim.10
  8.3 9.0 %all-to-all-start.2 = ((bf16[8,24,1152]{2,1,0:T(8,128)(2,1)}), bf16[8,24,1152]{2,1,0:T(8,128)(2,1)S(1)}, u32[]{:S(2)}, u32[]{:S(2)}) async-start(bf16[8,24,1152]{2,1,0:T(8,128)(2,1)} %broadcast_in_dim.10), calls=%async_computation.2 | async-start | bytes 884736 | tf_op jit(solution)/shard_map/all_to_all | solution.py:292
  17.4 0.0 all-gather.2.cloned.1.call-start
  17.4 1.5 %first.1 = (bf16[64,1152]{1,0:T(8,128)(2,1)S(1)}, bf16[64,1152]{1,0:T(8,128)(2,1)S(1)}, bf16[128,1280]{1,0:T(8,128)(2,1)S(1)}) custom-call(s32[2]{0:T(128)} %refs_0_.1, f32[64,6912]{1,0:T(8,128)} %refs_1_.3, bf16[2,64,1152]{2,1,0:T(8,128)(2,1)} %refs_2_.1), custom_call_target="tpu_custom_call" | custom-call | flops 40000000 | bytes 1500000 | tf_op jit(solution)/shard_map/first/pallas_call | solution.py:74
  18.9 2.7 %collective-permute-start.7 = (bf16[64,1152]{1,0:T(8,128)(2,1)S(1)}, bf16[64,1152]{1,0:T(8,128)(2,1)S(1)}, u32[]{:S(2)}, u32[]{:S(2)}) collective-permute-start(bf16[64,1152]{1,0:T(8,128)(2,1)S(1)} %get-tuple-element.10.refs_10_), channel_id=1, source_target_pairs={{0,7},{1,0},{2,1},{3,2},{4,3},{5,4},{6,5},{7,6},{8,15},{9,8},{10,9... | collective-permute-start | bytes 442376 | tf_op jit(solution)/shard_map/ppermute | solution.py:276
  21.6 0.0 collective-permute-start.3
  21.6 0.2 collective-permute-start.11
  21.9 2.5 %collective-permute-start = (bf16[64,1152]{1,0:T(8,128)(2,1)S(1)}, bf16[64,1152]{1,0:T(8,128)(2,1)S(1)}, u32[]{:S(2)}, u32[]{:S(2)}) collective-permute-start(bf16[64,1152]{1,0:T(8,128)(2,1)S(1)} %get-tuple-element.9.refs_2_), channel_id=1, source_target_pairs={{0,7},{1,0},{2,1},{3,2},{4,3},{5,4},{6,5},{7,6},{8,15},{9,8},{10,9... | collective-permute-start | bytes 442376 | tf_op jit(solution)/shard_map/ppermute | solution.py:276
  24.3 7.0 %collective-permute-done.7.refs_11_ = bf16[64,1152]{1,0:T(8,128)(2,1)S(1)} collective-permute-done((bf16[64,1152]{1,0:T(8,128)(2,1)S(1)}, bf16[64,1152]{1,0:T(8,128)(2,1)S(1)}, u32[]{:S(2)}, u32[]{:S(2)}) %collective-permute-start.7) | collective-permute-done | bytes 147488 | tf_op jit(solution)/shard_map/ppermute | solution.py:276
  31.3 0.9 collective-permute-done.3.refs_9_
  32.2 4.0 %collective-permute-done.11.refs_17_ = bf16[64,1152]{1,0:T(8,128)(2,1)S(1)} collective-permute-done((bf16[64,1152]{1,0:T(8,128)(2,1)S(1)}, bf16[64,1152]{1,0:T(8,128)(2,1)S(1)}, u32[]{:S(2)}, u32[]{:S(2)}) %collective-permute-start.11) | collective-permute-done | bytes 147488 | tf_op jit(solution)/shard_map/ppermute | solution.py:273
  36.2 0.0 collective-permute-done.refs_3_
  36.2 0.0 all-to-all-done.2
  36.2 0.8 copy-done
  37.0 0.0 all-gather.2.cloned.1.call-update
  37.0 1.3 collective-permute-start.8
  38.3 0.2 collective-permute-start.4
  38.6 0.0 collective-permute-start.12
  38.6 2.6 %collective-permute-start.1 = (bf16[64,1152]{1,0:T(8,128)(2,1)S(1)}, bf16[64,1152]{1,0:T(8,128)(2,1)S(1)}, u32[]{:S(2)}, u32[]{:S(2)}) collective-permute-start(bf16[64,1152]{1,0:T(8,128)(2,1)S(1)} %collective-permute-done.refs_3_), channel_id=1, source_target_pairs={{0,7},{1,0},{2,1},{3,2},{4,3},{5,4},{6,5},{7,6},{8,15},{9,8},{10,9... | collective-permute-start | bytes 442376 | tf_op jit(solution)/shard_map/ppermute | solution.py:276
  41.3 0.0 collective-permute-done.8.refs_12_
  41.3 2.3 %collective-permute-start.9 = (bf16[64,1152]{1,0:T(8,128)(2,1)S(1)}, bf16[64,1152]{1,0:T(8,128)(2,1)S(1)}, u32[]{:S(2)}, u32[]{:S(2)}) collective-permute-start(bf16[64,1152]{1,0:T(8,128)(2,1)S(1)} %collective-permute-done.8.refs_12_), channel_id=1, source_target_pairs={{0,7},{1,0},{2,1},{3,2},{4,3},{5,4},{6,5},{7,6},{8,15},{9,8},{10,9... | collective-permute-start | bytes 442376 | tf_op jit(solution)/shard_map/ppermute | solution.py:276
  43.6 2.8 %collective-permute-done.12.refs_16_ = bf16[64,1152]{1,0:T(8,128)(2,1)S(1)} collective-permute-done((bf16[64,1152]{1,0:T(8,128)(2,1)S(1)}, bf16[64,1152]{1,0:T(8,128)(2,1)S(1)}, u32[]{:S(2)}, u32[]{:S(2)}) %collective-permute-start.12) | collective-permute-done | bytes 147488 | tf_op jit(solution)/shard_map/ppermute | solution.py:273
  46.3 2.7 %collective-permute-start.2 = (bf16[64,1152]{1,0:T(8,128)(2,1)S(1)}, bf16[64,1152]{1,0:T(8,128)(2,1)S(1)}, u32[]{:S(2)}, u32[]{:S(2)}) collective-permute-start(bf16[64,1152]{1,0:T(8,128)(2,1)S(1)} %collective-permute-done.1.refs_4_), channel_id=1, source_target_pairs={{0,7},{1,0},{2,1},{3,2},{4,3},{5,4},{6,5},{7,6},{8,15},{9,8},{10,9... | collective-permute-start | bytes 442376 | tf_op jit(solution)/shard_map/ppermute | solution.py:276
  49.0 0.0 collective-permute-done.9.refs_13_
  49.0 1.2 collective-permute-start.10
  50.2 0.2 collective-permute-start.6
  50.5 1.0 collective-permute-done.13.refs_15_
  51.5 1.9 %collective-permute-done.10.refs_14_ = bf16[64,1152]{1,0:T(8,128)(2,1)S(1)} collective-permute-done((bf16[64,1152]{1,0:T(8,128)(2,1)S(1)}, bf16[64,1152]{1,0:T(8,128)(2,1)S(1)}, u32[]{:S(2)}, u32[]{:S(2)}) %collective-permute-start.10) | collective-permute-done | bytes 147488 | tf_op jit(solution)/shard_map/ppermute | solution.py:276
  53.5 3.6 %collective-permute-done.6.refs_6_ = bf16[64,1152]{1,0:T(8,128)(2,1)S(1)} collective-permute-done((bf16[64,1152]{1,0:T(8,128)(2,1)S(1)}, bf16[64,1152]{1,0:T(8,128)(2,1)S(1)}, u32[]{:S(2)}, u32[]{:S(2)}) %collective-permute-start.6) | collective-permute-done | bytes 147488 | tf_op jit(solution)/shard_map/ppermute | solution.py:273
  57.1 5.6 %spatial.1 = bf16[8,144,128]{2,1,0:T(8,128)(2,1)S(1)} custom-call(s32[1]{0:T(128)} %bitcast.refs_0_, bf16[3,144,1152]{2,1,0:T(8,128)(2,1)} %bitcast.14, bf16[64,1152]{1,0:T(8,128)(2,1)S(1)} %get-tuple-element.9.refs_2_, bf16[64,1152]{1,0:T(8,128)(2,1)S(1)} %collective-permute-done.refs_3_, bf16[64,1152]{1,0:T(8,128)(2,1)S(1)} %collective-permute-done.1.refs_4_, ...), custom_call_target="tpu_custom_call" | custom-call | flops 1556086784 | bytes 5000000 | tf_op jit(solution)/shard_map/spatial/pallas_call | solution.py:121
  62.7 0.0 copy-start.1
  62.7 15.5 %all_to_all.20.refs_0_ = bf16[8,144,128]{2,1,0:T(8,128)(2,1)S(1)} all-to-all(bf16[8,144,128]{2,1,0:T(8,128)(2,1)S(1)} %spatial.1), channel_id=1, replica_groups=mesh['queue'=32,'tok'=8] {'tok'}, dimensions={0} | all-to-all | bytes 589824 | tf_op jit(solution)/shard_map/all_to_all | solution.py:316
  78.2 0.2 bundle.1
  78.5 0.1 reshape.20
  78.6 29.3 %all_to_all.21 = bf16[32,4,2432]{2,1,0:T(4,128)(2,1)S(1)} all-to-all(bf16[32,4,2432]{2,1,0:T(4,128)(2,1)S(1)} %reshape.20), channel_id=1, replica_groups=mesh['queue'=32,'tok'=8] {'queue'}, dimensions={0} | all-to-all | bytes 1245184 | tf_op jit(solution)/shard_map/all_to_all | solution.py:320
  107.9 0.1 reshape.21.refs_0_
  108.0 7.5 %all-gather.2.cloned.1.call-done.refs_2_ = bf16[32,192,1152]{2,1,0:T(8,128)(2,1)} async-done(((bf16[1,192,1152]{2,1,0:T(8,128)(2,1)}), bf16[32,192,1152]{2,1,0:T(8,128)(2,1)}) %all-gather.2.cloned.1.call-update) | async-done | bytes 14155792 | tf_op jit(solution)/shard_map/all_gather | solution.py:306
  115.5 10.2 %temporal.1 = bf16[128,1152]{1,0:T(8,128)(2,1)S(1)} custom-call(bf16[128,2432]{1,0:T(8,128)(2,1)S(1)} %reshape.21.refs_0_, f32[64,6912]{1,0:T(8,128)} %refs_1_.3, bf16[32,192,1152]{2,1,0:T(8,128)(2,1)} %all-gather.2.cloned.1.call-done.refs_2_), custom_call_target="tpu_custom_call" | custom-call | flops 1698693120 | bytes 15000000 | tf_op jit(solution)/shard_map/temporal/pallas_call | solution.py:237
  125.6 0.8 reshape.23
  126.4 5.4 %all-to-all-start.3 = ((bf16[32,4,1152]{2,1,0:T(4,128)(2,1)}), bf16[32,4,1152]{2,1,0:T(4,128)(2,1)S(1)}, u32[]{:S(2)}, u32[]{:S(2)}) async-start(bf16[32,4,1152]{2,1,0:T(4,128)(2,1)} %reshape.23), calls=%async_computation.3 | async-start | bytes 589824 | tf_op jit(solution)/shard_map/all_to_all | solution.py:322
  131.9 9.2 %all-to-all-done.3 = bf16[32,4,1152]{2,1,0:T(4,128)(2,1)S(1)} async-done(((bf16[32,4,1152]{2,1,0:T(4,128)(2,1)}), bf16[32,4,1152]{2,1,0:T(4,128)(2,1)S(1)}, u32[]{:S(2)}, u32[]{:S(2)}) %all-to-all-start.3) | async-done | bytes 294944 | tf_op jit(solution)/shard_map/all_to_all | solution.py:322
  141.1 0.1 reshape.24
  141.2 0.2 copy.12
  141.4 0.2 fusion
  141.6 0.1 squeeze.3
  141.7 0.1 slice.11
  141.8 0.7 pad_maximum_fusion
  (9 shorter events, 0.0 us)
Async XLA Ops:
  8.3 27.9 %all-to-all-start.2 = ((bf16[8,24,1152]{2,1,0:T(8,128)(2,1)}), bf16[8,24,1152]{2,1,0:T(8,128)(2,1)S(1)}, u32[]{:S(2)}, u32[]{:S(2)}) async-start(bf16[8,24,1152]{2,1,0:T(8,128)(2,1)} %broadcast_in_dim.10), calls=%async_computation.2 | async-start | bytes 884736 | tf_op jit(solution)/shard_map/all_to_all | solution.py:292
  17.4 98.1 %all-gather.2.cloned.1.call-start = ((), (), s32[]{:S(2)}) async-start(), calls=%async_computation.4 | async-start | bytes 14598144 | tf_op jit(solution)/shard_map/all_gather | solution.py:306
  18.9 12.4 %collective-permute-start.7 = (bf16[64,1152]{1,0:T(8,128)(2,1)S(1)}, bf16[64,1152]{1,0:T(8,128)(2,1)S(1)}, u32[]{:S(2)}, u32[]{:S(2)}) collective-permute-start(bf16[64,1152]{1,0:T(8,128)(2,1)S(1)} %get-tuple-element.10.refs_10_), channel_id=1, source_target_pairs={{0,7},{1,0},{2,1},{3,2},{4,3},{5,4},{6,5},{7,6},{8,15},{9,8},{10,9... | collective-permute-start | bytes 442376 | tf_op jit(solution)/shard_map/ppermute | solution.py:276
  21.6 10.6 %collective-permute-start.3 = (bf16[64,1152]{1,0:T(8,128)(2,1)S(1)}, bf16[64,1152]{1,0:T(8,128)(2,1)S(1)}, u32[]{:S(2)}, u32[]{:S(2)}) collective-permute-start(bf16[64,1152]{1,0:T(8,128)(2,1)S(1)} %get-tuple-element.9.refs_2_), channel_id=1, source_target_pairs={{0,1},{1,2},{2,3},{3,4},{4,5},{5,6},{6,7},{7,0},{8,9},{9,10},{10,1... | collective-permute-start | bytes 442376 | tf_op jit(solution)/shard_map/ppermute | solution.py:273
  21.6 14.6 %collective-permute-start.11 = (bf16[64,1152]{1,0:T(8,128)(2,1)S(1)}, bf16[64,1152]{1,0:T(8,128)(2,1)S(1)}, u32[]{:S(2)}, u32[]{:S(2)}) collective-permute-start(bf16[64,1152]{1,0:T(8,128)(2,1)S(1)} %get-tuple-element.10.refs_10_), channel_id=1, source_target_pairs={{0,1},{1,2},{2,3},{3,4},{4,5},{5,6},{6,7},{7,0},{8,9},{9,10},{10,1... | collective-permute-start | bytes 442376 | tf_op jit(solution)/shard_map/ppermute | solution.py:273
  21.9 14.4 %collective-permute-start = (bf16[64,1152]{1,0:T(8,128)(2,1)S(1)}, bf16[64,1152]{1,0:T(8,128)(2,1)S(1)}, u32[]{:S(2)}, u32[]{:S(2)}) collective-permute-start(bf16[64,1152]{1,0:T(8,128)(2,1)S(1)} %get-tuple-element.9.refs_2_), channel_id=1, source_target_pairs={{0,7},{1,0},{2,1},{3,2},{4,3},{5,4},{6,5},{7,6},{8,15},{9,8},{10,9... | collective-permute-start | bytes 442376 | tf_op jit(solution)/shard_map/ppermute | solution.py:276
  36.2 0.8 copy-start
  37.0 4.2 %collective-permute-start.8 = (bf16[64,1152]{1,0:T(8,128)(2,1)S(1)}, bf16[64,1152]{1,0:T(8,128)(2,1)S(1)}, u32[]{:S(2)}, u32[]{:S(2)}) collective-permute-start(bf16[64,1152]{1,0:T(8,128)(2,1)S(1)} %collective-permute-done.7.refs_11_), channel_id=1, source_target_pairs={{0,7},{1,0},{2,1},{3,2},{4,3},{5,4},{6,5},{7,6},{8,15},{9,8},{10,9... | collective-permute-start | bytes 442376 | tf_op jit(solution)/shard_map/ppermute | solution.py:276
  38.3 5.2 %collective-permute-start.4 = (bf16[64,1152]{1,0:T(8,128)(2,1)S(1)}, bf16[64,1152]{1,0:T(8,128)(2,1)S(1)}, u32[]{:S(2)}, u32[]{:S(2)}) collective-permute-start(bf16[64,1152]{1,0:T(8,128)(2,1)S(1)} %collective-permute-done.3.refs_9_), channel_id=1, source_target_pairs={{0,1},{1,2},{2,3},{3,4},{4,5},{5,6},{6,7},{7,0},{8,9},{9,10},{10,1... | collective-permute-start | bytes 442376 | tf_op jit(solution)/shard_map/ppermute | solution.py:273
  38.6 7.7 %collective-permute-start.12 = (bf16[64,1152]{1,0:T(8,128)(2,1)S(1)}, bf16[64,1152]{1,0:T(8,128)(2,1)S(1)}, u32[]{:S(2)}, u32[]{:S(2)}) collective-permute-start(bf16[64,1152]{1,0:T(8,128)(2,1)S(1)} %collective-permute-done.11.refs_17_), channel_id=1, source_target_pairs={{0,1},{1,2},{2,3},{3,4},{4,5},{5,6},{6,7},{7,0},{8,9},{9,10},{10,1... | collective-permute-start | bytes 442376 | tf_op jit(solution)/shard_map/ppermute | solution.py:273
  38.6 7.7 %collective-permute-start.1 = (bf16[64,1152]{1,0:T(8,128)(2,1)S(1)}, bf16[64,1152]{1,0:T(8,128)(2,1)S(1)}, u32[]{:S(2)}, u32[]{:S(2)}) collective-permute-start(bf16[64,1152]{1,0:T(8,128)(2,1)S(1)} %collective-permute-done.refs_3_), channel_id=1, source_target_pairs={{0,7},{1,0},{2,1},{3,2},{4,3},{5,4},{6,5},{7,6},{8,15},{9,8},{10,9... | collective-permute-start | bytes 442376 | tf_op jit(solution)/shard_map/ppermute | solution.py:276
  41.3 7.7 %collective-permute-start.9 = (bf16[64,1152]{1,0:T(8,128)(2,1)S(1)}, bf16[64,1152]{1,0:T(8,128)(2,1)S(1)}, u32[]{:S(2)}, u32[]{:S(2)}) collective-permute-start(bf16[64,1152]{1,0:T(8,128)(2,1)S(1)} %collective-permute-done.8.refs_12_), channel_id=1, source_target_pairs={{0,7},{1,0},{2,1},{3,2},{4,3},{5,4},{6,5},{7,6},{8,15},{9,8},{10,9... | collective-permute-start | bytes 442376 | tf_op jit(solution)/shard_map/ppermute | solution.py:276
  43.6 6.7 %collective-permute-start.5 = (bf16[64,1152]{1,0:T(8,128)(2,1)S(1)}, bf16[64,1152]{1,0:T(8,128)(2,1)S(1)}, u32[]{:S(2)}, u32[]{:S(2)}) collective-permute-start(bf16[64,1152]{1,0:T(8,128)(2,1)S(1)} %collective-permute-done.4.refs_8_), channel_id=1, source_target_pairs={{0,1},{1,2},{2,3},{3,4},{4,5},{5,6},{6,7},{7,0},{8,9},{9,10},{10,1... | collective-permute-start | bytes 442376 | tf_op jit(solution)/shard_map/ppermute | solution.py:273
  46.3 5.2 %collective-permute-start.13 = (bf16[64,1152]{1,0:T(8,128)(2,1)S(1)}, bf16[64,1152]{1,0:T(8,128)(2,1)S(1)}, u32[]{:S(2)}, u32[]{:S(2)}) collective-permute-start(bf16[64,1152]{1,0:T(8,128)(2,1)S(1)} %collective-permute-done.12.refs_16_), channel_id=1, source_target_pairs={{0,1},{1,2},{2,3},{3,4},{4,5},{5,6},{6,7},{7,0},{8,9},{9,10},{10,1... | collective-permute-start | bytes 442376 | tf_op jit(solution)/shard_map/ppermute | solution.py:273
  46.3 5.2 %collective-permute-start.2 = (bf16[64,1152]{1,0:T(8,128)(2,1)S(1)}, bf16[64,1152]{1,0:T(8,128)(2,1)S(1)}, u32[]{:S(2)}, u32[]{:S(2)}) collective-permute-start(bf16[64,1152]{1,0:T(8,128)(2,1)S(1)} %collective-permute-done.1.refs_4_), channel_id=1, source_target_pairs={{0,7},{1,0},{2,1},{3,2},{4,3},{5,4},{6,5},{7,6},{8,15},{9,8},{10,9... | collective-permute-start | bytes 442376 | tf_op jit(solution)/shard_map/ppermute | solution.py:276
  49.0 4.4 %collective-permute-start.10 = (bf16[64,1152]{1,0:T(8,128)(2,1)S(1)}, bf16[64,1152]{1,0:T(8,128)(2,1)S(1)}, u32[]{:S(2)}, u32[]{:S(2)}) collective-permute-start(bf16[64,1152]{1,0:T(8,128)(2,1)S(1)} %collective-permute-done.9.refs_13_), channel_id=1, source_target_pairs={{0,7},{1,0},{2,1},{3,2},{4,3},{5,4},{6,5},{7,6},{8,15},{9,8},{10,9... | collective-permute-start | bytes 442376 | tf_op jit(solution)/shard_map/ppermute | solution.py:276
  50.2 6.8 %collective-permute-start.6 = (bf16[64,1152]{1,0:T(8,128)(2,1)S(1)}, bf16[64,1152]{1,0:T(8,128)(2,1)S(1)}, u32[]{:S(2)}, u32[]{:S(2)}) collective-permute-start(bf16[64,1152]{1,0:T(8,128)(2,1)S(1)} %collective-permute-done.5.refs_7_), channel_id=1, source_target_pairs={{0,1},{1,2},{2,3},{3,4},{4,5},{5,6},{6,7},{7,0},{8,9},{9,10},{10,1... | collective-permute-start | bytes 442376 | tf_op jit(solution)/shard_map/ppermute | solution.py:273
  62.7 79.1 %copy-start.1 = (bf16[64,1152]{1,0:T(8,128)(2,1)S(1)}, bf16[64,1152]{1,0:T(8,128)(2,1)}, u32[]{:S(2)}) copy-start(bf16[64,1152]{1,0:T(8,128)(2,1)} %param.9) | copy-start | bytes 442372
  126.4 14.7 %all-to-all-start.3 = ((bf16[32,4,1152]{2,1,0:T(4,128)(2,1)}), bf16[32,4,1152]{2,1,0:T(4,128)(2,1)S(1)}, u32[]{:S(2)}, u32[]{:S(2)}) async-start(bf16[32,4,1152]{2,1,0:T(4,128)(2,1)} %reshape.23), calls=%async_computation.3 | async-start | bytes 589824 | tf_op jit(solution)/shard_map/all_to_all | solution.py:322
Sparse Core Ops, SparseCore 0:
  37.2 78.2 all-gather.1

commit v5 on v4

--- a/solution.py
+++ b/solution.py
@@ -94,19 +94,23 @@
     copy.start()
     rows = refs[0].shape[0]
     ring = len(offsets[0])
-    copy.wait()
     for j in range(2):
         hidden = jnp.concatenate([ref[...] for ref in refs[j * ring : (j + 1) * ring]], axis=0)
-        query = turned(w_ref[0], hidden).astype(BF16)
-        keyed = turned(hidden, w_ref[1]).astype(BF16)
-        valued = turned(w_ref[2], hidden).astype(BF16)
+        if j == 0:
+            copy.wait()
+        projected = turned(w_ref[...], hidden).astype(BF16)
+        side = projected.shape[0] // 3
         heads = []
-        for h in range(query.shape[0] // HDIM):
-            cut = slice(h * HDIM, (h + 1) * HDIM)
-            scores = FACTOR * jnp.dot(keyed[:, cut], query[cut], preferred_element_type=F32)
+        for h in range(side // HDIM):
+            query, keyed, valued = [
+                projected[m * side + h * HDIM : m * side + (h + 1) * HDIM] for m in range(3)
+            ]
+            scores = FACTOR * lax.dot_general(
+                keyed, query, (((0,), (0,)), ((), ())), preferred_element_type=F32
+            )
             weights = jnp.exp(scores - jnp.max(scores, axis=0, keepdims=True))
             total = jnp.sum(weights, axis=0, keepdims=True)
-            mixed = jnp.dot(valued[cut], weights.astype(BF16), preferred_element_type=F32)
+            mixed = jnp.dot(valued, weights.astype(BF16), preferred_element_type=F32)
             heads.append((mixed / total).astype(BF16))
         attended = jnp.concatenate(heads, axis=0)
         for n, offset in enumerate(offsets[j]):
@@ -120,7 +124,7 @@
     whole = rows * ring
     return pl.pallas_call(
         lambda *refs: spatial_kernel(offsets, *refs),
-        out_shape=jax.ShapeDtypeStruct((ring, w_qkv.shape[1], 2 * rows), BF16),
+        out_shape=jax.ShapeDtypeStruct((ring, w_qkv.shape[0] // 3, 2 * rows), BF16),
         in_specs=[pl.BlockSpec(memory_space=pltpu.SMEM), pl.BlockSpec(memory_space=pl.ANY)]
         + [vspec()] * len(blocks),
         out_specs=vspec(),
@@ -201,34 +205,40 @@
     x1 = got_ref[:, width : 2 * width].astype(F32) + mods(0) * branch
     hidden = (normalize(x1) * (1.0 + mods(2)) + mods(1)).astype(BF16)
 
-    lane = lax.broadcasted_iota(jnp.int32, (1, half), 1)
-    owned = []
-    for z in range(ring):
-        mask = jnp.zeros((1, half), jnp.bool_)
-        for a in range(some):
-            low = a * depth + z * size
-            mask = mask | ((lane >= low) & (lane < low + size))
-        owned.append(mask)
-    along = lax.broadcasted_iota(jnp.int32, (ring * rows, rows), 0) % per
-    across = lax.broadcasted_iota(jnp.int32, (ring * rows, rows), 1) % per
+    row = lax.broadcasted_iota(jnp.int32, (half, 1), 0)
+    owner = row // size % ring
+    along = lax.broadcasted_iota(jnp.int32, (rows, ring * rows), 0) % per
+    across = lax.broadcasted_iota(jnp.int32, (rows, ring * rows), 1) % per
     same = along == across
 
-    query = [turned(hidden, matrix(0, s)) for s in range(2)]
+    query = [turned(matrix(0, s), hidden) for s in range(2)]
     keyed = [turned(hidden, matrix(1, s)).astype(BF16) for s in range(2)]
-    valued = [turned(hidden, matrix(2, s)).astype(BF16) for s in range(2)]
+    valued = [turned(matrix(2, s), hidden).astype(BF16) for s in range(2)]
     branch = jnp.zeros((rows, width), F32)
     for s in range(2):
-        spread = jnp.concatenate([jnp.where(m, query[s], 0.0) for m in owned], axis=0).astype(BF16)
-        scores = jnp.where(same, FACTOR * turned(spread, keyed[s]), -jnp.inf)
-        weights = jnp.exp(scores - jnp.max(scores, axis=-1, keepdims=True))
-        total = jnp.sum(weights, axis=-1, keepdims=True)
-        mixed = jnp.dot(weights.astype(BF16), valued[s], preferred_element_type=F32) / total
-        attended = jnp.zeros((rows, half), F32)
-        for z, m in enumerate(owned):
-            attended = jnp.where(m, mixed[z * rows : (z + 1) * rows], attended)
-        branch += jnp.dot(attended.astype(BF16), matrix(3, s), preferred_element_type=F32)
+        spread = jnp.concatenate(
+            [jnp.where(owner == z, query[s], 0.0).astype(BF16) for z in range(ring)], axis=1
+        )
+        scores = FACTOR * jnp.dot(keyed[s], spread, preferred_element_type=F32)
+        scores = jnp.where(same, scores, -jnp.inf)
+        weights = jnp.exp(scores - jnp.max(scores, axis=0, keepdims=True))
+        inverse = 1.0 / jnp.sum(weights, axis=0, keepdims=True)
+        mixed = jnp.dot(valued[s], weights.astype(BF16), preferred_element_type=F32)
+        attended = jnp.concatenate(
+            [
+                mixed[a * depth + z * size : a * depth + (z + 1) * size, z * rows : (z + 1) * rows]
+                * inverse[:, z * rows : (z + 1) * rows]
+                for a in range(some)
+                for z in range(ring)
+            ],
+            axis=0,
+        ).astype(BF16)
+        branch += lax.dot_general(
+            attended, matrix(3, s), (((0,), (0,)), ((), ())), preferred_element_type=F32
+        )
     y = x1 + mods(3) * branch
-    out_ref[...] = jnp.concatenate([y[per:], y[:per]], axis=0).astype(BF16)
+    y = jnp.concatenate([y[per:], y[:per]], axis=0)
+    out_ref[...] = y.astype(BF16)
 
 
 def temporal(ring, size, per, got, table, weights):
@@ -250,6 +260,37 @@
         ),
         name="temporal",
     )(got, in_hbm(table), in_hbm(weights))
+
+
+def last_kernel(line, tail_ref, got_ref, fresh_ref, out_ref):
+    rows = fresh_ref.shape[0]
+    per = rows // line
+    spot = lax.broadcasted_iota(jnp.int32, (2 * rows, 2 * rows), 1)
+    source = spot // per % 2 * rows + spot // (2 * per) * per + spot % per
+    back = (lax.broadcasted_iota(jnp.int32, (2 * rows, 2 * rows), 0) == source).astype(BF16)
+    values = jnp.dot(back, got_ref[...], preferred_element_type=F32).astype(BF16)
+    out_ref[0] = values[:rows]
+
+    @pl.when(tail_ref[0] == 0)
+    def _():
+        out_ref[1] = values[rows:]
+
+    @pl.when(tail_ref[0] != 0)
+    def _():
+        out_ref[1] = fresh_ref[...]
+
+
+def last(tail, line, got, fresh):
+    rows, width = fresh.shape
+    return pl.pallas_call(
+        lambda *refs: last_kernel(line, *refs),
+        out_shape=jax.ShapeDtypeStruct((2, rows, width), BF16),
+        in_specs=[pl.BlockSpec(memory_space=pltpu.SMEM), vspec(), vspec()],
+        out_specs=vspec(),
+        compiler_params=params(8),
+        cost_estimate=pl.CostEstimate(flops=40000000, bytes_accessed=1000000, transcendentals=0),
+        name="last",
+    )(tail, got, fresh)
 
 
 def per_device(
@@ -294,6 +335,8 @@
     )
 
     *hidden, side_rows = first(line, levels, mod_table, queue_tokens)
+    tail = (spot == line - 1).astype(jnp.int32)[None]
+    hidden[0], tail = lax.optimization_barrier((hidden[0], tail))
     frames = [{0: h} for h in hidden]
     reach = ((4, 3), (3, 4))
     for step in range(1, 5):
@@ -302,7 +345,6 @@
                 frames[j][-step] = send_up(frames[j][1 - step])
             if step <= reach[j][1]:
                 frames[j][step] = send_down(frames[j][step - 1])
-    chunks, *_ = lax.optimization_barrier((chunks, *[frames[j][o] for j in range(2) for o in (-1, 1)]))
     weights = lax.all_gather(chunks.reshape(ring * size, width), "queue", axis=0, tiled=False)
 
     offsets = [[0, 1, 2, 3, -4, -3, -2, -1], [0, 1, 2, 3, 4, -3, -2, -1]]
@@ -310,7 +352,7 @@
     mixed = spatial(
         offsets,
         place,
-        jnp.swapaxes(w_qkv_spatial, 1, 2),
+        jnp.swapaxes(w_qkv_spatial, 1, 2).reshape(3 * side, width),
         [frames[j][o] for j in range(2) for o in offsets[j]],
     )
     mixed = lax.all_to_all(mixed, "tok", 0, 0, tiled=True)
@@ -320,9 +362,7 @@
     got = lax.all_to_all(sent.reshape(line, 2 * per, sent.shape[1]), "queue", 0, 0, tiled=True)
     moved = temporal(ring, size, per, got.reshape(sent.shape), mod_table, weights)
     got = lax.all_to_all(moved.reshape(line, 2 * per, width), "queue", 0, 0, tiled=True)
-    got = jnp.transpose(got.reshape(line, 2, per, width), (1, 0, 2, 3)).reshape(2, rows, width)
-    tail = jnp.where(spot == line - 1, fresh_frame, got[1])
-    return jnp.stack([got[0], tail])
+    return last(tail, line, got.reshape(2 * rows, width), fresh_frame)
 
 
 def solution(mesh):

time: 150 us -> 140 us (0.933)
  blocking collectives: 44.8 us -> 81.7 us
  waiting for transfers between devices: 38 us -> 9.34 us
  starting transfers between devices: 30.6 us -> 16.1 us
  local copies, waits for them, and re-layouts: 3.3 us -> 0.47 us
    all_to_all x0 -> x2, blocking collectives: none -> 38 us  [the longest x1 23 us: per_device(): lax.all_to_all(jnp.broadcast_to(chunk[None], (ring, size, width)), 'tok',...]
    all_to_all x2 -> x0, starting transfers between devices: 14.5 us -> none  [the longest x1 9.01 us: per_device(): lax.all_to_all(jnp.broadcast_to(chunk[None], (ring, size, width)), 'tok',...]
    all_to_all x2 -> x0, waiting for transfers between devices: 9.22 us -> none  [the longest x1 9.21 us: per_device(): lax.all_to_all(moved.reshape(line, 2 * per, width), 'queue', 0, 0, tiled=...]
    ppermute x7, waiting for transfers between devices: 8.93 us -> 0.99 us  [send_down(): return lax.ppermute(v, 'tok', down)]
    all_gather x1, waiting for transfers between devices: 7.46 us -> 0.02 us  [per_device(): lax.all_gather(chunks.reshape(ring * size, width), 'queue', axis=0, tiled...]
    ppermute x7, waiting for transfers between devices: 12.4 us -> 8.31 us  [send_up(): return lax.ppermute(v, 'tok', up)]
    all_to_all x1, blocking collectives: 15.5 us -> 13.2 us  [per_device(): mixed = lax.all_to_all(mixed, 'tok', 0, 0, tiled=True)]
    ppermute x7, starting transfers between devices: 0.77 us -> 2.42 us  [send_up(): return lax.ppermute(v, 'tok', up)]
  transfers between devices with their start and end apart: 17 -> 15, of which waited for: 9 -> 6; matrix products, arithmetic and copies ran while one was open for 0% -> 0% of each run, Pallas kernels for 5% -> 5%
where the time goes in v5:
time: 140 us
  blocking collectives  81.7 us (58%)
  Pallas kernels  17.7 us (13%)
  starting transfers between devices  16.1 us (12%)
  between operations  13.5 us (10%)
  waiting for transfers between devices  9.34 us (7%)
    all_to_all x1, blocking collectives, per_device(): lax.all_to_all(sent.reshape(line, 2 * per, sent.shape[1]), 'queue', 0, 0,...  30.5 us
    all_to_all x1, blocking collectives, per_device(): lax.all_to_all(jnp.broadcast_to(chunk[None], (ring, size, width)), 'tok',...  23 us
    all_to_all x1, blocking collectives, per_device(): lax.all_to_all(moved.reshape(line, 2 * per, width), 'queue', 0, 0, tiled=...  14.9 us
    ppermute x7, starting transfers between devices, send_down(): return lax.ppermute(v, 'tok', down)  13.7 us
    all_to_all x1, blocking collectives, per_device(): mixed = lax.all_to_all(mixed, 'tok', 0, 0, tiled=True)  13.2 us
    pallas_call x1, Pallas kernels, temporal(): pl.pallas_call(lambda *refs: temporal_kernel(ring, size, per, *refs), out...  9.94 us
    ppermute x7, waiting for transfers between devices, send_up(): return lax.ppermute(v, 'tok', up)  8.31 us
    pallas_call x1, Pallas kernels, spatial(): pl.pallas_call(lambda *refs: spatial_kernel(offsets, *refs), out_shape=ja...  5.08 us
  transfers between devices with their start and end apart: 15, of which 6 were waited for; matrix products, arithmetic and copies ran while one was open for 0% of the time, Pallas kernels for 5%

profile of v5, /device:TPU:1, one launch (start us, length us, event | category | flops | bytes accessed | tf_op | source)
XLA Modules:
  0.0 139.9 jit_solution(15285555152152058534)
XLA Ops:
  6.5 0.0 all-gather.2.cloned.1.call-start
  6.5 1.0 select_select_fusion
  7.6 23.0 %all_to_all.20 = bf16[8,24,1152]{2,1,0:T(8,128)(2,1)} all-to-all(bf16[8,24,1152]{2,1,0:T(8,128)(2,1)S(1)} %broadcast_in_dim.18), channel_id=1, replica_groups=mesh['queue'=32,'tok'=8] {'tok'}, dimensions={0} | all-to-all | bytes 884736 | tf_op jit(solution)/shard_map/all_to_all | solution.py:333
  30.6 0.0 all-gather.2.cloned.1.call-update
  30.6 1.5 %first.1 = (bf16[64,1152]{1,0:T(8,128)(2,1)S(1)}, bf16[64,1152]{1,0:T(8,128)(2,1)S(1)}, bf16[128,1280]{1,0:T(8,128)(2,1)S(1)}) custom-call(s32[2]{0:T(128)} %refs_0_.1, f32[64,6912]{1,0:T(8,128)} %refs_1_.3, bf16[2,64,1152]{2,1,0:T(8,128)(2,1)} %refs_2_.2), custom_call_target="tpu_custom_call" | custom-call | flops 40000000 | bytes 1500000 | tf_op jit(solution)/shard_map/first/pallas_call | solution.py:74
  32.2 0.3 collective-permute-start.3
  32.5 2.4 %collective-permute-start.7 = (bf16[64,1152]{1,0:T(8,128)(2,1)S(1)}, bf16[64,1152]{1,0:T(8,128)(2,1)S(1)}, u32[]{:S(2)}, u32[]{:S(2)}) collective-permute-start(bf16[64,1152]{1,0:T(8,128)(2,1)S(1)} %get-tuple-element.13.refs_10_), channel_id=1, source_target_pairs={{0,7},{1,0},{2,1},{3,2},{4,3},{5,4},{6,5},{7,6},{8,15},{9,8},{10,9... | collective-permute-start | bytes 442376 | tf_op jit(solution)/shard_map/ppermute | solution.py:317
  34.9 0.0 collective-permute-start
  34.9 1.4 %collective-permute-start.11 = (bf16[64,1152]{1,0:T(8,128)(2,1)S(1)}, bf16[64,1152]{1,0:T(8,128)(2,1)S(1)}, u32[]{:S(2)}, u32[]{:S(2)}) collective-permute-start(bf16[64,1152]{1,0:T(8,128)(2,1)S(1)} %get-tuple-element.13.refs_10_), channel_id=1, source_target_pairs={{0,1},{1,2},{2,3},{3,4},{4,5},{5,6},{6,7},{7,0},{8,9},{9,10},{10,1... | collective-permute-start | bytes 442376 | tf_op jit(solution)/shard_map/ppermute | solution.py:314
  36.4 1.1 collective-permute-done.3.refs_9_
  37.4 0.0 collective-permute-start.4
  37.4 0.0 collective-permute-done.7.refs_11_
  37.4 2.7 %collective-permute-start.8 = (bf16[64,1152]{1,0:T(8,128)(2,1)S(1)}, bf16[64,1152]{1,0:T(8,128)(2,1)S(1)}, u32[]{:S(2)}, u32[]{:S(2)}) collective-permute-start(bf16[64,1152]{1,0:T(8,128)(2,1)S(1)} %collective-permute-done.7.refs_11_), channel_id=1, source_target_pairs={{0,7},{1,0},{2,1},{3,2},{4,3},{5,4},{6,5},{7,6},{8,15},{9,8},{10,9... | collective-permute-start | bytes 442376 | tf_op jit(solution)/shard_map/ppermute | solution.py:317
  40.1 0.0 collective-permute-done.refs_3_
  40.1 1.6 %collective-permute-start.1 = (bf16[64,1152]{1,0:T(8,128)(2,1)S(1)}, bf16[64,1152]{1,0:T(8,128)(2,1)S(1)}, u32[]{:S(2)}, u32[]{:S(2)}) collective-permute-start(bf16[64,1152]{1,0:T(8,128)(2,1)S(1)} %collective-permute-done.refs_3_), channel_id=1, source_target_pairs={{0,7},{1,0},{2,1},{3,2},{4,3},{5,4},{6,5},{7,6},{8,15},{9,8},{10,9... | collective-permute-start | bytes 442376 | tf_op jit(solution)/shard_map/ppermute | solution.py:317
  41.7 0.0 collective-permute-done.11.refs_17_
  41.7 0.0 collective-permute-start.12
  41.7 3.0 %collective-permute-done.4.refs_8_ = bf16[64,1152]{1,0:T(8,128)(2,1)S(1)} collective-permute-done((bf16[64,1152]{1,0:T(8,128)(2,1)S(1)}, bf16[64,1152]{1,0:T(8,128)(2,1)S(1)}, u32[]{:S(2)}, u32[]{:S(2)}) %collective-permute-start.4) | collective-permute-done | bytes 147488 | tf_op jit(solution)/shard_map/ppermute | solution.py:314
  44.7 0.0 collective-permute-start.5
  44.7 0.0 collective-permute-done.8.refs_12_
  44.7 2.7 %collective-permute-start.9 = (bf16[64,1152]{1,0:T(8,128)(2,1)S(1)}, bf16[64,1152]{1,0:T(8,128)(2,1)S(1)}, u32[]{:S(2)}, u32[]{:S(2)}) collective-permute-start(bf16[64,1152]{1,0:T(8,128)(2,1)S(1)} %collective-permute-done.8.refs_12_), channel_id=1, source_target_pairs={{0,7},{1,0},{2,1},{3,2},{4,3},{5,4},{6,5},{7,6},{8,15},{9,8},{10,9... | collective-permute-start | bytes 442376 | tf_op jit(solution)/shard_map/ppermute | solution.py:317
  47.4 0.0 collective-permute-done.1.refs_4_
  47.4 0.8 collective-permute-start.2
  48.2 0.0 collective-permute-done.12.refs_16_
  48.2 0.6 collective-permute-start.13
  48.8 1.2 collective-permute-done.5.refs_7_
  50.1 0.0 collective-permute-start.6
  50.1 1.0 collective-permute-done.9.refs_13_
  51.0 3.5 %collective-permute-start.10 = (bf16[64,1152]{1,0:T(8,128)(2,1)S(1)}, bf16[64,1152]{1,0:T(8,128)(2,1)S(1)}, u32[]{:S(2)}, u32[]{:S(2)}) collective-permute-start(bf16[64,1152]{1,0:T(8,128)(2,1)S(1)} %collective-permute-done.9.refs_13_), channel_id=1, source_target_pairs={{0,7},{1,0},{2,1},{3,2},{4,3},{5,4},{6,5},{7,6},{8,15},{9,8},{10,9... | collective-permute-start | bytes 442376 | tf_op jit(solution)/shard_map/ppermute | solution.py:317
  54.6 0.0 collective-permute-done.2.refs_5_
  54.6 0.7 collective-permute-done.13.refs_15_
  55.3 2.3 %collective-permute-done.6.refs_6_ = bf16[64,1152]{1,0:T(8,128)(2,1)S(1)} collective-permute-done((bf16[64,1152]{1,0:T(8,128)(2,1)S(1)}, bf16[64,1152]{1,0:T(8,128)(2,1)S(1)}, u32[]{:S(2)}, u32[]{:S(2)}) %collective-permute-start.6) | collective-permute-done | bytes 147488 | tf_op jit(solution)/shard_map/ppermute | solution.py:314
  57.6 0.0 collective-permute-done.10.refs_14_
  57.6 0.0 copy-start
  57.6 5.1 %spatial.1 = bf16[8,144,128]{2,1,0:T(8,128)(2,1)S(1)} custom-call(s32[1]{0:T(128)} %bitcast.1.refs_0_, bf16[432,1152]{1,0:T(8,128)(2,1)} %bitcast.11, bf16[64,1152]{1,0:T(8,128)(2,1)S(1)} %get-tuple-element.12.refs_2_, bf16[64,1152]{1,0:T(8,128)(2,1)S(1)} %collective-permute-done.refs_3_, bf16[64,1152]{1,0:T(8,128)(2,1)S(1)} %collective-permute-done.1.refs_4_, ...), custom_call_target="tpu_custom_call" | custom-call | flops 1556086784 | bytes 5000000 | tf_op jit(solution)/shard_map/spatial/pallas_call | solution.py:125
  62.7 13.2 %all_to_all.21.refs_0_ = bf16[8,144,128]{2,1,0:T(8,128)(2,1)S(1)} all-to-all(bf16[8,144,128]{2,1,0:T(8,128)(2,1)S(1)} %spatial.1), channel_id=1, replica_groups=mesh['queue'=32,'tok'=8] {'tok'}, dimensions={0} | all-to-all | bytes 589824 | tf_op jit(solution)/shard_map/all_to_all | solution.py:358
  75.9 0.2 bundle.1
  76.2 0.1 reshape.20
  76.3 30.5 %all_to_all.22 = bf16[32,4,2432]{2,1,0:T(4,128)(2,1)S(1)} all-to-all(bf16[32,4,2432]{2,1,0:T(4,128)(2,1)S(1)} %reshape.20), channel_id=1, replica_groups=mesh['queue'=32,'tok'=8] {'queue'}, dimensions={0} | all-to-all | bytes 1245184 | tf_op jit(solution)/shard_map/all_to_all | solution.py:362
  106.8 0.1 reshape.21.refs_0_
  107.0 0.0 all-gather.2.cloned.1.call-done.refs_2_
  107.0 9.9 %temporal.1 = bf16[128,1152]{1,0:T(8,128)(2,1)S(1)} custom-call(bf16[128,2432]{1,0:T(8,128)(2,1)S(1)} %reshape.21.refs_0_, f32[64,6912]{1,0:T(8,128)} %refs_1_.3, bf16[32,192,1152]{2,1,0:T(8,128)(2,1)} %all-gather.2.cloned.1.call-done.refs_2_), custom_call_target="tpu_custom_call" | custom-call | flops 1698693120 | bytes 15000000 | tf_op jit(solution)/shard_map/temporal/pallas_call | solution.py:247
  117.0 0.1 reshape.23
  117.0 14.9 %all_to_all.23 = bf16[32,4,1152]{2,1,0:T(4,128)(2,1)S(1)} all-to-all(bf16[32,4,1152]{2,1,0:T(4,128)(2,1)S(1)} %reshape.23), channel_id=1, replica_groups=mesh['queue'=32,'tok'=8] {'queue'}, dimensions={0} | all-to-all | bytes 589824 | tf_op jit(solution)/shard_map/all_to_all | solution.py:364
  132.0 0.1 reshape.24.refs_1_
  132.1 0.0 copy-done
  132.1 1.0 last.1
  (1 shorter events, 0.0 us)
Async XLA Ops:
  6.5 100.5 %all-gather.2.cloned.1.call-start = ((), (), s32[]{:S(2)}) async-start(), calls=%async_computation.4 | async-start | bytes 14598144 | tf_op jit(solution)/shard_map/all_gather | solution.py:348
  32.2 5.3 %collective-permute-start.3 = (bf16[64,1152]{1,0:T(8,128)(2,1)S(1)}, bf16[64,1152]{1,0:T(8,128)(2,1)S(1)}, u32[]{:S(2)}, u32[]{:S(2)}) collective-permute-start(bf16[64,1152]{1,0:T(8,128)(2,1)S(1)} %get-tuple-element.12.refs_2_), channel_id=1, source_target_pairs={{0,1},{1,2},{2,3},{3,4},{4,5},{5,6},{6,7},{7,0},{8,9},{9,10},{10,1... | collective-permute-start | bytes 442376 | tf_op jit(solution)/shard_map/ppermute | solution.py:314
  32.5 5.0 %collective-permute-start.7 = (bf16[64,1152]{1,0:T(8,128)(2,1)S(1)}, bf16[64,1152]{1,0:T(8,128)(2,1)S(1)}, u32[]{:S(2)}, u32[]{:S(2)}) collective-permute-start(bf16[64,1152]{1,0:T(8,128)(2,1)S(1)} %get-tuple-element.13.refs_10_), channel_id=1, source_target_pairs={{0,7},{1,0},{2,1},{3,2},{4,3},{5,4},{6,5},{7,6},{8,15},{9,8},{10,9... | collective-permute-start | bytes 442376 | tf_op jit(solution)/shard_map/ppermute | solution.py:317
  34.9 5.2 %collective-permute-start = (bf16[64,1152]{1,0:T(8,128)(2,1)S(1)}, bf16[64,1152]{1,0:T(8,128)(2,1)S(1)}, u32[]{:S(2)}, u32[]{:S(2)}) collective-permute-start(bf16[64,1152]{1,0:T(8,128)(2,1)S(1)} %get-tuple-element.12.refs_2_), channel_id=1, source_target_pairs={{0,7},{1,0},{2,1},{3,2},{4,3},{5,4},{6,5},{7,6},{8,15},{9,8},{10,9... | collective-permute-start | bytes 442376 | tf_op jit(solution)/shard_map/ppermute | solution.py:317
  34.9 6.8 %collective-permute-start.11 = (bf16[64,1152]{1,0:T(8,128)(2,1)S(1)}, bf16[64,1152]{1,0:T(8,128)(2,1)S(1)}, u32[]{:S(2)}, u32[]{:S(2)}) collective-permute-start(bf16[64,1152]{1,0:T(8,128)(2,1)S(1)} %get-tuple-element.13.refs_10_), channel_id=1, source_target_pairs={{0,1},{1,2},{2,3},{3,4},{4,5},{5,6},{6,7},{7,0},{8,9},{9,10},{10,1... | collective-permute-start | bytes 442376 | tf_op jit(solution)/shard_map/ppermute | solution.py:314
  37.4 7.2 %collective-permute-start.4 = (bf16[64,1152]{1,0:T(8,128)(2,1)S(1)}, bf16[64,1152]{1,0:T(8,128)(2,1)S(1)}, u32[]{:S(2)}, u32[]{:S(2)}) collective-permute-start(bf16[64,1152]{1,0:T(8,128)(2,1)S(1)} %collective-permute-done.3.refs_9_), channel_id=1, source_target_pairs={{0,1},{1,2},{2,3},{3,4},{4,5},{5,6},{6,7},{7,0},{8,9},{9,10},{10,1... | collective-permute-start | bytes 442376 | tf_op jit(solution)/shard_map/ppermute | solution.py:314
  37.4 7.2 %collective-permute-start.8 = (bf16[64,1152]{1,0:T(8,128)(2,1)S(1)}, bf16[64,1152]{1,0:T(8,128)(2,1)S(1)}, u32[]{:S(2)}, u32[]{:S(2)}) collective-permute-start(bf16[64,1152]{1,0:T(8,128)(2,1)S(1)} %collective-permute-done.7.refs_11_), channel_id=1, source_target_pairs={{0,7},{1,0},{2,1},{3,2},{4,3},{5,4},{6,5},{7,6},{8,15},{9,8},{10,9... | collective-permute-start | bytes 442376 | tf_op jit(solution)/shard_map/ppermute | solution.py:317
  40.1 7.2 %collective-permute-start.1 = (bf16[64,1152]{1,0:T(8,128)(2,1)S(1)}, bf16[64,1152]{1,0:T(8,128)(2,1)S(1)}, u32[]{:S(2)}, u32[]{:S(2)}) collective-permute-start(bf16[64,1152]{1,0:T(8,128)(2,1)S(1)} %collective-permute-done.refs_3_), channel_id=1, source_target_pairs={{0,7},{1,0},{2,1},{3,2},{4,3},{5,4},{6,5},{7,6},{8,15},{9,8},{10,9... | collective-permute-start | bytes 442376 | tf_op jit(solution)/shard_map/ppermute | solution.py:317
  41.7 6.5 %collective-permute-start.12 = (bf16[64,1152]{1,0:T(8,128)(2,1)S(1)}, bf16[64,1152]{1,0:T(8,128)(2,1)S(1)}, u32[]{:S(2)}, u32[]{:S(2)}) collective-permute-start(bf16[64,1152]{1,0:T(8,128)(2,1)S(1)} %collective-permute-done.11.refs_17_), channel_id=1, source_target_pairs={{0,1},{1,2},{2,3},{3,4},{4,5},{5,6},{6,7},{7,0},{8,9},{9,10},{10,1... | collective-permute-start | bytes 442376 | tf_op jit(solution)/shard_map/ppermute | solution.py:314
  44.7 5.4 %collective-permute-start.5 = (bf16[64,1152]{1,0:T(8,128)(2,1)S(1)}, bf16[64,1152]{1,0:T(8,128)(2,1)S(1)}, u32[]{:S(2)}, u32[]{:S(2)}) collective-permute-start(bf16[64,1152]{1,0:T(8,128)(2,1)S(1)} %collective-permute-done.4.refs_8_), channel_id=1, source_target_pairs={{0,1},{1,2},{2,3},{3,4},{4,5},{5,6},{6,7},{7,0},{8,9},{9,10},{10,1... | collective-permute-start | bytes 442376 | tf_op jit(solution)/shard_map/ppermute | solution.py:314
  44.7 6.4 %collective-permute-start.9 = (bf16[64,1152]{1,0:T(8,128)(2,1)S(1)}, bf16[64,1152]{1,0:T(8,128)(2,1)S(1)}, u32[]{:S(2)}, u32[]{:S(2)}) collective-permute-start(bf16[64,1152]{1,0:T(8,128)(2,1)S(1)} %collective-permute-done.8.refs_12_), channel_id=1, source_target_pairs={{0,7},{1,0},{2,1},{3,2},{4,3},{5,4},{6,5},{7,6},{8,15},{9,8},{10,9... | collective-permute-start | bytes 442376 | tf_op jit(solution)/shard_map/ppermute | solution.py:317
  47.4 7.2 %collective-permute-start.2 = (bf16[64,1152]{1,0:T(8,128)(2,1)S(1)}, bf16[64,1152]{1,0:T(8,128)(2,1)S(1)}, u32[]{:S(2)}, u32[]{:S(2)}) collective-permute-start(bf16[64,1152]{1,0:T(8,128)(2,1)S(1)} %collective-permute-done.1.refs_4_), channel_id=1, source_target_pairs={{0,7},{1,0},{2,1},{3,2},{4,3},{5,4},{6,5},{7,6},{8,15},{9,8},{10,9... | collective-permute-start | bytes 442376 | tf_op jit(solution)/shard_map/ppermute | solution.py:317
  48.2 7.1 %collective-permute-start.13 = (bf16[64,1152]{1,0:T(8,128)(2,1)S(1)}, bf16[64,1152]{1,0:T(8,128)(2,1)S(1)}, u32[]{:S(2)}, u32[]{:S(2)}) collective-permute-start(bf16[64,1152]{1,0:T(8,128)(2,1)S(1)} %collective-permute-done.12.refs_16_), channel_id=1, source_target_pairs={{0,1},{1,2},{2,3},{3,4},{4,5},{5,6},{6,7},{7,0},{8,9},{9,10},{10,1... | collective-permute-start | bytes 442376 | tf_op jit(solution)/shard_map/ppermute | solution.py:314
  50.1 7.5 %collective-permute-start.6 = (bf16[64,1152]{1,0:T(8,128)(2,1)S(1)}, bf16[64,1152]{1,0:T(8,128)(2,1)S(1)}, u32[]{:S(2)}, u32[]{:S(2)}) collective-permute-start(bf16[64,1152]{1,0:T(8,128)(2,1)S(1)} %collective-permute-done.5.refs_7_), channel_id=1, source_target_pairs={{0,1},{1,2},{2,3},{3,4},{4,5},{5,6},{6,7},{7,0},{8,9},{9,10},{10,1... | collective-permute-start | bytes 442376 | tf_op jit(solution)/shard_map/ppermute | solution.py:314
  51.0 6.6 %collective-permute-start.10 = (bf16[64,1152]{1,0:T(8,128)(2,1)S(1)}, bf16[64,1152]{1,0:T(8,128)(2,1)S(1)}, u32[]{:S(2)}, u32[]{:S(2)}) collective-permute-start(bf16[64,1152]{1,0:T(8,128)(2,1)S(1)} %collective-permute-done.9.refs_13_), channel_id=1, source_target_pairs={{0,7},{1,0},{2,1},{3,2},{4,3},{5,4},{6,5},{7,6},{8,15},{9,8},{10,9... | collective-permute-start | bytes 442376 | tf_op jit(solution)/shard_map/ppermute | solution.py:317
  57.6 74.5 %copy-start = (bf16[64,1152]{1,0:T(8,128)(2,1)S(1)}, bf16[64,1152]{1,0:T(8,128)(2,1)}, u32[]{:S(2)}) copy-start(bf16[64,1152]{1,0:T(8,128)(2,1)} %refs_2_.3) | copy-start | bytes 442372
Sparse Core Ops, SparseCore 0:
  30.8 75.8 all-gather.1

commit v6 on v5

--- a/solution.py
+++ b/solution.py
@@ -86,6 +86,25 @@
         cost_estimate=pl.CostEstimate(flops=40000000, bytes_accessed=1500000, transcendentals=0),
         name="first",
     )(in_hbm(levels), in_hbm(table), in_hbm(tokens))
+
+
+def others_kernel(place_ref, chunks_ref, out_ref):
+    ring, size, width = chunks_ref.shape
+    pieces = [chunks_ref[lax.rem(place_ref[0] + offset, ring)].astype(F32) for offset in range(1, ring)]
+    spare = out_ref.shape[0] - (ring - 1) * size
+    out_ref[...] = jnp.concatenate(pieces + [jnp.zeros((spare, width), F32)], axis=0).astype(BF16)
+
+
+def others(place, chunks, rows):
+    return pl.pallas_call(
+        others_kernel,
+        out_shape=jax.ShapeDtypeStruct((rows, chunks.shape[2]), BF16),
+        in_specs=[pl.BlockSpec(memory_space=pltpu.SMEM), vspec()],
+        out_specs=vspec(),
+        compiler_params=params(8),
+        cost_estimate=pl.CostEstimate(flops=0, bytes_accessed=900000, transcendentals=0),
+        name="others",
+    )(place, chunks)
 
 
 def spatial_kernel(offsets, place_ref, w_hbm, *refs):
@@ -139,57 +158,72 @@
     )(place, in_hbm(w_qkv), *blocks)
 
 
-def bundle_kernel(line, size, mixed_ref, side_ref, out_ref):
+def bundle_kernel(line, size, group, place_ref, mixed_ref, side_ref, out_ref):
     ring, side, rows = mixed_ref.shape
     width = ring * side
-    mixed = jnp.concatenate(
-        [mixed_ref[z, a * size : (a + 1) * size].astype(F32) for a in range(side // size) for z in range(ring)],
-        axis=0,
-    ).astype(BF16)
+    pieces = []
+    for s in range(2):
+        for k in range(3 * s, 3 * s + 3):
+            for offset in range(1, ring):
+                z = lax.rem(place_ref[0] + offset, ring)
+                pieces.append(mixed_ref[z, k * size : (k + 1) * size].astype(F32))
+            pieces.append(jnp.zeros((group - (ring - 1) * size, rows), F32))
+        if s == 0:
+            pieces.append(mixed_ref[place_ref[0]].astype(F32))
+    mixed = jnp.concatenate(pieces, axis=0).astype(BF16)
     moved, _ = order_matrix(line, rows)
-    out_ref[:, :width] = turned(moved, mixed).astype(BF16)
-    out_ref[:, width:] = side_ref[...]
-
-
-def bundle(line, size, mixed, tokens):
+    end = width + mixed.shape[0]
+    out_ref[:, :width] = side_ref[:, :width]
+    out_ref[:, width:end] = turned(moved, mixed).astype(BF16)
+    out_ref[:, end:] = side_ref[:, width : width + out_ref.shape[1] - end]
+
+
+def bundle(line, size, group, place, mixed, tokens):
     ring, side, rows = mixed.shape
-    return pl.pallas_call(
-        lambda *refs: bundle_kernel(line, size, *refs),
-        out_shape=jax.ShapeDtypeStruct((rows, ring * side + tokens.shape[1]), BF16),
-        in_specs=[vspec(), vspec()],
+    whole = ring * side + 6 * group + side
+    lanes = -(-(whole + 64) // 128) * 128
+    return pl.pallas_call(
+        lambda *refs: bundle_kernel(line, size, group, *refs),
+        out_shape=jax.ShapeDtypeStruct((rows, lanes), BF16),
+        in_specs=[pl.BlockSpec(memory_space=pltpu.SMEM), vspec(), vspec()],
         out_specs=vspec(),
         compiler_params=params(12),
         cost_estimate=pl.CostEstimate(flops=40000000, bytes_accessed=1500000, transcendentals=0),
         name="bundle",
-    )(mixed, tokens)
-
-
-def temporal_kernel(ring, size, per, got_ref, table_hbm, weights_hbm, out_ref, held, table_ref, sems):
-    depth, width = held.shape[1:]
-    some = 6 // 2
-    half = width // 2
-
-    def copy(n):
-        part = pl.ds(n * some, some)
-        return pltpu.make_async_copy(weights_hbm.at[part], held.at[part], sems.at[n])
+    )(place, mixed, tokens)
+
+
+def temporal_kernel(
+    size, per, got_ref, table_hbm, own_qkv, own_temporal, own_spatial, weights_hbm, out_ref, one_ref, two_ref, table_ref, sems
+):
+    group, width = weights_hbm.shape[1:]
+    side = own_temporal.shape[0]
+    ring = width // side
+    held = (one_ref, two_ref)
+    gathered = 3 * group
+
+    def start(m, s):
+        for k in range(3):
+            pltpu.make_async_copy(
+                weights_hbm.at[6 * m + 3 * s + k], held[s].at[m, pl.ds(k * group, group)], sems.at[2 * m + s]
+            ).start()
+        if s == 0:
+            own = own_qkv.at[m] if m < 3 else (own_temporal, own_spatial)[m - 3]
+            pltpu.make_async_copy(own, one_ref.at[m, pl.ds(gathered, side)], sems.at[2 * m]).start()
 
     table_copy = pltpu.make_async_copy(table_hbm.at[:, pl.ds(2 * width, 4 * width)], table_ref, sems.at[10])
-    for n in (8, 9):
-        copy(n).start()
     table_copy.start()
-    for n in range(8):
-        copy(n).start()
+    for m, s in ((4, 0), (4, 1), (0, 0), (1, 0), (2, 0), (3, 0), (0, 1), (1, 1), (2, 1), (3, 1)):
+        start(m, s)
     rows = got_ref.shape[0]
 
     def matrix(m, s):
-        n = 2 * m + s
-        copy(n).wait()
-        return held[n * some : (n + 1) * some].reshape(half, width)
-
-    branch = jnp.zeros((rows, width), F32)
-    for s in range(2):
-        branch += jnp.dot(got_ref[:, s * half : (s + 1) * half], matrix(4, s), preferred_element_type=F32)
-    level = got_ref[:, 2 * width :].astype(F32)[:, : table_ref.shape[0]]
+        pltpu.make_async_copy(held[s].at[m], held[s].at[m], sems.at[2 * m + s]).wait()
+        return held[s][m]
+
+    split = width + gathered + side
+    end = split + gathered
+    level = got_ref[:, end : end + table_ref.shape[0]].astype(F32)
     column = lax.broadcasted_iota(jnp.int32, level.shape, 1).astype(F32)
     onehot = (level == column).astype(BF16)
     table_copy.wait()
@@ -202,55 +236,63 @@
             onehot, small, preferred_element_type=F32
         )
 
-    x1 = got_ref[:, width : 2 * width].astype(F32) + mods(0) * branch
-    hidden = (normalize(x1) * (1.0 + mods(2)) + mods(1)).astype(BF16)
-
-    row = lax.broadcasted_iota(jnp.int32, (half, 1), 0)
-    owner = row // size % ring
-    along = lax.broadcasted_iota(jnp.int32, (rows, ring * rows), 0) % per
-    across = lax.broadcasted_iota(jnp.int32, (rows, ring * rows), 1) % per
-    same = along == across
-
-    query = [turned(matrix(0, s), hidden) for s in range(2)]
-    keyed = [turned(hidden, matrix(1, s)).astype(BF16) for s in range(2)]
-    valued = [turned(matrix(2, s), hidden).astype(BF16) for s in range(2)]
+    gate1, shift2, scale2, gate2 = [mods(n) for n in range(4)]
+    branch = jnp.dot(got_ref[:, width:split], matrix(4, 0), preferred_element_type=F32)
+    branch += jnp.dot(got_ref[:, split:end], matrix(4, 1), preferred_element_type=F32)
+    x1 = got_ref[:, :width].astype(F32) + gate1 * branch
+    hidden = (normalize(x1) * (1.0 + scale2) + shift2).astype(BF16)
+
     branch = jnp.zeros((rows, width), F32)
     for s in range(2):
+        heads = ring + 1 if s == 0 else ring - 1
+        query = turned(matrix(0, s), hidden)
+        keyed = turned(hidden, matrix(1, s)).astype(BF16)
+        valued = turned(matrix(2, s), hidden).astype(BF16)
+        row = lax.broadcasted_iota(jnp.int32, (query.shape[0], 1), 0)
+        inside = row % group
+        owner = jnp.where(inside < (ring - 1) * size, inside // size, -1)
+        owner = jnp.where(row >= gathered, ring - 1 + (row - gathered) // HDIM, owner)
+        along = lax.broadcasted_iota(jnp.int32, (rows, heads * rows), 0) % per
+        across = lax.broadcasted_iota(jnp.int32, (rows, heads * rows), 1) % per
         spread = jnp.concatenate(
-            [jnp.where(owner == z, query[s], 0.0).astype(BF16) for z in range(ring)], axis=1
+            [jnp.where(owner == h, query, 0.0).astype(BF16) for h in range(heads)], axis=1
         )
-        scores = FACTOR * jnp.dot(keyed[s], spread, preferred_element_type=F32)
-        scores = jnp.where(same, scores, -jnp.inf)
+        scores = FACTOR * jnp.dot(keyed, spread, preferred_element_type=F32)
+        scores = jnp.where(along == across, scores, -jnp.inf)
         weights = jnp.exp(scores - jnp.max(scores, axis=0, keepdims=True))
         inverse = 1.0 / jnp.sum(weights, axis=0, keepdims=True)
-        mixed = jnp.dot(valued[s], weights.astype(BF16), preferred_element_type=F32)
-        attended = jnp.concatenate(
-            [
-                mixed[a * depth + z * size : a * depth + (z + 1) * size, z * rows : (z + 1) * rows]
-                * inverse[:, z * rows : (z + 1) * rows]
-                for a in range(some)
-                for z in range(ring)
-            ],
-            axis=0,
-        ).astype(BF16)
+        mixed = jnp.dot(valued, weights.astype(BF16), preferred_element_type=F32)
+
+        def piece(first_row, count, h):
+            columns = slice(h * rows, (h + 1) * rows)
+            return mixed[first_row : first_row + count, columns] * inverse[:, columns]
+
+        pieces = []
+        for k in range(3):
+            pieces += [piece(k * group + h * size, size, h) for h in range(ring - 1)]
+            pieces.append(jnp.zeros((group - (ring - 1) * size, rows), F32))
+        pieces += [piece(gathered + (h - ring + 1) * HDIM, HDIM, h) for h in range(ring - 1, heads)]
+        attended = jnp.concatenate(pieces, axis=0).astype(BF16)
         branch += lax.dot_general(
             attended, matrix(3, s), (((0,), (0,)), ((), ())), preferred_element_type=F32
         )
-    y = x1 + mods(3) * branch
+    y = x1 + gate2 * branch
     y = jnp.concatenate([y[per:], y[:per]], axis=0)
     out_ref[...] = y.astype(BF16)
 
 
-def temporal(ring, size, per, got, table, weights):
-    _, depth, width = weights.shape
+def temporal(size, per, got, table, own, weights):
+    group, width = weights.shape[1:]
+    side = own[1].shape[0]
     rows = got.shape[0]
     return pl.pallas_call(
-        lambda *refs: temporal_kernel(ring, size, per, *refs),
+        lambda *refs: temporal_kernel(size, per, *refs),
         out_shape=jax.ShapeDtypeStruct((rows, width), BF16),
-        in_specs=[vspec(), pl.BlockSpec(memory_space=pl.ANY), pl.BlockSpec(memory_space=pl.ANY)],
+        in_specs=[vspec()] + [pl.BlockSpec(memory_space=pl.ANY)] * 5,
         out_specs=vspec(),
         scratch_shapes=[
-            VMEM((30, depth, width), BF16),
+            VMEM((5, 3 * group + side, width), BF16),
+            VMEM((5, 3 * group, width), BF16),
             VMEM((table.shape[0], 4 * width), F32),
             pltpu.SemaphoreType.DMA((11,)),
         ],
@@ -259,7 +301,7 @@
             flops=2 * rows * width * width * 5, bytes_accessed=15000000, transcendentals=16 * rows * rows
         ),
         name="temporal",
-    )(got, in_hbm(table), in_hbm(weights))
+    )(got, in_hbm(table), *[in_hbm(v) for v in own], in_hbm(weights))
 
 
 def last_kernel(line, tail_ref, got_ref, fresh_ref, out_ref):
@@ -330,13 +372,14 @@
         rows_from(turned_qkv, 0),
         jnp.where(start < 4 * side, rows_from(w_out_temporal, 3 * side), rows_from(w_out_spatial, 4 * side)),
     )
+    place = lax.axis_index("tok").astype(jnp.int32)[None]
+    tail = (spot == line - 1).astype(jnp.int32)[None]
+    chunk, place, tail = lax.optimization_barrier((chunk, place, tail))
     chunks = lax.all_to_all(
         jnp.broadcast_to(chunk[None], (ring, size, width)), "tok", 0, 0, tiled=True
     )
 
     *hidden, side_rows = first(line, levels, mod_table, queue_tokens)
-    tail = (spot == line - 1).astype(jnp.int32)[None]
-    hidden[0], tail = lax.optimization_barrier((hidden[0], tail))
     frames = [{0: h} for h in hidden]
     reach = ((4, 3), (3, 4))
     for step in range(1, 5):
@@ -345,10 +388,10 @@
                 frames[j][-step] = send_up(frames[j][1 - step])
             if step <= reach[j][1]:
                 frames[j][step] = send_down(frames[j][step - 1])
-    weights = lax.all_gather(chunks.reshape(ring * size, width), "queue", axis=0, tiled=False)
+    group = -(-(ring - 1) * size // 16) * 16
+    weights = lax.all_gather(others(place, chunks, group), "queue", axis=0, tiled=False)
 
     offsets = [[0, 1, 2, 3, -4, -3, -2, -1], [0, 1, 2, 3, 4, -3, -2, -1]]
-    place = lax.axis_index("tok").astype(jnp.int32)[None]
     mixed = spatial(
         offsets,
         place,
@@ -358,9 +401,10 @@
     mixed = lax.all_to_all(mixed, "tok", 0, 0, tiled=True)
 
     per = rows // line
-    sent = bundle(line, size, mixed, side_rows)
+    sent = bundle(line, size, group, place, mixed, side_rows)
     got = lax.all_to_all(sent.reshape(line, 2 * per, sent.shape[1]), "queue", 0, 0, tiled=True)
-    moved = temporal(ring, size, per, got.reshape(sent.shape), mod_table, weights)
+    own = (turned_qkv.reshape(3, side, width), w_out_temporal, w_out_spatial)
+    moved = temporal(size, per, got.reshape(sent.shape), mod_table, own, weights)
     got = lax.all_to_all(moved.reshape(line, 2 * per, width), "queue", 0, 0, tiled=True)
     return last(tail, line, got.reshape(2 * rows, width), fresh_frame)
 

time: 140 us -> 137 us (0.979)
  blocking collectives: 81.7 us -> 77.3 us
  Pallas kernels: 17.7 us -> 19.1 us
    all_to_all x1, blocking collectives: 30.5 us -> 27.9 us  [per_device(): lax.all_to_all(sent.reshape(line, 2 * per, sent.shape[1]), 'queue', 0, 0,...]
    all_to_all x1, blocking collectives: 14.9 us -> 13.1 us  [per_device(): lax.all_to_all(moved.reshape(line, 2 * per, width), 'queue', 0, 0, tiled=...]
    pallas_call x2 -> x3, Pallas kernels: 10.2 us -> 11.6 us  [the longest x1 10.5 us: temporal(): pl.pallas_call(lambda *refs: temporal_kernel(size, per, *refs), out_shape...]
where the time goes in v6:
time: 137 us
  blocking collectives  77.3 us (56%)
  Pallas kernels  19.1 us (14%)
  starting transfers between devices  16.1 us (12%)
  between operations  13.5 us (10%)
  waiting for transfers between devices  9.34 us (7%)
    all_to_all x1, blocking collectives, per_device(): lax.all_to_all(sent.reshape(line, 2 * per, sent.shape[1]), 'queue', 0, 0,...  27.9 us
    all_to_all x1, blocking collectives, per_device(): lax.all_to_all(jnp.broadcast_to(chunk[None], (ring, size, width)), 'tok',...  22.9 us
    ppermute x7, starting transfers between devices, send_down(): return lax.ppermute(v, 'tok', down)  13.7 us
    all_to_all x1, blocking collectives, per_device(): mixed = lax.all_to_all(mixed, 'tok', 0, 0, tiled=True)  13.4 us
    all_to_all x1, blocking collectives, per_device(): lax.all_to_all(moved.reshape(line, 2 * per, width), 'queue', 0, 0, tiled=...  13.1 us
    pallas_call x1, Pallas kernels, temporal(): pl.pallas_call(lambda *refs: temporal_kernel(size, per, *refs), out_shape...  10.5 us
    ppermute x7, waiting for transfers between devices, send_up(): return lax.ppermute(v, 'tok', up)  8.31 us
    pallas_call x1, Pallas kernels, spatial(): pl.pallas_call(lambda *refs: spatial_kernel(offsets, *refs), out_shape=ja...  5.06 us
  transfers between devices with their start and end apart: 15, of which 6 were waited for; matrix products, arithmetic and copies ran while one was open for 0% of the time, Pallas kernels for 5%

profile of v6, /device:TPU:1, one launch (start us, length us, event | category | flops | bytes accessed | tf_op | source)
XLA Modules:
  0.0 136.9 jit_solution(16826973068382993382)
XLA Ops:
  6.5 0.0 all-gather.3.cloned.1.call-start
  6.5 1.0 select_select_fusion
  7.6 22.9 %all_to_all.20.chunks_ref = bf16[8,24,1152]{2,1,0:T(8,128)(2,1)S(1)} all-to-all(bf16[8,24,1152]{2,1,0:T(8,128)(2,1)S(1)} %broadcast_in_dim.18), channel_id=1, replica_groups=mesh['queue'=32,'tok'=8] {'tok'}, dimensions={0} | all-to-all | bytes 884736 | tf_op jit(solution)/shard_map/all_to_all | solution.py:378
  30.5 0.8 others.1
  31.3 0.0 all-gather.3.cloned.1.call-update
  31.3 1.5 %first.1 = (bf16[64,1152]{1,0:T(8,128)(2,1)S(1)}, bf16[64,1152]{1,0:T(8,128)(2,1)S(1)}, bf16[128,1280]{1,0:T(8,128)(2,1)S(1)}) custom-call(s32[2]{0:T(128)} %refs_0_.1, f32[64,6912]{1,0:T(8,128)} %refs_1_.3, bf16[2,64,1152]{2,1,0:T(8,128)(2,1)} %refs_2_.2), custom_call_target="tpu_custom_call" | custom-call | flops 40000000 | bytes 1500000 | tf_op jit(solution)/shard_map/first/pallas_call | solution.py:74
  32.9 0.3 collective-permute-start.3
  33.2 2.4 %collective-permute-start.7 = (bf16[64,1152]{1,0:T(8,128)(2,1)S(1)}, bf16[64,1152]{1,0:T(8,128)(2,1)S(1)}, u32[]{:S(2)}, u32[]{:S(2)}) collective-permute-start(bf16[64,1152]{1,0:T(8,128)(2,1)S(1)} %get-tuple-element.14.refs_10_), channel_id=1, source_target_pairs={{0,7},{1,0},{2,1},{3,2},{4,3},{5,4},{6,5},{7,6},{8,15},{9,8},{10,9... | collective-permute-start | bytes 442376 | tf_op jit(solution)/shard_map/ppermute | solution.py:359
  35.6 0.0 collective-permute-start
  35.6 1.4 %collective-permute-start.11 = (bf16[64,1152]{1,0:T(8,128)(2,1)S(1)}, bf16[64,1152]{1,0:T(8,128)(2,1)S(1)}, u32[]{:S(2)}, u32[]{:S(2)}) collective-permute-start(bf16[64,1152]{1,0:T(8,128)(2,1)S(1)} %get-tuple-element.14.refs_10_), channel_id=1, source_target_pairs={{0,1},{1,2},{2,3},{3,4},{4,5},{5,6},{6,7},{7,0},{8,9},{9,10},{10,1... | collective-permute-start | bytes 442376 | tf_op jit(solution)/shard_map/ppermute | solution.py:356
  37.1 1.1 collective-permute-done.3.refs_9_
  38.1 0.0 collective-permute-start.4
  38.1 0.0 collective-permute-done.7.refs_11_
  38.1 2.7 %collective-permute-start.8 = (bf16[64,1152]{1,0:T(8,128)(2,1)S(1)}, bf16[64,1152]{1,0:T(8,128)(2,1)S(1)}, u32[]{:S(2)}, u32[]{:S(2)}) collective-permute-start(bf16[64,1152]{1,0:T(8,128)(2,1)S(1)} %collective-permute-done.7.refs_11_), channel_id=1, source_target_pairs={{0,7},{1,0},{2,1},{3,2},{4,3},{5,4},{6,5},{7,6},{8,15},{9,8},{10,9... | collective-permute-start | bytes 442376 | tf_op jit(solution)/shard_map/ppermute | solution.py:359
  40.8 0.0 collective-permute-done.refs_3_
  40.8 1.6 %collective-permute-start.1 = (bf16[64,1152]{1,0:T(8,128)(2,1)S(1)}, bf16[64,1152]{1,0:T(8,128)(2,1)S(1)}, u32[]{:S(2)}, u32[]{:S(2)}) collective-permute-start(bf16[64,1152]{1,0:T(8,128)(2,1)S(1)} %collective-permute-done.refs_3_), channel_id=1, source_target_pairs={{0,7},{1,0},{2,1},{3,2},{4,3},{5,4},{6,5},{7,6},{8,15},{9,8},{10,9... | collective-permute-start | bytes 442376 | tf_op jit(solution)/shard_map/ppermute | solution.py:359
  42.4 0.0 collective-permute-done.11.refs_17_
  42.4 0.0 collective-permute-start.12
  42.4 3.0 %collective-permute-done.4.refs_8_ = bf16[64,1152]{1,0:T(8,128)(2,1)S(1)} collective-permute-done((bf16[64,1152]{1,0:T(8,128)(2,1)S(1)}, bf16[64,1152]{1,0:T(8,128)(2,1)S(1)}, u32[]{:S(2)}, u32[]{:S(2)}) %collective-permute-start.4) | collective-permute-done | bytes 147488 | tf_op jit(solution)/shard_map/ppermute | solution.py:356
  45.4 0.0 collective-permute-start.5
  45.4 0.0 collective-permute-done.8.refs_12_
  45.4 2.7 %collective-permute-start.9 = (bf16[64,1152]{1,0:T(8,128)(2,1)S(1)}, bf16[64,1152]{1,0:T(8,128)(2,1)S(1)}, u32[]{:S(2)}, u32[]{:S(2)}) collective-permute-start(bf16[64,1152]{1,0:T(8,128)(2,1)S(1)} %collective-permute-done.8.refs_12_), channel_id=1, source_target_pairs={{0,7},{1,0},{2,1},{3,2},{4,3},{5,4},{6,5},{7,6},{8,15},{9,8},{10,9... | collective-permute-start | bytes 442376 | tf_op jit(solution)/shard_map/ppermute | solution.py:359
  48.1 0.0 collective-permute-done.1.refs_4_
  48.1 0.8 collective-permute-start.2
  48.9 0.0 collective-permute-done.12.refs_16_
  48.9 0.6 collective-permute-start.13
  49.5 1.2 collective-permute-done.5.refs_7_
  50.8 0.0 collective-permute-start.6
  50.8 1.0 collective-permute-done.9.refs_13_
  51.7 3.5 %collective-permute-start.10 = (bf16[64,1152]{1,0:T(8,128)(2,1)S(1)}, bf16[64,1152]{1,0:T(8,128)(2,1)S(1)}, u32[]{:S(2)}, u32[]{:S(2)}) collective-permute-start(bf16[64,1152]{1,0:T(8,128)(2,1)S(1)} %collective-permute-done.9.refs_13_), channel_id=1, source_target_pairs={{0,7},{1,0},{2,1},{3,2},{4,3},{5,4},{6,5},{7,6},{8,15},{9,8},{10,9... | collective-permute-start | bytes 442376 | tf_op jit(solution)/shard_map/ppermute | solution.py:359
  55.3 0.0 collective-permute-done.2.refs_5_
  55.3 0.7 collective-permute-done.13.refs_15_
  56.0 2.3 %collective-permute-done.6.refs_6_ = bf16[64,1152]{1,0:T(8,128)(2,1)S(1)} collective-permute-done((bf16[64,1152]{1,0:T(8,128)(2,1)S(1)}, bf16[64,1152]{1,0:T(8,128)(2,1)S(1)}, u32[]{:S(2)}, u32[]{:S(2)}) %collective-permute-start.6) | collective-permute-done | bytes 147488 | tf_op jit(solution)/shard_map/ppermute | solution.py:356
  58.3 0.0 collective-permute-done.10.refs_14_
  58.3 5.1 %spatial.1 = bf16[8,144,128]{2,1,0:T(8,128)(2,1)S(1)} custom-call(s32[1]{0:T(128)} %bitcast.2.refs_0_.place_ref, bf16[432,1152]{1,0:T(8,128)(2,1)} %bitcast.12, bf16[64,1152]{1,0:T(8,128)(2,1)S(1)} %get-tuple-element.13.refs_2_, bf16[64,1152]{1,0:T(8,128)(2,1)S(1)} %collective-permute-done.refs_3_, bf16[64,1152]{1,0:T(8,128)(2,1)S(1)} %collective-permute-done.1.refs_4_, ...), custom_call_target="tpu_custom_call" | custom-call | flops 1556086784 | bytes 5000000 | tf_op jit(solution)/shard_map/spatial/pallas_call | solution.py:144
  63.4 0.0 copy-start
  63.4 13.4 %all_to_all.21.refs_1_ = bf16[8,144,128]{2,1,0:T(8,128)(2,1)S(1)} all-to-all(bf16[8,144,128]{2,1,0:T(8,128)(2,1)S(1)} %spatial.1), channel_id=1, replica_groups=mesh['queue'=32,'tok'=8] {'tok'}, dimensions={0} | all-to-all | bytes 589824 | tf_op jit(solution)/shard_map/all_to_all | solution.py:401
  76.8 0.3 bundle.1
  77.0 0.1 reshape.21
  77.2 27.9 %all_to_all.22 = bf16[32,4,2432]{2,1,0:T(4,128)(2,1)S(1)} all-to-all(bf16[32,4,2432]{2,1,0:T(4,128)(2,1)S(1)} %reshape.21), channel_id=1, replica_groups=mesh['queue'=32,'tok'=8] {'queue'}, dimensions={0} | all-to-all | bytes 1245184 | tf_op jit(solution)/shard_map/all_to_all | solution.py:405
  105.1 0.1 reshape.22.refs_0_
  105.2 0.0 all-gather.3.cloned.1.call-done
  105.3 10.5 %temporal.1 = bf16[128,1152]{1,0:T(8,128)(2,1)S(1)} custom-call(bf16[128,2432]{1,0:T(8,128)(2,1)S(1)} %reshape.22.refs_0_, f32[64,6912]{1,0:T(8,128)} %refs_1_.3, bf16[3,144,1152]{2,1,0:T(8,128)(2,1)} %bitcast.11, bf16[144,1152]{1,0:T(8,128)(2,1)} %refs_3_.1, bf16[144,1152]{1,0:T(8,128)(2,1)} %refs_4_.1, bf16[32,176,1152]{2,1,0:T(8,128)(2,1)} %bitcast.9), custom_call_target="tpu_custom_call" | custom-call | flops 1698693120 | bytes 15000000 | tf_op jit(solution)/shard_map/temporal/pallas_call | solution.py:288
  115.8 0.1 reshape.23
  115.9 13.1 %all_to_all.23 = bf16[32,4,1152]{2,1,0:T(4,128)(2,1)S(1)} all-to-all(bf16[32,4,1152]{2,1,0:T(4,128)(2,1)S(1)} %reshape.23), channel_id=1, replica_groups=mesh['queue'=32,'tok'=8] {'queue'}, dimensions={0} | all-to-all | bytes 589824 | tf_op jit(solution)/shard_map/all_to_all | solution.py:408
  129.0 0.1 reshape.24.refs_1_
  129.0 0.0 copy-done
  129.1 1.0 last.1
  (1 shorter events, 0.0 us)
Async XLA Ops:
  6.5 98.7 %all-gather.3.cloned.1.call-start = ((), (), s32[]{:S(2)}) async-start(), calls=%async_computation.4 | async-start | bytes 13381632 | tf_op jit(solution)/shard_map/all_gather | solution.py:392
  32.9 5.3 %collective-permute-start.3 = (bf16[64,1152]{1,0:T(8,128)(2,1)S(1)}, bf16[64,1152]{1,0:T(8,128)(2,1)S(1)}, u32[]{:S(2)}, u32[]{:S(2)}) collective-permute-start(bf16[64,1152]{1,0:T(8,128)(2,1)S(1)} %get-tuple-element.13.refs_2_), channel_id=1, source_target_pairs={{0,1},{1,2},{2,3},{3,4},{4,5},{5,6},{6,7},{7,0},{8,9},{9,10},{10,1... | collective-permute-start | bytes 442376 | tf_op jit(solution)/shard_map/ppermute | solution.py:356
  33.2 5.0 %collective-permute-start.7 = (bf16[64,1152]{1,0:T(8,128)(2,1)S(1)}, bf16[64,1152]{1,0:T(8,128)(2,1)S(1)}, u32[]{:S(2)}, u32[]{:S(2)}) collective-permute-start(bf16[64,1152]{1,0:T(8,128)(2,1)S(1)} %get-tuple-element.14.refs_10_), channel_id=1, source_target_pairs={{0,7},{1,0},{2,1},{3,2},{4,3},{5,4},{6,5},{7,6},{8,15},{9,8},{10,9... | collective-permute-start | bytes 442376 | tf_op jit(solution)/shard_map/ppermute | solution.py:359
  35.6 5.2 %collective-permute-start = (bf16[64,1152]{1,0:T(8,128)(2,1)S(1)}, bf16[64,1152]{1,0:T(8,128)(2,1)S(1)}, u32[]{:S(2)}, u32[]{:S(2)}) collective-permute-start(bf16[64,1152]{1,0:T(8,128)(2,1)S(1)} %get-tuple-element.13.refs_2_), channel_id=1, source_target_pairs={{0,7},{1,0},{2,1},{3,2},{4,3},{5,4},{6,5},{7,6},{8,15},{9,8},{10,9... | collective-permute-start | bytes 442376 | tf_op jit(solution)/shard_map/ppermute | solution.py:359
  35.6 6.8 %collective-permute-start.11 = (bf16[64,1152]{1,0:T(8,128)(2,1)S(1)}, bf16[64,1152]{1,0:T(8,128)(2,1)S(1)}, u32[]{:S(2)}, u32[]{:S(2)}) collective-permute-start(bf16[64,1152]{1,0:T(8,128)(2,1)S(1)} %get-tuple-element.14.refs_10_), channel_id=1, source_target_pairs={{0,1},{1,2},{2,3},{3,4},{4,5},{5,6},{6,7},{7,0},{8,9},{9,10},{10,1... | collective-permute-start | bytes 442376 | tf_op jit(solution)/shard_map/ppermute | solution.py:356
  38.1 7.2 %collective-permute-start.4 = (bf16[64,1152]{1,0:T(8,128)(2,1)S(1)}, bf16[64,1152]{1,0:T(8,128)(2,1)S(1)}, u32[]{:S(2)}, u32[]{:S(2)}) collective-permute-start(bf16[64,1152]{1,0:T(8,128)(2,1)S(1)} %collective-permute-done.3.refs_9_), channel_id=1, source_target_pairs={{0,1},{1,2},{2,3},{3,4},{4,5},{5,6},{6,7},{7,0},{8,9},{9,10},{10,1... | collective-permute-start | bytes 442376 | tf_op jit(solution)/shard_map/ppermute | solution.py:356
  38.1 7.2 %collective-permute-start.8 = (bf16[64,1152]{1,0:T(8,128)(2,1)S(1)}, bf16[64,1152]{1,0:T(8,128)(2,1)S(1)}, u32[]{:S(2)}, u32[]{:S(2)}) collective-permute-start(bf16[64,1152]{1,0:T(8,128)(2,1)S(1)} %collective-permute-done.7.refs_11_), channel_id=1, source_target_pairs={{0,7},{1,0},{2,1},{3,2},{4,3},{5,4},{6,5},{7,6},{8,15},{9,8},{10,9... | collective-permute-start | bytes 442376 | tf_op jit(solution)/shard_map/ppermute | solution.py:359
  40.8 7.2 %collective-permute-start.1 = (bf16[64,1152]{1,0:T(8,128)(2,1)S(1)}, bf16[64,1152]{1,0:T(8,128)(2,1)S(1)}, u32[]{:S(2)}, u32[]{:S(2)}) collective-permute-start(bf16[64,1152]{1,0:T(8,128)(2,1)S(1)} %collective-permute-done.refs_3_), channel_id=1, source_target_pairs={{0,7},{1,0},{2,1},{3,2},{4,3},{5,4},{6,5},{7,6},{8,15},{9,8},{10,9... | collective-permute-start | bytes 442376 | tf_op jit(solution)/shard_map/ppermute | solution.py:359
  42.4 6.5 %collective-permute-start.12 = (bf16[64,1152]{1,0:T(8,128)(2,1)S(1)}, bf16[64,1152]{1,0:T(8,128)(2,1)S(1)}, u32[]{:S(2)}, u32[]{:S(2)}) collective-permute-start(bf16[64,1152]{1,0:T(8,128)(2,1)S(1)} %collective-permute-done.11.refs_17_), channel_id=1, source_target_pairs={{0,1},{1,2},{2,3},{3,4},{4,5},{5,6},{6,7},{7,0},{8,9},{9,10},{10,1... | collective-permute-start | bytes 442376 | tf_op jit(solution)/shard_map/ppermute | solution.py:356
  45.4 5.4 %collective-permute-start.5 = (bf16[64,1152]{1,0:T(8,128)(2,1)S(1)}, bf16[64,1152]{1,0:T(8,128)(2,1)S(1)}, u32[]{:S(2)}, u32[]{:S(2)}) collective-permute-start(bf16[64,1152]{1,0:T(8,128)(2,1)S(1)} %collective-permute-done.4.refs_8_), channel_id=1, source_target_pairs={{0,1},{1,2},{2,3},{3,4},{4,5},{5,6},{6,7},{7,0},{8,9},{9,10},{10,1... | collective-permute-start | bytes 442376 | tf_op jit(solution)/shard_map/ppermute | solution.py:356
  45.4 6.4 %collective-permute-start.9 = (bf16[64,1152]{1,0:T(8,128)(2,1)S(1)}, bf16[64,1152]{1,0:T(8,128)(2,1)S(1)}, u32[]{:S(2)}, u32[]{:S(2)}) collective-permute-start(bf16[64,1152]{1,0:T(8,128)(2,1)S(1)} %collective-permute-done.8.refs_12_), channel_id=1, source_target_pairs={{0,7},{1,0},{2,1},{3,2},{4,3},{5,4},{6,5},{7,6},{8,15},{9,8},{10,9... | collective-permute-start | bytes 442376 | tf_op jit(solution)/shard_map/ppermute | solution.py:359
  48.1 7.2 %collective-permute-start.2 = (bf16[64,1152]{1,0:T(8,128)(2,1)S(1)}, bf16[64,1152]{1,0:T(8,128)(2,1)S(1)}, u32[]{:S(2)}, u32[]{:S(2)}) collective-permute-start(bf16[64,1152]{1,0:T(8,128)(2,1)S(1)} %collective-permute-done.1.refs_4_), channel_id=1, source_target_pairs={{0,7},{1,0},{2,1},{3,2},{4,3},{5,4},{6,5},{7,6},{8,15},{9,8},{10,9... | collective-permute-start | bytes 442376 | tf_op jit(solution)/shard_map/ppermute | solution.py:359
  48.9 7.1 %collective-permute-start.13 = (bf16[64,1152]{1,0:T(8,128)(2,1)S(1)}, bf16[64,1152]{1,0:T(8,128)(2,1)S(1)}, u32[]{:S(2)}, u32[]{:S(2)}) collective-permute-start(bf16[64,1152]{1,0:T(8,128)(2,1)S(1)} %collective-permute-done.12.refs_16_), channel_id=1, source_target_pairs={{0,1},{1,2},{2,3},{3,4},{4,5},{5,6},{6,7},{7,0},{8,9},{9,10},{10,1... | collective-permute-start | bytes 442376 | tf_op jit(solution)/shard_map/ppermute | solution.py:356
  50.8 7.5 %collective-permute-start.6 = (bf16[64,1152]{1,0:T(8,128)(2,1)S(1)}, bf16[64,1152]{1,0:T(8,128)(2,1)S(1)}, u32[]{:S(2)}, u32[]{:S(2)}) collective-permute-start(bf16[64,1152]{1,0:T(8,128)(2,1)S(1)} %collective-permute-done.5.refs_7_), channel_id=1, source_target_pairs={{0,1},{1,2},{2,3},{3,4},{4,5},{5,6},{6,7},{7,0},{8,9},{9,10},{10,1... | collective-permute-start | bytes 442376 | tf_op jit(solution)/shard_map/ppermute | solution.py:356
  51.7 6.6 %collective-permute-start.10 = (bf16[64,1152]{1,0:T(8,128)(2,1)S(1)}, bf16[64,1152]{1,0:T(8,128)(2,1)S(1)}, u32[]{:S(2)}, u32[]{:S(2)}) collective-permute-start(bf16[64,1152]{1,0:T(8,128)(2,1)S(1)} %collective-permute-done.9.refs_13_), channel_id=1, source_target_pairs={{0,7},{1,0},{2,1},{3,2},{4,3},{5,4},{6,5},{7,6},{8,15},{9,8},{10,9... | collective-permute-start | bytes 442376 | tf_op jit(solution)/shard_map/ppermute | solution.py:359
  63.4 65.7 %copy-start = (bf16[64,1152]{1,0:T(8,128)(2,1)S(1)}, bf16[64,1152]{1,0:T(8,128)(2,1)}, u32[]{:S(2)}) copy-start(bf16[64,1152]{1,0:T(8,128)(2,1)} %refs_2_.3) | copy-start | bytes 442372
Sparse Core Ops, SparseCore 0:
  31.5 67.5 all-gather.2

commit v7 on v6

--- a/solution.py
+++ b/solution.py
@@ -8,7 +8,7 @@
 HEADS = 16
 HDIM = 72
 EPS = 1e-06
-FACTOR = HDIM ** (-0.5)
+FACTOR = HDIM ** (-0.5) * 1.4426950408889634
 BF16 = jnp.bfloat16
 F32 = jnp.float32
 VMEM = pltpu.VMEM
@@ -117,17 +117,18 @@
         hidden = jnp.concatenate([ref[...] for ref in refs[j * ring : (j + 1) * ring]], axis=0)
         if j == 0:
             copy.wait()
-        projected = turned(w_ref[...], hidden).astype(BF16)
+        projected = turned(w_ref[...], hidden)
         side = projected.shape[0] // 3
+        projected = jnp.concatenate([FACTOR * projected[:side], projected[side:]], axis=0).astype(BF16)
         heads = []
         for h in range(side // HDIM):
             query, keyed, valued = [
                 projected[m * side + h * HDIM : m * side + (h + 1) * HDIM] for m in range(3)
             ]
-            scores = FACTOR * lax.dot_general(
+            scores = lax.dot_general(
                 keyed, query, (((0,), (0,)), ((), ())), preferred_element_type=F32
             )
-            weights = jnp.exp(scores - jnp.max(scores, axis=0, keepdims=True))
+            weights = jnp.exp2(scores - jnp.max(scores, axis=0, keepdims=True))
             total = jnp.sum(weights, axis=0, keepdims=True)
             mixed = jnp.dot(valued, weights.astype(BF16), preferred_element_type=F32)
             heads.append((mixed / total).astype(BF16))
@@ -161,15 +162,14 @@
 def bundle_kernel(line, size, group, place_ref, mixed_ref, side_ref, out_ref):
     ring, side, rows = mixed_ref.shape
     width = ring * side
+    parts = [mixed_ref[lax.rem(place_ref[0] + offset, ring)].astype(F32) for offset in range(ring)]
     pieces = []
     for s in range(2):
         for k in range(3 * s, 3 * s + 3):
-            for offset in range(1, ring):
-                z = lax.rem(place_ref[0] + offset, ring)
-                pieces.append(mixed_ref[z, k * size : (k + 1) * size].astype(F32))
+            pieces += [parts[offset][k * size : (k + 1) * size] for offset in range(1, ring)]
             pieces.append(jnp.zeros((group - (ring - 1) * size, rows), F32))
         if s == 0:
-            pieces.append(mixed_ref[place_ref[0]].astype(F32))
+            pieces.append(parts[0])
     mixed = jnp.concatenate(pieces, axis=0).astype(BF16)
     moved, _ = order_matrix(line, rows)
     end = width + mixed.shape[0]
@@ -245,7 +245,7 @@
     branch = jnp.zeros((rows, width), F32)
     for s in range(2):
         heads = ring + 1 if s == 0 else ring - 1
-        query = turned(matrix(0, s), hidden)
+        query = FACTOR * turned(matrix(0, s), hidden)
         keyed = turned(hidden, matrix(1, s)).astype(BF16)
         valued = turned(matrix(2, s), hidden).astype(BF16)
         row = lax.broadcasted_iota(jnp.int32, (query.shape[0], 1), 0)
@@ -257,9 +257,9 @@
         spread = jnp.concatenate(
             [jnp.where(owner == h, query, 0.0).astype(BF16) for h in range(heads)], axis=1
         )
-        scores = FACTOR * jnp.dot(keyed, spread, preferred_element_type=F32)
+        scores = jnp.dot(keyed, spread, preferred_element_type=F32)
         scores = jnp.where(along == across, scores, -jnp.inf)
-        weights = jnp.exp(scores - jnp.max(scores, axis=0, keepdims=True))
+        weights = jnp.exp2(scores - jnp.max(scores, axis=0, keepdims=True))
         inverse = 1.0 / jnp.sum(weights, axis=0, keepdims=True)
         mixed = jnp.dot(valued, weights.astype(BF16), preferred_element_type=F32)
 

time: 137 us -> 137 us (level)
  no operation moved by 1% of the time
where the time goes in v7:
time: 137 us
  blocking collectives  77.5 us (57%)
  Pallas kernels  18.9 us (14%)
  starting transfers between devices  16.1 us (12%)
  between operations  13.5 us (10%)
  waiting for transfers between devices  9.34 us (7%)
    all_to_all x1, blocking collectives, per_device(): lax.all_to_all(sent.reshape(line, 2 * per, sent.shape[1]), 'queue', 0, 0,...  27.9 us
    all_to_all x1, blocking collectives, per_device(): lax.all_to_all(jnp.broadcast_to(chunk[None], (ring, size, width)), 'tok',...  22.9 us
    ppermute x7, starting transfers between devices, send_down(): return lax.ppermute(v, 'tok', down)  13.7 us
    all_to_all x1, blocking collectives, per_device(): mixed = lax.all_to_all(mixed, 'tok', 0, 0, tiled=True)  13.4 us
    all_to_all x1, blocking collectives, per_device(): lax.all_to_all(moved.reshape(line, 2 * per, width), 'queue', 0, 0, tiled=...  13.3 us
    pallas_call x1, Pallas kernels, temporal(): pl.pallas_call(lambda *refs: temporal_kernel(size, per, *refs), out_shape...  10.5 us
    ppermute x7, waiting for transfers between devices, send_up(): return lax.ppermute(v, 'tok', up)  8.31 us
    pallas_call x1, Pallas kernels, spatial(): pl.pallas_call(lambda *refs: spatial_kernel(offsets, *refs), out_shape=ja...  4.85 us
  transfers between devices with their start and end apart: 15, of which 6 were waited for; matrix products, arithmetic and copies ran while one was open for 0% of the time, Pallas kernels for 5%

profile of v7, /device:TPU:1, one launch (start us, length us, event | category | flops | bytes accessed | tf_op | source)
XLA Modules:
  0.0 136.9 jit_solution(10484536850245059773)
XLA Ops:
  6.5 0.0 all-gather.3.cloned.1.call-start
  6.5 1.0 select_select_fusion
  7.6 22.9 %all_to_all.20.chunks_ref = bf16[8,24,1152]{2,1,0:T(8,128)(2,1)S(1)} all-to-all(bf16[8,24,1152]{2,1,0:T(8,128)(2,1)S(1)} %broadcast_in_dim.18), channel_id=1, replica_groups=mesh['queue'=32,'tok'=8] {'tok'}, dimensions={0} | all-to-all | bytes 884736 | tf_op jit(solution)/shard_map/all_to_all | solution.py:378
  30.5 0.8 others.1
  31.3 0.0 all-gather.3.cloned.1.call-update
  31.3 1.5 %first.1 = (bf16[64,1152]{1,0:T(8,128)(2,1)S(1)}, bf16[64,1152]{1,0:T(8,128)(2,1)S(1)}, bf16[128,1280]{1,0:T(8,128)(2,1)S(1)}) custom-call(s32[2]{0:T(128)} %refs_0_.1, f32[64,6912]{1,0:T(8,128)} %refs_1_.3, bf16[2,64,1152]{2,1,0:T(8,128)(2,1)} %refs_2_.2), custom_call_target="tpu_custom_call" | custom-call | flops 40000000 | bytes 1500000 | tf_op jit(solution)/shard_map/first/pallas_call | solution.py:74
  32.9 0.3 collective-permute-start.3
  33.2 2.4 %collective-permute-start.7 = (bf16[64,1152]{1,0:T(8,128)(2,1)S(1)}, bf16[64,1152]{1,0:T(8,128)(2,1)S(1)}, u32[]{:S(2)}, u32[]{:S(2)}) collective-permute-start(bf16[64,1152]{1,0:T(8,128)(2,1)S(1)} %get-tuple-element.14.refs_10_), channel_id=1, source_target_pairs={{0,7},{1,0},{2,1},{3,2},{4,3},{5,4},{6,5},{7,6},{8,15},{9,8},{10,9... | collective-permute-start | bytes 442376 | tf_op jit(solution)/shard_map/ppermute | solution.py:359
  35.6 0.0 collective-permute-start
  35.6 1.4 %collective-permute-start.11 = (bf16[64,1152]{1,0:T(8,128)(2,1)S(1)}, bf16[64,1152]{1,0:T(8,128)(2,1)S(1)}, u32[]{:S(2)}, u32[]{:S(2)}) collective-permute-start(bf16[64,1152]{1,0:T(8,128)(2,1)S(1)} %get-tuple-element.14.refs_10_), channel_id=1, source_target_pairs={{0,1},{1,2},{2,3},{3,4},{4,5},{5,6},{6,7},{7,0},{8,9},{9,10},{10,1... | collective-permute-start | bytes 442376 | tf_op jit(solution)/shard_map/ppermute | solution.py:356
  37.1 1.1 collective-permute-done.3.refs_9_
  38.1 0.0 collective-permute-start.4
  38.1 0.0 collective-permute-done.7.refs_11_
  38.1 2.7 %collective-permute-start.8 = (bf16[64,1152]{1,0:T(8,128)(2,1)S(1)}, bf16[64,1152]{1,0:T(8,128)(2,1)S(1)}, u32[]{:S(2)}, u32[]{:S(2)}) collective-permute-start(bf16[64,1152]{1,0:T(8,128)(2,1)S(1)} %collective-permute-done.7.refs_11_), channel_id=1, source_target_pairs={{0,7},{1,0},{2,1},{3,2},{4,3},{5,4},{6,5},{7,6},{8,15},{9,8},{10,9... | collective-permute-start | bytes 442376 | tf_op jit(solution)/shard_map/ppermute | solution.py:359
  40.8 0.0 collective-permute-done.refs_3_
  40.8 1.6 %collective-permute-start.1 = (bf16[64,1152]{1,0:T(8,128)(2,1)S(1)}, bf16[64,1152]{1,0:T(8,128)(2,1)S(1)}, u32[]{:S(2)}, u32[]{:S(2)}) collective-permute-start(bf16[64,1152]{1,0:T(8,128)(2,1)S(1)} %collective-permute-done.refs_3_), channel_id=1, source_target_pairs={{0,7},{1,0},{2,1},{3,2},{4,3},{5,4},{6,5},{7,6},{8,15},{9,8},{10,9... | collective-permute-start | bytes 442376 | tf_op jit(solution)/shard_map/ppermute | solution.py:359
  42.4 0.0 collective-permute-done.11.refs_17_
  42.4 0.0 collective-permute-start.12
  42.4 3.0 %collective-permute-done.4.refs_8_ = bf16[64,1152]{1,0:T(8,128)(2,1)S(1)} collective-permute-done((bf16[64,1152]{1,0:T(8,128)(2,1)S(1)}, bf16[64,1152]{1,0:T(8,128)(2,1)S(1)}, u32[]{:S(2)}, u32[]{:S(2)}) %collective-permute-start.4) | collective-permute-done | bytes 147488 | tf_op jit(solution)/shard_map/ppermute | solution.py:356
  45.4 0.0 collective-permute-start.5
  45.4 0.0 collective-permute-done.8.refs_12_
  45.4 2.7 %collective-permute-start.9 = (bf16[64,1152]{1,0:T(8,128)(2,1)S(1)}, bf16[64,1152]{1,0:T(8,128)(2,1)S(1)}, u32[]{:S(2)}, u32[]{:S(2)}) collective-permute-start(bf16[64,1152]{1,0:T(8,128)(2,1)S(1)} %collective-permute-done.8.refs_12_), channel_id=1, source_target_pairs={{0,7},{1,0},{2,1},{3,2},{4,3},{5,4},{6,5},{7,6},{8,15},{9,8},{10,9... | collective-permute-start | bytes 442376 | tf_op jit(solution)/shard_map/ppermute | solution.py:359
  48.1 0.0 collective-permute-done.1.refs_4_
  48.1 0.8 collective-permute-start.2
  48.9 0.0 collective-permute-done.12.refs_16_
  48.9 0.6 collective-permute-start.13
  49.5 1.2 collective-permute-done.5.refs_7_
  50.8 0.0 collective-permute-start.6
  50.8 1.0 collective-permute-done.9.refs_13_
  51.7 3.5 %collective-permute-start.10 = (bf16[64,1152]{1,0:T(8,128)(2,1)S(1)}, bf16[64,1152]{1,0:T(8,128)(2,1)S(1)}, u32[]{:S(2)}, u32[]{:S(2)}) collective-permute-start(bf16[64,1152]{1,0:T(8,128)(2,1)S(1)} %collective-permute-done.9.refs_13_), channel_id=1, source_target_pairs={{0,7},{1,0},{2,1},{3,2},{4,3},{5,4},{6,5},{7,6},{8,15},{9,8},{10,9... | collective-permute-start | bytes 442376 | tf_op jit(solution)/shard_map/ppermute | solution.py:359
  55.3 0.0 collective-permute-done.2.refs_5_
  55.3 0.7 collective-permute-done.13.refs_15_
  56.0 2.3 %collective-permute-done.6.refs_6_ = bf16[64,1152]{1,0:T(8,128)(2,1)S(1)} collective-permute-done((bf16[64,1152]{1,0:T(8,128)(2,1)S(1)}, bf16[64,1152]{1,0:T(8,128)(2,1)S(1)}, u32[]{:S(2)}, u32[]{:S(2)}) %collective-permute-start.6) | collective-permute-done | bytes 147488 | tf_op jit(solution)/shard_map/ppermute | solution.py:356
  58.3 0.0 collective-permute-done.10.refs_14_
  58.3 4.8 %spatial.1 = bf16[8,144,128]{2,1,0:T(8,128)(2,1)S(1)} custom-call(s32[1]{0:T(128)} %bitcast.2.refs_0_.place_ref, bf16[432,1152]{1,0:T(8,128)(2,1)} %bitcast.12, bf16[64,1152]{1,0:T(8,128)(2,1)S(1)} %get-tuple-element.13.refs_2_, bf16[64,1152]{1,0:T(8,128)(2,1)S(1)} %collective-permute-done.refs_3_, bf16[64,1152]{1,0:T(8,128)(2,1)S(1)} %collective-permute-done.1.refs_4_, ...), custom_call_target="tpu_custom_call" | custom-call | flops 1556086784 | bytes 5000000 | tf_op jit(solution)/shard_map/spatial/pallas_call | solution.py:145
  63.2 0.0 copy-start
  63.2 13.4 %all_to_all.21.refs_1_ = bf16[8,144,128]{2,1,0:T(8,128)(2,1)S(1)} all-to-all(bf16[8,144,128]{2,1,0:T(8,128)(2,1)S(1)} %spatial.1), channel_id=1, replica_groups=mesh['queue'=32,'tok'=8] {'tok'}, dimensions={0} | all-to-all | bytes 589824 | tf_op jit(solution)/shard_map/all_to_all | solution.py:401
  76.5 0.3 bundle.1
  76.8 0.1 reshape.21
  77.0 27.9 %all_to_all.22 = bf16[32,4,2432]{2,1,0:T(4,128)(2,1)S(1)} all-to-all(bf16[32,4,2432]{2,1,0:T(4,128)(2,1)S(1)} %reshape.21), channel_id=1, replica_groups=mesh['queue'=32,'tok'=8] {'queue'}, dimensions={0} | all-to-all | bytes 1245184 | tf_op jit(solution)/shard_map/all_to_all | solution.py:405
  104.9 0.1 reshape.22.refs_0_
  105.0 0.0 all-gather.3.cloned.1.call-done
  105.0 10.5 %temporal.1 = bf16[128,1152]{1,0:T(8,128)(2,1)S(1)} custom-call(bf16[128,2432]{1,0:T(8,128)(2,1)S(1)} %reshape.22.refs_0_, f32[64,6912]{1,0:T(8,128)} %refs_1_.3, bf16[3,144,1152]{2,1,0:T(8,128)(2,1)} %bitcast.11, bf16[144,1152]{1,0:T(8,128)(2,1)} %refs_3_.1, bf16[144,1152]{1,0:T(8,128)(2,1)} %refs_4_.1, bf16[32,176,1152]{2,1,0:T(8,128)(2,1)} %bitcast.9), custom_call_target="tpu_custom_call" | custom-call | flops 1698693120 | bytes 15000000 | tf_op jit(solution)/shard_map/temporal/pallas_call | solution.py:288
  115.6 0.1 reshape.23
  115.6 13.3 %all_to_all.23 = bf16[32,4,1152]{2,1,0:T(4,128)(2,1)S(1)} all-to-all(bf16[32,4,1152]{2,1,0:T(4,128)(2,1)S(1)} %reshape.23), channel_id=1, replica_groups=mesh['queue'=32,'tok'=8] {'queue'}, dimensions={0} | all-to-all | bytes 589824 | tf_op jit(solution)/shard_map/all_to_all | solution.py:408
  129.0 0.1 reshape.24.refs_1_
  129.1 0.0 copy-done
  129.1 1.0 last.1
  (1 shorter events, 0.0 us)
Async XLA Ops:
  6.5 98.5 %all-gather.3.cloned.1.call-start = ((), (), s32[]{:S(2)}) async-start(), calls=%async_computation.4 | async-start | bytes 13381632 | tf_op jit(solution)/shard_map/all_gather | solution.py:392
  32.9 5.3 %collective-permute-start.3 = (bf16[64,1152]{1,0:T(8,128)(2,1)S(1)}, bf16[64,1152]{1,0:T(8,128)(2,1)S(1)}, u32[]{:S(2)}, u32[]{:S(2)}) collective-permute-start(bf16[64,1152]{1,0:T(8,128)(2,1)S(1)} %get-tuple-element.13.refs_2_), channel_id=1, source_target_pairs={{0,1},{1,2},{2,3},{3,4},{4,5},{5,6},{6,7},{7,0},{8,9},{9,10},{10,1... | collective-permute-start | bytes 442376 | tf_op jit(solution)/shard_map/ppermute | solution.py:356
  33.2 5.0 %collective-permute-start.7 = (bf16[64,1152]{1,0:T(8,128)(2,1)S(1)}, bf16[64,1152]{1,0:T(8,128)(2,1)S(1)}, u32[]{:S(2)}, u32[]{:S(2)}) collective-permute-start(bf16[64,1152]{1,0:T(8,128)(2,1)S(1)} %get-tuple-element.14.refs_10_), channel_id=1, source_target_pairs={{0,7},{1,0},{2,1},{3,2},{4,3},{5,4},{6,5},{7,6},{8,15},{9,8},{10,9... | collective-permute-start | bytes 442376 | tf_op jit(solution)/shard_map/ppermute | solution.py:359
  35.6 5.2 %collective-permute-start = (bf16[64,1152]{1,0:T(8,128)(2,1)S(1)}, bf16[64,1152]{1,0:T(8,128)(2,1)S(1)}, u32[]{:S(2)}, u32[]{:S(2)}) collective-permute-start(bf16[64,1152]{1,0:T(8,128)(2,1)S(1)} %get-tuple-element.13.refs_2_), channel_id=1, source_target_pairs={{0,7},{1,0},{2,1},{3,2},{4,3},{5,4},{6,5},{7,6},{8,15},{9,8},{10,9... | collective-permute-start | bytes 442376 | tf_op jit(solution)/shard_map/ppermute | solution.py:359
  35.6 6.8 %collective-permute-start.11 = (bf16[64,1152]{1,0:T(8,128)(2,1)S(1)}, bf16[64,1152]{1,0:T(8,128)(2,1)S(1)}, u32[]{:S(2)}, u32[]{:S(2)}) collective-permute-start(bf16[64,1152]{1,0:T(8,128)(2,1)S(1)} %get-tuple-element.14.refs_10_), channel_id=1, source_target_pairs={{0,1},{1,2},{2,3},{3,4},{4,5},{5,6},{6,7},{7,0},{8,9},{9,10},{10,1... | collective-permute-start | bytes 442376 | tf_op jit(solution)/shard_map/ppermute | solution.py:356
  38.1 7.2 %collective-permute-start.4 = (bf16[64,1152]{1,0:T(8,128)(2,1)S(1)}, bf16[64,1152]{1,0:T(8,128)(2,1)S(1)}, u32[]{:S(2)}, u32[]{:S(2)}) collective-permute-start(bf16[64,1152]{1,0:T(8,128)(2,1)S(1)} %collective-permute-done.3.refs_9_), channel_id=1, source_target_pairs={{0,1},{1,2},{2,3},{3,4},{4,5},{5,6},{6,7},{7,0},{8,9},{9,10},{10,1... | collective-permute-start | bytes 442376 | tf_op jit(solution)/shard_map/ppermute | solution.py:356
  38.1 7.2 %collective-permute-start.8 = (bf16[64,1152]{1,0:T(8,128)(2,1)S(1)}, bf16[64,1152]{1,0:T(8,128)(2,1)S(1)}, u32[]{:S(2)}, u32[]{:S(2)}) collective-permute-start(bf16[64,1152]{1,0:T(8,128)(2,1)S(1)} %collective-permute-done.7.refs_11_), channel_id=1, source_target_pairs={{0,7},{1,0},{2,1},{3,2},{4,3},{5,4},{6,5},{7,6},{8,15},{9,8},{10,9... | collective-permute-start | bytes 442376 | tf_op jit(solution)/shard_map/ppermute | solution.py:359
  40.8 7.2 %collective-permute-start.1 = (bf16[64,1152]{1,0:T(8,128)(2,1)S(1)}, bf16[64,1152]{1,0:T(8,128)(2,1)S(1)}, u32[]{:S(2)}, u32[]{:S(2)}) collective-permute-start(bf16[64,1152]{1,0:T(8,128)(2,1)S(1)} %collective-permute-done.refs_3_), channel_id=1, source_target_pairs={{0,7},{1,0},{2,1},{3,2},{4,3},{5,4},{6,5},{7,6},{8,15},{9,8},{10,9... | collective-permute-start | bytes 442376 | tf_op jit(solution)/shard_map/ppermute | solution.py:359
  42.4 6.5 %collective-permute-start.12 = (bf16[64,1152]{1,0:T(8,128)(2,1)S(1)}, bf16[64,1152]{1,0:T(8,128)(2,1)S(1)}, u32[]{:S(2)}, u32[]{:S(2)}) collective-permute-start(bf16[64,1152]{1,0:T(8,128)(2,1)S(1)} %collective-permute-done.11.refs_17_), channel_id=1, source_target_pairs={{0,1},{1,2},{2,3},{3,4},{4,5},{5,6},{6,7},{7,0},{8,9},{9,10},{10,1... | collective-permute-start | bytes 442376 | tf_op jit(solution)/shard_map/ppermute | solution.py:356
  45.4 5.4 %collective-permute-start.5 = (bf16[64,1152]{1,0:T(8,128)(2,1)S(1)}, bf16[64,1152]{1,0:T(8,128)(2,1)S(1)}, u32[]{:S(2)}, u32[]{:S(2)}) collective-permute-start(bf16[64,1152]{1,0:T(8,128)(2,1)S(1)} %collective-permute-done.4.refs_8_), channel_id=1, source_target_pairs={{0,1},{1,2},{2,3},{3,4},{4,5},{5,6},{6,7},{7,0},{8,9},{9,10},{10,1... | collective-permute-start | bytes 442376 | tf_op jit(solution)/shard_map/ppermute | solution.py:356
  45.4 6.4 %collective-permute-start.9 = (bf16[64,1152]{1,0:T(8,128)(2,1)S(1)}, bf16[64,1152]{1,0:T(8,128)(2,1)S(1)}, u32[]{:S(2)}, u32[]{:S(2)}) collective-permute-start(bf16[64,1152]{1,0:T(8,128)(2,1)S(1)} %collective-permute-done.8.refs_12_), channel_id=1, source_target_pairs={{0,7},{1,0},{2,1},{3,2},{4,3},{5,4},{6,5},{7,6},{8,15},{9,8},{10,9... | collective-permute-start | bytes 442376 | tf_op jit(solution)/shard_map/ppermute | solution.py:359
  48.1 7.2 %collective-permute-start.2 = (bf16[64,1152]{1,0:T(8,128)(2,1)S(1)}, bf16[64,1152]{1,0:T(8,128)(2,1)S(1)}, u32[]{:S(2)}, u32[]{:S(2)}) collective-permute-start(bf16[64,1152]{1,0:T(8,128)(2,1)S(1)} %collective-permute-done.1.refs_4_), channel_id=1, source_target_pairs={{0,7},{1,0},{2,1},{3,2},{4,3},{5,4},{6,5},{7,6},{8,15},{9,8},{10,9... | collective-permute-start | bytes 442376 | tf_op jit(solution)/shard_map/ppermute | solution.py:359
  48.9 7.1 %collective-permute-start.13 = (bf16[64,1152]{1,0:T(8,128)(2,1)S(1)}, bf16[64,1152]{1,0:T(8,128)(2,1)S(1)}, u32[]{:S(2)}, u32[]{:S(2)}) collective-permute-start(bf16[64,1152]{1,0:T(8,128)(2,1)S(1)} %collective-permute-done.12.refs_16_), channel_id=1, source_target_pairs={{0,1},{1,2},{2,3},{3,4},{4,5},{5,6},{6,7},{7,0},{8,9},{9,10},{10,1... | collective-permute-start | bytes 442376 | tf_op jit(solution)/shard_map/ppermute | solution.py:356
  50.8 7.5 %collective-permute-start.6 = (bf16[64,1152]{1,0:T(8,128)(2,1)S(1)}, bf16[64,1152]{1,0:T(8,128)(2,1)S(1)}, u32[]{:S(2)}, u32[]{:S(2)}) collective-permute-start(bf16[64,1152]{1,0:T(8,128)(2,1)S(1)} %collective-permute-done.5.refs_7_), channel_id=1, source_target_pairs={{0,1},{1,2},{2,3},{3,4},{4,5},{5,6},{6,7},{7,0},{8,9},{9,10},{10,1... | collective-permute-start | bytes 442376 | tf_op jit(solution)/shard_map/ppermute | solution.py:356
  51.7 6.6 %collective-permute-start.10 = (bf16[64,1152]{1,0:T(8,128)(2,1)S(1)}, bf16[64,1152]{1,0:T(8,128)(2,1)S(1)}, u32[]{:S(2)}, u32[]{:S(2)}) collective-permute-start(bf16[64,1152]{1,0:T(8,128)(2,1)S(1)} %collective-permute-done.9.refs_13_), channel_id=1, source_target_pairs={{0,7},{1,0},{2,1},{3,2},{4,3},{5,4},{6,5},{7,6},{8,15},{9,8},{10,9... | collective-permute-start | bytes 442376 | tf_op jit(solution)/shard_map/ppermute | solution.py:359
  63.2 65.9 %copy-start = (bf16[64,1152]{1,0:T(8,128)(2,1)S(1)}, bf16[64,1152]{1,0:T(8,128)(2,1)}, u32[]{:S(2)}) copy-start(bf16[64,1152]{1,0:T(8,128)(2,1)} %refs_2_.3) | copy-start | bytes 442372
Sparse Core Ops, SparseCore 0:
  31.5 68.2 all-gather.2

commit v8 on v7

--- a/solution.py
+++ b/solution.py
@@ -107,10 +107,15 @@
     )(place, chunks)
 
 
-def spatial_kernel(offsets, place_ref, w_hbm, *refs):
-    *refs, out_ref, w_ref, sem = refs
-    copy = pltpu.make_async_copy(w_hbm, w_ref, sem)
+def spatial_kernel(offsets, place_ref, w_hbm, table_hbm, *refs):
+    *refs, out_ref, large_ref, small_ref, w_ref, table_ref, sems = refs
+    copy = pltpu.make_async_copy(w_hbm, w_ref, sems.at[0])
     copy.start()
+    count = table_ref.shape[1]
+    table_copy = pltpu.make_async_copy(
+        table_hbm.at[:, pl.ds(table_hbm.shape[1] - count, count)], table_ref, sems.at[1]
+    )
+    table_copy.start()
     rows = refs[0].shape[0]
     ring = len(offsets[0])
     for j in range(2):
@@ -136,27 +141,41 @@
         for n, offset in enumerate(offsets[j]):
             owner = lax.rem(place_ref[0] + offset + ring, ring)
             out_ref[owner, :, j * rows : (j + 1) * rows] = attended[:, n * rows : (n + 1) * rows]
-
-
-def spatial(offsets, place, w_qkv, blocks):
+    table_copy.wait()
+    values = table_ref[...]
+    large = values.astype(BF16)
+    large_ref[...] = large
+    small_ref[...] = (values - large.astype(F32)).astype(BF16)
+
+
+def spatial(offsets, place, w_qkv, table, blocks):
     rows, width = blocks[0].shape
     ring = len(offsets[0])
     whole = rows * ring
     return pl.pallas_call(
         lambda *refs: spatial_kernel(offsets, *refs),
-        out_shape=jax.ShapeDtypeStruct((ring, w_qkv.shape[0] // 3, 2 * rows), BF16),
-        in_specs=[pl.BlockSpec(memory_space=pltpu.SMEM), pl.BlockSpec(memory_space=pl.ANY)]
+        out_shape=(
+            jax.ShapeDtypeStruct((ring, w_qkv.shape[0] // 3, 2 * rows), BF16),
+            jax.ShapeDtypeStruct((table.shape[0], 4 * width), BF16),
+            jax.ShapeDtypeStruct((table.shape[0], 4 * width), BF16),
+        ),
+        in_specs=[pl.BlockSpec(memory_space=pltpu.SMEM)]
+        + [pl.BlockSpec(memory_space=pl.ANY)] * 2
         + [vspec()] * len(blocks),
-        out_specs=vspec(),
-        scratch_shapes=[VMEM(w_qkv.shape, BF16), pltpu.SemaphoreType.DMA],
+        out_specs=(vspec(), vspec(), vspec()),
+        scratch_shapes=[
+            VMEM(w_qkv.shape, BF16),
+            VMEM((table.shape[0], 4 * width), F32),
+            pltpu.SemaphoreType.DMA((2,)),
+        ],
         compiler_params=params(20),
         cost_estimate=pl.CostEstimate(
             flops=4 * whole * width * 144 * 3 + 8 * whole * whole * 256,
-            bytes_accessed=5000000,
+            bytes_accessed=8000000,
             transcendentals=4 * whole * whole,
         ),
         name="spatial",
-    )(place, in_hbm(w_qkv), *blocks)
+    )(place, in_hbm(w_qkv), in_hbm(table), *blocks)
 
 
 def bundle_kernel(line, size, group, place_ref, mixed_ref, side_ref, out_ref):
@@ -194,7 +213,7 @@
 
 
 def temporal_kernel(
-    size, per, got_ref, table_hbm, own_qkv, own_temporal, own_spatial, weights_hbm, out_ref, one_ref, two_ref, table_ref, sems
+    size, per, got_ref, large_ref, small_ref, own_qkv, own_temporal, own_spatial, weights_hbm, out_ref, one_ref, two_ref, sems
 ):
     group, width = weights_hbm.shape[1:]
     side = own_temporal.shape[0]
@@ -211,8 +230,6 @@
             own = own_qkv.at[m] if m < 3 else (own_temporal, own_spatial)[m - 3]
             pltpu.make_async_copy(own, one_ref.at[m, pl.ds(gathered, side)], sems.at[2 * m]).start()
 
-    table_copy = pltpu.make_async_copy(table_hbm.at[:, pl.ds(2 * width, 4 * width)], table_ref, sems.at[10])
-    table_copy.start()
     for m, s in ((4, 0), (4, 1), (0, 0), (1, 0), (2, 0), (3, 0), (0, 1), (1, 1), (2, 1), (3, 1)):
         start(m, s)
     rows = got_ref.shape[0]
@@ -223,17 +240,14 @@
 
     split = width + gathered + side
     end = split + gathered
-    level = got_ref[:, end : end + table_ref.shape[0]].astype(F32)
+    level = got_ref[:, end : end + large_ref.shape[0]].astype(F32)
     column = lax.broadcasted_iota(jnp.int32, level.shape, 1).astype(F32)
     onehot = (level == column).astype(BF16)
-    table_copy.wait()
 
     def mods(n):
-        values = table_ref[:, n * width : (n + 1) * width]
-        large = values.astype(BF16)
-        small = (values - large.astype(F32)).astype(BF16)
-        return jnp.dot(onehot, large, preferred_element_type=F32) + jnp.dot(
-            onehot, small, preferred_element_type=F32
+        part = slice(n * width, (n + 1) * width)
+        return jnp.dot(onehot, large_ref[:, part], preferred_element_type=F32) + jnp.dot(
+            onehot, small_ref[:, part], preferred_element_type=F32
         )
 
     gate1, shift2, scale2, gate2 = [mods(n) for n in range(4)]
@@ -281,27 +295,26 @@
     out_ref[...] = y.astype(BF16)
 
 
-def temporal(size, per, got, table, own, weights):
+def temporal(size, per, got, staged, own, weights):
     group, width = weights.shape[1:]
     side = own[1].shape[0]
     rows = got.shape[0]
     return pl.pallas_call(
         lambda *refs: temporal_kernel(size, per, *refs),
         out_shape=jax.ShapeDtypeStruct((rows, width), BF16),
-        in_specs=[vspec()] + [pl.BlockSpec(memory_space=pl.ANY)] * 5,
+        in_specs=[vspec()] * 3 + [pl.BlockSpec(memory_space=pl.ANY)] * 4,
         out_specs=vspec(),
         scratch_shapes=[
             VMEM((5, 3 * group + side, width), BF16),
             VMEM((5, 3 * group, width), BF16),
-            VMEM((table.shape[0], 4 * width), F32),
-            pltpu.SemaphoreType.DMA((11,)),
+            pltpu.SemaphoreType.DMA((10,)),
         ],
         compiler_params=params(40),
         cost_estimate=pl.CostEstimate(
             flops=2 * rows * width * width * 5, bytes_accessed=15000000, transcendentals=16 * rows * rows
         ),
         name="temporal",
-    )(got, in_hbm(table), *[in_hbm(v) for v in own], in_hbm(weights))
+    )(got, *staged, *[in_hbm(v) for v in own], in_hbm(weights))
 
 
 def last_kernel(line, tail_ref, got_ref, fresh_ref, out_ref):
@@ -392,10 +405,12 @@
     weights = lax.all_gather(others(place, chunks, group), "queue", axis=0, tiled=False)
 
     offsets = [[0, 1, 2, 3, -4, -3, -2, -1], [0, 1, 2, 3, 4, -3, -2, -1]]
-    mixed = spatial(
+    own = (turned_qkv.reshape(3, side, width), w_out_temporal, w_out_spatial)
+    mixed, *staged = spatial(
         offsets,
         place,
         jnp.swapaxes(w_qkv_spatial, 1, 2).reshape(3 * side, width),
+        mod_table,
         [frames[j][o] for j in range(2) for o in offsets[j]],
     )
     mixed = lax.all_to_all(mixed, "tok", 0, 0, tiled=True)
@@ -403,8 +418,7 @@
     per = rows // line
     sent = bundle(line, size, group, place, mixed, side_rows)
     got = lax.all_to_all(sent.reshape(line, 2 * per, sent.shape[1]), "queue", 0, 0, tiled=True)
-    own = (turned_qkv.reshape(3, side, width), w_out_temporal, w_out_spatial)
-    moved = temporal(size, per, got.reshape(sent.shape), mod_table, own, weights)
+    moved = temporal(size, per, got.reshape(sent.shape), staged, own, weights)
     got = lax.all_to_all(moved.reshape(line, 2 * per, width), "queue", 0, 0, tiled=True)
     return last(tail, line, got.reshape(2 * rows, width), fresh_frame)
 

time: 137 us -> 137 us (level)
  no operation moved by 1% of the time
where the time goes in v8:
time: 137 us; the launch traced here: 136 us
  blocking collectives  77.3 us (56%)
  Pallas kernels  18.6 us (14%)
  starting transfers between devices  16.1 us (12%)
  between operations  13.5 us (10%)
  waiting for transfers between devices  9.34 us (7%)
    all_to_all x1, blocking collectives, per_device(): lax.all_to_all(sent.reshape(line, 2 * per, sent.shape[1]), 'queue', 0, 0,...  28 us
    all_to_all x1, blocking collectives, per_device(): lax.all_to_all(jnp.broadcast_to(chunk[None], (ring, size, width)), 'tok',...  22.9 us
    ppermute x7, starting transfers between devices, send_down(): return lax.ppermute(v, 'tok', down)  13.7 us
    all_to_all x1, blocking collectives, per_device(): mixed = lax.all_to_all(mixed, 'tok', 0, 0, tiled=True)  13.4 us
    all_to_all x1, blocking collectives, per_device(): lax.all_to_all(moved.reshape(line, 2 * per, width), 'queue', 0, 0, tiled=...  13.1 us
    pallas_call x1, Pallas kernels, temporal(): pl.pallas_call(lambda *refs: temporal_kernel(size, per, *refs), out_shape...  10 us
    ppermute x7, waiting for transfers between devices, send_up(): return lax.ppermute(v, 'tok', up)  8.31 us
    pallas_call x1, Pallas kernels, spatial(): pl.pallas_call(lambda *refs: spatial_kernel(offsets, *refs), out_shape=(j...  5.02 us
  transfers between devices with their start and end apart: 15, of which 6 were waited for; matrix products, arithmetic and copies ran while one was open for 0% of the time, Pallas kernels for 5%

profile of v8, /device:TPU:1, one launch (start us, length us, event | category | flops | bytes accessed | tf_op | source)
XLA Modules:
  0.0 136.3 jit_solution(10946546770371758455)
XLA Ops:
  6.5 0.0 all-gather.3.cloned.1.call-start
  6.5 1.0 select_select_fusion
  7.6 22.9 %all_to_all.20.chunks_ref = bf16[8,24,1152]{2,1,0:T(8,128)(2,1)S(1)} all-to-all(bf16[8,24,1152]{2,1,0:T(8,128)(2,1)S(1)} %broadcast_in_dim.18), channel_id=1, replica_groups=mesh['queue'=32,'tok'=8] {'tok'}, dimensions={0} | all-to-all | bytes 884736 | tf_op jit(solution)/shard_map/all_to_all | solution.py:391
  30.5 0.8 others.1
  31.3 0.0 all-gather.3.cloned.1.call-update
  31.3 1.5 %first.1 = (bf16[64,1152]{1,0:T(8,128)(2,1)S(1)}, bf16[64,1152]{1,0:T(8,128)(2,1)S(1)}, bf16[128,1280]{1,0:T(8,128)(2,1)S(1)}) custom-call(s32[2]{0:T(128)} %refs_0_.1, f32[64,6912]{1,0:T(8,128)} %refs_2_.4, bf16[2,64,1152]{2,1,0:T(8,128)(2,1)} %refs_2_.3), custom_call_target="tpu_custom_call" | custom-call | flops 40000000 | bytes 1500000 | tf_op jit(solution)/shard_map/first/pallas_call | solution.py:74
  32.9 0.3 collective-permute-start.3
  33.2 2.4 %collective-permute-start.7 = (bf16[64,1152]{1,0:T(8,128)(2,1)S(1)}, bf16[64,1152]{1,0:T(8,128)(2,1)S(1)}, u32[]{:S(2)}, u32[]{:S(2)}) collective-permute-start(bf16[64,1152]{1,0:T(8,128)(2,1)S(1)} %get-tuple-element.17.refs_11_), channel_id=1, source_target_pairs={{0,7},{1,0},{2,1},{3,2},{4,3},{5,4},{6,5},{7,6},{8,15},{9,8},{10,9... | collective-permute-start | bytes 442376 | tf_op jit(solution)/shard_map/ppermute | solution.py:372
  35.6 0.0 collective-permute-start
  35.6 1.4 %collective-permute-start.11 = (bf16[64,1152]{1,0:T(8,128)(2,1)S(1)}, bf16[64,1152]{1,0:T(8,128)(2,1)S(1)}, u32[]{:S(2)}, u32[]{:S(2)}) collective-permute-start(bf16[64,1152]{1,0:T(8,128)(2,1)S(1)} %get-tuple-element.17.refs_11_), channel_id=1, source_target_pairs={{0,1},{1,2},{2,3},{3,4},{4,5},{5,6},{6,7},{7,0},{8,9},{9,10},{10,1... | collective-permute-start | bytes 442376 | tf_op jit(solution)/shard_map/ppermute | solution.py:369
  37.1 1.1 collective-permute-done.3.refs_10_
  38.1 0.0 collective-permute-start.4
  38.1 0.0 collective-permute-done.7.refs_12_
  38.1 2.7 %collective-permute-start.8 = (bf16[64,1152]{1,0:T(8,128)(2,1)S(1)}, bf16[64,1152]{1,0:T(8,128)(2,1)S(1)}, u32[]{:S(2)}, u32[]{:S(2)}) collective-permute-start(bf16[64,1152]{1,0:T(8,128)(2,1)S(1)} %collective-permute-done.7.refs_12_), channel_id=1, source_target_pairs={{0,7},{1,0},{2,1},{3,2},{4,3},{5,4},{6,5},{7,6},{8,15},{9,8},{10,9... | collective-permute-start | bytes 442376 | tf_op jit(solution)/shard_map/ppermute | solution.py:372
  40.8 0.0 collective-permute-done.refs_4_
  40.8 1.6 %collective-permute-start.1 = (bf16[64,1152]{1,0:T(8,128)(2,1)S(1)}, bf16[64,1152]{1,0:T(8,128)(2,1)S(1)}, u32[]{:S(2)}, u32[]{:S(2)}) collective-permute-start(bf16[64,1152]{1,0:T(8,128)(2,1)S(1)} %collective-permute-done.refs_4_), channel_id=1, source_target_pairs={{0,7},{1,0},{2,1},{3,2},{4,3},{5,4},{6,5},{7,6},{8,15},{9,8},{10,9... | collective-permute-start | bytes 442376 | tf_op jit(solution)/shard_map/ppermute | solution.py:372
  42.4 0.0 collective-permute-done.11.refs_18_
  42.4 0.0 collective-permute-start.12
  42.4 3.0 %collective-permute-done.4.refs_9_ = bf16[64,1152]{1,0:T(8,128)(2,1)S(1)} collective-permute-done((bf16[64,1152]{1,0:T(8,128)(2,1)S(1)}, bf16[64,1152]{1,0:T(8,128)(2,1)S(1)}, u32[]{:S(2)}, u32[]{:S(2)}) %collective-permute-start.4) | collective-permute-done | bytes 147488 | tf_op jit(solution)/shard_map/ppermute | solution.py:369
  45.4 0.0 collective-permute-start.5
  45.4 0.0 collective-permute-done.8.refs_13_
  45.4 2.7 %collective-permute-start.9 = (bf16[64,1152]{1,0:T(8,128)(2,1)S(1)}, bf16[64,1152]{1,0:T(8,128)(2,1)S(1)}, u32[]{:S(2)}, u32[]{:S(2)}) collective-permute-start(bf16[64,1152]{1,0:T(8,128)(2,1)S(1)} %collective-permute-done.8.refs_13_), channel_id=1, source_target_pairs={{0,7},{1,0},{2,1},{3,2},{4,3},{5,4},{6,5},{7,6},{8,15},{9,8},{10,9... | collective-permute-start | bytes 442376 | tf_op jit(solution)/shard_map/ppermute | solution.py:372
  48.1 0.0 collective-permute-done.1.refs_5_
  48.1 0.8 collective-permute-start.2
  48.9 0.0 collective-permute-done.12.refs_17_
  48.9 0.6 collective-permute-start.13
  49.5 1.2 collective-permute-done.5.refs_8_
  50.8 0.0 collective-permute-start.6
  50.8 1.0 collective-permute-done.9.refs_14_
  51.7 3.5 %collective-permute-start.10 = (bf16[64,1152]{1,0:T(8,128)(2,1)S(1)}, bf16[64,1152]{1,0:T(8,128)(2,1)S(1)}, u32[]{:S(2)}, u32[]{:S(2)}) collective-permute-start(bf16[64,1152]{1,0:T(8,128)(2,1)S(1)} %collective-permute-done.9.refs_14_), channel_id=1, source_target_pairs={{0,7},{1,0},{2,1},{3,2},{4,3},{5,4},{6,5},{7,6},{8,15},{9,8},{10,9... | collective-permute-start | bytes 442376 | tf_op jit(solution)/shard_map/ppermute | solution.py:372
  55.3 0.0 collective-permute-done.2.refs_6_
  55.3 0.7 collective-permute-done.13.refs_16_
  56.0 2.3 %collective-permute-done.6.refs_7_ = bf16[64,1152]{1,0:T(8,128)(2,1)S(1)} collective-permute-done((bf16[64,1152]{1,0:T(8,128)(2,1)S(1)}, bf16[64,1152]{1,0:T(8,128)(2,1)S(1)}, u32[]{:S(2)}, u32[]{:S(2)}) %collective-permute-start.6) | collective-permute-done | bytes 147488 | tf_op jit(solution)/shard_map/ppermute | solution.py:369
  58.3 0.0 collective-permute-done.10.refs_15_
  58.3 5.0 %spatial.1 = (bf16[8,144,128]{2,1,0:T(8,128)(2,1)S(1)}, bf16[64,4608]{1,0:T(8,128)(2,1)S(1)}, bf16[64,4608]{1,0:T(8,128)(2,1)S(1)}) custom-call(s32[1]{0:T(128)} %bitcast.2.refs_0_.place_ref, bf16[432,1152]{1,0:T(8,128)(2,1)} %bitcast.12, f32[64,6912]{1,0:T(8,128)} %refs_2_.4, bf16[64,1152]{1,0:T(8,128)(2,1)S(1)} %get-tuple-element.16.refs_3_, ...), custom_call_target="tpu_custom_call" | custom-call | flops 1556086784 | bytes 8000000 | tf_op jit(solution)/shard_map/spatial/pallas_call | solution.py:155
  63.3 0.0 copy-start
  63.3 13.4 %all_to_all.21.refs_1_ = bf16[8,144,128]{2,1,0:T(8,128)(2,1)S(1)} all-to-all(bf16[8,144,128]{2,1,0:T(8,128)(2,1)S(1)} %get-tuple-element.18), channel_id=1, replica_groups=mesh['queue'=32,'tok'=8] {'tok'}, dimensions={0} | all-to-all | bytes 589824 | tf_op jit(solution)/shard_map/all_to_all | solution.py:416
  76.7 0.3 bundle.1
  77.0 0.1 reshape.21
  77.1 28.0 %all_to_all.22 = bf16[32,4,2432]{2,1,0:T(4,128)(2,1)S(1)} all-to-all(bf16[32,4,2432]{2,1,0:T(4,128)(2,1)S(1)} %reshape.21), channel_id=1, replica_groups=mesh['queue'=32,'tok'=8] {'queue'}, dimensions={0} | all-to-all | bytes 1245184 | tf_op jit(solution)/shard_map/all_to_all | solution.py:420
  105.1 0.1 reshape.22.refs_0_
  105.3 0.0 all-gather.3.cloned.1.call-done
  105.3 10.0 %temporal.1 = bf16[128,1152]{1,0:T(8,128)(2,1)S(1)} custom-call(bf16[128,2432]{1,0:T(8,128)(2,1)S(1)} %reshape.22.refs_0_, bf16[64,4608]{1,0:T(8,128)(2,1)S(1)} %get-tuple-element.20.refs_1_, bf16[64,4608]{1,0:T(8,128)(2,1)S(1)} %get-tuple-element.21.refs_2_, bf16[3,144,1152]{2,1,0:T(8,128)(2,1)} %bitcast.11, bf16[144,1152]{1,0:T(8,128)(2,1)} %refs_4_.1, ...), custom_call_target="tpu_custom_call" | custom-call | flops 1698693120 | bytes 15000000 | tf_op jit(solution)/shard_map/temporal/pallas_call | solution.py:302
  115.3 0.1 reshape.23
  115.4 13.1 %all_to_all.23 = bf16[32,4,1152]{2,1,0:T(4,128)(2,1)S(1)} all-to-all(bf16[32,4,1152]{2,1,0:T(4,128)(2,1)S(1)} %reshape.23), channel_id=1, replica_groups=mesh['queue'=32,'tok'=8] {'queue'}, dimensions={0} | all-to-all | bytes 589824 | tf_op jit(solution)/shard_map/all_to_all | solution.py:422
  128.4 0.1 reshape.24.refs_1_
  128.5 0.0 copy-done
  128.5 1.0 last.1
  (1 shorter events, 0.0 us)
Async XLA Ops:
  6.5 98.8 %all-gather.3.cloned.1.call-start = ((), (), s32[]{:S(2)}) async-start(), calls=%async_computation.4 | async-start | bytes 13381632 | tf_op jit(solution)/shard_map/all_gather | solution.py:405
  32.9 5.3 %collective-permute-start.3 = (bf16[64,1152]{1,0:T(8,128)(2,1)S(1)}, bf16[64,1152]{1,0:T(8,128)(2,1)S(1)}, u32[]{:S(2)}, u32[]{:S(2)}) collective-permute-start(bf16[64,1152]{1,0:T(8,128)(2,1)S(1)} %get-tuple-element.16.refs_3_), channel_id=1, source_target_pairs={{0,1},{1,2},{2,3},{3,4},{4,5},{5,6},{6,7},{7,0},{8,9},{9,10},{10,1... | collective-permute-start | bytes 442376 | tf_op jit(solution)/shard_map/ppermute | solution.py:369
  33.2 5.0 %collective-permute-start.7 = (bf16[64,1152]{1,0:T(8,128)(2,1)S(1)}, bf16[64,1152]{1,0:T(8,128)(2,1)S(1)}, u32[]{:S(2)}, u32[]{:S(2)}) collective-permute-start(bf16[64,1152]{1,0:T(8,128)(2,1)S(1)} %get-tuple-element.17.refs_11_), channel_id=1, source_target_pairs={{0,7},{1,0},{2,1},{3,2},{4,3},{5,4},{6,5},{7,6},{8,15},{9,8},{10,9... | collective-permute-start | bytes 442376 | tf_op jit(solution)/shard_map/ppermute | solution.py:372
  35.6 5.2 %collective-permute-start = (bf16[64,1152]{1,0:T(8,128)(2,1)S(1)}, bf16[64,1152]{1,0:T(8,128)(2,1)S(1)}, u32[]{:S(2)}, u32[]{:S(2)}) collective-permute-start(bf16[64,1152]{1,0:T(8,128)(2,1)S(1)} %get-tuple-element.16.refs_3_), channel_id=1, source_target_pairs={{0,7},{1,0},{2,1},{3,2},{4,3},{5,4},{6,5},{7,6},{8,15},{9,8},{10,9... | collective-permute-start | bytes 442376 | tf_op jit(solution)/shard_map/ppermute | solution.py:372
  35.6 6.8 %collective-permute-start.11 = (bf16[64,1152]{1,0:T(8,128)(2,1)S(1)}, bf16[64,1152]{1,0:T(8,128)(2,1)S(1)}, u32[]{:S(2)}, u32[]{:S(2)}) collective-permute-start(bf16[64,1152]{1,0:T(8,128)(2,1)S(1)} %get-tuple-element.17.refs_11_), channel_id=1, source_target_pairs={{0,1},{1,2},{2,3},{3,4},{4,5},{5,6},{6,7},{7,0},{8,9},{9,10},{10,1... | collective-permute-start | bytes 442376 | tf_op jit(solution)/shard_map/ppermute | solution.py:369
  38.1 7.2 %collective-permute-start.4 = (bf16[64,1152]{1,0:T(8,128)(2,1)S(1)}, bf16[64,1152]{1,0:T(8,128)(2,1)S(1)}, u32[]{:S(2)}, u32[]{:S(2)}) collective-permute-start(bf16[64,1152]{1,0:T(8,128)(2,1)S(1)} %collective-permute-done.3.refs_10_), channel_id=1, source_target_pairs={{0,1},{1,2},{2,3},{3,4},{4,5},{5,6},{6,7},{7,0},{8,9},{9,10},{10,1... | collective-permute-start | bytes 442376 | tf_op jit(solution)/shard_map/ppermute | solution.py:369
  38.1 7.2 %collective-permute-start.8 = (bf16[64,1152]{1,0:T(8,128)(2,1)S(1)}, bf16[64,1152]{1,0:T(8,128)(2,1)S(1)}, u32[]{:S(2)}, u32[]{:S(2)}) collective-permute-start(bf16[64,1152]{1,0:T(8,128)(2,1)S(1)} %collective-permute-done.7.refs_12_), channel_id=1, source_target_pairs={{0,7},{1,0},{2,1},{3,2},{4,3},{5,4},{6,5},{7,6},{8,15},{9,8},{10,9... | collective-permute-start | bytes 442376 | tf_op jit(solution)/shard_map/ppermute | solution.py:372
  40.8 7.2 %collective-permute-start.1 = (bf16[64,1152]{1,0:T(8,128)(2,1)S(1)}, bf16[64,1152]{1,0:T(8,128)(2,1)S(1)}, u32[]{:S(2)}, u32[]{:S(2)}) collective-permute-start(bf16[64,1152]{1,0:T(8,128)(2,1)S(1)} %collective-permute-done.refs_4_), channel_id=1, source_target_pairs={{0,7},{1,0},{2,1},{3,2},{4,3},{5,4},{6,5},{7,6},{8,15},{9,8},{10,9... | collective-permute-start | bytes 442376 | tf_op jit(solution)/shard_map/ppermute | solution.py:372
  42.4 6.5 %collective-permute-start.12 = (bf16[64,1152]{1,0:T(8,128)(2,1)S(1)}, bf16[64,1152]{1,0:T(8,128)(2,1)S(1)}, u32[]{:S(2)}, u32[]{:S(2)}) collective-permute-start(bf16[64,1152]{1,0:T(8,128)(2,1)S(1)} %collective-permute-done.11.refs_18_), channel_id=1, source_target_pairs={{0,1},{1,2},{2,3},{3,4},{4,5},{5,6},{6,7},{7,0},{8,9},{9,10},{10,1... | collective-permute-start | bytes 442376 | tf_op jit(solution)/shard_map/ppermute | solution.py:369
  45.4 5.4 %collective-permute-start.5 = (bf16[64,1152]{1,0:T(8,128)(2,1)S(1)}, bf16[64,1152]{1,0:T(8,128)(2,1)S(1)}, u32[]{:S(2)}, u32[]{:S(2)}) collective-permute-start(bf16[64,1152]{1,0:T(8,128)(2,1)S(1)} %collective-permute-done.4.refs_9_), channel_id=1, source_target_pairs={{0,1},{1,2},{2,3},{3,4},{4,5},{5,6},{6,7},{7,0},{8,9},{9,10},{10,1... | collective-permute-start | bytes 442376 | tf_op jit(solution)/shard_map/ppermute | solution.py:369
  45.4 6.4 %collective-permute-start.9 = (bf16[64,1152]{1,0:T(8,128)(2,1)S(1)}, bf16[64,1152]{1,0:T(8,128)(2,1)S(1)}, u32[]{:S(2)}, u32[]{:S(2)}) collective-permute-start(bf16[64,1152]{1,0:T(8,128)(2,1)S(1)} %collective-permute-done.8.refs_13_), channel_id=1, source_target_pairs={{0,7},{1,0},{2,1},{3,2},{4,3},{5,4},{6,5},{7,6},{8,15},{9,8},{10,9... | collective-permute-start | bytes 442376 | tf_op jit(solution)/shard_map/ppermute | solution.py:372
  48.1 7.2 %collective-permute-start.2 = (bf16[64,1152]{1,0:T(8,128)(2,1)S(1)}, bf16[64,1152]{1,0:T(8,128)(2,1)S(1)}, u32[]{:S(2)}, u32[]{:S(2)}) collective-permute-start(bf16[64,1152]{1,0:T(8,128)(2,1)S(1)} %collective-permute-done.1.refs_5_), channel_id=1, source_target_pairs={{0,7},{1,0},{2,1},{3,2},{4,3},{5,4},{6,5},{7,6},{8,15},{9,8},{10,9... | collective-permute-start | bytes 442376 | tf_op jit(solution)/shard_map/ppermute | solution.py:372
  48.9 7.1 %collective-permute-start.13 = (bf16[64,1152]{1,0:T(8,128)(2,1)S(1)}, bf16[64,1152]{1,0:T(8,128)(2,1)S(1)}, u32[]{:S(2)}, u32[]{:S(2)}) collective-permute-start(bf16[64,1152]{1,0:T(8,128)(2,1)S(1)} %collective-permute-done.12.refs_17_), channel_id=1, source_target_pairs={{0,1},{1,2},{2,3},{3,4},{4,5},{5,6},{6,7},{7,0},{8,9},{9,10},{10,1... | collective-permute-start | bytes 442376 | tf_op jit(solution)/shard_map/ppermute | solution.py:369
  50.8 7.5 %collective-permute-start.6 = (bf16[64,1152]{1,0:T(8,128)(2,1)S(1)}, bf16[64,1152]{1,0:T(8,128)(2,1)S(1)}, u32[]{:S(2)}, u32[]{:S(2)}) collective-permute-start(bf16[64,1152]{1,0:T(8,128)(2,1)S(1)} %collective-permute-done.5.refs_8_), channel_id=1, source_target_pairs={{0,1},{1,2},{2,3},{3,4},{4,5},{5,6},{6,7},{7,0},{8,9},{9,10},{10,1... | collective-permute-start | bytes 442376 | tf_op jit(solution)/shard_map/ppermute | solution.py:369
  51.7 6.6 %collective-permute-start.10 = (bf16[64,1152]{1,0:T(8,128)(2,1)S(1)}, bf16[64,1152]{1,0:T(8,128)(2,1)S(1)}, u32[]{:S(2)}, u32[]{:S(2)}) collective-permute-start(bf16[64,1152]{1,0:T(8,128)(2,1)S(1)} %collective-permute-done.9.refs_14_), channel_id=1, source_target_pairs={{0,7},{1,0},{2,1},{3,2},{4,3},{5,4},{6,5},{7,6},{8,15},{9,8},{10,9... | collective-permute-start | bytes 442376 | tf_op jit(solution)/shard_map/ppermute | solution.py:372
  63.3 65.2 %copy-start = (bf16[64,1152]{1,0:T(8,128)(2,1)S(1)}, bf16[64,1152]{1,0:T(8,128)(2,1)}, u32[]{:S(2)}) copy-start(bf16[64,1152]{1,0:T(8,128)(2,1)} %refs_2_.5) | copy-start | bytes 442372
Sparse Core Ops, SparseCore 0:
  31.5 67.5 all-gather.2

commit v9 on v8

--- a/solution.py
+++ b/solution.py
@@ -266,8 +266,8 @@
         inside = row % group
         owner = jnp.where(inside < (ring - 1) * size, inside // size, -1)
         owner = jnp.where(row >= gathered, ring - 1 + (row - gathered) // HDIM, owner)
-        along = lax.broadcasted_iota(jnp.int32, (rows, heads * rows), 0) % per
-        across = lax.broadcasted_iota(jnp.int32, (rows, heads * rows), 1) % per
+        along = lax.broadcasted_iota(jnp.int32, (rows, 1), 0) % per
+        across = lax.broadcasted_iota(jnp.int32, (1, heads * rows), 1) % per
         spread = jnp.concatenate(
             [jnp.where(owner == h, query, 0.0).astype(BF16) for h in range(heads)], axis=1
         )

time: 137 us -> 137 us (level)
  no operation moved by 1% of the time
where the time goes in v9:
time: 137 us; the launch traced here: 136 us
  blocking collectives  77.3 us (56%)
  Pallas kernels  18.6 us (14%)
  starting transfers between devices  16.1 us (12%)
  between operations  13.5 us (10%)
  waiting for transfers between devices  9.34 us (7%)
    all_to_all x1, blocking collectives, per_device(): lax.all_to_all(sent.reshape(line, 2 * per, sent.shape[1]), 'queue', 0, 0,...  28 us
    all_to_all x1, blocking collectives, per_device(): lax.all_to_all(jnp.broadcast_to(chunk[None], (ring, size, width)), 'tok',...  22.9 us
    ppermute x7, starting transfers between devices, send_down(): return lax.ppermute(v, 'tok', down)  13.7 us
    all_to_all x1, blocking collectives, per_device(): mixed = lax.all_to_all(mixed, 'tok', 0, 0, tiled=True)  13.4 us
    all_to_all x1, blocking collectives, per_device(): lax.all_to_all(moved.reshape(line, 2 * per, width), 'queue', 0, 0, tiled=...  13.1 us
    pallas_call x1, Pallas kernels, temporal(): pl.pallas_call(lambda *refs: temporal_kernel(size, per, *refs), out_shape...  10 us
    ppermute x7, waiting for transfers between devices, send_up(): return lax.ppermute(v, 'tok', up)  8.31 us
    pallas_call x1, Pallas kernels, spatial(): pl.pallas_call(lambda *refs: spatial_kernel(offsets, *refs), out_shape=(j...  5.02 us
  transfers between devices with their start and end apart: 15, of which 6 were waited for; matrix products, arithmetic and copies ran while one was open for 0% of the time, Pallas kernels for 5%

profile of v9, /device:TPU:1, one launch (start us, length us, event | category | flops | bytes accessed | tf_op | source)
XLA Modules:
  0.0 136.3 jit_solution(10946546770371758455)
XLA Ops:
  6.5 0.0 all-gather.3.cloned.1.call-start
  6.5 1.0 select_select_fusion
  7.6 22.9 %all_to_all.20.chunks_ref = bf16[8,24,1152]{2,1,0:T(8,128)(2,1)S(1)} all-to-all(bf16[8,24,1152]{2,1,0:T(8,128)(2,1)S(1)} %broadcast_in_dim.18), channel_id=1, replica_groups=mesh['queue'=32,'tok'=8] {'tok'}, dimensions={0} | all-to-all | bytes 884736 | tf_op jit(solution)/shard_map/all_to_all | solution.py:391
  30.5 0.8 others.1
  31.3 0.0 all-gather.3.cloned.1.call-update
  31.3 1.5 %first.1 = (bf16[64,1152]{1,0:T(8,128)(2,1)S(1)}, bf16[64,1152]{1,0:T(8,128)(2,1)S(1)}, bf16[128,1280]{1,0:T(8,128)(2,1)S(1)}) custom-call(s32[2]{0:T(128)} %refs_0_.1, f32[64,6912]{1,0:T(8,128)} %refs_2_.4, bf16[2,64,1152]{2,1,0:T(8,128)(2,1)} %refs_2_.3), custom_call_target="tpu_custom_call" | custom-call | flops 40000000 | bytes 1500000 | tf_op jit(solution)/shard_map/first/pallas_call | solution.py:74
  32.9 0.3 collective-permute-start.3
  33.2 2.4 %collective-permute-start.7 = (bf16[64,1152]{1,0:T(8,128)(2,1)S(1)}, bf16[64,1152]{1,0:T(8,128)(2,1)S(1)}, u32[]{:S(2)}, u32[]{:S(2)}) collective-permute-start(bf16[64,1152]{1,0:T(8,128)(2,1)S(1)} %get-tuple-element.17.refs_11_), channel_id=1, source_target_pairs={{0,7},{1,0},{2,1},{3,2},{4,3},{5,4},{6,5},{7,6},{8,15},{9,8},{10,9... | collective-permute-start | bytes 442376 | tf_op jit(solution)/shard_map/ppermute | solution.py:372
  35.6 0.0 collective-permute-start
  35.6 1.4 %collective-permute-start.11 = (bf16[64,1152]{1,0:T(8,128)(2,1)S(1)}, bf16[64,1152]{1,0:T(8,128)(2,1)S(1)}, u32[]{:S(2)}, u32[]{:S(2)}) collective-permute-start(bf16[64,1152]{1,0:T(8,128)(2,1)S(1)} %get-tuple-element.17.refs_11_), channel_id=1, source_target_pairs={{0,1},{1,2},{2,3},{3,4},{4,5},{5,6},{6,7},{7,0},{8,9},{9,10},{10,1... | collective-permute-start | bytes 442376 | tf_op jit(solution)/shard_map/ppermute | solution.py:369
  37.1 1.1 collective-permute-done.3.refs_10_
  38.1 0.0 collective-permute-start.4
  38.1 0.0 collective-permute-done.7.refs_12_
  38.1 2.7 %collective-permute-start.8 = (bf16[64,1152]{1,0:T(8,128)(2,1)S(1)}, bf16[64,1152]{1,0:T(8,128)(2,1)S(1)}, u32[]{:S(2)}, u32[]{:S(2)}) collective-permute-start(bf16[64,1152]{1,0:T(8,128)(2,1)S(1)} %collective-permute-done.7.refs_12_), channel_id=1, source_target_pairs={{0,7},{1,0},{2,1},{3,2},{4,3},{5,4},{6,5},{7,6},{8,15},{9,8},{10,9... | collective-permute-start | bytes 442376 | tf_op jit(solution)/shard_map/ppermute | solution.py:372
  40.8 0.0 collective-permute-done.refs_4_
  40.8 1.6 %collective-permute-start.1 = (bf16[64,1152]{1,0:T(8,128)(2,1)S(1)}, bf16[64,1152]{1,0:T(8,128)(2,1)S(1)}, u32[]{:S(2)}, u32[]{:S(2)}) collective-permute-start(bf16[64,1152]{1,0:T(8,128)(2,1)S(1)} %collective-permute-done.refs_4_), channel_id=1, source_target_pairs={{0,7},{1,0},{2,1},{3,2},{4,3},{5,4},{6,5},{7,6},{8,15},{9,8},{10,9... | collective-permute-start | bytes 442376 | tf_op jit(solution)/shard_map/ppermute | solution.py:372
  42.4 0.0 collective-permute-done.11.refs_18_
  42.4 0.0 collective-permute-start.12
  42.4 3.0 %collective-permute-done.4.refs_9_ = bf16[64,1152]{1,0:T(8,128)(2,1)S(1)} collective-permute-done((bf16[64,1152]{1,0:T(8,128)(2,1)S(1)}, bf16[64,1152]{1,0:T(8,128)(2,1)S(1)}, u32[]{:S(2)}, u32[]{:S(2)}) %collective-permute-start.4) | collective-permute-done | bytes 147488 | tf_op jit(solution)/shard_map/ppermute | solution.py:369
  45.4 0.0 collective-permute-start.5
  45.4 0.0 collective-permute-done.8.refs_13_
  45.4 2.7 %collective-permute-start.9 = (bf16[64,1152]{1,0:T(8,128)(2,1)S(1)}, bf16[64,1152]{1,0:T(8,128)(2,1)S(1)}, u32[]{:S(2)}, u32[]{:S(2)}) collective-permute-start(bf16[64,1152]{1,0:T(8,128)(2,1)S(1)} %collective-permute-done.8.refs_13_), channel_id=1, source_target_pairs={{0,7},{1,0},{2,1},{3,2},{4,3},{5,4},{6,5},{7,6},{8,15},{9,8},{10,9... | collective-permute-start | bytes 442376 | tf_op jit(solution)/shard_map/ppermute | solution.py:372
  48.1 0.0 collective-permute-done.1.refs_5_
  48.1 0.8 collective-permute-start.2
  48.9 0.0 collective-permute-done.12.refs_17_
  48.9 0.6 collective-permute-start.13
  49.5 1.2 collective-permute-done.5.refs_8_
  50.8 0.0 collective-permute-start.6
  50.8 1.0 collective-permute-done.9.refs_14_
  51.7 3.5 %collective-permute-start.10 = (bf16[64,1152]{1,0:T(8,128)(2,1)S(1)}, bf16[64,1152]{1,0:T(8,128)(2,1)S(1)}, u32[]{:S(2)}, u32[]{:S(2)}) collective-permute-start(bf16[64,1152]{1,0:T(8,128)(2,1)S(1)} %collective-permute-done.9.refs_14_), channel_id=1, source_target_pairs={{0,7},{1,0},{2,1},{3,2},{4,3},{5,4},{6,5},{7,6},{8,15},{9,8},{10,9... | collective-permute-start | bytes 442376 | tf_op jit(solution)/shard_map/ppermute | solution.py:372
  55.3 0.0 collective-permute-done.2.refs_6_
  55.3 0.7 collective-permute-done.13.refs_16_
  56.0 2.3 %collective-permute-done.6.refs_7_ = bf16[64,1152]{1,0:T(8,128)(2,1)S(1)} collective-permute-done((bf16[64,1152]{1,0:T(8,128)(2,1)S(1)}, bf16[64,1152]{1,0:T(8,128)(2,1)S(1)}, u32[]{:S(2)}, u32[]{:S(2)}) %collective-permute-start.6) | collective-permute-done | bytes 147488 | tf_op jit(solution)/shard_map/ppermute | solution.py:369
  58.3 0.0 collective-permute-done.10.refs_15_
  58.3 5.0 %spatial.1 = (bf16[8,144,128]{2,1,0:T(8,128)(2,1)S(1)}, bf16[64,4608]{1,0:T(8,128)(2,1)S(1)}, bf16[64,4608]{1,0:T(8,128)(2,1)S(1)}) custom-call(s32[1]{0:T(128)} %bitcast.2.refs_0_.place_ref, bf16[432,1152]{1,0:T(8,128)(2,1)} %bitcast.12, f32[64,6912]{1,0:T(8,128)} %refs_2_.4, bf16[64,1152]{1,0:T(8,128)(2,1)S(1)} %get-tuple-element.16.refs_3_, ...), custom_call_target="tpu_custom_call" | custom-call | flops 1556086784 | bytes 8000000 | tf_op jit(solution)/shard_map/spatial/pallas_call | solution.py:155
  63.3 0.0 copy-start
  63.3 13.4 %all_to_all.21.refs_1_ = bf16[8,144,128]{2,1,0:T(8,128)(2,1)S(1)} all-to-all(bf16[8,144,128]{2,1,0:T(8,128)(2,1)S(1)} %get-tuple-element.18), channel_id=1, replica_groups=mesh['queue'=32,'tok'=8] {'tok'}, dimensions={0} | all-to-all | bytes 589824 | tf_op jit(solution)/shard_map/all_to_all | solution.py:416
  76.7 0.3 bundle.1
  77.0 0.1 reshape.21
  77.1 28.0 %all_to_all.22 = bf16[32,4,2432]{2,1,0:T(4,128)(2,1)S(1)} all-to-all(bf16[32,4,2432]{2,1,0:T(4,128)(2,1)S(1)} %reshape.21), channel_id=1, replica_groups=mesh['queue'=32,'tok'=8] {'queue'}, dimensions={0} | all-to-all | bytes 1245184 | tf_op jit(solution)/shard_map/all_to_all | solution.py:420
  105.1 0.1 reshape.22.refs_0_
  105.3 0.0 all-gather.3.cloned.1.call-done
  105.3 10.0 %temporal.1 = bf16[128,1152]{1,0:T(8,128)(2,1)S(1)} custom-call(bf16[128,2432]{1,0:T(8,128)(2,1)S(1)} %reshape.22.refs_0_, bf16[64,4608]{1,0:T(8,128)(2,1)S(1)} %get-tuple-element.20.refs_1_, bf16[64,4608]{1,0:T(8,128)(2,1)S(1)} %get-tuple-element.21.refs_2_, bf16[3,144,1152]{2,1,0:T(8,128)(2,1)} %bitcast.11, bf16[144,1152]{1,0:T(8,128)(2,1)} %refs_4_.1, ...), custom_call_target="tpu_custom_call" | custom-call | flops 1698693120 | bytes 15000000 | tf_op jit(solution)/shard_map/temporal/pallas_call | solution.py:302
  115.3 0.1 reshape.23
  115.4 13.1 %all_to_all.23 = bf16[32,4,1152]{2,1,0:T(4,128)(2,1)S(1)} all-to-all(bf16[32,4,1152]{2,1,0:T(4,128)(2,1)S(1)} %reshape.23), channel_id=1, replica_groups=mesh['queue'=32,'tok'=8] {'queue'}, dimensions={0} | all-to-all | bytes 589824 | tf_op jit(solution)/shard_map/all_to_all | solution.py:422
  128.4 0.1 reshape.24.refs_1_
  128.5 0.0 copy-done
  128.5 1.0 last.1
  (1 shorter events, 0.0 us)
Async XLA Ops:
  6.5 98.8 %all-gather.3.cloned.1.call-start = ((), (), s32[]{:S(2)}) async-start(), calls=%async_computation.4 | async-start | bytes 13381632 | tf_op jit(solution)/shard_map/all_gather | solution.py:405
  32.9 5.3 %collective-permute-start.3 = (bf16[64,1152]{1,0:T(8,128)(2,1)S(1)}, bf16[64,1152]{1,0:T(8,128)(2,1)S(1)}, u32[]{:S(2)}, u32[]{:S(2)}) collective-permute-start(bf16[64,1152]{1,0:T(8,128)(2,1)S(1)} %get-tuple-element.16.refs_3_), channel_id=1, source_target_pairs={{0,1},{1,2},{2,3},{3,4},{4,5},{5,6},{6,7},{7,0},{8,9},{9,10},{10,1... | collective-permute-start | bytes 442376 | tf_op jit(solution)/shard_map/ppermute | solution.py:369
  33.2 5.0 %collective-permute-start.7 = (bf16[64,1152]{1,0:T(8,128)(2,1)S(1)}, bf16[64,1152]{1,0:T(8,128)(2,1)S(1)}, u32[]{:S(2)}, u32[]{:S(2)}) collective-permute-start(bf16[64,1152]{1,0:T(8,128)(2,1)S(1)} %get-tuple-element.17.refs_11_), channel_id=1, source_target_pairs={{0,7},{1,0},{2,1},{3,2},{4,3},{5,4},{6,5},{7,6},{8,15},{9,8},{10,9... | collective-permute-start | bytes 442376 | tf_op jit(solution)/shard_map/ppermute | solution.py:372
  35.6 5.2 %collective-permute-start = (bf16[64,1152]{1,0:T(8,128)(2,1)S(1)}, bf16[64,1152]{1,0:T(8,128)(2,1)S(1)}, u32[]{:S(2)}, u32[]{:S(2)}) collective-permute-start(bf16[64,1152]{1,0:T(8,128)(2,1)S(1)} %get-tuple-element.16.refs_3_), channel_id=1, source_target_pairs={{0,7},{1,0},{2,1},{3,2},{4,3},{5,4},{6,5},{7,6},{8,15},{9,8},{10,9... | collective-permute-start | bytes 442376 | tf_op jit(solution)/shard_map/ppermute | solution.py:372
  35.6 6.8 %collective-permute-start.11 = (bf16[64,1152]{1,0:T(8,128)(2,1)S(1)}, bf16[64,1152]{1,0:T(8,128)(2,1)S(1)}, u32[]{:S(2)}, u32[]{:S(2)}) collective-permute-start(bf16[64,1152]{1,0:T(8,128)(2,1)S(1)} %get-tuple-element.17.refs_11_), channel_id=1, source_target_pairs={{0,1},{1,2},{2,3},{3,4},{4,5},{5,6},{6,7},{7,0},{8,9},{9,10},{10,1... | collective-permute-start | bytes 442376 | tf_op jit(solution)/shard_map/ppermute | solution.py:369
  38.1 7.2 %collective-permute-start.4 = (bf16[64,1152]{1,0:T(8,128)(2,1)S(1)}, bf16[64,1152]{1,0:T(8,128)(2,1)S(1)}, u32[]{:S(2)}, u32[]{:S(2)}) collective-permute-start(bf16[64,1152]{1,0:T(8,128)(2,1)S(1)} %collective-permute-done.3.refs_10_), channel_id=1, source_target_pairs={{0,1},{1,2},{2,3},{3,4},{4,5},{5,6},{6,7},{7,0},{8,9},{9,10},{10,1... | collective-permute-start | bytes 442376 | tf_op jit(solution)/shard_map/ppermute | solution.py:369
  38.1 7.2 %collective-permute-start.8 = (bf16[64,1152]{1,0:T(8,128)(2,1)S(1)}, bf16[64,1152]{1,0:T(8,128)(2,1)S(1)}, u32[]{:S(2)}, u32[]{:S(2)}) collective-permute-start(bf16[64,1152]{1,0:T(8,128)(2,1)S(1)} %collective-permute-done.7.refs_12_), channel_id=1, source_target_pairs={{0,7},{1,0},{2,1},{3,2},{4,3},{5,4},{6,5},{7,6},{8,15},{9,8},{10,9... | collective-permute-start | bytes 442376 | tf_op jit(solution)/shard_map/ppermute | solution.py:372
  40.8 7.2 %collective-permute-start.1 = (bf16[64,1152]{1,0:T(8,128)(2,1)S(1)}, bf16[64,1152]{1,0:T(8,128)(2,1)S(1)}, u32[]{:S(2)}, u32[]{:S(2)}) collective-permute-start(bf16[64,1152]{1,0:T(8,128)(2,1)S(1)} %collective-permute-done.refs_4_), channel_id=1, source_target_pairs={{0,7},{1,0},{2,1},{3,2},{4,3},{5,4},{6,5},{7,6},{8,15},{9,8},{10,9... | collective-permute-start | bytes 442376 | tf_op jit(solution)/shard_map/ppermute | solution.py:372
  42.4 6.5 %collective-permute-start.12 = (bf16[64,1152]{1,0:T(8,128)(2,1)S(1)}, bf16[64,1152]{1,0:T(8,128)(2,1)S(1)}, u32[]{:S(2)}, u32[]{:S(2)}) collective-permute-start(bf16[64,1152]{1,0:T(8,128)(2,1)S(1)} %collective-permute-done.11.refs_18_), channel_id=1, source_target_pairs={{0,1},{1,2},{2,3},{3,4},{4,5},{5,6},{6,7},{7,0},{8,9},{9,10},{10,1... | collective-permute-start | bytes 442376 | tf_op jit(solution)/shard_map/ppermute | solution.py:369
  45.4 5.4 %collective-permute-start.5 = (bf16[64,1152]{1,0:T(8,128)(2,1)S(1)}, bf16[64,1152]{1,0:T(8,128)(2,1)S(1)}, u32[]{:S(2)}, u32[]{:S(2)}) collective-permute-start(bf16[64,1152]{1,0:T(8,128)(2,1)S(1)} %collective-permute-done.4.refs_9_), channel_id=1, source_target_pairs={{0,1},{1,2},{2,3},{3,4},{4,5},{5,6},{6,7},{7,0},{8,9},{9,10},{10,1... | collective-permute-start | bytes 442376 | tf_op jit(solution)/shard_map/ppermute | solution.py:369
  45.4 6.4 %collective-permute-start.9 = (bf16[64,1152]{1,0:T(8,128)(2,1)S(1)}, bf16[64,1152]{1,0:T(8,128)(2,1)S(1)}, u32[]{:S(2)}, u32[]{:S(2)}) collective-permute-start(bf16[64,1152]{1,0:T(8,128)(2,1)S(1)} %collective-permute-done.8.refs_13_), channel_id=1, source_target_pairs={{0,7},{1,0},{2,1},{3,2},{4,3},{5,4},{6,5},{7,6},{8,15},{9,8},{10,9... | collective-permute-start | bytes 442376 | tf_op jit(solution)/shard_map/ppermute | solution.py:372
  48.1 7.2 %collective-permute-start.2 = (bf16[64,1152]{1,0:T(8,128)(2,1)S(1)}, bf16[64,1152]{1,0:T(8,128)(2,1)S(1)}, u32[]{:S(2)}, u32[]{:S(2)}) collective-permute-start(bf16[64,1152]{1,0:T(8,128)(2,1)S(1)} %collective-permute-done.1.refs_5_), channel_id=1, source_target_pairs={{0,7},{1,0},{2,1},{3,2},{4,3},{5,4},{6,5},{7,6},{8,15},{9,8},{10,9... | collective-permute-start | bytes 442376 | tf_op jit(solution)/shard_map/ppermute | solution.py:372
  48.9 7.1 %collective-permute-start.13 = (bf16[64,1152]{1,0:T(8,128)(2,1)S(1)}, bf16[64,1152]{1,0:T(8,128)(2,1)S(1)}, u32[]{:S(2)}, u32[]{:S(2)}) collective-permute-start(bf16[64,1152]{1,0:T(8,128)(2,1)S(1)} %collective-permute-done.12.refs_17_), channel_id=1, source_target_pairs={{0,1},{1,2},{2,3},{3,4},{4,5},{5,6},{6,7},{7,0},{8,9},{9,10},{10,1... | collective-permute-start | bytes 442376 | tf_op jit(solution)/shard_map/ppermute | solution.py:369
  50.8 7.5 %collective-permute-start.6 = (bf16[64,1152]{1,0:T(8,128)(2,1)S(1)}, bf16[64,1152]{1,0:T(8,128)(2,1)S(1)}, u32[]{:S(2)}, u32[]{:S(2)}) collective-permute-start(bf16[64,1152]{1,0:T(8,128)(2,1)S(1)} %collective-permute-done.5.refs_8_), channel_id=1, source_target_pairs={{0,1},{1,2},{2,3},{3,4},{4,5},{5,6},{6,7},{7,0},{8,9},{9,10},{10,1... | collective-permute-start | bytes 442376 | tf_op jit(solution)/shard_map/ppermute | solution.py:369
  51.7 6.6 %collective-permute-start.10 = (bf16[64,1152]{1,0:T(8,128)(2,1)S(1)}, bf16[64,1152]{1,0:T(8,128)(2,1)S(1)}, u32[]{:S(2)}, u32[]{:S(2)}) collective-permute-start(bf16[64,1152]{1,0:T(8,128)(2,1)S(1)} %collective-permute-done.9.refs_14_), channel_id=1, source_target_pairs={{0,7},{1,0},{2,1},{3,2},{4,3},{5,4},{6,5},{7,6},{8,15},{9,8},{10,9... | collective-permute-start | bytes 442376 | tf_op jit(solution)/shard_map/ppermute | solution.py:372
  63.3 65.2 %copy-start = (bf16[64,1152]{1,0:T(8,128)(2,1)S(1)}, bf16[64,1152]{1,0:T(8,128)(2,1)}, u32[]{:S(2)}) copy-start(bf16[64,1152]{1,0:T(8,128)(2,1)} %refs_2_.5) | copy-start | bytes 442372
Sparse Core Ops, SparseCore 0:
  31.5 67.5 all-gather.2

commit v10 on v9

--- a/solution.py
+++ b/solution.py
@@ -56,12 +56,12 @@
     tokens = held[...].reshape(2 * rows, width)
     side_ref[:, :width] = jnp.dot(moved, tokens, preferred_element_type=F32).astype(BF16)
     one, two = levels_ref[0].astype(F32), levels_ref[1].astype(F32)
-    side_ref[:, width:] = jnp.where(frame == 0, one, two).astype(BF16)
+    side_ref[:, width:] = jnp.broadcast_to(jnp.where(frame == 0, one, two), (2 * rows, 2 * rows)).astype(BF16)
 
 
 def order_matrix(line, rows):
     per = rows // (2 * line)
-    spot = lax.broadcasted_iota(jnp.int32, (rows, rows), 0)
+    spot = lax.broadcasted_iota(jnp.int32, (rows, 1), 0)
     frame = spot // per % 2
     source = frame * (rows // 2) + spot // (2 * per) * per + spot % per
     moved = (lax.broadcasted_iota(jnp.int32, (rows, rows), 1) == source).astype(BF16)
@@ -320,7 +320,7 @@
 def last_kernel(line, tail_ref, got_ref, fresh_ref, out_ref):
     rows = fresh_ref.shape[0]
     per = rows // line
-    spot = lax.broadcasted_iota(jnp.int32, (2 * rows, 2 * rows), 1)
+    spot = lax.broadcasted_iota(jnp.int32, (1, 2 * rows), 1)
     source = spot // per % 2 * rows + spot // (2 * per) * per + spot % per
     back = (lax.broadcasted_iota(jnp.int32, (2 * rows, 2 * rows), 0) == source).astype(BF16)
     values = jnp.dot(back, got_ref[...], preferred_element_type=F32).astype(BF16)

time: 137 us -> 137 us (level)
  no operation moved by 1% of the time
where the time goes in v10:
time: 137 us; the launch traced here: 136 us
  blocking collectives  77.3 us (56%)
  Pallas kernels  18.6 us (14%)
  starting transfers between devices  16.1 us (12%)
  between operations  13.5 us (10%)
  waiting for transfers between devices  9.34 us (7%)
    all_to_all x1, blocking collectives, per_device(): lax.all_to_all(sent.reshape(line, 2 * per, sent.shape[1]), 'queue', 0, 0,...  28 us
    all_to_all x1, blocking collectives, per_device(): lax.all_to_all(jnp.broadcast_to(chunk[None], (ring, size, width)), 'tok',...  22.9 us
    ppermute x7, starting transfers between devices, send_down(): return lax.ppermute(v, 'tok', down)  13.7 us
    all_to_all x1, blocking collectives, per_device(): mixed = lax.all_to_all(mixed, 'tok', 0, 0, tiled=True)  13.4 us
    all_to_all x1, blocking collectives, per_device(): lax.all_to_all(moved.reshape(line, 2 * per, width), 'queue', 0, 0, tiled=...  13.1 us
    pallas_call x1, Pallas kernels, temporal(): pl.pallas_call(lambda *refs: temporal_kernel(size, per, *refs), out_shape...  10 us
    ppermute x7, waiting for transfers between devices, send_up(): return lax.ppermute(v, 'tok', up)  8.31 us
    pallas_call x1, Pallas kernels, spatial(): pl.pallas_call(lambda *refs: spatial_kernel(offsets, *refs), out_shape=(j...  5.02 us
  transfers between devices with their start and end apart: 15, of which 6 were waited for; matrix products, arithmetic and copies ran while one was open for 0% of the time, Pallas kernels for 5%

profile of v10, /device:TPU:1, one launch (start us, length us, event | category | flops | bytes accessed | tf_op | source)
XLA Modules:
  0.0 136.3 jit_solution(10946546770371758455)
XLA Ops:
  6.5 0.0 all-gather.3.cloned.1.call-start
  6.5 1.0 select_select_fusion
  7.6 22.9 %all_to_all.20.chunks_ref = bf16[8,24,1152]{2,1,0:T(8,128)(2,1)S(1)} all-to-all(bf16[8,24,1152]{2,1,0:T(8,128)(2,1)S(1)} %broadcast_in_dim.18), channel_id=1, replica_groups=mesh['queue'=32,'tok'=8] {'tok'}, dimensions={0} | all-to-all | bytes 884736 | tf_op jit(solution)/shard_map/all_to_all | solution.py:391
  30.5 0.8 others.1
  31.3 0.0 all-gather.3.cloned.1.call-update
  31.3 1.5 %first.1 = (bf16[64,1152]{1,0:T(8,128)(2,1)S(1)}, bf16[64,1152]{1,0:T(8,128)(2,1)S(1)}, bf16[128,1280]{1,0:T(8,128)(2,1)S(1)}) custom-call(s32[2]{0:T(128)} %refs_0_.1, f32[64,6912]{1,0:T(8,128)} %refs_2_.4, bf16[2,64,1152]{2,1,0:T(8,128)(2,1)} %refs_2_.3), custom_call_target="tpu_custom_call" | custom-call | flops 40000000 | bytes 1500000 | tf_op jit(solution)/shard_map/first/pallas_call | solution.py:74
  32.9 0.3 collective-permute-start.3
  33.2 2.4 %collective-permute-start.7 = (bf16[64,1152]{1,0:T(8,128)(2,1)S(1)}, bf16[64,1152]{1,0:T(8,128)(2,1)S(1)}, u32[]{:S(2)}, u32[]{:S(2)}) collective-permute-start(bf16[64,1152]{1,0:T(8,128)(2,1)S(1)} %get-tuple-element.17.refs_11_), channel_id=1, source_target_pairs={{0,7},{1,0},{2,1},{3,2},{4,3},{5,4},{6,5},{7,6},{8,15},{9,8},{10,9... | collective-permute-start | bytes 442376 | tf_op jit(solution)/shard_map/ppermute | solution.py:372
  35.6 0.0 collective-permute-start
  35.6 1.4 %collective-permute-start.11 = (bf16[64,1152]{1,0:T(8,128)(2,1)S(1)}, bf16[64,1152]{1,0:T(8,128)(2,1)S(1)}, u32[]{:S(2)}, u32[]{:S(2)}) collective-permute-start(bf16[64,1152]{1,0:T(8,128)(2,1)S(1)} %get-tuple-element.17.refs_11_), channel_id=1, source_target_pairs={{0,1},{1,2},{2,3},{3,4},{4,5},{5,6},{6,7},{7,0},{8,9},{9,10},{10,1... | collective-permute-start | bytes 442376 | tf_op jit(solution)/shard_map/ppermute | solution.py:369
  37.1 1.1 collective-permute-done.3.refs_10_
  38.1 0.0 collective-permute-start.4
  38.1 0.0 collective-permute-done.7.refs_12_
  38.1 2.7 %collective-permute-start.8 = (bf16[64,1152]{1,0:T(8,128)(2,1)S(1)}, bf16[64,1152]{1,0:T(8,128)(2,1)S(1)}, u32[]{:S(2)}, u32[]{:S(2)}) collective-permute-start(bf16[64,1152]{1,0:T(8,128)(2,1)S(1)} %collective-permute-done.7.refs_12_), channel_id=1, source_target_pairs={{0,7},{1,0},{2,1},{3,2},{4,3},{5,4},{6,5},{7,6},{8,15},{9,8},{10,9... | collective-permute-start | bytes 442376 | tf_op jit(solution)/shard_map/ppermute | solution.py:372
  40.8 0.0 collective-permute-done.refs_4_
  40.8 1.6 %collective-permute-start.1 = (bf16[64,1152]{1,0:T(8,128)(2,1)S(1)}, bf16[64,1152]{1,0:T(8,128)(2,1)S(1)}, u32[]{:S(2)}, u32[]{:S(2)}) collective-permute-start(bf16[64,1152]{1,0:T(8,128)(2,1)S(1)} %collective-permute-done.refs_4_), channel_id=1, source_target_pairs={{0,7},{1,0},{2,1},{3,2},{4,3},{5,4},{6,5},{7,6},{8,15},{9,8},{10,9... | collective-permute-start | bytes 442376 | tf_op jit(solution)/shard_map/ppermute | solution.py:372
  42.4 0.0 collective-permute-done.11.refs_18_
  42.4 0.0 collective-permute-start.12
  42.4 3.0 %collective-permute-done.4.refs_9_ = bf16[64,1152]{1,0:T(8,128)(2,1)S(1)} collective-permute-done((bf16[64,1152]{1,0:T(8,128)(2,1)S(1)}, bf16[64,1152]{1,0:T(8,128)(2,1)S(1)}, u32[]{:S(2)}, u32[]{:S(2)}) %collective-permute-start.4) | collective-permute-done | bytes 147488 | tf_op jit(solution)/shard_map/ppermute | solution.py:369
  45.4 0.0 collective-permute-start.5
  45.4 0.0 collective-permute-done.8.refs_13_
  45.4 2.7 %collective-permute-start.9 = (bf16[64,1152]{1,0:T(8,128)(2,1)S(1)}, bf16[64,1152]{1,0:T(8,128)(2,1)S(1)}, u32[]{:S(2)}, u32[]{:S(2)}) collective-permute-start(bf16[64,1152]{1,0:T(8,128)(2,1)S(1)} %collective-permute-done.8.refs_13_), channel_id=1, source_target_pairs={{0,7},{1,0},{2,1},{3,2},{4,3},{5,4},{6,5},{7,6},{8,15},{9,8},{10,9... | collective-permute-start | bytes 442376 | tf_op jit(solution)/shard_map/ppermute | solution.py:372
  48.1 0.0 collective-permute-done.1.refs_5_
  48.1 0.8 collective-permute-start.2
  48.9 0.0 collective-permute-done.12.refs_17_
  48.9 0.6 collective-permute-start.13
  49.5 1.2 collective-permute-done.5.refs_8_
  50.8 0.0 collective-permute-start.6
  50.8 1.0 collective-permute-done.9.refs_14_
  51.7 3.5 %collective-permute-start.10 = (bf16[64,1152]{1,0:T(8,128)(2,1)S(1)}, bf16[64,1152]{1,0:T(8,128)(2,1)S(1)}, u32[]{:S(2)}, u32[]{:S(2)}) collective-permute-start(bf16[64,1152]{1,0:T(8,128)(2,1)S(1)} %collective-permute-done.9.refs_14_), channel_id=1, source_target_pairs={{0,7},{1,0},{2,1},{3,2},{4,3},{5,4},{6,5},{7,6},{8,15},{9,8},{10,9... | collective-permute-start | bytes 442376 | tf_op jit(solution)/shard_map/ppermute | solution.py:372
  55.3 0.0 collective-permute-done.2.refs_6_
  55.3 0.7 collective-permute-done.13.refs_16_
  56.0 2.3 %collective-permute-done.6.refs_7_ = bf16[64,1152]{1,0:T(8,128)(2,1)S(1)} collective-permute-done((bf16[64,1152]{1,0:T(8,128)(2,1)S(1)}, bf16[64,1152]{1,0:T(8,128)(2,1)S(1)}, u32[]{:S(2)}, u32[]{:S(2)}) %collective-permute-start.6) | collective-permute-done | bytes 147488 | tf_op jit(solution)/shard_map/ppermute | solution.py:369
  58.3 0.0 collective-permute-done.10.refs_15_
  58.3 5.0 %spatial.1 = (bf16[8,144,128]{2,1,0:T(8,128)(2,1)S(1)}, bf16[64,4608]{1,0:T(8,128)(2,1)S(1)}, bf16[64,4608]{1,0:T(8,128)(2,1)S(1)}) custom-call(s32[1]{0:T(128)} %bitcast.2.refs_0_.place_ref, bf16[432,1152]{1,0:T(8,128)(2,1)} %bitcast.12, f32[64,6912]{1,0:T(8,128)} %refs_2_.4, bf16[64,1152]{1,0:T(8,128)(2,1)S(1)} %get-tuple-element.16.refs_3_, ...), custom_call_target="tpu_custom_call" | custom-call | flops 1556086784 | bytes 8000000 | tf_op jit(solution)/shard_map/spatial/pallas_call | solution.py:155
  63.3 0.0 copy-start
  63.3 13.4 %all_to_all.21.refs_1_ = bf16[8,144,128]{2,1,0:T(8,128)(2,1)S(1)} all-to-all(bf16[8,144,128]{2,1,0:T(8,128)(2,1)S(1)} %get-tuple-element.18), channel_id=1, replica_groups=mesh['queue'=32,'tok'=8] {'tok'}, dimensions={0} | all-to-all | bytes 589824 | tf_op jit(solution)/shard_map/all_to_all | solution.py:416
  76.7 0.3 bundle.1
  77.0 0.1 reshape.21
  77.1 28.0 %all_to_all.22 = bf16[32,4,2432]{2,1,0:T(4,128)(2,1)S(1)} all-to-all(bf16[32,4,2432]{2,1,0:T(4,128)(2,1)S(1)} %reshape.21), channel_id=1, replica_groups=mesh['queue'=32,'tok'=8] {'queue'}, dimensions={0} | all-to-all | bytes 1245184 | tf_op jit(solution)/shard_map/all_to_all | solution.py:420
  105.1 0.1 reshape.22.refs_0_
  105.3 0.0 all-gather.3.cloned.1.call-done
  105.3 10.0 %temporal.1 = bf16[128,1152]{1,0:T(8,128)(2,1)S(1)} custom-call(bf16[128,2432]{1,0:T(8,128)(2,1)S(1)} %reshape.22.refs_0_, bf16[64,4608]{1,0:T(8,128)(2,1)S(1)} %get-tuple-element.20.refs_1_, bf16[64,4608]{1,0:T(8,128)(2,1)S(1)} %get-tuple-element.21.refs_2_, bf16[3,144,1152]{2,1,0:T(8,128)(2,1)} %bitcast.11, bf16[144,1152]{1,0:T(8,128)(2,1)} %refs_4_.1, ...), custom_call_target="tpu_custom_call" | custom-call | flops 1698693120 | bytes 15000000 | tf_op jit(solution)/shard_map/temporal/pallas_call | solution.py:302
  115.3 0.1 reshape.23
  115.4 13.1 %all_to_all.23 = bf16[32,4,1152]{2,1,0:T(4,128)(2,1)S(1)} all-to-all(bf16[32,4,1152]{2,1,0:T(4,128)(2,1)S(1)} %reshape.23), channel_id=1, replica_groups=mesh['queue'=32,'tok'=8] {'queue'}, dimensions={0} | all-to-all | bytes 589824 | tf_op jit(solution)/shard_map/all_to_all | solution.py:422
  128.4 0.1 reshape.24.refs_1_
  128.5 0.0 copy-done
  128.5 1.0 last.1
  (1 shorter events, 0.0 us)
Async XLA Ops:
  6.5 98.8 %all-gather.3.cloned.1.call-start = ((), (), s32[]{:S(2)}) async-start(), calls=%async_computation.4 | async-start | bytes 13381632 | tf_op jit(solution)/shard_map/all_gather | solution.py:405
  32.9 5.3 %collective-permute-start.3 = (bf16[64,1152]{1,0:T(8,128)(2,1)S(1)}, bf16[64,1152]{1,0:T(8,128)(2,1)S(1)}, u32[]{:S(2)}, u32[]{:S(2)}) collective-permute-start(bf16[64,1152]{1,0:T(8,128)(2,1)S(1)} %get-tuple-element.16.refs_3_), channel_id=1, source_target_pairs={{0,1},{1,2},{2,3},{3,4},{4,5},{5,6},{6,7},{7,0},{8,9},{9,10},{10,1... | collective-permute-start | bytes 442376 | tf_op jit(solution)/shard_map/ppermute | solution.py:369
  33.2 5.0 %collective-permute-start.7 = (bf16[64,1152]{1,0:T(8,128)(2,1)S(1)}, bf16[64,1152]{1,0:T(8,128)(2,1)S(1)}, u32[]{:S(2)}, u32[]{:S(2)}) collective-permute-start(bf16[64,1152]{1,0:T(8,128)(2,1)S(1)} %get-tuple-element.17.refs_11_), channel_id=1, source_target_pairs={{0,7},{1,0},{2,1},{3,2},{4,3},{5,4},{6,5},{7,6},{8,15},{9,8},{10,9... | collective-permute-start | bytes 442376 | tf_op jit(solution)/shard_map/ppermute | solution.py:372
  35.6 5.2 %collective-permute-start = (bf16[64,1152]{1,0:T(8,128)(2,1)S(1)}, bf16[64,1152]{1,0:T(8,128)(2,1)S(1)}, u32[]{:S(2)}, u32[]{:S(2)}) collective-permute-start(bf16[64,1152]{1,0:T(8,128)(2,1)S(1)} %get-tuple-element.16.refs_3_), channel_id=1, source_target_pairs={{0,7},{1,0},{2,1},{3,2},{4,3},{5,4},{6,5},{7,6},{8,15},{9,8},{10,9... | collective-permute-start | bytes 442376 | tf_op jit(solution)/shard_map/ppermute | solution.py:372
  35.6 6.8 %collective-permute-start.11 = (bf16[64,1152]{1,0:T(8,128)(2,1)S(1)}, bf16[64,1152]{1,0:T(8,128)(2,1)S(1)}, u32[]{:S(2)}, u32[]{:S(2)}) collective-permute-start(bf16[64,1152]{1,0:T(8,128)(2,1)S(1)} %get-tuple-element.17.refs_11_), channel_id=1, source_target_pairs={{0,1},{1,2},{2,3},{3,4},{4,5},{5,6},{6,7},{7,0},{8,9},{9,10},{10,1... | collective-permute-start | bytes 442376 | tf_op jit(solution)/shard_map/ppermute | solution.py:369
  38.1 7.2 %collective-permute-start.4 = (bf16[64,1152]{1,0:T(8,128)(2,1)S(1)}, bf16[64,1152]{1,0:T(8,128)(2,1)S(1)}, u32[]{:S(2)}, u32[]{:S(2)}) collective-permute-start(bf16[64,1152]{1,0:T(8,128)(2,1)S(1)} %collective-permute-done.3.refs_10_), channel_id=1, source_target_pairs={{0,1},{1,2},{2,3},{3,4},{4,5},{5,6},{6,7},{7,0},{8,9},{9,10},{10,1... | collective-permute-start | bytes 442376 | tf_op jit(solution)/shard_map/ppermute | solution.py:369
  38.1 7.2 %collective-permute-start.8 = (bf16[64,1152]{1,0:T(8,128)(2,1)S(1)}, bf16[64,1152]{1,0:T(8,128)(2,1)S(1)}, u32[]{:S(2)}, u32[]{:S(2)}) collective-permute-start(bf16[64,1152]{1,0:T(8,128)(2,1)S(1)} %collective-permute-done.7.refs_12_), channel_id=1, source_target_pairs={{0,7},{1,0},{2,1},{3,2},{4,3},{5,4},{6,5},{7,6},{8,15},{9,8},{10,9... | collective-permute-start | bytes 442376 | tf_op jit(solution)/shard_map/ppermute | solution.py:372
  40.8 7.2 %collective-permute-start.1 = (bf16[64,1152]{1,0:T(8,128)(2,1)S(1)}, bf16[64,1152]{1,0:T(8,128)(2,1)S(1)}, u32[]{:S(2)}, u32[]{:S(2)}) collective-permute-start(bf16[64,1152]{1,0:T(8,128)(2,1)S(1)} %collective-permute-done.refs_4_), channel_id=1, source_target_pairs={{0,7},{1,0},{2,1},{3,2},{4,3},{5,4},{6,5},{7,6},{8,15},{9,8},{10,9... | collective-permute-start | bytes 442376 | tf_op jit(solution)/shard_map/ppermute | solution.py:372
  42.4 6.5 %collective-permute-start.12 = (bf16[64,1152]{1,0:T(8,128)(2,1)S(1)}, bf16[64,1152]{1,0:T(8,128)(2,1)S(1)}, u32[]{:S(2)}, u32[]{:S(2)}) collective-permute-start(bf16[64,1152]{1,0:T(8,128)(2,1)S(1)} %collective-permute-done.11.refs_18_), channel_id=1, source_target_pairs={{0,1},{1,2},{2,3},{3,4},{4,5},{5,6},{6,7},{7,0},{8,9},{9,10},{10,1... | collective-permute-start | bytes 442376 | tf_op jit(solution)/shard_map/ppermute | solution.py:369
  45.4 5.4 %collective-permute-start.5 = (bf16[64,1152]{1,0:T(8,128)(2,1)S(1)}, bf16[64,1152]{1,0:T(8,128)(2,1)S(1)}, u32[]{:S(2)}, u32[]{:S(2)}) collective-permute-start(bf16[64,1152]{1,0:T(8,128)(2,1)S(1)} %collective-permute-done.4.refs_9_), channel_id=1, source_target_pairs={{0,1},{1,2},{2,3},{3,4},{4,5},{5,6},{6,7},{7,0},{8,9},{9,10},{10,1... | collective-permute-start | bytes 442376 | tf_op jit(solution)/shard_map/ppermute | solution.py:369
  45.4 6.4 %collective-permute-start.9 = (bf16[64,1152]{1,0:T(8,128)(2,1)S(1)}, bf16[64,1152]{1,0:T(8,128)(2,1)S(1)}, u32[]{:S(2)}, u32[]{:S(2)}) collective-permute-start(bf16[64,1152]{1,0:T(8,128)(2,1)S(1)} %collective-permute-done.8.refs_13_), channel_id=1, source_target_pairs={{0,7},{1,0},{2,1},{3,2},{4,3},{5,4},{6,5},{7,6},{8,15},{9,8},{10,9... | collective-permute-start | bytes 442376 | tf_op jit(solution)/shard_map/ppermute | solution.py:372
  48.1 7.2 %collective-permute-start.2 = (bf16[64,1152]{1,0:T(8,128)(2,1)S(1)}, bf16[64,1152]{1,0:T(8,128)(2,1)S(1)}, u32[]{:S(2)}, u32[]{:S(2)}) collective-permute-start(bf16[64,1152]{1,0:T(8,128)(2,1)S(1)} %collective-permute-done.1.refs_5_), channel_id=1, source_target_pairs={{0,7},{1,0},{2,1},{3,2},{4,3},{5,4},{6,5},{7,6},{8,15},{9,8},{10,9... | collective-permute-start | bytes 442376 | tf_op jit(solution)/shard_map/ppermute | solution.py:372
  48.9 7.1 %collective-permute-start.13 = (bf16[64,1152]{1,0:T(8,128)(2,1)S(1)}, bf16[64,1152]{1,0:T(8,128)(2,1)S(1)}, u32[]{:S(2)}, u32[]{:S(2)}) collective-permute-start(bf16[64,1152]{1,0:T(8,128)(2,1)S(1)} %collective-permute-done.12.refs_17_), channel_id=1, source_target_pairs={{0,1},{1,2},{2,3},{3,4},{4,5},{5,6},{6,7},{7,0},{8,9},{9,10},{10,1... | collective-permute-start | bytes 442376 | tf_op jit(solution)/shard_map/ppermute | solution.py:369
  50.8 7.5 %collective-permute-start.6 = (bf16[64,1152]{1,0:T(8,128)(2,1)S(1)}, bf16[64,1152]{1,0:T(8,128)(2,1)S(1)}, u32[]{:S(2)}, u32[]{:S(2)}) collective-permute-start(bf16[64,1152]{1,0:T(8,128)(2,1)S(1)} %collective-permute-done.5.refs_8_), channel_id=1, source_target_pairs={{0,1},{1,2},{2,3},{3,4},{4,5},{5,6},{6,7},{7,0},{8,9},{9,10},{10,1... | collective-permute-start | bytes 442376 | tf_op jit(solution)/shard_map/ppermute | solution.py:369
  51.7 6.6 %collective-permute-start.10 = (bf16[64,1152]{1,0:T(8,128)(2,1)S(1)}, bf16[64,1152]{1,0:T(8,128)(2,1)S(1)}, u32[]{:S(2)}, u32[]{:S(2)}) collective-permute-start(bf16[64,1152]{1,0:T(8,128)(2,1)S(1)} %collective-permute-done.9.refs_14_), channel_id=1, source_target_pairs={{0,7},{1,0},{2,1},{3,2},{4,3},{5,4},{6,5},{7,6},{8,15},{9,8},{10,9... | collective-permute-start | bytes 442376 | tf_op jit(solution)/shard_map/ppermute | solution.py:372
  63.3 65.2 %copy-start = (bf16[64,1152]{1,0:T(8,128)(2,1)S(1)}, bf16[64,1152]{1,0:T(8,128)(2,1)}, u32[]{:S(2)}) copy-start(bf16[64,1152]{1,0:T(8,128)(2,1)} %refs_2_.5) | copy-start | bytes 442372
Sparse Core Ops, SparseCore 0:
  31.5 67.5 all-gather.2

commit v11 on v9

--- a/solution.py
+++ b/solution.py
@@ -136,7 +136,7 @@
             weights = jnp.exp2(scores - jnp.max(scores, axis=0, keepdims=True))
             total = jnp.sum(weights, axis=0, keepdims=True)
             mixed = jnp.dot(valued, weights.astype(BF16), preferred_element_type=F32)
-            heads.append((mixed / total).astype(BF16))
+            heads.append((mixed * (1.0 / total)).astype(BF16))
         attended = jnp.concatenate(heads, axis=0)
         for n, offset in enumerate(offsets[j]):
             owner = lax.rem(place_ref[0] + offset + ring, ring)

time: 137 us -> 137 us (level)
  no operation moved by 1% of the time
where the time goes in v11:
time: 137 us; the launch traced here: 136 us
  blocking collectives  77.3 us (56%)
  Pallas kernels  18.6 us (14%)
  starting transfers between devices  16.1 us (12%)
  between operations  13.5 us (10%)
  waiting for transfers between devices  9.34 us (7%)
    all_to_all x1, blocking collectives, per_device(): lax.all_to_all(sent.reshape(line, 2 * per, sent.shape[1]), 'queue', 0, 0,...  28 us
    all_to_all x1, blocking collectives, per_device(): lax.all_to_all(jnp.broadcast_to(chunk[None], (ring, size, width)), 'tok',...  22.9 us
    ppermute x7, starting transfers between devices, send_down(): return lax.ppermute(v, 'tok', down)  13.7 us
    all_to_all x1, blocking collectives, per_device(): mixed = lax.all_to_all(mixed, 'tok', 0, 0, tiled=True)  13.4 us
    all_to_all x1, blocking collectives, per_device(): lax.all_to_all(moved.reshape(line, 2 * per, width), 'queue', 0, 0, tiled=...  13.1 us
    pallas_call x1, Pallas kernels, temporal(): pl.pallas_call(lambda *refs: temporal_kernel(size, per, *refs), out_shape...  10 us
    ppermute x7, waiting for transfers between devices, send_up(): return lax.ppermute(v, 'tok', up)  8.31 us
    pallas_call x1, Pallas kernels, spatial(): pl.pallas_call(lambda *refs: spatial_kernel(offsets, *refs), out_shape=(j...  5.02 us
  transfers between devices with their start and end apart: 15, of which 6 were waited for; matrix products, arithmetic and copies ran while one was open for 0% of the time, Pallas kernels for 5%

profile of v11, /device:TPU:1, one launch (start us, length us, event | category | flops | bytes accessed | tf_op | source)
XLA Modules:
  0.0 136.3 jit_solution(10946546770371758455)
XLA Ops:
  6.5 0.0 all-gather.3.cloned.1.call-start
  6.5 1.0 select_select_fusion
  7.6 22.9 %all_to_all.20.chunks_ref = bf16[8,24,1152]{2,1,0:T(8,128)(2,1)S(1)} all-to-all(bf16[8,24,1152]{2,1,0:T(8,128)(2,1)S(1)} %broadcast_in_dim.18), channel_id=1, replica_groups=mesh['queue'=32,'tok'=8] {'tok'}, dimensions={0} | all-to-all | bytes 884736 | tf_op jit(solution)/shard_map/all_to_all | solution.py:391
  30.5 0.8 others.1
  31.3 0.0 all-gather.3.cloned.1.call-update
  31.3 1.5 %first.1 = (bf16[64,1152]{1,0:T(8,128)(2,1)S(1)}, bf16[64,1152]{1,0:T(8,128)(2,1)S(1)}, bf16[128,1280]{1,0:T(8,128)(2,1)S(1)}) custom-call(s32[2]{0:T(128)} %refs_0_.1, f32[64,6912]{1,0:T(8,128)} %refs_2_.4, bf16[2,64,1152]{2,1,0:T(8,128)(2,1)} %refs_2_.3), custom_call_target="tpu_custom_call" | custom-call | flops 40000000 | bytes 1500000 | tf_op jit(solution)/shard_map/first/pallas_call | solution.py:74
  32.9 0.3 collective-permute-start.3
  33.2 2.4 %collective-permute-start.7 = (bf16[64,1152]{1,0:T(8,128)(2,1)S(1)}, bf16[64,1152]{1,0:T(8,128)(2,1)S(1)}, u32[]{:S(2)}, u32[]{:S(2)}) collective-permute-start(bf16[64,1152]{1,0:T(8,128)(2,1)S(1)} %get-tuple-element.17.refs_11_), channel_id=1, source_target_pairs={{0,7},{1,0},{2,1},{3,2},{4,3},{5,4},{6,5},{7,6},{8,15},{9,8},{10,9... | collective-permute-start | bytes 442376 | tf_op jit(solution)/shard_map/ppermute | solution.py:372
  35.6 0.0 collective-permute-start
  35.6 1.4 %collective-permute-start.11 = (bf16[64,1152]{1,0:T(8,128)(2,1)S(1)}, bf16[64,1152]{1,0:T(8,128)(2,1)S(1)}, u32[]{:S(2)}, u32[]{:S(2)}) collective-permute-start(bf16[64,1152]{1,0:T(8,128)(2,1)S(1)} %get-tuple-element.17.refs_11_), channel_id=1, source_target_pairs={{0,1},{1,2},{2,3},{3,4},{4,5},{5,6},{6,7},{7,0},{8,9},{9,10},{10,1... | collective-permute-start | bytes 442376 | tf_op jit(solution)/shard_map/ppermute | solution.py:369
  37.1 1.1 collective-permute-done.3.refs_10_
  38.1 0.0 collective-permute-start.4
  38.1 0.0 collective-permute-done.7.refs_12_
  38.1 2.7 %collective-permute-start.8 = (bf16[64,1152]{1,0:T(8,128)(2,1)S(1)}, bf16[64,1152]{1,0:T(8,128)(2,1)S(1)}, u32[]{:S(2)}, u32[]{:S(2)}) collective-permute-start(bf16[64,1152]{1,0:T(8,128)(2,1)S(1)} %collective-permute-done.7.refs_12_), channel_id=1, source_target_pairs={{0,7},{1,0},{2,1},{3,2},{4,3},{5,4},{6,5},{7,6},{8,15},{9,8},{10,9... | collective-permute-start | bytes 442376 | tf_op jit(solution)/shard_map/ppermute | solution.py:372
  40.8 0.0 collective-permute-done.refs_4_
  40.8 1.6 %collective-permute-start.1 = (bf16[64,1152]{1,0:T(8,128)(2,1)S(1)}, bf16[64,1152]{1,0:T(8,128)(2,1)S(1)}, u32[]{:S(2)}, u32[]{:S(2)}) collective-permute-start(bf16[64,1152]{1,0:T(8,128)(2,1)S(1)} %collective-permute-done.refs_4_), channel_id=1, source_target_pairs={{0,7},{1,0},{2,1},{3,2},{4,3},{5,4},{6,5},{7,6},{8,15},{9,8},{10,9... | collective-permute-start | bytes 442376 | tf_op jit(solution)/shard_map/ppermute | solution.py:372
  42.4 0.0 collective-permute-done.11.refs_18_
  42.4 0.0 collective-permute-start.12
  42.4 3.0 %collective-permute-done.4.refs_9_ = bf16[64,1152]{1,0:T(8,128)(2,1)S(1)} collective-permute-done((bf16[64,1152]{1,0:T(8,128)(2,1)S(1)}, bf16[64,1152]{1,0:T(8,128)(2,1)S(1)}, u32[]{:S(2)}, u32[]{:S(2)}) %collective-permute-start.4) | collective-permute-done | bytes 147488 | tf_op jit(solution)/shard_map/ppermute | solution.py:369
  45.4 0.0 collective-permute-start.5
  45.4 0.0 collective-permute-done.8.refs_13_
  45.4 2.7 %collective-permute-start.9 = (bf16[64,1152]{1,0:T(8,128)(2,1)S(1)}, bf16[64,1152]{1,0:T(8,128)(2,1)S(1)}, u32[]{:S(2)}, u32[]{:S(2)}) collective-permute-start(bf16[64,1152]{1,0:T(8,128)(2,1)S(1)} %collective-permute-done.8.refs_13_), channel_id=1, source_target_pairs={{0,7},{1,0},{2,1},{3,2},{4,3},{5,4},{6,5},{7,6},{8,15},{9,8},{10,9... | collective-permute-start | bytes 442376 | tf_op jit(solution)/shard_map/ppermute | solution.py:372
  48.1 0.0 collective-permute-done.1.refs_5_
  48.1 0.8 collective-permute-start.2
  48.9 0.0 collective-permute-done.12.refs_17_
  48.9 0.6 collective-permute-start.13
  49.5 1.2 collective-permute-done.5.refs_8_
  50.8 0.0 collective-permute-start.6
  50.8 1.0 collective-permute-done.9.refs_14_
  51.7 3.5 %collective-permute-start.10 = (bf16[64,1152]{1,0:T(8,128)(2,1)S(1)}, bf16[64,1152]{1,0:T(8,128)(2,1)S(1)}, u32[]{:S(2)}, u32[]{:S(2)}) collective-permute-start(bf16[64,1152]{1,0:T(8,128)(2,1)S(1)} %collective-permute-done.9.refs_14_), channel_id=1, source_target_pairs={{0,7},{1,0},{2,1},{3,2},{4,3},{5,4},{6,5},{7,6},{8,15},{9,8},{10,9... | collective-permute-start | bytes 442376 | tf_op jit(solution)/shard_map/ppermute | solution.py:372
  55.3 0.0 collective-permute-done.2.refs_6_
  55.3 0.7 collective-permute-done.13.refs_16_
  56.0 2.3 %collective-permute-done.6.refs_7_ = bf16[64,1152]{1,0:T(8,128)(2,1)S(1)} collective-permute-done((bf16[64,1152]{1,0:T(8,128)(2,1)S(1)}, bf16[64,1152]{1,0:T(8,128)(2,1)S(1)}, u32[]{:S(2)}, u32[]{:S(2)}) %collective-permute-start.6) | collective-permute-done | bytes 147488 | tf_op jit(solution)/shard_map/ppermute | solution.py:369
  58.3 0.0 collective-permute-done.10.refs_15_
  58.3 5.0 %spatial.1 = (bf16[8,144,128]{2,1,0:T(8,128)(2,1)S(1)}, bf16[64,4608]{1,0:T(8,128)(2,1)S(1)}, bf16[64,4608]{1,0:T(8,128)(2,1)S(1)}) custom-call(s32[1]{0:T(128)} %bitcast.2.refs_0_.place_ref, bf16[432,1152]{1,0:T(8,128)(2,1)} %bitcast.12, f32[64,6912]{1,0:T(8,128)} %refs_2_.4, bf16[64,1152]{1,0:T(8,128)(2,1)S(1)} %get-tuple-element.16.refs_3_, ...), custom_call_target="tpu_custom_call" | custom-call | flops 1556086784 | bytes 8000000 | tf_op jit(solution)/shard_map/spatial/pallas_call | solution.py:155
  63.3 0.0 copy-start
  63.3 13.4 %all_to_all.21.refs_1_ = bf16[8,144,128]{2,1,0:T(8,128)(2,1)S(1)} all-to-all(bf16[8,144,128]{2,1,0:T(8,128)(2,1)S(1)} %get-tuple-element.18), channel_id=1, replica_groups=mesh['queue'=32,'tok'=8] {'tok'}, dimensions={0} | all-to-all | bytes 589824 | tf_op jit(solution)/shard_map/all_to_all | solution.py:416
  76.7 0.3 bundle.1
  77.0 0.1 reshape.21
  77.1 28.0 %all_to_all.22 = bf16[32,4,2432]{2,1,0:T(4,128)(2,1)S(1)} all-to-all(bf16[32,4,2432]{2,1,0:T(4,128)(2,1)S(1)} %reshape.21), channel_id=1, replica_groups=mesh['queue'=32,'tok'=8] {'queue'}, dimensions={0} | all-to-all | bytes 1245184 | tf_op jit(solution)/shard_map/all_to_all | solution.py:420
  105.1 0.1 reshape.22.refs_0_
  105.3 0.0 all-gather.3.cloned.1.call-done
  105.3 10.0 %temporal.1 = bf16[128,1152]{1,0:T(8,128)(2,1)S(1)} custom-call(bf16[128,2432]{1,0:T(8,128)(2,1)S(1)} %reshape.22.refs_0_, bf16[64,4608]{1,0:T(8,128)(2,1)S(1)} %get-tuple-element.20.refs_1_, bf16[64,4608]{1,0:T(8,128)(2,1)S(1)} %get-tuple-element.21.refs_2_, bf16[3,144,1152]{2,1,0:T(8,128)(2,1)} %bitcast.11, bf16[144,1152]{1,0:T(8,128)(2,1)} %refs_4_.1, ...), custom_call_target="tpu_custom_call" | custom-call | flops 1698693120 | bytes 15000000 | tf_op jit(solution)/shard_map/temporal/pallas_call | solution.py:302
  115.3 0.1 reshape.23
  115.4 13.1 %all_to_all.23 = bf16[32,4,1152]{2,1,0:T(4,128)(2,1)S(1)} all-to-all(bf16[32,4,1152]{2,1,0:T(4,128)(2,1)S(1)} %reshape.23), channel_id=1, replica_groups=mesh['queue'=32,'tok'=8] {'queue'}, dimensions={0} | all-to-all | bytes 589824 | tf_op jit(solution)/shard_map/all_to_all | solution.py:422
  128.4 0.1 reshape.24.refs_1_
  128.5 0.0 copy-done
  128.5 1.0 last.1
  (1 shorter events, 0.0 us)
Async XLA Ops:
  6.5 98.8 %all-gather.3.cloned.1.call-start = ((), (), s32[]{:S(2)}) async-start(), calls=%async_computation.4 | async-start | bytes 13381632 | tf_op jit(solution)/shard_map/all_gather | solution.py:405
  32.9 5.3 %collective-permute-start.3 = (bf16[64,1152]{1,0:T(8,128)(2,1)S(1)}, bf16[64,1152]{1,0:T(8,128)(2,1)S(1)}, u32[]{:S(2)}, u32[]{:S(2)}) collective-permute-start(bf16[64,1152]{1,0:T(8,128)(2,1)S(1)} %get-tuple-element.16.refs_3_), channel_id=1, source_target_pairs={{0,1},{1,2},{2,3},{3,4},{4,5},{5,6},{6,7},{7,0},{8,9},{9,10},{10,1... | collective-permute-start | bytes 442376 | tf_op jit(solution)/shard_map/ppermute | solution.py:369
  33.2 5.0 %collective-permute-start.7 = (bf16[64,1152]{1,0:T(8,128)(2,1)S(1)}, bf16[64,1152]{1,0:T(8,128)(2,1)S(1)}, u32[]{:S(2)}, u32[]{:S(2)}) collective-permute-start(bf16[64,1152]{1,0:T(8,128)(2,1)S(1)} %get-tuple-element.17.refs_11_), channel_id=1, source_target_pairs={{0,7},{1,0},{2,1},{3,2},{4,3},{5,4},{6,5},{7,6},{8,15},{9,8},{10,9... | collective-permute-start | bytes 442376 | tf_op jit(solution)/shard_map/ppermute | solution.py:372
  35.6 5.2 %collective-permute-start = (bf16[64,1152]{1,0:T(8,128)(2,1)S(1)}, bf16[64,1152]{1,0:T(8,128)(2,1)S(1)}, u32[]{:S(2)}, u32[]{:S(2)}) collective-permute-start(bf16[64,1152]{1,0:T(8,128)(2,1)S(1)} %get-tuple-element.16.refs_3_), channel_id=1, source_target_pairs={{0,7},{1,0},{2,1},{3,2},{4,3},{5,4},{6,5},{7,6},{8,15},{9,8},{10,9... | collective-permute-start | bytes 442376 | tf_op jit(solution)/shard_map/ppermute | solution.py:372
  35.6 6.8 %collective-permute-start.11 = (bf16[64,1152]{1,0:T(8,128)(2,1)S(1)}, bf16[64,1152]{1,0:T(8,128)(2,1)S(1)}, u32[]{:S(2)}, u32[]{:S(2)}) collective-permute-start(bf16[64,1152]{1,0:T(8,128)(2,1)S(1)} %get-tuple-element.17.refs_11_), channel_id=1, source_target_pairs={{0,1},{1,2},{2,3},{3,4},{4,5},{5,6},{6,7},{7,0},{8,9},{9,10},{10,1... | collective-permute-start | bytes 442376 | tf_op jit(solution)/shard_map/ppermute | solution.py:369
  38.1 7.2 %collective-permute-start.4 = (bf16[64,1152]{1,0:T(8,128)(2,1)S(1)}, bf16[64,1152]{1,0:T(8,128)(2,1)S(1)}, u32[]{:S(2)}, u32[]{:S(2)}) collective-permute-start(bf16[64,1152]{1,0:T(8,128)(2,1)S(1)} %collective-permute-done.3.refs_10_), channel_id=1, source_target_pairs={{0,1},{1,2},{2,3},{3,4},{4,5},{5,6},{6,7},{7,0},{8,9},{9,10},{10,1... | collective-permute-start | bytes 442376 | tf_op jit(solution)/shard_map/ppermute | solution.py:369
  38.1 7.2 %collective-permute-start.8 = (bf16[64,1152]{1,0:T(8,128)(2,1)S(1)}, bf16[64,1152]{1,0:T(8,128)(2,1)S(1)}, u32[]{:S(2)}, u32[]{:S(2)}) collective-permute-start(bf16[64,1152]{1,0:T(8,128)(2,1)S(1)} %collective-permute-done.7.refs_12_), channel_id=1, source_target_pairs={{0,7},{1,0},{2,1},{3,2},{4,3},{5,4},{6,5},{7,6},{8,15},{9,8},{10,9... | collective-permute-start | bytes 442376 | tf_op jit(solution)/shard_map/ppermute | solution.py:372
  40.8 7.2 %collective-permute-start.1 = (bf16[64,1152]{1,0:T(8,128)(2,1)S(1)}, bf16[64,1152]{1,0:T(8,128)(2,1)S(1)}, u32[]{:S(2)}, u32[]{:S(2)}) collective-permute-start(bf16[64,1152]{1,0:T(8,128)(2,1)S(1)} %collective-permute-done.refs_4_), channel_id=1, source_target_pairs={{0,7},{1,0},{2,1},{3,2},{4,3},{5,4},{6,5},{7,6},{8,15},{9,8},{10,9... | collective-permute-start | bytes 442376 | tf_op jit(solution)/shard_map/ppermute | solution.py:372
  42.4 6.5 %collective-permute-start.12 = (bf16[64,1152]{1,0:T(8,128)(2,1)S(1)}, bf16[64,1152]{1,0:T(8,128)(2,1)S(1)}, u32[]{:S(2)}, u32[]{:S(2)}) collective-permute-start(bf16[64,1152]{1,0:T(8,128)(2,1)S(1)} %collective-permute-done.11.refs_18_), channel_id=1, source_target_pairs={{0,1},{1,2},{2,3},{3,4},{4,5},{5,6},{6,7},{7,0},{8,9},{9,10},{10,1... | collective-permute-start | bytes 442376 | tf_op jit(solution)/shard_map/ppermute | solution.py:369
  45.4 5.4 %collective-permute-start.5 = (bf16[64,1152]{1,0:T(8,128)(2,1)S(1)}, bf16[64,1152]{1,0:T(8,128)(2,1)S(1)}, u32[]{:S(2)}, u32[]{:S(2)}) collective-permute-start(bf16[64,1152]{1,0:T(8,128)(2,1)S(1)} %collective-permute-done.4.refs_9_), channel_id=1, source_target_pairs={{0,1},{1,2},{2,3},{3,4},{4,5},{5,6},{6,7},{7,0},{8,9},{9,10},{10,1... | collective-permute-start | bytes 442376 | tf_op jit(solution)/shard_map/ppermute | solution.py:369
  45.4 6.4 %collective-permute-start.9 = (bf16[64,1152]{1,0:T(8,128)(2,1)S(1)}, bf16[64,1152]{1,0:T(8,128)(2,1)S(1)}, u32[]{:S(2)}, u32[]{:S(2)}) collective-permute-start(bf16[64,1152]{1,0:T(8,128)(2,1)S(1)} %collective-permute-done.8.refs_13_), channel_id=1, source_target_pairs={{0,7},{1,0},{2,1},{3,2},{4,3},{5,4},{6,5},{7,6},{8,15},{9,8},{10,9... | collective-permute-start | bytes 442376 | tf_op jit(solution)/shard_map/ppermute | solution.py:372
  48.1 7.2 %collective-permute-start.2 = (bf16[64,1152]{1,0:T(8,128)(2,1)S(1)}, bf16[64,1152]{1,0:T(8,128)(2,1)S(1)}, u32[]{:S(2)}, u32[]{:S(2)}) collective-permute-start(bf16[64,1152]{1,0:T(8,128)(2,1)S(1)} %collective-permute-done.1.refs_5_), channel_id=1, source_target_pairs={{0,7},{1,0},{2,1},{3,2},{4,3},{5,4},{6,5},{7,6},{8,15},{9,8},{10,9... | collective-permute-start | bytes 442376 | tf_op jit(solution)/shard_map/ppermute | solution.py:372
  48.9 7.1 %collective-permute-start.13 = (bf16[64,1152]{1,0:T(8,128)(2,1)S(1)}, bf16[64,1152]{1,0:T(8,128)(2,1)S(1)}, u32[]{:S(2)}, u32[]{:S(2)}) collective-permute-start(bf16[64,1152]{1,0:T(8,128)(2,1)S(1)} %collective-permute-done.12.refs_17_), channel_id=1, source_target_pairs={{0,1},{1,2},{2,3},{3,4},{4,5},{5,6},{6,7},{7,0},{8,9},{9,10},{10,1... | collective-permute-start | bytes 442376 | tf_op jit(solution)/shard_map/ppermute | solution.py:369
  50.8 7.5 %collective-permute-start.6 = (bf16[64,1152]{1,0:T(8,128)(2,1)S(1)}, bf16[64,1152]{1,0:T(8,128)(2,1)S(1)}, u32[]{:S(2)}, u32[]{:S(2)}) collective-permute-start(bf16[64,1152]{1,0:T(8,128)(2,1)S(1)} %collective-permute-done.5.refs_8_), channel_id=1, source_target_pairs={{0,1},{1,2},{2,3},{3,4},{4,5},{5,6},{6,7},{7,0},{8,9},{9,10},{10,1... | collective-permute-start | bytes 442376 | tf_op jit(solution)/shard_map/ppermute | solution.py:369
  51.7 6.6 %collective-permute-start.10 = (bf16[64,1152]{1,0:T(8,128)(2,1)S(1)}, bf16[64,1152]{1,0:T(8,128)(2,1)S(1)}, u32[]{:S(2)}, u32[]{:S(2)}) collective-permute-start(bf16[64,1152]{1,0:T(8,128)(2,1)S(1)} %collective-permute-done.9.refs_14_), channel_id=1, source_target_pairs={{0,7},{1,0},{2,1},{3,2},{4,3},{5,4},{6,5},{7,6},{8,15},{9,8},{10,9... | collective-permute-start | bytes 442376 | tf_op jit(solution)/shard_map/ppermute | solution.py:372
  63.3 65.2 %copy-start = (bf16[64,1152]{1,0:T(8,128)(2,1)S(1)}, bf16[64,1152]{1,0:T(8,128)(2,1)}, u32[]{:S(2)}) copy-start(bf16[64,1152]{1,0:T(8,128)(2,1)} %refs_2_.5) | copy-start | bytes 442372
Sparse Core Ops, SparseCore 0:
  31.5 67.5 all-gather.2
